TPU v7x, 32 devices: a whole 2x2x4 slice. The times are simulated.
32 devices in a mesh: shard: 8 (over y, x, core), rep: 4 (over z).
Axes of the slice: x: 2, y: 2, z: 4, core: 2. Of those that a mesh axis runs over, the one named last changes fastest.
Arguments:
- hidden_in: bfloat16 [32, 128, 2048], P(('shard', 'rep')), may hold values from -6 to 6
- segments: int32 [32, 128], P(('shard', 'rep')), may hold values from 0 to 3, never falling along the last dimension, each value on 1 to 64 neighbouring positions
- ln1_gain: bfloat16 [2, 2048], P(None, 'shard'), may hold values from 0.099609375 to 1.8984375
- ln1_bias: bfloat16 [2, 2048], P(None, 'shard'), may hold values from -4 to 4
- qkv_weight: bfloat16 [2, 2048, 6144], P(None, 'shard'), may hold values from -0.125 to 0.125
- qkv_bias: bfloat16 [2, 6144], P(None, 'shard'), may hold values from -6 to 6
- out_weight: bfloat16 [2, 2048, 2048], P(None, 'shard'), may hold values from -0.5 to 0.5
- ln2_gain: bfloat16 [2, 2048], P(None, 'shard'), may hold values from 0.099609375 to 1.8984375
- ln2_bias: bfloat16 [2, 2048], P(None, 'shard'), may hold values from -4 to 4
- gate_weight: bfloat16 [2, 2048, 5632], P(None, 'shard'), may hold values from -0.125 to 0.125
- up_weight: bfloat16 [2, 2048, 5632], P(None, 'shard'), may hold values from -0.125 to 0.125
- down_weight: bfloat16 [2, 5632, 2048], P(None, 'shard'), may hold values from -0.109375 to 0.109375
- cotangent: bfloat16 [32, 128, 2048], P(('shard', 'rep')), may hold values from -6 to 6
Outputs:
- block_out: bfloat16 [32, 128, 2048], P(('shard', 'rep'))
- input_grad: bfloat16 [32, 128, 2048], P(('shard', 'rep'))
- ln1_gain_grad: float32 [2, 2048], P(None, 'shard')
- ln1_bias_grad: float32 [2, 2048], P(None, 'shard')
- qkv_weight_grad: float32 [2, 2048, 6144], P(None, 'shard')
- qkv_bias_grad: float32 [2, 6144], P(None, 'shard')
- out_weight_grad: float32 [2, 2048, 2048], P(None, 'shard')
- ln2_gain_grad: float32 [2, 2048], P(None, 'shard')
- ln2_bias_grad: float32 [2, 2048], P(None, 'shard')
- gate_weight_grad: float32 [2, 2048, 5632], P(None, 'shard')
- up_weight_grad: float32 [2, 2048, 5632], P(None, 'shard')
- down_weight_grad: float32 [2, 5632, 2048], P(None, 'shard')
Inputs may be any that keep to these rules, and one draw needn't show every extreme that they name: `segments`: along each sequence the numbers never fall; each of the 4 documents holds one token or more and at most half of 128.
All inputs are finite; a program needn't handle non-finite values.
Results may differ from a plain program's by a relative error of at most 0.02.
Values may be sent and summed in bfloat16 or wider, within the bound.
No kernel may reach another device: no remote copies, remote signals or barrier semaphores. Data moves between devices by JAX's collectives and lax.ppermute only.
A program may use at most 512 MiB of HBM per device.

v0:
```python
import jax
import jax.numpy as jnp
from jax import lax
from jax.sharding import PartitionSpec as P

HEADS = 32
ROTARY = 16


norm_eps = 1e-05


def layer_norm(values, norm_gain, norm_shift):
    centred = values - jnp.mean(values, axis=-1, keepdims=True)
    variance = jnp.mean(centred * centred, axis=-1, keepdims=True)
    return centred * lax.rsqrt(variance + norm_eps) * norm_gain + norm_shift


def positions_and_mask(segments):
    length = segments.shape[-1]
    earlier = (segments[..., None, :] < segments[..., :, None]).astype(jnp.int32)
    starts = jnp.sum(earlier, axis=-1)
    places = jnp.arange(length, dtype=jnp.int32)
    positions = places - starts
    allowed = (segments[..., None, :] == segments[..., :, None]) & (
        places[None, :] <= places[:, None]
    )
    return (positions, allowed)


def rotary_tables(positions):
    half_dims = ROTARY // 2
    exponents = jnp.arange(half_dims, dtype=jnp.float32) * (2.0 / ROTARY)
    inverse = 10000.0 ** (-exponents)
    angles = positions.astype(jnp.float32)[..., None] * inverse
    return (jnp.cos(angles)[..., None, :], jnp.sin(angles)[..., None, :])


def rotate(heads_in, cosine, sine_table):
    half_dims = ROTARY // 2
    leading = heads_in[..., :half_dims]
    trailing = heads_in[..., half_dims:ROTARY]
    unturned = heads_in[..., ROTARY:]
    return jnp.concatenate(
        [
            leading * cosine - trailing * sine_table,
            trailing * cosine + leading * sine_table,
            unturned,
        ],
        axis=-1,
    )


def unrotate(heads_grad, cosine, sine_table):
    half_dims = ROTARY // 2
    leading = heads_grad[..., :half_dims]
    trailing = heads_grad[..., half_dims:ROTARY]
    unturned = heads_grad[..., ROTARY:]
    return jnp.concatenate(
        [
            leading * cosine + trailing * sine_table,
            trailing * cosine - leading * sine_table,
            unturned,
        ],
        axis=-1,
    )


def swiglu(gate, upper):
    return jax.nn.silu(gate) * upper


def fetch_attention_again(ln1_gain, ln1_bias, qkv_weight, qkv_bias, out_weight, layer):
    return (
        lax.all_gather(ln1_gain[layer], "shard", axis=0, tiled=True),
        lax.all_gather(ln1_bias[layer], "shard", axis=0, tiled=True),
        lax.all_gather(qkv_weight[layer], "shard", axis=0, tiled=True),
        lax.all_gather(qkv_bias[layer], "shard", axis=0, tiled=True),
        lax.all_gather(out_weight[layer], "shard", axis=0, tiled=True),
    )


def fetch_mlp_again(ln2_gain, ln2_bias, gate_weight, up_weight, down_weight, layer):
    return (
        lax.all_gather(ln2_gain[layer], "shard", axis=0, tiled=True),
        lax.all_gather(ln2_bias[layer], "shard", axis=0, tiled=True),
        lax.all_gather(gate_weight[layer], "shard", axis=0, tiled=True),
        lax.all_gather(up_weight[layer], "shard", axis=0, tiled=True),
        lax.all_gather(down_weight[layer], "shard", axis=0, tiled=True),
    )


def sum_replicas(shards):
    return (
        lax.psum(shards[0].astype(jnp.bfloat16), "rep").astype(jnp.float32),
        lax.psum(shards[1].astype(jnp.bfloat16), "rep").astype(jnp.float32),
        lax.psum(shards[2].astype(jnp.bfloat16), "rep").astype(jnp.float32),
        lax.psum(shards[3].astype(jnp.bfloat16), "rep").astype(jnp.float32),
        lax.psum(shards[4].astype(jnp.bfloat16), "rep").astype(jnp.float32),
    )


def local(
    hidden_in,
    segments,
    ln1_gain,
    ln1_bias,
    qkv_weight,
    qkv_bias,
    out_weight,
    ln2_gain,
    ln2_bias,
    gate_weight,
    up_weight,
    down_weight,
    cotangent,
):
    layers = qkv_weight.shape[0]
    width = hidden_in.shape[2]
    head_size = width // HEADS
    scale = head_size ** (-0.5)
    bias_rows = qkv_bias.shape[1]
    positions, allowed = positions_and_mask(segments[0])
    cosine, sine_table = rotary_tables(positions)
    state = hidden_in[0].astype(jnp.float32)
    tokens = state.shape[0]
    kept_attention = []
    kept_mlp = []
    saved = []
    for layer in range(layers):
        attn_full = (
            lax.all_gather(ln1_gain[layer], "shard", axis=0, tiled=True),
            lax.all_gather(ln1_bias[layer], "shard", axis=0, tiled=True),
            lax.all_gather(qkv_weight[layer], "shard", axis=0, tiled=True),
            lax.all_gather(qkv_bias[layer], "shard", axis=0, tiled=True),
            lax.all_gather(out_weight[layer], "shard", axis=0, tiled=True),
        )
        kept_attention.append(attn_full)
        norm_gain, norm_shift, proj_in, proj_bias, proj_out = attn_full
        normed, norm_pull = jax.vjp(
            layer_norm, state, norm_gain.astype(jnp.float32), norm_shift.astype(jnp.float32)
        )
        normed_low = normed.astype(jnp.bfloat16)
        joined = jnp.dot(
            normed_low, proj_in, preferred_element_type=jnp.float32
        ) + proj_bias.astype(jnp.float32)
        split = joined.reshape(tokens, 3, HEADS, head_size)
        query_low = rotate(split[:, 0], cosine, sine_table).astype(jnp.bfloat16)
        key_low = rotate(split[:, 1], cosine, sine_table).astype(jnp.bfloat16)
        value_low = split[:, 2].astype(jnp.bfloat16)
        scores = (
            jnp.einsum("qhd,khd->hqk", query_low, key_low, preferred_element_type=jnp.float32)
            * scale
        )
        masked = jnp.where(allowed[None], scores, -1000000000.0)
        peak_score = jnp.max(masked, axis=-1, keepdims=True)
        weights_exp = jnp.exp(masked - peak_score)
        row_total = jnp.sum(weights_exp, axis=-1, keepdims=True)
        probs_low = (weights_exp / row_total).astype(jnp.bfloat16)
        log_total = peak_score + jnp.log(row_total)
        mixed_low = (
            jnp.einsum("hqk,khd->qhd", probs_low, value_low, preferred_element_type=jnp.float32)
            .astype(jnp.bfloat16)
            .reshape(tokens, width)
        )
        state_mid = state + jnp.dot(mixed_low, proj_out, preferred_element_type=jnp.float32)
        mlp_full = (
            lax.all_gather(ln2_gain[layer], "shard", axis=0, tiled=True),
            lax.all_gather(ln2_bias[layer], "shard", axis=0, tiled=True),
            lax.all_gather(gate_weight[layer], "shard", axis=0, tiled=True),
            lax.all_gather(up_weight[layer], "shard", axis=0, tiled=True),
            lax.all_gather(down_weight[layer], "shard", axis=0, tiled=True),
        )
        kept_mlp.append(mlp_full)
        second_gain, second_shift, weight_gate, weight_up, weight_down = mlp_full
        normed_two, norm_two_pull = jax.vjp(
            layer_norm, state_mid, second_gain.astype(jnp.float32), second_shift.astype(jnp.float32)
        )
        normed_two_low = normed_two.astype(jnp.bfloat16)
        gate = jnp.dot(normed_two_low, weight_gate, preferred_element_type=jnp.float32)
        upper = jnp.dot(normed_two_low, weight_up, preferred_element_type=jnp.float32)
        inner, act_pull = jax.vjp(swiglu, gate, upper)
        inner_low = inner.astype(jnp.bfloat16)
        state = state_mid + jnp.dot(inner_low, weight_down, preferred_element_type=jnp.float32)
        saved.append(
            (
                norm_pull,
                normed_low,
                query_low,
                key_low,
                value_low,
                log_total,
                mixed_low,
                norm_two_pull,
                normed_two_low,
                act_pull,
                inner_low,
            )
        )
    block_out = state.astype(jnp.bfloat16)[None]
    grad_state = cotangent[0].astype(jnp.float32)
    attention_parts = [None] * layers
    mlp_parts = [None] * layers
    for layer in reversed(range(layers)):
        (
            norm_pull,
            normed_low,
            query_low,
            key_low,
            value_low,
            log_total,
            mixed_low,
            norm_two_pull,
            normed_two_low,
            act_pull,
            inner_low,
        ) = saved[layer]
        mlp_full = (
            kept_mlp[layer]
            if layer == layers - 1
            else fetch_mlp_again(ln2_gain, ln2_bias, gate_weight, up_weight, down_weight, layer)
        )
        second_gain, second_shift, weight_gate, weight_up, weight_down = mlp_full
        down_in = grad_state.astype(jnp.bfloat16)
        grad_inner = jnp.einsum(
            "td,fd->tf", down_in, weight_down, preferred_element_type=jnp.float32
        )
        grad_gate, grad_up = act_pull(grad_inner)
        gate_low = grad_gate.astype(jnp.bfloat16)
        up_low = grad_up.astype(jnp.bfloat16)
        grad_normed_two = jnp.einsum(
            "tf,df->td", gate_low, weight_gate, preferred_element_type=jnp.float32
        ) + jnp.einsum("tf,df->td", up_low, weight_up, preferred_element_type=jnp.float32)
        grad_mid_norm, grad_second_gain, grad_second_shift = norm_two_pull(grad_normed_two)
        grad_state = grad_state + grad_mid_norm
        owned_gain, owned_shift = (
            lax.psum_scatter(grad_second_gain, "shard", scatter_dimension=0, tiled=True),
            lax.psum_scatter(grad_second_shift, "shard", scatter_dimension=0, tiled=True),
        )
        all_down, all_gate, all_up = (
            lax.all_gather(down_in, "shard", axis=0, tiled=True),
            lax.all_gather(gate_low, "shard", axis=0, tiled=True),
            lax.all_gather(up_low, "shard", axis=0, tiled=True),
        )
        column_normed, column_inner = (
            lax.all_to_all(normed_two_low, "shard", split_axis=1, concat_axis=0, tiled=True),
            lax.all_to_all(inner_low, "shard", split_axis=1, concat_axis=0, tiled=True),
        )
        owned_gate = jnp.einsum(
            "td,tf->df", column_normed, all_gate, preferred_element_type=jnp.float32
        )
        owned_up = jnp.einsum(
            "td,tf->df", column_normed, all_up, preferred_element_type=jnp.float32
        )
        owned_down = jnp.einsum(
            "tf,td->fd", column_inner, all_down, preferred_element_type=jnp.float32
        )
        mlp_shards = (owned_gain, owned_shift, owned_gate, owned_up, owned_down)
        mlp_shards = sum_replicas(mlp_shards)
        mlp_parts[layer] = mlp_shards
        attn_full = (
            kept_attention[layer]
            if layer == layers - 1
            else fetch_attention_again(ln1_gain, ln1_bias, qkv_weight, qkv_bias, out_weight, layer)
        )
        norm_gain, norm_shift, proj_in, proj_bias, proj_out = attn_full
        branch_low = grad_state.astype(jnp.bfloat16)
        grad_mixed = (
            jnp.einsum("te,de->td", branch_low, proj_out, preferred_element_type=jnp.float32)
            .astype(jnp.bfloat16)
            .reshape(tokens, HEADS, head_size)
        )
        scores = (
            jnp.einsum("qhd,khd->hqk", query_low, key_low, preferred_element_type=jnp.float32)
            * scale
        )
        probs = jnp.where(allowed[None], jnp.exp(scores - log_total), 0.0)
        probs_low = probs.astype(jnp.bfloat16)
        grad_probs = jnp.einsum(
            "qhd,khd->hqk", grad_mixed, value_low, preferred_element_type=jnp.float32
        )
        grad_value = jnp.einsum(
            "hqk,qhd->khd", probs_low, grad_mixed, preferred_element_type=jnp.float32
        )
        inner_sum = jnp.sum(probs * grad_probs, axis=-1, keepdims=True)
        grad_scores = (probs * (grad_probs - inner_sum)).astype(jnp.bfloat16)
        grad_query = (
            jnp.einsum("hqk,khd->qhd", grad_scores, key_low, preferred_element_type=jnp.float32)
            * scale
        )
        grad_key = (
            jnp.einsum("hqk,qhd->khd", grad_scores, query_low, preferred_element_type=jnp.float32)
            * scale
        )
        grad_query = unrotate(grad_query, cosine, sine_table)
        grad_key = unrotate(grad_key, cosine, sine_table)
        grad_joined = jnp.concatenate(
            [
                grad_query.reshape(tokens, width),
                grad_key.reshape(tokens, width),
                grad_value.reshape(tokens, width),
            ],
            axis=1,
        ).astype(jnp.bfloat16)
        grad_normed = jnp.einsum(
            "te,de->td", grad_joined, proj_in, preferred_element_type=jnp.float32
        )
        grad_before, grad_first_gain, grad_first_shift = norm_pull(grad_normed)
        grad_state = grad_state + grad_before
        owned_gain, owned_shift = (
            lax.psum_scatter(grad_first_gain, "shard", scatter_dimension=0, tiled=True),
            lax.psum_scatter(grad_first_shift, "shard", scatter_dimension=0, tiled=True),
        )
        all_joined, all_branch = (
            lax.all_gather(grad_joined, "shard", axis=0, tiled=True),
            lax.all_gather(branch_low, "shard", axis=0, tiled=True),
        )
        column_normed, column_mixed = (
            lax.all_to_all(normed_low, "shard", split_axis=1, concat_axis=0, tiled=True),
            lax.all_to_all(mixed_low, "shard", split_axis=1, concat_axis=0, tiled=True),
        )
        owned_in = jnp.einsum(
            "td,te->de", column_normed, all_joined, preferred_element_type=jnp.float32
        )
        owned_out = jnp.einsum(
            "td,te->de", column_mixed, all_branch, preferred_element_type=jnp.float32
        )
        column_total = jnp.sum(all_joined.astype(jnp.float32), axis=0)
        owned_bias = lax.dynamic_slice_in_dim(
            column_total, lax.axis_index("shard") * bias_rows, bias_rows, 0
        )
        attention_shards = (owned_gain, owned_shift, owned_in, owned_bias, owned_out)
        attention_shards = sum_replicas(attention_shards)
        attention_parts[layer] = attention_shards
    stacked = [
        jnp.stack([attention_parts[layer][index] for layer in range(layers)]) for index in range(5)
    ]
    stacked = stacked + [
        jnp.stack([mlp_parts[layer][index] for layer in range(layers)]) for index in range(5)
    ]
    input_grad = grad_state.astype(jnp.bfloat16)[None]
    return (
        block_out,
        input_grad,
        stacked[0],
        stacked[1],
        stacked[2],
        stacked[3],
        stacked[4],
        stacked[5],
        stacked[6],
        stacked[7],
        stacked[8],
        stacked[9],
    )


def solution(mesh):
    in_specs = (
        P(("shard", "rep"), None, None),
        P(("shard", "rep"), None),
        P(None, "shard"),
        P(None, "shard"),
        P(None, "shard", None),
        P(None, "shard"),
        P(None, "shard", None),
        P(None, "shard"),
        P(None, "shard"),
        P(None, "shard", None),
        P(None, "shard", None),
        P(None, "shard", None),
        P(("shard", "rep"), None, None),
    )
    out_specs = (
        P(("shard", "rep"), None, None),
        P(("shard", "rep"), None, None),
        P(None, "shard"),
        P(None, "shard"),
        P(None, "shard", None),
        P(None, "shard"),
        P(None, "shard", None),
        P(None, "shard"),
        P(None, "shard"),
        P(None, "shard", None),
        P(None, "shard", None),
        P(None, "shard", None),
    )
    return jax.shard_map(local, mesh=mesh, in_specs=in_specs, out_specs=out_specs, check_vma=False)
```

profile of v0, /device:TPU:0, one launch (start us, length us, event | category | flops | bytes accessed | tf_op | source)
XLA Modules:
  0.0 2668.8 jit_solution(4218134554305357537)
XLA Ops:
  7.2 6.2 fusion.173
  13.5 6.3 fusion.172
  23.0 7.0 fusion.174
  41.3 9.9 all-gather
  51.3 8.9 all-gather.1
  60.2 8.1 all-gather.3
  68.3 8.9 all-gather.5
  77.2 7.9 all-gather.6
  85.2 8.9 all-gather.10
  94.1 7.9 all-gather.11
  102.1 9.1 all-gather.13
  111.2 7.9 all-gather.15
  119.7 9.2 all-gather.16
  133.1 13.8 fusion.8
  146.8 114.1 %all-gather.60.cloned.1.call-done = bf16[1,2048,6144]{2,1,0:T(8,128)(2,1)} async-done(((bf16[1,256,6144]{2,1,0:T(8,128)(2,1)}), bf16[1,2048,6144]{2,1,0:T(8,128)(2,1)}) %all-gather.60.cloned.1.call-update) | async-done | bytes 25165840 | tf_op jit(solution)/shard_map/all_gather | solution.py:134
  260.9 13.4 fusion.46
  284.1 33.1 %all-gather.62.cloned.1.call-done = bf16[1,2048,2048]{2,1,0:T(8,128)(2,1)} async-done(((bf16[1,256,2048]{2,1,0:T(8,128)(2,1)}), bf16[1,2048,2048]{2,1,0:T(8,128)(2,1)}) %all-gather.62.cloned.1.call-update) | async-done | bytes 8388624 | tf_op jit(solution)/shard_map/all_gather | solution.py:136
  322.5 113.5 %all-gather.64.cloned.1.call-done = bf16[1,2048,5632]{2,1,0:T(8,128)(2,1)} async-done(((bf16[1,256,5632]{2,1,0:T(8,128)(2,1)}), bf16[1,2048,5632]{2,1,0:T(8,128)(2,1)}) %all-gather.64.cloned.1.call-update) | async-done | bytes 23068688 | tf_op jit(solution)/shard_map/all_gather | solution.py:170
  436.0 12.3 fusion.30
  448.3 105.9 %all-gather.66.cloned.1.call-done = bf16[1,2048,5632]{2,1,0:T(8,128)(2,1)} async-done(((bf16[1,256,5632]{2,1,0:T(8,128)(2,1)}), bf16[1,2048,5632]{2,1,0:T(8,128)(2,1)}) %all-gather.66.cloned.1.call-update) | async-done | bytes 23068688 | tf_op jit(solution)/shard_map/all_gather | solution.py:171
  554.2 14.7 multiply_convert_fusion.3
  569.0 103.5 %all-gather.68.cloned.1.call-done = bf16[1,5632,2048]{2,1,0:T(8,128)(2,1)} async-done(((bf16[1,704,2048]{2,1,0:T(8,128)(2,1)}), bf16[1,5632,2048]{2,1,0:T(8,128)(2,1)}) %all-gather.68.cloned.1.call-update) | async-done | bytes 23068688 | tf_op jit(solution)/shard_map/all_gather | solution.py:172
  672.5 10.0 fusion.183
  683.1 117.2 %all-gather.70.cloned.1.call-done = bf16[1,2048,6144]{2,1,0:T(8,128)(2,1)} async-done(((bf16[1,256,6144]{2,1,0:T(8,128)(2,1)}), bf16[1,2048,6144]{2,1,0:T(8,128)(2,1)}) %all-gather.70.cloned.1.call-update) | async-done | bytes 25165840 | tf_op jit(solution)/shard_map/all_gather | solution.py:134
  800.3 13.2 fusion.49
  824.3 32.3 %all-gather.72.cloned.1.call-done = bf16[1,2048,2048]{2,1,0:T(8,128)(2,1)} async-done(((bf16[1,256,2048]{2,1,0:T(8,128)(2,1)}), bf16[1,2048,2048]{2,1,0:T(8,128)(2,1)}) %all-gather.72.cloned.1.call-update) | async-done | bytes 8388624 | tf_op jit(solution)/shard_map/all_gather | solution.py:136
  864.0 110.9 %all-gather.76.cloned.1.call-done = bf16[1,2048,5632]{2,1,0:T(8,128)(2,1)} async-done(((bf16[1,256,5632]{2,1,0:T(8,128)(2,1)}), bf16[1,2048,5632]{2,1,0:T(8,128)(2,1)}) %all-gather.76.cloned.1.call-update) | async-done | bytes 23068688 | tf_op jit(solution)/shard_map/all_gather | solution.py:171
  975.0 12.5 fusion.14
  987.5 106.3 %all-gather.74.cloned.1.call-done = bf16[1,2048,5632]{2,1,0:T(8,128)(2,1)} async-done(((bf16[1,256,5632]{2,1,0:T(8,128)(2,1)}), bf16[1,2048,5632]{2,1,0:T(8,128)(2,1)}) %all-gather.74.cloned.1.call-update) | async-done | bytes 23068688 | tf_op jit(solution)/shard_map/all_gather | solution.py:170
  1093.8 15.7 fusion.63
  1109.5 13.3 fusion.12
  1122.8 15.7 multiply_reduce_fusion.2
  1140.1 6.5 fusion.92
  1156.0 14.9 multiply_reduce_fusion.4
  1174.7 15.0 fusion.66
  1189.7 13.5 fusion.24
  1203.2 16.0 multiply_reduce_fusion.3
  1224.3 6.4 fusion.89
  1249.6 8.2 all-to-all-done.3
  1263.7 21.1 all-to-all-done.7
  1294.4 7.3 fusion.58
  1301.7 8.5 all-to-all-done.6
  1314.1 7.4 fusion.57
  1321.5 8.2 all-to-all-done.2
  1346.5 35.3 %all-gather.56.cloned.1.call-done = bf16[1024,5632]{1,0:T(8,128)(2,1)} async-done(((bf16[128,5632]{1,0:T(8,128)(2,1)}), bf16[1024,5632]{1,0:T(8,128)(2,1)}) %all-gather.56.cloned.1.call-update) | async-done | bytes 11534352 | tf_op jit(solution)/shard_map/all_gather | solution.py:243
  1381.7 8.8 fusion.45
  1390.5 61.2 %all-gather.52.cloned.1.call-done = bf16[1024,5632]{1,0:T(8,128)(2,1)} async-done(((bf16[128,5632]{1,0:T(8,128)(2,1)}), bf16[1024,5632]{1,0:T(8,128)(2,1)}) %all-gather.52.cloned.1.call-update) | async-done | bytes 11534352 | tf_op jit(solution)/shard_map/all_gather | solution.py:242
  1451.8 8.8 fusion.43
  1464.1 62.8 %all-gather.50.cloned.1.call-done = bf16[1024,5632]{1,0:T(8,128)(2,1)} async-done(((bf16[128,5632]{1,0:T(8,128)(2,1)}), bf16[1024,5632]{1,0:T(8,128)(2,1)}) %all-gather.50.cloned.1.call-update) | async-done | bytes 11534352 | tf_op jit(solution)/shard_map/all_gather | solution.py:242
  1526.9 8.8 fusion.42
  1535.7 60.6 %all-gather.54.cloned.1.call-done = bf16[1024,5632]{1,0:T(8,128)(2,1)} async-done(((bf16[128,5632]{1,0:T(8,128)(2,1)}), bf16[1024,5632]{1,0:T(8,128)(2,1)}) %all-gather.54.cloned.1.call-update) | async-done | bytes 11534352 | tf_op jit(solution)/shard_map/all_gather | solution.py:243
  1596.3 8.9 fusion.44
  1609.0 70.0 %all-gather.42.cloned.1.call-done = bf16[1024,6144]{0,1:T(8,128)(2,1)} async-done(((bf16[128,6144]{0,1:T(8,128)(2,1)}), bf16[1024,6144]{0,1:T(8,128)(2,1)}) %all-gather.42.cloned.1.call-update) | async-done | bytes 12582928 | tf_op jit(solution)/shard_map/all_gather | solution.py:315
  1679.0 14.2 fusion.40
  1693.2 62.6 %all-gather.44.cloned.1.call-done = bf16[1024,6144]{0,1:T(8,128)(2,1)} async-done(((bf16[128,6144]{0,1:T(8,128)(2,1)}), bf16[1024,6144]{0,1:T(8,128)(2,1)}) %all-gather.44.cloned.1.call-update) | async-done | bytes 12582928 | tf_op jit(solution)/shard_map/all_gather | solution.py:315
  1755.8 14.2 fusion.41
  1772.1 22.0 fusion.167
  1796.0 24.9 all-reduce.8
  1824.4 11.8 fusion.98
  1836.1 6.4 convert_reduce_fusion.1
  1842.7 6.4 convert_reduce_fusion
  1849.2 20.6 all-reduce.9
  1872.7 760.1 %all-reduce.13.cloned.1.call-done = (bf16[1,256,6144]{2,1,0:T(8,128)(2,1)}, bf16[1,256,6144]{2,1,0:T(8,128)(2,1)}, bf16[1,256,2048]{2,1,0:T(8,128)(2,1)}, bf16[1...) async-done(((bf16[1,256,6144]{2,1,0:T(8,128)(2,1)}, ...) | async-done | bytes 25690128 | tf_op jit(solution)/shard_map/psum | solution.py:97
  2632.8 8.0 maximum_convert_fusion.3
  (473 shorter events, 164.6 us)
Async XLA Ops:
  7.2 125.9 %all-gather.78.cloned.1.call-start = ((), (), s32[]{:S(2)}) async-start(), calls=%async_computation.26 | async-start | bytes 25952256 | tf_op jit(solution)/shard_map/all_gather | solution.py:172
  13.5 247.4 %all-gather.60.cloned.1.call-start = ((), (), s32[]{:S(2)}) async-start(), calls=%async_computation.17 | async-start | bytes 28311552 | tf_op jit(solution)/shard_map/all_gather | solution.py:134
  19.9 297.3 %all-gather.62.cloned.1.call-start = ((), (), s32[]{:S(2)}) async-start(), calls=%async_computation.18 | async-start | bytes 9437184 | tf_op jit(solution)/shard_map/all_gather | solution.py:136
  23.0 413.0 %all-gather.64.cloned.1.call-start = ((), (), s32[]{:S(2)}) async-start(), calls=%async_computation.19 | async-start | bytes 25952256 | tf_op jit(solution)/shard_map/all_gather | solution.py:170
  30.0 524.2 %all-gather.66.cloned.1.call-start = ((), (), s32[]{:S(2)}) async-start(), calls=%async_computation.20 | async-start | bytes 25952256 | tf_op jit(solution)/shard_map/all_gather | solution.py:171
  35.7 636.7 %all-gather.68.cloned.1.call-start = ((), (), s32[]{:S(2)}) async-start(), calls=%async_computation.21 | async-start | bytes 25952256 | tf_op jit(solution)/shard_map/all_gather | solution.py:172
  36.3 764.0 %all-gather.70.cloned.1.call-start = ((), (), s32[]{:S(2)}) async-start(), calls=%async_computation.22 | async-start | bytes 28311552 | tf_op jit(solution)/shard_map/all_gather | solution.py:134
  37.1 819.5 %all-gather.72.cloned.1.call-start = ((), (), s32[]{:S(2)}) async-start(), calls=%async_computation.23 | async-start | bytes 9437184 | tf_op jit(solution)/shard_map/all_gather | solution.py:136
  37.8 937.2 %all-gather.76.cloned.1.call-start = ((), (), s32[]{:S(2)}) async-start(), calls=%async_computation.25 | async-start | bytes 25952256 | tf_op jit(solution)/shard_map/all_gather | solution.py:171
  38.6 29.7 %copy-start.118 = (bf16[2,256]{1,0:T(2,128)(2,1)S(1)}, bf16[2,256]{1,0:T(2,128)(2,1)}, u32[]{:S(2)}) copy-start(bf16[2,256]{1,0:T(2,128)(2,1)} %param.20) | copy-start | bytes 3076
  38.6 38.6 %copy-start.119 = (bf16[2,256]{1,0:T(2,128)(2,1)S(1)}, bf16[2,256]{1,0:T(2,128)(2,1)}, u32[]{:S(2)}) copy-start(bf16[2,256]{1,0:T(2,128)(2,1)} %param.21) | copy-start | bytes 3076
  38.6 94.5 %copy-start.9 = (bf16[1,128,2048]{2,1,0:T(8,128)(2,1)S(1)}, bf16[1,128,2048]{2,1,0:T(8,128)(2,1)}, u32[]{:S(2)}) copy-start(bf16[1,128,2048]{2,1,0:T(8,128)(2,1)} %param.25) | copy-start | bytes 1572868
  38.6 1055.2 %all-gather.74.cloned.1.call-start = ((), (), s32[]{:S(2)}) async-start(), calls=%async_computation.24 | async-start | bytes 25952256 | tf_op jit(solution)/shard_map/all_gather | solution.py:170
  39.2 1255.2 %all-gather.80.cloned.1.call-start = ((), (), s32[]{:S(2)}) async-start(), calls=%async_computation.27 | async-start | bytes 4718592 | tf_op jit(solution)/shard_map/all_gather | solution.py:241
  39.9 1274.2 %all-gather.58.cloned.1.call-start = ((), (), s32[]{:S(2)}) async-start(), calls=%async_computation.16 | async-start | bytes 4718592 | tf_op jit(solution)/shard_map/all_gather | solution.py:241
  40.4 220.5 %copy-start.99 = (f32[128]{0:T(128)}, f32[128]{0:T(128)S(1)}, u32[]{:S(2)}) copy-start(f32[128]{0:T(128)S(1)} %broadcast_multiply_fusion.3) | copy-start | bytes 1540
  41.2 219.6 %copy-start.101 = (f32[128]{0:T(128)}, f32[128]{0:T(128)S(1)}, u32[]{:S(2)}) copy-start(f32[128]{0:T(128)S(1)} %fusion.148) | copy-start | bytes 1540
  51.2 77.7 %copy-start.86 = (bf16[1,2048]{1,0:T(2,128)(2,1)}, bf16[1,2048]{1,0:T(2,128)(2,1)S(1)}, u32[]{:S(2)}) copy-start(bf16[1,2048]{1,0:T(2,128)(2,1)S(1)} %all-gather) | copy-start | bytes 12292
  51.2 209.6 %copy-start.70 = (f32[1,2048]{1,0:T(1,128)}, f32[1,2048]{1,0:T(1,128)S(1)}, u32[]{:S(2)}) copy-start(f32[1,2048]{1,0:T(1,128)S(1)} %convert_element_type.310) | copy-start | bytes 24580
  60.1 25.1 copy-start.88
  77.2 245.0 %copy-start.72 = (f32[1,2048]{1,0:T(1,128)}, f32[1,2048]{1,0:T(1,128)S(1)}, u32[]{:S(2)}) copy-start(f32[1,2048]{1,0:T(1,128)S(1)} %convert_element_type.313) | copy-start | bytes 24580
  94.1 588.7 %copy-start.84 = (f32[1,2048]{1,0:T(1,128)}, f32[1,2048]{1,0:T(1,128)S(1)}, u32[]{:S(2)}) copy-start(f32[1,2048]{1,0:T(1,128)S(1)} %convert_element_type.315) | copy-start | bytes 24580
  129.6 150.5 %copy-start.76 = (f32[128,8]{0,1:T(8,128)}, f32[128,8]{0,1:T(8,128)S(1)}, u32[]{:S(2)}) copy-start(f32[128,8]{0,1:T(8,128)S(1)} %get-tuple-element.114) | copy-start | bytes 12292
  129.6 150.5 %copy-start.80 = (f32[128,8]{0,1:T(8,128)}, f32[128,8]{0,1:T(8,128)S(1)}, u32[]{:S(2)}) copy-start(f32[128,8]{0,1:T(8,128)S(1)} %get-tuple-element.115) | copy-start | bytes 12292
  284.1 37.8 %copy-start.27 = (bf16[32,64,128]{2,1,0:T(8,128)(2,1)}, bf16[32,64,128]{2,1,0:T(8,128)(2,1)S(1)}, u32[]{:S(2)}) copy-start(bf16[32,64,128]{2,1,0:T(8,128)(2,1)S(1)} %convolution_convert_fusion.12) | copy-start | bytes 1572868
  321.9 126.4 %copy-start.106 = (f32[128]{0:T(128)}, f32[128]{0:T(128)S(1)}, u32[]{:S(2)}) copy-start(f32[128]{0:T(128)S(1)} %broadcast_multiply_fusion.2) | copy-start | bytes 1540
  322.2 126.1 %copy-start.127 = (f32[128]{0:T(128)}, f32[128]{0:T(128)S(1)}, u32[]{:S(2)}) copy-start(f32[128]{0:T(128)S(1)} %multiply_reduce_fusion.12) | copy-start | bytes 1540
  322.2 126.1 %copy-start.112 = (f32[128]{0:T(128)}, f32[128]{0:T(128)S(1)}, u32[]{:S(2)}) copy-start(f32[128]{0:T(128)S(1)} %fusion.149) | copy-start | bytes 1540
  322.5 231.7 %copy-start.20 = (bf16[128,2048]{1,0:T(8,128)(2,1)}, bf16[128,2048]{1,0:T(8,128)(2,1)S(1)}, u32[]{:S(2)}) copy-start(bf16[128,2048]{1,0:T(8,128)(2,1)S(1)} %add_convert_fusion.3) | copy-start | bytes 1572868
  682.5 131.0 %copy-start.110 = (f32[128]{0:T(128)}, f32[128]{0:T(128)S(1)}, u32[]{:S(2)}) copy-start(f32[128]{0:T(128)S(1)} %broadcast_multiply_fusion.1) | copy-start | bytes 1540
  682.8 130.8 %copy-start.129 = (f32[128]{0:T(128)}, f32[128]{0:T(128)S(1)}, u32[]{:S(2)}) copy-start(f32[128]{0:T(128)S(1)} %multiply_reduce_fusion.11) | copy-start | bytes 1540
  682.8 130.7 %copy-start.125 = (f32[128]{0:T(128)}, f32[128]{0:T(128)S(1)}, u32[]{:S(2)}) copy-start(f32[128]{0:T(128)S(1)} %fusion.150) | copy-start | bytes 1540
  683.1 130.5 %copy-start.22 = (bf16[128,2048]{1,0:T(8,128)(2,1)}, bf16[128,2048]{1,0:T(8,128)(2,1)S(1)}, u32[]{:S(2)}) copy-start(bf16[128,2048]{1,0:T(8,128)(2,1)S(1)} %add_convert_fusion.2) | copy-start | bytes 1572868
  861.5 277.0 %copy-start = (f32[128,2048]{1,0:T(8,128)}, f32[128,2048]{1,0:T(8,128)S(1)}, u32[]{:S(2)}) copy-start(f32[128,2048]{1,0:T(8,128)S(1)} %get-tuple-element.127) | copy-start | bytes 3145732
  1173.9 45.8 %copy-start.14 = (f32[128,2048]{1,0:T(8,128)}, f32[128,2048]{1,0:T(8,128)S(1)}, u32[]{:S(2)}) copy-start(f32[128,2048]{1,0:T(8,128)S(1)} %get-tuple-element.56) | copy-start | bytes 3145732
  1173.9 159.3 %all-gather.48.cloned.1.call-start = ((), (), s32[]{:S(2)}) async-start(), calls=%async_computation.11 | async-start | bytes 4718592 | tf_op jit(solution)/shard_map/all_gather | solution.py:316
  1174.6 163.2 %all-gather.46.cloned.1.call-start = ((), (), s32[]{:S(2)}) async-start(), calls=%async_computation.10 | async-start | bytes 4718592 | tf_op jit(solution)/shard_map/all_gather | solution.py:316
  1221.7 160.0 %all-gather.56.cloned.1.call-start = ((), (), s32[]{:S(2)}) async-start(), calls=%async_computation.15 | async-start | bytes 12976128 | tf_op jit(solution)/shard_map/all_gather | solution.py:243
  1222.3 229.5 %all-gather.52.cloned.1.call-start = ((), (), s32[]{:S(2)}) async-start(), calls=%async_computation.13 | async-start | bytes 12976128 | tf_op jit(solution)/shard_map/all_gather | solution.py:242
  1222.9 304.0 %all-gather.50.cloned.1.call-start = ((), (), s32[]{:S(2)}) async-start(), calls=%async_computation.12 | async-start | bytes 12976128 | tf_op jit(solution)/shard_map/all_gather | solution.py:242
  1223.5 372.8 %all-gather.54.cloned.1.call-start = ((), (), s32[]{:S(2)}) async-start(), calls=%async_computation.14 | async-start | bytes 12976128 | tf_op jit(solution)/shard_map/all_gather | solution.py:243
  1224.1 454.9 %all-gather.42.cloned.1.call-start = ((), (), s32[]{:S(2)}) async-start(), calls=%async_computation.8 | async-start | bytes 14155776 | tf_op jit(solution)/shard_map/all_gather | solution.py:315
  1240.1 515.7 %all-gather.44.cloned.1.call-start = ((), (), s32[]{:S(2)}) async-start(), calls=%async_computation.9 | async-start | bytes 14155776 | tf_op jit(solution)/shard_map/all_gather | solution.py:315
  1243.9 13.9 all-to-all-start.3
  1257.8 27.0 %all-to-all-start.7 = ((bf16[128,8,704]{0,2,1:T(8,128)(2,1)}), bf16[128,8,704]{0,2,1:T(8,128)(2,1)}, u32[]{:S(2)}, u32[]{:S(2)}) async-start(bf16[128,8,704]{0,2,1:T(8,128)(2,1)} %bitcast.314), calls=%async_computation.7 | async-start | bytes 2883584 | tf_op jit(solution)/shard_map/all_to_all | solution.py:247
  1262.1 27.1 %copy-start.89 = (bf16[1,2048]{1,0:T(2,128)(2,1)S(1)}, bf16[1,2048]{1,0:T(2,128)(2,1)}, u32[]{:S(2)}) copy-start(bf16[1,2048]{1,0:T(2,128)(2,1)} %copy-done.88) | copy-start | bytes 12292
  1262.2 27.2 %copy-start.87 = (bf16[1,2048]{1,0:T(2,128)(2,1)S(1)}, bf16[1,2048]{1,0:T(2,128)(2,1)}, u32[]{:S(2)}) copy-start(bf16[1,2048]{1,0:T(2,128)(2,1)} %copy-done.86) | copy-start | bytes 12292
  1262.2 27.2 %copy-start.3 = (bf16[1,128,2048]{2,1,0:T(8,128)(2,1)S(1)}, bf16[1,128,2048]{2,1,0:T(8,128)(2,1)}, u32[]{:S(2)}) copy-start(bf16[1,128,2048]{2,1,0:T(8,128)(2,1)} %param.13) | copy-start | bytes 1572868
  1263.7 25.8 copy-start.100
  1263.7 25.8 copy-start.102
  1284.8 25.3 all-to-all-start.6
  1310.2 19.5 all-to-all-start.2
  1329.7 13.2 all-to-all-start.5
  1342.9 117.7 %all-to-all-start.4 = ((bf16[128,8,256]{2,0,1:T(8,128)(2,1)}), bf16[128,8,256]{2,0,1:T(8,128)(2,1)S(1)}, u32[]{:S(2)}, u32[]{:S(2)}) async-start(bf16[128,8,256]{2,0,1:T(8,128)(2,1)} %bitcast.304), calls=%async_computation.4 | async-start | bytes 1048576 | tf_op jit(solution)/shard_map/all_to_all | solution.py:246
  1460.6 144.6 %all-to-all-start = ((bf16[128,8,256]{2,0,1:T(8,128)(2,1)}), bf16[128,8,256]{2,0,1:T(8,128)(2,1)S(1)}, u32[]{:S(2)}, u32[]{:S(2)}) async-start(bf16[128,8,256]{2,0,1:T(8,128)(2,1)} %fusion.118), calls=%async_computation | async-start | bytes 1048576 | tf_op jit(solution)/shard_map/all_to_all | solution.py:319
  1605.2 88.0 %all-to-all-start.1 = ((bf16[128,8,256]{2,0,1:T(8,128)(2,1)}), bf16[128,8,256]{2,0,1:T(8,128)(2,1)S(1)}, u32[]{:S(2)}, u32[]{:S(2)}) async-start(bf16[128,8,256]{2,0,1:T(8,128)(2,1)} %bitcast.305), calls=%async_computation.1 | async-start | bytes 1048576 | tf_op jit(solution)/shard_map/all_to_all | solution.py:319
  1608.7 1024.1 %all-reduce.13.cloned.1.call-start = ((), (), s32[]{:S(2)}) async-start(), calls=%async_computation.28 | async-start | bytes 51380224 | tf_op jit(solution)/shard_map/psum | solution.py:97
  1772.0 23.9 copy-start.95
  1772.0 23.9 copy-start.96
  1772.0 23.9 copy-start.97
  1772.0 23.9 copy-start.98
  1772.1 49.5 %copy-start.15 = (f32[128,2048]{1,0:T(8,128)S(1)}, f32[128,2048]{1,0:T(8,128)}, u32[]{:S(2)}) copy-start(f32[128,2048]{1,0:T(8,128)} %copy-done.14) | copy-start | bytes 3145732
  1772.1 49.5 %copy-start.124 = (f32[128]{0:T(128)S(1)}, f32[128]{0:T(128)}, u32[]{:S(2)}) copy-start(f32[128]{0:T(128)} %copy-done.123) | copy-start | bytes 1540
  1794.1 30.3 %copy-start.1 = (f32[128,2048]{1,0:T(8,128)S(1)}, f32[128,2048]{1,0:T(8,128)}, u32[]{:S(2)}) copy-start(f32[128,2048]{1,0:T(8,128)} %copy-done) | copy-start | bytes 3145732
  (101 other events, 508.1 us)
Sparse Core Ops, SparseCore 0:
  13.6 119.3 all-gather.77
  135.5 125.3 all-gather.59
  262.8 54.3 all-gather.61
  319.5 116.4 all-gather.63
  437.7 116.4 all-gather.65
  556.0 116.4 all-gather.67
  674.9 125.3 all-gather.69
  802.2 54.3 all-gather.71
  858.5 116.4 all-gather.75
  977.3 116.4 all-gather.73
  1095.7 36.7 all-gather.79
  1174.0 36.6 all-gather.57
  1212.6 36.8 all-gather.47
  1251.2 47.1 all-gather.45
  1300.1 81.5 all-gather.55
  1384.0 67.6 all-gather.51
  1453.5 73.2 all-gather.49
  1528.6 67.6 all-gather.53
  1598.8 80.1 all-gather.41
  1681.3 74.5 all-gather.43
  1770.2 862.5 all-reduce.12
where the time goes:
time: 2680 us; the launch traced here: 2670 us
  waiting for transfers between devices  2010 us (75%)
  matrix products  354 us (13%)
  blocking collectives  132 us (5%)
  other arithmetic  66.3 us (2%)
  local copies, waits for them, and re-layouts  61.4 us (2%)
  starting transfers between devices  32.1 us (1%)
    psum x1, waiting for transfers between devices, sum_replicas(): lax.psum(shards[2].astype(jnp.bfloat16), 'rep').astype(jnp.float32)  760 us
    all_gather x2, waiting for transfers between devices, local(): lax.all_gather(qkv_weight[layer], 'shard', axis=0, tiled=True)  231 us
    all_gather x2, waiting for transfers between devices, local(): lax.all_gather(gate_weight[layer], 'shard', axis=0, tiled=True)  220 us
    all_gather x2, waiting for transfers between devices, local(): lax.all_gather(up_weight[layer], 'shard', axis=0, tiled=True)  217 us
    all_gather x2, waiting for transfers between devices, local(): lax.all_gather(grad_joined, 'shard', axis=0, tiled=True)  133 us
    all_gather x2, waiting for transfers between devices, local(): lax.all_gather(gate_low, 'shard', axis=0, tiled=True)  124 us
    all_gather x2, waiting for transfers between devices, local(): lax.all_gather(down_weight[layer], 'shard', axis=0, tiled=True)  107 us
    all_gather x2, waiting for transfers between devices, local(): lax.all_gather(up_low, 'shard', axis=0, tiled=True)  95.9 us
  transfers between devices with their start and end apart: 29, of which 22 were waited for; matrix products, arithmetic and copies ran while one was open for 16% of the time, Pallas kernels for 0%

commit v1 on v0

v1 whole, which is shorter than its diff:
```python
import jax
import jax.numpy as jnp
from jax import lax
from jax.sharding import PartitionSpec as P

HEADS = 32
ROTARY = 16
HALF = ROTARY // 2

norm_eps = 1e-05
bf16 = jnp.bfloat16
f32 = jnp.float32


def dot(a, b):
    return jnp.dot(a, b, preferred_element_type=f32)


def dot_t(a, b):
    return lax.dot_general(a, b, (((1,), (1,)), ((), ())), preferred_element_type=f32)


def t_dot(a, b):
    return lax.dot_general(a, b, (((0,), (0,)), ((), ())), preferred_element_type=f32)


def normalize(values):
    centred = values - jnp.mean(values, axis=-1, keepdims=True)
    variance = jnp.mean(centred * centred, axis=-1, keepdims=True)
    inverse = lax.rsqrt(variance + norm_eps)
    return centred * inverse, inverse


def normalize_back(grad, xhat, inverse, gain):
    scaled = grad * gain
    inner = jnp.mean(scaled * xhat, axis=-1, keepdims=True)
    grad_in = inverse * (scaled - jnp.mean(scaled, axis=-1, keepdims=True) - xhat * inner)
    return grad_in, jnp.sum(grad * xhat, axis=0), jnp.sum(grad, axis=0)


def positions_and_mask(segments):
    length = segments.shape[-1]
    earlier = (segments[..., None, :] < segments[..., :, None]).astype(jnp.int32)
    starts = jnp.sum(earlier, axis=-1)
    places = jnp.arange(length, dtype=jnp.int32)
    positions = places - starts
    allowed = (segments[..., None, :] == segments[..., :, None]) & (
        places[None, :] <= places[:, None]
    )
    return positions, allowed


def rotary_tables(positions):
    exponents = jnp.arange(HALF, dtype=f32) * (2.0 / ROTARY)
    inverse = 10000.0 ** (-exponents)
    angles = positions.astype(f32)[..., None] * inverse
    return jnp.cos(angles)[..., None, :], jnp.sin(angles)[..., None, :]


def rotate(heads_in, cosine, sine):
    leading = heads_in[..., :HALF]
    trailing = heads_in[..., HALF:ROTARY]
    return jnp.concatenate(
        [
            leading * cosine - trailing * sine,
            trailing * cosine + leading * sine,
            heads_in[..., ROTARY:],
        ],
        axis=-1,
    )


class Exchange:
    def __init__(self, mesh):
        self.shards = mesh.shape["shard"]
        self.reps = mesh.shape["rep"]
        self.cube = self.shards == 8
        self.line = self.reps == 4

    def swap(self, values, bit):
        pairs = [(i, i ^ bit) for i in range(self.shards)]
        return lax.ppermute(values, "shard", pairs)

    def gather(self, own):
        if not self.cube:
            return lax.all_gather(own, "shard", axis=0, tiled=False)
        first = self.swap(own, 1)
        x, y, d = self.swap(own, 2), self.swap(own, 4), self.swap(own, 6)
        others = self.swap(jnp.stack([x, y, d]), 1)
        return jnp.stack([own, first, x, others[0], y, others[1], d, others[2]])

    def scatter_sum(self, blocks):
        if not self.cube:
            return lax.psum_scatter(blocks.astype(bf16), "shard", scatter_dimension=0, tiled=False).astype(f32)
        low = blocks.astype(bf16)
        arrived = self.swap(jnp.stack([low[1], low[3], low[5], low[7]]), 1).astype(f32)
        x = self.swap((blocks[2] + arrived[1]).astype(bf16), 2)
        y = self.swap((blocks[4] + arrived[2]).astype(bf16), 4)
        d = self.swap((blocks[6] + arrived[3]).astype(bf16), 6)
        own = blocks[0] + arrived[0]
        return own + x.astype(f32) + (y.astype(f32) + d.astype(f32))

    def spread(self, blocks):
        return lax.all_to_all(blocks, "shard", split_axis=0, concat_axis=0, tiled=False)

    def total(self, grad, turn=None):
        turn = turn or (lambda v: v)
        if not self.line:
            full = lax.psum(grad.astype(bf16), "rep")
            return jnp.stack([turn(full[0]), turn(full[1])]).astype(f32)
        rep = lax.axis_index("rep")
        low = grad.astype(bf16)
        inward = lax.ppermute(low, "rep", [(0, 1), (3, 2)])
        part = (grad + inward.astype(f32)).astype(bf16)
        lower = rep < 2
        sent = jnp.where(lower, part[0], part[1])
        kept = jnp.where(lower, part[1], part[0])
        middle = lax.ppermute(sent, "rep", [(1, 2), (2, 1)])
        final = turn((kept.astype(f32) + middle.astype(f32)).astype(bf16))
        other = lax.ppermute(final, "rep", [(1, 2), (2, 1)])
        whole = jnp.where(lower, jnp.stack([other, final]), jnp.stack([final, other]))
        outward = lax.ppermute(whole, "rep", [(1, 0), (2, 3)])
        return jnp.where((rep == 1) | (rep == 2), whole, outward).astype(f32)


def make_local(mesh):
    net = Exchange(mesh)
    shards = net.shards

    def local(
        hidden_in,
        segments,
        ln1_gain,
        ln1_bias,
        qkv_weight,
        qkv_bias,
        out_weight,
        ln2_gain,
        ln2_bias,
        gate_weight,
        up_weight,
        down_weight,
        cotangent,
    ):
        layers, rows = qkv_weight.shape[:2]
        width = hidden_in.shape[2]
        tokens = hidden_in.shape[1]
        head_size = width // HEADS
        scale = head_size ** (-0.5)
        own_heads = HEADS // shards
        cols = own_heads * head_size
        hidden_units = down_weight.shape[1]
        everyone = shards * tokens
        me = lax.axis_index("shard")

        small = jnp.concatenate(
            [v.reshape(-1) for v in (ln1_gain, ln1_bias, ln2_gain, ln2_bias, qkv_bias)]
        )
        small = lax.all_gather(small, "shard", axis=0, tiled=False)
        cuts = [0]
        for v in (ln1_gain, ln1_bias, ln2_gain, ln2_bias, qkv_bias):
            cuts.append(cuts[-1] + v.size)

        def whole_of(index, like):
            part = small[:, cuts[index] : cuts[index + 1]].reshape(shards, layers, like.shape[1])
            return part.transpose(1, 0, 2).reshape(layers, -1).astype(f32)

        gain1, shift1 = whole_of(0, ln1_gain), whole_of(1, ln1_bias)
        gain2, shift2 = whole_of(2, ln2_gain), whole_of(3, ln2_bias)
        bias_all = whole_of(4, qkv_bias).reshape(layers, 3, shards, cols)
        bias_own = lax.dynamic_index_in_dim(bias_all, me, axis=2, keepdims=False)
        bias_own = bias_own.reshape(layers, 3 * cols)

        group_segments = net.gather(segments[0].astype(bf16)).astype(jnp.int32)
        positions, allowed = positions_and_mask(group_segments)
        cosine, sine = rotary_tables(positions)
        allowed = allowed[:, None]

        def columns_of(weight):
            cut = weight.reshape(rows, shards, -1).transpose(1, 0, 2)
            return net.spread(cut).reshape(width, -1)

        def qkv_columns(weight):
            cut = weight.reshape(rows, 3, shards, cols).transpose(2, 0, 1, 3)
            return net.spread(cut).reshape(width, 3 * cols)

        proj_in = [qkv_columns(qkv_weight[layer]) for layer in range(layers)]
        weight_gate = [columns_of(gate_weight[layer]) for layer in range(layers)]
        weight_up = [columns_of(up_weight[layer]) for layer in range(layers)]

        def gather(values):
            return net.gather(values).reshape(everyone, -1)

        def scatter_sum(values):
            return net.scatter_sum(values.reshape(shards, tokens, -1))

        state = hidden_in[0].astype(f32)
        saved = []
        for layer in range(layers):
            xhat1, inverse1 = normalize(state)
            normed1 = gather((xhat1 * gain1[layer] + shift1[layer]).astype(bf16))
            joined = dot(normed1, proj_in[layer]) + bias_own[layer]
            split = joined.reshape(shards, tokens, 3, own_heads, head_size)
            query = rotate(split[:, :, 0], cosine, sine).astype(bf16)
            keys = rotate(split[:, :, 1], cosine, sine).astype(bf16)
            value = split[:, :, 2].astype(bf16)
            scores = (
                jnp.einsum("gqhd,gkhd->ghqk", query, keys, preferred_element_type=f32) * scale
            )
            masked = jnp.where(allowed, scores, -1000000000.0)
            peak = jnp.max(masked, axis=-1, keepdims=True)
            raised = jnp.exp(masked - peak)
            probs = raised / jnp.sum(raised, axis=-1, keepdims=True)
            probs_low = probs.astype(bf16)
            mixed = (
                jnp.einsum("ghqk,gkhd->gqhd", probs_low, value, preferred_element_type=f32)
                .astype(bf16)
                .reshape(everyone, cols)
            )
            state_mid = state + scatter_sum(dot(mixed, out_weight[layer]))
            xhat2, inverse2 = normalize(state_mid)
            normed2 = gather((xhat2 * gain2[layer] + shift2[layer]).astype(bf16))
            gate = dot(normed2, weight_gate[layer])
            upper = dot(normed2, weight_up[layer])
            inner = (jax.nn.silu(gate) * upper).astype(bf16)
            state = state_mid + scatter_sum(dot(inner, down_weight[layer]))
            saved.append(
                (xhat1, inverse1, normed1, query, keys, value, probs, mixed)
                + (xhat2, inverse2, normed2, gate, upper, inner)
            )
        block_out = state.astype(bf16)[None]

        def from_columns(grad):
            return grad.reshape(shards, 2, rows // 2, -1).transpose(1, 0, 2, 3)

        def turn_columns(half):
            return net.spread(half).transpose(1, 0, 2).reshape(rows // 2, -1)

        def turn_qkv(half):
            whole = net.spread(half).reshape(shards, rows // 2, 3, cols)
            return whole.transpose(1, 2, 0, 3).reshape(rows // 2, -1)

        def halves(grad):
            return grad.reshape(2, grad.shape[0] // 2, -1)

        grad_state = cotangent[0].astype(f32)
        weight_grads = [None] * layers
        small_grads = [None] * layers
        for layer in reversed(range(layers)):
            xhat1, inverse1, normed1, query, keys, value, probs, mixed = saved[layer][:8]
            xhat2, inverse2, normed2, gate, upper, inner = saved[layer][8:]
            down_in = gather(grad_state.astype(bf16))
            grad_inner = dot_t(down_in, down_weight[layer])
            sigmoid = jax.nn.sigmoid(gate)
            silu = gate * sigmoid
            grad_gate = (grad_inner * upper * (sigmoid * (1.0 + gate * (1.0 - sigmoid)))).astype(bf16)
            grad_up = (grad_inner * silu).astype(bf16)
            grad_normed2 = scatter_sum(
                dot_t(grad_gate, weight_gate[layer]) + dot_t(grad_up, weight_up[layer])
            )
            grad_down_weight = net.total(halves(t_dot(inner, down_in)))
            grad_gate_weight = net.total(from_columns(t_dot(normed2, grad_gate)), turn_columns)
            grad_up_weight = net.total(from_columns(t_dot(normed2, grad_up)), turn_columns)
            back2, gain2_grad, shift2_grad = normalize_back(
                grad_normed2, xhat2, inverse2, gain2[layer]
            )
            grad_state = grad_state + back2

            branch = gather(grad_state.astype(bf16))
            grad_mixed = dot_t(branch, out_weight[layer]).astype(bf16)
            grad_out_weight = net.total(halves(t_dot(mixed, branch)))
            grad_mixed = grad_mixed.reshape(shards, tokens, own_heads, head_size)
            grad_probs = jnp.einsum(
                "gqhd,gkhd->ghqk", grad_mixed, value, preferred_element_type=f32
            )
            grad_value = jnp.einsum(
                "ghqk,gqhd->gkhd", probs.astype(bf16), grad_mixed, preferred_element_type=f32
            )
            inner_sum = jnp.sum(probs * grad_probs, axis=-1, keepdims=True)
            grad_scores = (probs * (grad_probs - inner_sum)).astype(bf16)
            grad_query = (
                jnp.einsum("ghqk,gkhd->gqhd", grad_scores, keys, preferred_element_type=f32) * scale
            )
            grad_key = (
                jnp.einsum("ghqk,gqhd->gkhd", grad_scores, query, preferred_element_type=f32)
                * scale
            )
            grad_query = rotate(grad_query, cosine, -sine)
            grad_key = rotate(grad_key, cosine, -sine)
            grad_joined = jnp.stack([grad_query, grad_key, grad_value], axis=2)
            bias_grad = jnp.sum(grad_joined.astype(bf16).astype(f32), axis=(0, 1))
            grad_joined = grad_joined.reshape(everyone, 3 * cols).astype(bf16)
            grad_normed1 = scatter_sum(dot_t(grad_joined, proj_in[layer]))
            grad_qkv_weight = net.total(from_columns(t_dot(normed1, grad_joined)), turn_qkv)
            back1, gain1_grad, shift1_grad = normalize_back(
                grad_normed1, xhat1, inverse1, gain1[layer]
            )
            grad_state = grad_state + back1
            weight_grads[layer] = (
                grad_qkv_weight.reshape(rows, -1),
                grad_out_weight.reshape(rows, -1),
                grad_gate_weight.reshape(rows, -1),
                grad_up_weight.reshape(rows, -1),
                grad_down_weight.reshape(hidden_units, -1),
            )
            placed = jnp.where(
                (jnp.arange(shards) == me)[None, :, None], bias_grad.reshape(3, 1, cols), 0.0
            )
            small_grads[layer] = jnp.concatenate(
                [gain1_grad, shift1_grad, gain2_grad, shift2_grad, placed.reshape(-1)]
            )

        summed = lax.psum(jnp.stack(small_grads), ("shard", "rep"))

        def owned(begin, count):
            part = summed[:, begin : begin + count].reshape(layers, shards, count // shards)
            return lax.dynamic_index_in_dim(part, me, axis=1, keepdims=False)

        stacked = [
            jnp.stack([weight_grads[layer][index] for layer in range(layers)]) for index in range(5)
        ]
        return (
            block_out,
            grad_state.astype(bf16)[None],
            owned(0, width),
            owned(width, width),
            stacked[0],
            owned(4 * width, 3 * width),
            stacked[1],
            owned(2 * width, width),
            owned(3 * width, width),
            stacked[2],
            stacked[3],
            stacked[4],
        )

    return local


def solution(mesh):
    tokens3 = P(("shard", "rep"), None, None)
    vector = P(None, "shard")
    matrix = P(None, "shard", None)
    in_specs = (
        tokens3,
        P(("shard", "rep"), None),
        vector,
        vector,
        matrix,
        vector,
        matrix,
        vector,
        vector,
        matrix,
        matrix,
        matrix,
        tokens3,
    )
    out_specs = (
        tokens3,
        tokens3,
        vector,
        vector,
        matrix,
        vector,
        matrix,
        vector,
        vector,
        matrix,
        matrix,
        matrix,
    )
    return jax.shard_map(
        make_local(mesh), mesh=mesh, in_specs=in_specs, out_specs=out_specs, check_vma=False
    )
```

time: 2680 us -> 1920 us (0.72)
  waiting for transfers between devices: 2010 us -> 840 us
  starting transfers between devices: 32.1 us -> 365 us
  local copies, waits for them, and re-layouts: 61.4 us -> 255 us
  other arithmetic: 66.3 us -> 247 us
  matrix products: 354 us -> 178 us
  blocking collectives: 132 us -> 10.7 us
    all_gather x20 -> x0, waiting for transfers between devices: 1190 us -> none  [the longest x2 231 us: local(): lax.all_gather(qkv_weight[layer], 'shard', axis=0, tiled=True)]
    ppermute x0 -> x117, waiting for transfers between devices: none -> 664 us  [the longest x77 293 us: swap(): return lax.ppermute(values, 'shard', pairs)]
    psum x1, waiting for transfers between devices: 760 us -> 162 us  [local(): summed = lax.psum(jnp.stack(small_grads), ('shard', 'rep'))]
    ppermute x0 -> x117, starting transfers between devices: none -> 313 us  [the longest x10 194 us: total(): inward = lax.ppermute(low, 'rep', [(0, 1), (3, 2)])]
    dot_general x42 -> x40, matrix products: 354 us -> 173 us  [the longest x10 65.6 us: t_dot(): lax.dot_general(a, b, (((0,), (0,)), ((), ())), preferred_element_type=f32)]
    unnamed x282 -> x449, local copies, waits for them, and re-layouts: 14.2 us -> 103 us
    convert_element_type x22 -> x47, other arithmetic: 7.9 us -> 86.3 us  [the longest x10 26 us: total(): part = (grad + inward.astype(f32)).astype(bf16)]
    all_gather x10 -> x1, blocking collectives: 86.7 us -> 10.7 us  [local(): small = lax.all_gather(small, 'shard', axis=0, tiled=False)]
  transfers between devices with their start and end apart: 29 -> 130, of which waited for: 22 -> 42; matrix products, arithmetic and copies ran while one was open for 16% -> 27% of each run, Pallas kernels for 0% -> 0%
where the time goes in v1:
time: 1920 us; the launch traced here: 1910 us
  waiting for transfers between devices  840 us (44%)
  starting transfers between devices  365 us (19%)
  local copies, waits for them, and re-layouts  255 us (13%)
  other arithmetic  247 us (13%)
  matrix products  178 us (9%)
    ppermute x77, waiting for transfers between devices, swap(): return lax.ppermute(values, 'shard', pairs)  293 us
    ppermute x10, waiting for transfers between devices, total(): inward = lax.ppermute(low, 'rep', [(0, 1), (3, 2)])  208 us
    ppermute x10, starting transfers between devices, total(): inward = lax.ppermute(low, 'rep', [(0, 1), (3, 2)])  194 us
    ppermute x10, waiting for transfers between devices, total(): outward = lax.ppermute(whole, 'rep', [(1, 0), (2, 3)])  163 us
    psum x1, waiting for transfers between devices, local(): summed = lax.psum(jnp.stack(small_grads), ('shard', 'rep'))  162 us
    unnamed x449, local copies, waits for them, and re-layouts  103 us
    ppermute x77, starting transfers between devices, swap(): return lax.ppermute(values, 'shard', pairs)  80.1 us
    dot_general x10, matrix products, t_dot(): lax.dot_general(a, b, (((0,), (0,)), ((), ())), preferred_element_type=f32)  65.6 us
  transfers between devices with their start and end apart: 130, of which 42 were waited for; matrix products, arithmetic and copies ran while one was open for 27% of the time, Pallas kernels for 0%

profile of v1, /device:TPU:0, one launch (start us, length us, event | category | flops | bytes accessed | tf_op | source)
XLA Modules:
  0.0 1913.9 jit_solution(3396445815899176752)
XLA Ops:
  11.5 10.7 all-gather.1
  33.8 6.3 fusion.238
  55.0 33.2 %collective-permute-done.8 = bf16[128]{0:T(256)(128)(2,1)S(1)} collective-permute-done((bf16[128]{0:T(256)(128)(2,1)S(1)}, bf16[128]{0:T(256)(128)(2,1)S(1)}, u32[]{:S(2)}, u32[]{:S(2)}) %collective-permute-start.8) | collective-permute-done | bytes 288 | tf_op jit(solution)/shard_map/ppermute | solution.py:82
  114.9 6.3 reshape.763
  158.9 5.5 fusion.241
  180.6 13.8 all-to-all-done.1
  204.8 12.2 collective-permute-done.13
  224.6 33.6 %collective-permute-done.15 = bf16[128,2048]{1,0:T(8,128)(2,1)S(1)} collective-permute-done((bf16[128,2048]{1,0:T(8,128)(2,1)}, bf16[128,2048]{1,0:T(8,128)(2,1)S(1)}, u32[]{:S(2)}, u32[]{:S(2)}) %collective-permute-start.15) | collective-permute-done | bytes 524320 | tf_op jit(solution)/shard_map/ppermute | solution.py:82
  258.2 11.7 collective-permute-done.17
  315.8 9.8 collective-permute-done.22
  329.4 10.2 collective-permute-start.24
  341.1 29.5 %collective-permute-done.24 = bf16[128,2048]{1,0:T(8,128)(2,1)S(1)} collective-permute-done((bf16[128,2048]{1,0:T(8,128)(2,1)}, bf16[128,2048]{1,0:T(8,128)(2,1)S(1)}, u32[]{:S(2)}, u32[]{:S(2)}) %collective-permute-start.24) | collective-permute-done | bytes 524320 | tf_op jit(solution)/shard_map/ppermute | solution.py:82
  370.6 10.4 collective-permute-done.26
  399.6 6.3 reshape.764
  446.2 12.0 collective-permute-done.43
  472.7 8.4 collective-permute-start.29
  486.5 13.2 collective-permute-done.29
  500.6 10.9 collective-permute-done.31
  526.0 38.3 %collective-permute-done.33 = bf16[128,2048]{1,0:T(8,128)(2,1)S(1)} collective-permute-done((bf16[128,2048]{1,0:T(8,128)(2,1)}, bf16[128,2048]{1,0:T(8,128)(2,1)S(1)}, u32[]{:S(2)}, u32[]{:S(2)}) %collective-permute-start.33) | collective-permute-done | bytes 524320 | tf_op jit(solution)/shard_map/ppermute | solution.py:82
  564.3 11.7 collective-permute-done.35
  599.9 7.7 fusion.251
  610.7 5.8 multiply_convert_fusion.2
  620.1 5.8 fusion.250
  628.7 6.5 copy.296
  636.2 6.4 copy.313
  643.5 6.6 copy.306
  650.0 7.5 fusion.257
  662.6 6.5 copy.319
  669.1 6.1 bitcast_convert_fusion.2
  690.0 7.8 collective-permute-done.38
  698.4 9.0 collective-permute-done.39
  712.2 5.9 bitcast_convert_fusion.4
  723.2 7.3 collective-permute-done.48
  738.5 47.5 %collective-permute-done.105 = bf16[2,8,128,704]{2,3,1,0:T(8,128)(2,1)} collective-permute-done((bf16[2,8,128,704]{2,3,1,0:T(8,128)(2,1)}, bf16[2,8,128,704]{2,3,1,0:T(8,128)(2,1)}, u32[]{:S(2)}, u32[]{:S(2)}) %collective-permute-start.105) | collective-permute-done | bytes 2883616 | tf_op jit(solution)/shard_map/ppermute | solution.py:113
  792.9 53.9 %collective-permute-done.97 = bf16[2,8,128,704]{2,3,1,0:T(8,128)(2,1)} collective-permute-done((bf16[2,8,128,704]{2,3,1,0:T(8,128)(2,1)}, bf16[2,8,128,704]{2,3,1,0:T(8,128)(2,1)}, u32[]{:S(2)}, u32[]{:S(2)}) %collective-permute-start.97) | collective-permute-done | bytes 2883616 | tf_op jit(solution)/shard_map/ppermute | solution.py:113
  895.3 5.4 fusion.255
  900.7 80.1 %collective-permute-start.89 = (bf16[2,128,2048]{2,1,0:T(8,128)(2,1)S(1)}, bf16[2,128,2048]{2,1,0:T(8,128)(2,1)S(1)}, u32[]{:S(2)}, u32[]{:S(2)}) collective-permute-start(bf16[2,128,2048]{2,1,0:T(8,128)(2,1)S(1)} %get-tuple-element.208), channel_id=1, source_target_pairs={{0,1},{3,2},{4,5},{7,6},{8,9},{11,10},{12,13},{15,14},{16,17},{19,... | collective-permute-start | bytes 3145736 | tf_op jit(solution)/shard_map/ppermute | solution.py:113
  980.9 5.8 fusion.252
  992.1 7.6 collective-permute-done.89
  1003.0 5.9 bitcast_convert_fusion
  1010.3 8.5 collective-permute-start.81
  1045.8 6.2 collective-permute-done.57
  1059.1 21.0 %collective-permute-done.81 = bf16[2,8,128,768]{3,2,1,0:T(8,128)(2,1)} collective-permute-done((bf16[2,8,128,768]{3,2,1,0:T(8,128)(2,1)}, bf16[2,8,128,768]{3,2,1,0:T(8,128)(2,1)}, u32[]{:S(2)}, u32[]{:S(2)}) %collective-permute-start.81) | collective-permute-done | bytes 3145760 | tf_op jit(solution)/shard_map/ppermute | solution.py:113
  1088.1 64.0 %collective-permute-done.92 = bf16[2,128,2048]{2,1,0:T(8,128)(2,1)S(1)} collective-permute-done((bf16[2,128,2048]{2,1,0:T(8,128)(2,1)S(1)}, bf16[2,128,2048]{2,1,0:T(8,128)(2,1)S(1)}, u32[]{:S(2)}, u32[]{:S(2)}) %collective-permute-start.92) | collective-permute-done | bytes 1048608 | tf_op jit(solution)/shard_map/ppermute | solution.py:122
  1163.2 6.0 multiply_convert_fusion
  1172.7 5.5 bitcast_convert_fusion.5
  1178.2 5.4 bitcast_convert_fusion.3
  1190.8 5.9 fusion.253
  1206.0 9.4 fusion.258
  1215.4 5.3 broadcast_select_fusion.4
  1229.4 39.3 %collective-permute-done.100 = bf16[2,128,5632]{1,2,0:T(8,128)(2,1)} collective-permute-done((bf16[2,128,5632]{1,2,0:T(8,128)(2,1)}, bf16[2,128,5632]{1,2,0:T(8,128)(2,1)}, u32[]{:S(2)}, u32[]{:S(2)}) %collective-permute-start.100) | collective-permute-done | bytes 2883616 | tf_op jit(solution)/shard_map/ppermute | solution.py:122
  1295.4 16.0 collective-permute-done.93
  1318.0 42.7 %collective-permute-done.109 = bf16[2,352,2048]{2,1,0:T(8,128)(2,1)S(1)} collective-permute-done((bf16[2,352,2048]{2,1,0:T(8,128)(2,1)}, bf16[2,352,2048]{2,1,0:T(8,128)(2,1)S(1)}, u32[]{:S(2)}, u32[]{:S(2)}) %collective-permute-start.109) | collective-permute-done | bytes 2883616 | tf_op jit(solution)/shard_map/ppermute | solution.py:113
  1406.3 5.8 fusion.254
  1424.3 83.4 %collective-permute-start.85 = (bf16[2,128,2048]{2,1,0:T(8,128)(2,1)}, bf16[2,128,2048]{2,1,0:T(8,128)(2,1)}, u32[]{:S(2)}, u32[]{:S(2)}) collective-permute-start(bf16[2,128,2048]{2,1,0:T(8,128)(2,1)} %get-tuple-element.210), channel_id=1, source_target_pairs={{0,1},{3,2},{4,5},{7,6},{8,9},{11,10},{12,13},{15,14},{16,17},{19,... | collective-permute-start | bytes 3145736 | tf_op jit(solution)/shard_map/ppermute | solution.py:113
  1507.8 9.4 bitcast_convert_fusion.1
  1566.1 10.3 collective-permute-done.75
  1581.7 15.6 collective-permute-done.77
  1613.6 162.4 %all-reduce.2.cloned.1.call-done = f32[2,14336]{1,0:T(2,128)} async-done(((f32[2,14336]{1,0:T(2,128)}), f32[2,14336]{1,0:T(2,128)}) %all-reduce.2.cloned.1.call-update) | async-done | bytes 114704 | tf_op jit(solution)/shard_map/psum | solution.py:313
  1791.6 5.2 maximum_convert_fusion.3
  1800.4 5.4 broadcast_select_fusion.5
  1819.7 11.3 maximum_convert_fusion.1
  1831.0 60.1 %collective-permute-done.80 = bf16[2,128,6144]{1,2,0:T(8,128)(2,1)} collective-permute-done((bf16[2,128,6144]{1,2,0:T(8,128)(2,1)}, bf16[2,128,6144]{1,2,0:T(8,128)(2,1)}, u32[]{:S(2)}, u32[]{:S(2)}) %collective-permute-start.80) | collective-permute-done | bytes 3145760 | tf_op jit(solution)/shard_map/ppermute | solution.py:122
  1899.4 7.5 maximum_convert_fusion
  (933 shorter events, 695.5 us)
Async XLA Ops:
  27.6 63.2 %collective-permute-start.1 = (bf16[128,2048]{1,0:T(8,128)(2,1)}, bf16[128,2048]{1,0:T(8,128)(2,1)}, u32[]{:S(2)}, u32[]{:S(2)}) collective-permute-start(bf16[128,2048]{1,0:T(8,128)(2,1)} %fusion.83), channel_id=1, source_target_pairs={{0,8},{4,12},{8,0},{12,4},{16,24},{20,28},{24,16},{28,20},{1,9},{5... | collective-permute-start | bytes 1572872 | tf_op jit(solution)/shard_map/ppermute | solution.py:82
  29.1 61.7 %collective-permute-start.2 = (bf16[128,2048]{1,0:T(8,128)(2,1)}, bf16[128,2048]{1,0:T(8,128)(2,1)}, u32[]{:S(2)}, u32[]{:S(2)}) collective-permute-start(bf16[128,2048]{1,0:T(8,128)(2,1)} %fusion.83), channel_id=1, source_target_pairs={{0,16},{4,20},{8,24},{12,28},{16,0},{20,4},{24,8},{28,12},{1,17},{... | collective-permute-start | bytes 1572872 | tf_op jit(solution)/shard_map/ppermute | solution.py:82
  29.7 61.2 %collective-permute-start.3 = (bf16[128,2048]{1,0:T(8,128)(2,1)}, bf16[128,2048]{1,0:T(8,128)(2,1)}, u32[]{:S(2)}, u32[]{:S(2)}) collective-permute-start(bf16[128,2048]{1,0:T(8,128)(2,1)} %fusion.83), channel_id=1, source_target_pairs={{0,24},{4,28},{8,16},{12,20},{16,8},{20,12},{24,0},{28,4},{1,25},{... | collective-permute-start | bytes 1572872 | tf_op jit(solution)/shard_map/ppermute | solution.py:82
  45.2 58.1 %all-to-all-start = ((bf16[8,256,3,256]{1,3,2,0:T(8,128)(2,1)}), bf16[8,256,3,256]{1,3,2,0:T(8,128)(2,1)}, u32[]{:S(2)}, u32[]{:S(2)}) async-start(bf16[8,256,3,256]{1,3,2,0:T(8,128)(2,1)} %copy.257), calls=%async_computation | async-start | bytes 6291456 | tf_op jit(solution)/shard_map/all_to_all | solution.py:104
  55.0 39.4 %collective-permute-start = (bf16[128,2048]{1,0:T(8,128)(2,1)}, bf16[128,2048]{1,0:T(8,128)(2,1)S(1)}, u32[]{:S(2)}, u32[]{:S(2)}) collective-permute-start(bf16[128,2048]{1,0:T(8,128)(2,1)} %fusion.83), channel_id=1, source_target_pairs={{0,4},{4,0},{8,12},{12,8},{16,20},{20,16},{24,28},{28,24},{1,5},{5... | collective-permute-start | bytes 1572872 | tf_op jit(solution)/shard_map/ppermute | solution.py:82
  155.1 39.3 %all-to-all-start.1 = ((bf16[8,256,704]{1,2,0:T(8,128)(2,1)}), bf16[8,256,704]{1,2,0:T(8,128)(2,1)S(1)}, u32[]{:S(2)}, u32[]{:S(2)}) async-start(bf16[8,256,704]{1,2,0:T(8,128)(2,1)} %bitcast.995), calls=%async_computation.1 | async-start | bytes 5767168 | tf_op jit(solution)/shard_map/all_to_all | solution.py:104
  174.7 42.4 %collective-permute-start.13 = (bf16[128,2048]{1,0:T(8,128)(2,1)}, bf16[128,2048]{1,0:T(8,128)(2,1)}, u32[]{:S(2)}, u32[]{:S(2)}) collective-permute-start(bf16[128,2048]{1,0:T(8,128)(2,1)} %get-tuple-element.81), channel_id=1, source_target_pairs={{0,24},{4,28},{8,16},{12,20},{16,8},{20,12},{24,0},{28,4},{1,25},{... | collective-permute-start | bytes 1572872 | tf_op jit(solution)/shard_map/ppermute | solution.py:82
  196.0 77.7 %all-to-all-start.2 = ((bf16[8,256,704]{1,2,0:T(8,128)(2,1)}), bf16[8,256,704]{1,2,0:T(8,128)(2,1)}, u32[]{:S(2)}, u32[]{:S(2)}) async-start(bf16[8,256,704]{1,2,0:T(8,128)(2,1)} %bitcast.994), calls=%async_computation.2 | async-start | bytes 5767168 | tf_op jit(solution)/shard_map/all_to_all | solution.py:104
  221.1 37.1 %collective-permute-start.15 = (bf16[128,2048]{1,0:T(8,128)(2,1)}, bf16[128,2048]{1,0:T(8,128)(2,1)S(1)}, u32[]{:S(2)}, u32[]{:S(2)}) collective-permute-start(bf16[128,2048]{1,0:T(8,128)(2,1)} %get-tuple-element.56), channel_id=1, source_target_pairs={{0,8},{4,12},{8,0},{12,4},{16,24},{20,28},{24,16},{28,20},{1,9},{5... | collective-permute-start | bytes 1572872 | tf_op jit(solution)/shard_map/ppermute | solution.py:82
  221.8 48.1 %collective-permute-start.17 = (bf16[128,2048]{1,0:T(8,128)(2,1)}, bf16[128,2048]{1,0:T(8,128)(2,1)S(1)}, u32[]{:S(2)}, u32[]{:S(2)}) collective-permute-start(bf16[128,2048]{1,0:T(8,128)(2,1)} %get-tuple-element.56), channel_id=1, source_target_pairs={{0,24},{4,28},{8,16},{12,20},{16,8},{20,12},{24,0},{28,4},{1,25},{... | collective-permute-start | bytes 1572872 | tf_op jit(solution)/shard_map/ppermute | solution.py:82
  311.3 71.6 %all-to-all-start.3 = ((bf16[8,256,3,256]{1,3,2,0:T(8,128)(2,1)}), bf16[8,256,3,256]{1,3,2,0:T(8,128)(2,1)}, u32[]{:S(2)}, u32[]{:S(2)}) async-start(bf16[8,256,3,256]{1,3,2,0:T(8,128)(2,1)} %copy.270), calls=%async_computation.3 | async-start | bytes 6291456 | tf_op jit(solution)/shard_map/all_to_all | solution.py:104
  329.4 41.2 %collective-permute-start.24 = (bf16[128,2048]{1,0:T(8,128)(2,1)}, bf16[128,2048]{1,0:T(8,128)(2,1)S(1)}, u32[]{:S(2)}, u32[]{:S(2)}) collective-permute-start(bf16[128,2048]{1,0:T(8,128)(2,1)} %get-tuple-element.52), channel_id=1, source_target_pairs={{0,8},{4,12},{8,0},{12,4},{16,24},{20,28},{24,16},{28,20},{1,9},{5... | collective-permute-start | bytes 1572872 | tf_op jit(solution)/shard_map/ppermute | solution.py:82
  339.5 41.5 %collective-permute-start.26 = (bf16[128,2048]{1,0:T(8,128)(2,1)}, bf16[128,2048]{1,0:T(8,128)(2,1)S(1)}, u32[]{:S(2)}, u32[]{:S(2)}) collective-permute-start(bf16[128,2048]{1,0:T(8,128)(2,1)} %get-tuple-element.52), channel_id=1, source_target_pairs={{0,24},{4,28},{8,16},{12,20},{16,8},{20,12},{24,0},{28,4},{1,25},{... | collective-permute-start | bytes 1572872 | tf_op jit(solution)/shard_map/ppermute | solution.py:82
  431.4 36.9 %collective-permute-start.28 = (bf16[4,128,2048]{2,1,0:T(8,128)(2,1)}, bf16[4,128,2048]{2,1,0:T(8,128)(2,1)}, u32[]{:S(2)}, u32[]{:S(2)}) collective-permute-start(bf16[4,128,2048]{2,1,0:T(8,128)(2,1)} %pad_maximum_fusion.2), channel_id=1, source_target_pairs={{0,4},{4,0},{8,12},{12,8},{16,20},{20,16},{24,28},{28,24},{1,5},{5... | collective-permute-start | bytes 6291464 | tf_op jit(solution)/shard_map/ppermute | solution.py:82
  439.4 74.1 %all-to-all-start.4 = ((bf16[8,256,704]{1,2,0:T(8,128)(2,1)}), bf16[8,256,704]{1,2,0:T(8,128)(2,1)}, u32[]{:S(2)}, u32[]{:S(2)}) async-start(bf16[8,256,704]{1,2,0:T(8,128)(2,1)} %bitcast.993), calls=%async_computation.4 | async-start | bytes 5767168 | tf_op jit(solution)/shard_map/all_to_all | solution.py:104
  513.5 70.3 %all-to-all-start.5 = ((bf16[8,256,704]{1,2,0:T(8,128)(2,1)}), bf16[8,256,704]{1,2,0:T(8,128)(2,1)}, u32[]{:S(2)}, u32[]{:S(2)}) async-start(bf16[8,256,704]{1,2,0:T(8,128)(2,1)} %bitcast.991), calls=%async_computation.5 | async-start | bytes 5767168 | tf_op jit(solution)/shard_map/all_to_all | solution.py:104
  519.8 44.6 %collective-permute-start.33 = (bf16[128,2048]{1,0:T(8,128)(2,1)}, bf16[128,2048]{1,0:T(8,128)(2,1)S(1)}, u32[]{:S(2)}, u32[]{:S(2)}) collective-permute-start(bf16[128,2048]{1,0:T(8,128)(2,1)} %get-tuple-element.48), channel_id=1, source_target_pairs={{0,8},{4,12},{8,0},{12,4},{16,24},{20,28},{24,16},{28,20},{1,9},{5... | collective-permute-start | bytes 1572872 | tf_op jit(solution)/shard_map/ppermute | solution.py:82
  521.7 42.6 %collective-permute-start.34 = (bf16[128,2048]{1,0:T(8,128)(2,1)}, bf16[128,2048]{1,0:T(8,128)(2,1)S(1)}, u32[]{:S(2)}, u32[]{:S(2)}) collective-permute-start(bf16[128,2048]{1,0:T(8,128)(2,1)} %get-tuple-element.48), channel_id=1, source_target_pairs={{0,16},{4,20},{8,24},{12,28},{16,0},{20,4},{24,8},{28,12},{1,17},{... | collective-permute-start | bytes 1572872 | tf_op jit(solution)/shard_map/ppermute | solution.py:82
  523.2 52.8 %collective-permute-start.35 = (bf16[128,2048]{1,0:T(8,128)(2,1)}, bf16[128,2048]{1,0:T(8,128)(2,1)S(1)}, u32[]{:S(2)}, u32[]{:S(2)}) collective-permute-start(bf16[128,2048]{1,0:T(8,128)(2,1)} %get-tuple-element.48), channel_id=1, source_target_pairs={{0,24},{4,28},{8,16},{12,20},{16,8},{20,12},{24,0},{28,4},{1,25},{... | collective-permute-start | bytes 1572872 | tf_op jit(solution)/shard_map/ppermute | solution.py:82
  526.0 60.3 %collective-permute-start.32 = (bf16[128,2048]{1,0:T(8,128)(2,1)}, bf16[128,2048]{1,0:T(8,128)(2,1)}, u32[]{:S(2)}, u32[]{:S(2)}) collective-permute-start(bf16[128,2048]{1,0:T(8,128)(2,1)} %get-tuple-element.48), channel_id=1, source_target_pairs={{0,4},{4,0},{8,12},{12,8},{16,20},{20,16},{24,28},{28,24},{1,5},{5... | collective-permute-start | bytes 1572872 | tf_op jit(solution)/shard_map/ppermute | solution.py:82
  609.4 68.7 %collective-permute-start.37 = (bf16[4,128,2048]{2,1,0:T(8,128)(2,1)}, bf16[4,128,2048]{2,1,0:T(8,128)(2,1)}, u32[]{:S(2)}, u32[]{:S(2)}) collective-permute-start(bf16[4,128,2048]{2,1,0:T(8,128)(2,1)} %pad_maximum_fusion.3), channel_id=1, source_target_pairs={{0,4},{4,0},{8,12},{12,8},{16,20},{20,16},{24,28},{28,24},{1,5},{5... | collective-permute-start | bytes 6291464 | tf_op jit(solution)/shard_map/ppermute | solution.py:82
  627.7 56.2 %collective-permute-start.46 = (bf16[4,128,2048]{2,1,0:T(8,128)(2,1)}, bf16[4,128,2048]{2,1,0:T(8,128)(2,1)}, u32[]{:S(2)}, u32[]{:S(2)}) collective-permute-start(bf16[4,128,2048]{2,1,0:T(8,128)(2,1)} %pad_maximum_fusion.4), channel_id=1, source_target_pairs={{0,4},{4,0},{8,12},{12,8},{16,20},{20,16},{24,28},{28,24},{1,5},{5... | collective-permute-start | bytes 6291464 | tf_op jit(solution)/shard_map/ppermute | solution.py:82
  657.5 131.5 %collective-permute-start.113 = (bf16[2,352,2048]{2,1,0:T(8,128)(2,1)}, bf16[2,352,2048]{2,1,0:T(8,128)(2,1)}, u32[]{:S(2)}, u32[]{:S(2)}) collective-permute-start(bf16[2,352,2048]{2,1,0:T(8,128)(2,1)} %get-tuple-element.222), channel_id=1, source_target_pairs={{0,1},{3,2},{4,5},{7,6},{8,9},{11,10},{12,13},{15,14},{16,17},{19,... | collective-permute-start | bytes 8650760 | tf_op jit(solution)/shard_map/ppermute | solution.py:113
  675.3 110.7 %collective-permute-start.105 = (bf16[2,8,128,704]{2,3,1,0:T(8,128)(2,1)}, bf16[2,8,128,704]{2,3,1,0:T(8,128)(2,1)}, u32[]{:S(2)}, u32[]{:S(2)}) collective-permute-start(bf16[2,8,128,704]{2,3,1,0:T(8,128)(2,1)} %get-tuple-element.216), channel_id=1, source_target_pairs={{0,1},{3,2},{4,5},{7,6},{8,9},{11,10},{12,13},{15,14},{16,17},{19,... | collective-permute-start | bytes 8650760 | tf_op jit(solution)/shard_map/ppermute | solution.py:113
  720.3 126.5 %collective-permute-start.97 = (bf16[2,8,128,704]{2,3,1,0:T(8,128)(2,1)}, bf16[2,8,128,704]{2,3,1,0:T(8,128)(2,1)}, u32[]{:S(2)}, u32[]{:S(2)}) collective-permute-start(bf16[2,8,128,704]{2,3,1,0:T(8,128)(2,1)} %get-tuple-element.212), channel_id=1, source_target_pairs={{0,1},{3,2},{4,5},{7,6},{8,9},{11,10},{12,13},{15,14},{16,17},{19,... | collective-permute-start | bytes 8650760 | tf_op jit(solution)/shard_map/ppermute | solution.py:113
  736.5 115.0 %collective-permute-start.51 = (bf16[128,2048]{1,0:T(8,128)(2,1)}, bf16[128,2048]{1,0:T(8,128)(2,1)}, u32[]{:S(2)}, u32[]{:S(2)}) collective-permute-start(bf16[128,2048]{1,0:T(8,128)(2,1)} %get-tuple-element.44), channel_id=1, source_target_pairs={{0,8},{4,12},{8,0},{12,4},{16,24},{20,28},{24,16},{28,20},{1,9},{5... | collective-permute-start | bytes 1572872 | tf_op jit(solution)/shard_map/ppermute | solution.py:82
  738.0 114.3 %collective-permute-start.52 = (bf16[128,2048]{1,0:T(8,128)(2,1)}, bf16[128,2048]{1,0:T(8,128)(2,1)S(1)}, u32[]{:S(2)}, u32[]{:S(2)}) collective-permute-start(bf16[128,2048]{1,0:T(8,128)(2,1)} %get-tuple-element.44), channel_id=1, source_target_pairs={{0,16},{4,20},{8,24},{12,28},{16,0},{20,4},{24,8},{28,12},{1,17},{... | collective-permute-start | bytes 1572872 | tf_op jit(solution)/shard_map/ppermute | solution.py:82
  786.0 68.1 %collective-permute-start.53 = (bf16[128,2048]{1,0:T(8,128)(2,1)}, bf16[128,2048]{1,0:T(8,128)(2,1)S(1)}, u32[]{:S(2)}, u32[]{:S(2)}) collective-permute-start(bf16[128,2048]{1,0:T(8,128)(2,1)} %get-tuple-element.44), channel_id=1, source_target_pairs={{0,24},{4,28},{8,16},{12,20},{16,8},{20,12},{24,0},{28,4},{1,25},{... | collective-permute-start | bytes 1572872 | tf_op jit(solution)/shard_map/ppermute | solution.py:82
  789.0 67.6 %collective-permute-start.50 = (bf16[128,2048]{1,0:T(8,128)(2,1)}, bf16[128,2048]{1,0:T(8,128)(2,1)S(1)}, u32[]{:S(2)}, u32[]{:S(2)}) collective-permute-start(bf16[128,2048]{1,0:T(8,128)(2,1)} %get-tuple-element.44), channel_id=1, source_target_pairs={{0,4},{4,0},{8,12},{12,8},{16,20},{20,16},{24,28},{28,24},{1,5},{5... | collective-permute-start | bytes 1572872 | tf_op jit(solution)/shard_map/ppermute | solution.py:82
  861.3 159.2 %collective-permute-start.115 = (bf16[352,2048]{1,0:T(8,128)(2,1)}, bf16[352,2048]{1,0:T(8,128)(2,1)}, u32[]{:S(2)}, u32[]{:S(2)}) collective-permute-start(bf16[352,2048]{1,0:T(8,128)(2,1)} %fusion.18), channel_id=1, source_target_pairs={{1,2},{2,1},{5,6},{6,5},{9,10},{10,9},{13,14},{14,13},{17,18},{18,... | collective-permute-start | bytes 4325384 | tf_op jit(solution)/shard_map/ppermute | solution.py:120
  864.7 123.8 %all-to-all-start.11 = ((bf16[8,128,704]{1,2,0:T(8,128)(2,1)}), bf16[8,128,704]{1,2,0:T(8,128)(2,1)}, u32[]{:S(2)}, u32[]{:S(2)}) async-start(bf16[8,128,704]{1,2,0:T(8,128)(2,1)} %fusion.20), calls=%async_computation.11 | async-start | bytes 2883584 | tf_op jit(solution)/shard_map/all_to_all | solution.py:104
  900.7 99.0 %collective-permute-start.89 = (bf16[2,128,2048]{2,1,0:T(8,128)(2,1)S(1)}, bf16[2,128,2048]{2,1,0:T(8,128)(2,1)S(1)}, u32[]{:S(2)}, u32[]{:S(2)}) collective-permute-start(bf16[2,128,2048]{2,1,0:T(8,128)(2,1)S(1)} %get-tuple-element.208), channel_id=1, source_target_pairs={{0,1},{3,2},{4,5},{7,6},{8,9},{11,10},{12,13},{15,14},{16,17},{19,... | collective-permute-start | bytes 3145736 | tf_op jit(solution)/shard_map/ppermute | solution.py:113
  988.5 37.5 %collective-permute-start.55 = (bf16[4,128,2048]{2,1,0:T(8,128)(2,1)}, bf16[4,128,2048]{2,1,0:T(8,128)(2,1)}, u32[]{:S(2)}, u32[]{:S(2)}) collective-permute-start(bf16[4,128,2048]{2,1,0:T(8,128)(2,1)} %pad_maximum_fusion.5), channel_id=1, source_target_pairs={{0,4},{4,0},{8,12},{12,8},{16,20},{20,16},{24,28},{28,24},{1,5},{5... | collective-permute-start | bytes 6291464 | tf_op jit(solution)/shard_map/ppermute | solution.py:82
  1010.3 69.8 %collective-permute-start.81 = (bf16[2,8,128,768]{3,2,1,0:T(8,128)(2,1)}, bf16[2,8,128,768]{3,2,1,0:T(8,128)(2,1)}, u32[]{:S(2)}, u32[]{:S(2)}) collective-permute-start(bf16[2,8,128,768]{3,2,1,0:T(8,128)(2,1)} %get-tuple-element.204), channel_id=1, source_target_pairs={{0,1},{3,2},{4,5},{7,6},{8,9},{11,10},{12,13},{15,14},{16,17},{19,... | collective-permute-start | bytes 9437192 | tf_op jit(solution)/shard_map/ppermute | solution.py:113
  1024.5 130.6 %collective-permute-start.116 = (bf16[2,352,2048]{2,1,0:T(8,128)(2,1)S(1)}, bf16[2,352,2048]{2,1,0:T(8,128)(2,1)S(1)}, u32[]{:S(2)}, u32[]{:S(2)}) collective-permute-start(bf16[2,352,2048]{2,1,0:T(8,128)(2,1)S(1)} %maximum_select_fusion.7), channel_id=1, source_target_pairs={{1,0},{2,3},{5,4},{6,7},{9,8},{10,11},{13,12},{14,15},{17,16},{18,... | collective-permute-start | bytes 8650760 | tf_op jit(solution)/shard_map/ppermute | solution.py:122
  1083.0 69.0 %collective-permute-start.92 = (bf16[2,128,2048]{2,1,0:T(8,128)(2,1)S(1)}, bf16[2,128,2048]{2,1,0:T(8,128)(2,1)S(1)}, u32[]{:S(2)}, u32[]{:S(2)}) collective-permute-start(bf16[2,128,2048]{2,1,0:T(8,128)(2,1)S(1)} %maximum_select_fusion.9), channel_id=1, source_target_pairs={{1,0},{2,3},{5,4},{6,7},{9,8},{10,11},{13,12},{14,15},{17,16},{18,... | collective-permute-start | bytes 3145736 | tf_op jit(solution)/shard_map/ppermute | solution.py:122
  1084.6 130.8 %collective-permute-start.108 = (bf16[2,128,5632]{1,2,0:T(8,128)(2,1)}, bf16[2,128,5632]{1,2,0:T(8,128)(2,1)}, u32[]{:S(2)}, u32[]{:S(2)}) collective-permute-start(bf16[2,128,5632]{1,2,0:T(8,128)(2,1)} %maximum_select_fusion.5), channel_id=1, source_target_pairs={{1,0},{2,3},{5,4},{6,7},{9,8},{10,11},{13,12},{14,15},{17,16},{18,... | collective-permute-start | bytes 8650760 | tf_op jit(solution)/shard_map/ppermute | solution.py:122
  1085.9 182.8 %collective-permute-start.100 = (bf16[2,128,5632]{1,2,0:T(8,128)(2,1)}, bf16[2,128,5632]{1,2,0:T(8,128)(2,1)}, u32[]{:S(2)}, u32[]{:S(2)}) collective-permute-start(bf16[2,128,5632]{1,2,0:T(8,128)(2,1)} %maximum_select_fusion.3), channel_id=1, source_target_pairs={{1,0},{2,3},{5,4},{6,7},{9,8},{10,11},{13,12},{14,15},{17,16},{18,... | collective-permute-start | bytes 8650760 | tf_op jit(solution)/shard_map/ppermute | solution.py:122
  1087.4 72.4 %collective-permute-start.63 = (bf16[3,128,2048]{2,1,0:T(8,128)(2,1)S(1)}, bf16[3,128,2048]{2,1,0:T(8,128)(2,1)S(1)}, u32[]{:S(2)}, u32[]{:S(2)}) collective-permute-start(bf16[3,128,2048]{2,1,0:T(8,128)(2,1)S(1)} %pad_maximum_fusion.15), channel_id=1, source_target_pairs={{0,4},{4,0},{8,12},{12,8},{16,20},{20,16},{24,28},{28,24},{1,5},{5... | collective-permute-start | bytes 4718600 | tf_op jit(solution)/shard_map/ppermute | solution.py:82
  1152.0 46.6 %collective-permute-start.82 = (bf16[8,128,768]{2,1,0:T(8,128)(2,1)S(1)}, bf16[8,128,768]{2,1,0:T(8,128)(2,1)}, u32[]{:S(2)}, u32[]{:S(2)}) collective-permute-start(bf16[8,128,768]{2,1,0:T(8,128)(2,1)S(1)} %select_bitcast_fusion), channel_id=1, source_target_pairs={{1,2},{2,1},{5,6},{6,5},{9,10},{10,9},{13,14},{14,13},{17,18},{18,... | collective-permute-start | bytes 4718600 | tf_op jit(solution)/shard_map/ppermute | solution.py:118
  1183.6 108.3 %collective-permute-start.101 = (bf16[2,8,128,704]{2,3,1,0:T(8,128)(2,1)}, bf16[2,8,128,704]{2,3,1,0:T(8,128)(2,1)}, u32[]{:S(2)}, u32[]{:S(2)}) collective-permute-start(bf16[2,8,128,704]{2,3,1,0:T(8,128)(2,1)} %get-tuple-element.218), channel_id=1, source_target_pairs={{0,1},{3,2},{4,5},{7,6},{8,9},{11,10},{12,13},{15,14},{16,17},{19,... | collective-permute-start | bytes 8650760 | tf_op jit(solution)/shard_map/ppermute | solution.py:113
  1187.9 123.5 %collective-permute-start.93 = (bf16[2,8,128,704]{2,3,0,1:T(8,128)(2,1)}, bf16[2,8,128,704]{2,3,0,1:T(8,128)(2,1)}, u32[]{:S(2)}, u32[]{:S(2)}) collective-permute-start(bf16[2,8,128,704]{2,3,0,1:T(8,128)(2,1)} %get-tuple-element.214), channel_id=1, source_target_pairs={{0,1},{3,2},{4,5},{7,6},{8,9},{11,10},{12,13},{15,14},{16,17},{19,... | collective-permute-start | bytes 8650760 | tf_op jit(solution)/shard_map/ppermute | solution.py:113
  1201.7 80.1 %all-to-all-start.7 = ((bf16[8,128,768]{2,1,0:T(8,128)(2,1)}), bf16[8,128,768]{2,1,0:T(8,128)(2,1)}, u32[]{:S(2)}, u32[]{:S(2)}) async-start(bf16[8,128,768]{2,1,0:T(8,128)(2,1)} %fusion.16), calls=%async_computation.7 | async-start | bytes 3145728 | tf_op jit(solution)/shard_map/all_to_all | solution.py:104
  1226.0 57.9 %collective-permute-start.65 = (bf16[128,2048]{1,0:T(8,128)(2,1)}, bf16[128,2048]{1,0:T(8,128)(2,1)S(1)}, u32[]{:S(2)}, u32[]{:S(2)}) collective-permute-start(bf16[128,2048]{1,0:T(8,128)(2,1)} %get-tuple-element.62), channel_id=1, source_target_pairs={{0,8},{4,12},{8,0},{12,4},{16,24},{20,28},{24,16},{28,20},{1,9},{5... | collective-permute-start | bytes 1572872 | tf_op jit(solution)/shard_map/ppermute | solution.py:82
  1227.9 57.5 %collective-permute-start.66 = (bf16[128,2048]{1,0:T(8,128)(2,1)}, bf16[128,2048]{1,0:T(8,128)(2,1)}, u32[]{:S(2)}, u32[]{:S(2)}) collective-permute-start(bf16[128,2048]{1,0:T(8,128)(2,1)} %get-tuple-element.64), channel_id=1, source_target_pairs={{0,16},{4,20},{8,24},{12,28},{16,0},{20,4},{24,8},{28,12},{1,17},{... | collective-permute-start | bytes 1572872 | tf_op jit(solution)/shard_map/ppermute | solution.py:82
  1284.0 76.8 %collective-permute-start.109 = (bf16[2,352,2048]{2,1,0:T(8,128)(2,1)}, bf16[2,352,2048]{2,1,0:T(8,128)(2,1)S(1)}, u32[]{:S(2)}, u32[]{:S(2)}) collective-permute-start(bf16[2,352,2048]{2,1,0:T(8,128)(2,1)} %get-tuple-element.226), channel_id=1, source_target_pairs={{0,1},{3,2},{4,5},{7,6},{8,9},{11,10},{12,13},{15,14},{16,17},{19,... | collective-permute-start | bytes 8650760 | tf_op jit(solution)/shard_map/ppermute | solution.py:113
  1285.5 79.9 %collective-permute-start.83 = (bf16[128,6144]{0,1:T(8,128)(2,1)S(1)}, bf16[128,6144]{0,1:T(8,128)(2,1)S(1)}, u32[]{:S(2)}, u32[]{:S(2)}) collective-permute-start(bf16[128,6144]{0,1:T(8,128)(2,1)S(1)} %bitcast.973), channel_id=1, source_target_pairs={{1,2},{2,1},{5,6},{6,5},{9,10},{10,9},{13,14},{14,13},{17,18},{18,... | collective-permute-start | bytes 4718600 | tf_op jit(solution)/shard_map/ppermute | solution.py:120
  1291.6 76.5 %collective-permute-start.69 = (bf16[128,2048]{1,0:T(8,128)(2,1)S(1)}, bf16[128,2048]{1,0:T(8,128)(2,1)S(1)}, u32[]{:S(2)}, u32[]{:S(2)}) collective-permute-start(bf16[128,2048]{1,0:T(8,128)(2,1)S(1)} %get-tuple-element.36), channel_id=1, source_target_pairs={{0,8},{4,12},{8,0},{12,4},{16,24},{20,28},{24,16},{28,20},{1,9},{5... | collective-permute-start | bytes 1572872 | tf_op jit(solution)/shard_map/ppermute | solution.py:82
  1291.9 76.9 %collective-permute-start.70 = (bf16[128,2048]{1,0:T(8,128)(2,1)S(1)}, bf16[128,2048]{1,0:T(8,128)(2,1)S(1)}, u32[]{:S(2)}, u32[]{:S(2)}) collective-permute-start(bf16[128,2048]{1,0:T(8,128)(2,1)S(1)} %get-tuple-element.36), channel_id=1, source_target_pairs={{0,16},{4,20},{8,24},{12,28},{16,0},{20,4},{24,8},{28,12},{1,17},{... | collective-permute-start | bytes 1572872 | tf_op jit(solution)/shard_map/ppermute | solution.py:82
  1311.4 59.3 %collective-permute-start.71 = (bf16[128,2048]{1,0:T(8,128)(2,1)S(1)}, bf16[128,2048]{1,0:T(8,128)(2,1)S(1)}, u32[]{:S(2)}, u32[]{:S(2)}) collective-permute-start(bf16[128,2048]{1,0:T(8,128)(2,1)S(1)} %get-tuple-element.36), channel_id=1, source_target_pairs={{0,24},{4,28},{8,16},{12,20},{16,8},{20,12},{24,0},{28,4},{1,25},{... | collective-permute-start | bytes 1572872 | tf_op jit(solution)/shard_map/ppermute | solution.py:82
  1370.6 163.9 %collective-permute-start.84 = (bf16[2,128,6144]{1,2,0:T(8,128)(2,1)}, bf16[2,128,6144]{1,2,0:T(8,128)(2,1)}, u32[]{:S(2)}, u32[]{:S(2)}) collective-permute-start(bf16[2,128,6144]{1,2,0:T(8,128)(2,1)} %maximum_select_fusion.1), channel_id=1, source_target_pairs={{1,0},{2,3},{5,4},{6,7},{9,8},{10,11},{13,12},{14,15},{17,16},{18,... | collective-permute-start | bytes 9437192 | tf_op jit(solution)/shard_map/ppermute | solution.py:122
  1376.9 143.8 %collective-permute-start.111 = (bf16[352,2048]{1,0:T(8,128)(2,1)}, bf16[352,2048]{1,0:T(8,128)(2,1)}, u32[]{:S(2)}, u32[]{:S(2)}) collective-permute-start(bf16[352,2048]{1,0:T(8,128)(2,1)} %fusion.19), channel_id=1, source_target_pairs={{1,2},{2,1},{5,6},{6,5},{9,10},{10,9},{13,14},{14,13},{17,18},{18,... | collective-permute-start | bytes 4325384 | tf_op jit(solution)/shard_map/ppermute | solution.py:120
  1380.4 39.3 %all-to-all-start.10 = ((bf16[8,128,704]{1,2,0:T(8,128)(2,1)}), bf16[8,128,704]{1,2,0:T(8,128)(2,1)}, u32[]{:S(2)}, u32[]{:S(2)}) async-start(bf16[8,128,704]{1,2,0:T(8,128)(2,1)} %fusion.21), calls=%async_computation.10 | async-start | bytes 2883584 | tf_op jit(solution)/shard_map/all_to_all | solution.py:104
  1414.0 130.8 %collective-permute-start.73 = (bf16[4,128,2048]{2,1,0:T(8,128)(2,1)}, bf16[4,128,2048]{2,1,0:T(8,128)(2,1)}, u32[]{:S(2)}, u32[]{:S(2)}) collective-permute-start(bf16[4,128,2048]{2,1,0:T(8,128)(2,1)} %pad_maximum_fusion.7), channel_id=1, source_target_pairs={{0,4},{4,0},{8,12},{12,8},{16,20},{20,16},{24,28},{28,24},{1,5},{5... | collective-permute-start | bytes 6291464 | tf_op jit(solution)/shard_map/ppermute | solution.py:82
  1419.7 107.2 %all-to-all-start.8 = ((bf16[8,128,704]{1,2,0:T(8,128)(2,1)}), bf16[8,128,704]{1,2,0:T(8,128)(2,1)S(1)}, u32[]{:S(2)}, u32[]{:S(2)}) async-start(bf16[8,128,704]{1,2,0:T(8,128)(2,1)} %fusion.23), calls=%async_computation.8 | async-start | bytes 2883584 | tf_op jit(solution)/shard_map/all_to_all | solution.py:104
  1423.6 352.4 %all-reduce.2.cloned.1.call-start = ((), (), s32[]{:S(2)}) async-start(), calls=%async_computation.12 | async-start | bytes 229376 | tf_op jit(solution)/shard_map/psum | solution.py:313
  1424.3 106.0 %collective-permute-start.85 = (bf16[2,128,2048]{2,1,0:T(8,128)(2,1)}, bf16[2,128,2048]{2,1,0:T(8,128)(2,1)}, u32[]{:S(2)}, u32[]{:S(2)}) collective-permute-start(bf16[2,128,2048]{2,1,0:T(8,128)(2,1)} %get-tuple-element.210), channel_id=1, source_target_pairs={{0,1},{3,2},{4,5},{7,6},{8,9},{11,10},{12,13},{15,14},{16,17},{19,... | collective-permute-start | bytes 3145736 | tf_op jit(solution)/shard_map/ppermute | solution.py:113
  1517.2 80.2 %collective-permute-start.77 = (bf16[2,8,128,768]{3,2,0,1:T(8,128)(2,1)}, bf16[2,8,128,768]{3,2,0,1:T(8,128)(2,1)}, u32[]{:S(2)}, u32[]{:S(2)}) collective-permute-start(bf16[2,8,128,768]{3,2,0,1:T(8,128)(2,1)} %get-tuple-element.206), channel_id=1, source_target_pairs={{0,1},{3,2},{4,5},{7,6},{8,9},{11,10},{12,13},{15,14},{16,17},{19,... | collective-permute-start | bytes 9437192 | tf_op jit(solution)/shard_map/ppermute | solution.py:113
  1543.2 244.0 %collective-permute-start.112 = (bf16[2,352,2048]{2,1,0:T(8,128)(2,1)}, bf16[2,352,2048]{2,1,0:T(8,128)(2,1)}, u32[]{:S(2)}, u32[]{:S(2)}) collective-permute-start(bf16[2,352,2048]{2,1,0:T(8,128)(2,1)} %maximum_select_fusion.6), channel_id=1, source_target_pairs={{1,0},{2,3},{5,4},{6,7},{9,8},{10,11},{13,12},{14,15},{17,16},{18,... | collective-permute-start | bytes 8650760 | tf_op jit(solution)/shard_map/ppermute | solution.py:122
  1564.8 218.7 %collective-permute-start.88 = (bf16[2,128,2048]{2,1,0:T(8,128)(2,1)}, bf16[2,128,2048]{2,1,0:T(8,128)(2,1)}, u32[]{:S(2)}, u32[]{:S(2)}) collective-permute-start(bf16[2,128,2048]{2,1,0:T(8,128)(2,1)} %maximum_select_fusion.8), channel_id=1, source_target_pairs={{1,0},{2,3},{5,4},{6,7},{9,8},{10,11},{13,12},{14,15},{17,16},{18,... | collective-permute-start | bytes 3145736 | tf_op jit(solution)/shard_map/ppermute | solution.py:122
  1576.4 224.0 %collective-permute-start.104 = (bf16[2,128,5632]{1,2,0:T(8,128)(2,1)}, bf16[2,128,5632]{1,2,0:T(8,128)(2,1)}, u32[]{:S(2)}, u32[]{:S(2)}) collective-permute-start(bf16[2,128,5632]{1,2,0:T(8,128)(2,1)} %maximum_select_fusion.4), channel_id=1, source_target_pairs={{1,0},{2,3},{5,4},{6,7},{9,8},{10,11},{13,12},{14,15},{17,16},{18,... | collective-permute-start | bytes 8650760 | tf_op jit(solution)/shard_map/ppermute | solution.py:122
  1577.7 232.9 %collective-permute-start.96 = (bf16[2,128,5632]{1,2,0:T(8,128)(2,1)}, bf16[2,128,5632]{1,2,0:T(8,128)(2,1)}, u32[]{:S(2)}, u32[]{:S(2)}) collective-permute-start(bf16[2,128,5632]{1,2,0:T(8,128)(2,1)} %maximum_select_fusion.2), channel_id=1, source_target_pairs={{1,0},{2,3},{5,4},{6,7},{9,8},{10,11},{13,12},{14,15},{17,16},{18,... | collective-permute-start | bytes 8650760 | tf_op jit(solution)/shard_map/ppermute | solution.py:122
  1607.2 172.2 %all-to-all-start.6 = ((bf16[8,128,768]{2,1,0:T(8,128)(2,1)}), bf16[8,128,768]{2,1,0:T(8,128)(2,1)S(1)}, u32[]{:S(2)}, u32[]{:S(2)}) async-start(bf16[8,128,768]{2,1,0:T(8,128)(2,1)} %fusion.17), calls=%async_computation.6 | async-start | bytes 3145728 | tf_op jit(solution)/shard_map/all_to_all | solution.py:104
  1799.1 91.9 %collective-permute-start.80 = (bf16[2,128,6144]{1,2,0:T(8,128)(2,1)}, bf16[2,128,6144]{1,2,0:T(8,128)(2,1)}, u32[]{:S(2)}, u32[]{:S(2)}) collective-permute-start(bf16[2,128,6144]{1,2,0:T(8,128)(2,1)} %maximum_select_fusion), channel_id=1, source_target_pairs={{1,0},{2,3},{5,4},{6,7},{9,8},{10,11},{13,12},{14,15},{17,16},{18,... | collective-permute-start | bytes 9437192 | tf_op jit(solution)/shard_map/ppermute | solution.py:122
  (242 other events, 3476.1 us)
Sparse Core Ops, SparseCore 0:
  1604.1 171.8 all-reduce.1

commit v2 on v1

--- a/solution.py
+++ b/solution.py
@@ -1,6 +1,10 @@
+import functools
+
 import jax
 import jax.numpy as jnp
 from jax import lax
+from jax.experimental import pallas as pl
+from jax.experimental.pallas import tpu as pltpu
 from jax.sharding import PartitionSpec as P
 
 HEADS = 32
@@ -68,6 +72,608 @@
         ],
         axis=-1,
     )
+
+
+def call(kernel, grid, in_specs, out_specs, out_shape, flops, moved, vmem=48, scratch=()):
+    return pl.pallas_call(
+        kernel,
+        grid=grid or (),
+        in_specs=in_specs,
+        out_specs=out_specs,
+        out_shape=out_shape,
+        scratch_shapes=scratch,
+        compiler_params=pltpu.CompilerParams(vmem_limit_bytes=vmem << 20),
+        cost_estimate=pl.CostEstimate(flops=flops, bytes_accessed=moved, transcendentals=0),
+    )
+
+
+def whole(shape):
+    zeros = (0,) * len(shape)
+    return pl.BlockSpec(shape, lambda *_: zeros, pipeline_mode=pl.Buffered(1))
+
+
+def shape_of(shape, dtype):
+    return jax.ShapeDtypeStruct(shape, dtype)
+
+
+def head_lanes(values, head, head_size):
+    lanes = lax.broadcasted_iota(jnp.int32, values.shape, 1)
+    inside = (lanes >= head * head_size) & (lanes < (head + 1) * head_size)
+    return jnp.where(inside, values, jnp.zeros_like(values))
+
+
+def join_rows(own_ref, pair_ref):
+    pieces = []
+    for s in range(own_ref.shape[0]):
+        pieces += [own_ref[s], pair_ref[s]]
+    return jnp.concatenate(pieces, axis=0)
+
+
+def part_rows(values, keep_ref, send_ref):
+    count, half, _ = keep_ref.shape
+    for s in range(count):
+        first = 2 * s * half
+        keep_ref[s] = values[first : first + half]
+        send_ref[s] = values[first + half : first + 2 * half].astype(bf16)
+
+
+def attend_kernel(
+    own_ref, pair_ref, w_ref, bias_ref, cos_ref, low_ref, high_ref, mask_ref, out_w_ref,
+    keep_ref, send_ref, normed_ref, q_ref, k_ref, v_ref, mixed_ref,
+    *, heads, head_size,
+):
+    cols = heads * head_size
+    normed = join_rows(own_ref, pair_ref)
+    normed_ref[...] = normed
+    joined = dot(normed, w_ref[...]) + bias_ref[...]
+    cosine, low, high = cos_ref[...], low_ref[...], high_ref[...]
+
+    def turn(v):
+        return v * cosine + pltpu.roll(v, cols - HALF, 1) * low + pltpu.roll(v, HALF, 1) * high
+
+    q = turn(joined[:, :cols]).astype(bf16)
+    k = turn(joined[:, cols : 2 * cols]).astype(bf16)
+    v = joined[:, 2 * cols :].astype(bf16)
+    q_ref[...] = q
+    k_ref[...] = k
+    v_ref[...] = v
+    tokens = mask_ref.shape[1]
+    mixed = []
+    for s in range(mask_ref.shape[0]):
+        at = slice(s * tokens, (s + 1) * tokens)
+        allowed = mask_ref[s] > 0.5
+        total = None
+        for h in range(heads):
+            scores = dot_t(head_lanes(q[at], h, head_size), k[at]) * head_size ** (-0.5)
+            masked = jnp.where(allowed, scores, -1000000000.0)
+            raised = jnp.exp(masked - jnp.max(masked, axis=-1, keepdims=True))
+            probs = raised / jnp.sum(raised, axis=-1, keepdims=True)
+            term = dot(probs.astype(bf16), head_lanes(v[at], h, head_size))
+            total = term if total is None else total + term
+        mixed.append(total.astype(bf16))
+    mixed = jnp.concatenate(mixed, axis=0)
+    mixed_ref[...] = mixed
+    part_rows(dot(mixed, out_w_ref[...]), keep_ref, send_ref)
+
+
+def attend_back_kernel(
+    own_ref, pair_ref, w_ref, cos_ref, low_ref, high_ref, mask_ref, out_w_ref, q_ref, k_ref, v_ref,
+    keep_ref, send_ref, branch_ref, joined_ref, bias_ref,
+    *, heads, head_size,
+):
+    cols = heads * head_size
+    scale = head_size ** (-0.5)
+    branch = join_rows(own_ref, pair_ref)
+    branch_ref[...] = branch
+    grad_mixed = dot_t(branch, out_w_ref[...]).astype(bf16)
+    cosine, low, high = cos_ref[...], low_ref[...], high_ref[...]
+
+    def turn_back(v):
+        return v * cosine - pltpu.roll(v, cols - HALF, 1) * low - pltpu.roll(v, HALF, 1) * high
+
+    q, k, v = q_ref[...], k_ref[...], v_ref[...]
+    tokens = mask_ref.shape[1]
+    grad_q, grad_k, grad_v = [], [], []
+    for s in range(mask_ref.shape[0]):
+        at = slice(s * tokens, (s + 1) * tokens)
+        allowed = mask_ref[s] > 0.5
+        sums = [None, None, None]
+        for h in range(heads):
+            q_h = head_lanes(q[at], h, head_size)
+            g_h = head_lanes(grad_mixed[at], h, head_size)
+            scores = dot_t(q_h, k[at]) * scale
+            masked = jnp.where(allowed, scores, -1000000000.0)
+            raised = jnp.exp(masked - jnp.max(masked, axis=-1, keepdims=True))
+            probs = raised / jnp.sum(raised, axis=-1, keepdims=True)
+            grad_probs = dot_t(g_h, v[at])
+            inner = jnp.sum(probs * grad_probs, axis=-1, keepdims=True)
+            grad_scores = (probs * (grad_probs - inner)).astype(bf16)
+            terms = (
+                dot(grad_scores, head_lanes(k[at], h, head_size)),
+                t_dot(grad_scores, q_h),
+                t_dot(probs.astype(bf16), g_h),
+            )
+            sums = [t if a is None else a + t for a, t in zip(sums, terms)]
+        grad_q.append(sums[0] * scale)
+        grad_k.append(sums[1] * scale)
+        grad_v.append(sums[2])
+    joined = jnp.concatenate(
+        [
+            turn_back(jnp.concatenate(grad_q, axis=0)),
+            turn_back(jnp.concatenate(grad_k, axis=0)),
+            jnp.concatenate(grad_v, axis=0),
+        ],
+        axis=1,
+    ).astype(bf16)
+    joined_ref[...] = joined
+
+    @pl.when(pl.program_id(0) == 0)
+    def _():
+        bias_ref[...] = jnp.zeros_like(bias_ref)
+
+    bias_ref[...] += jnp.sum(joined.astype(f32), axis=0, keepdims=True)
+    part_rows(dot_t(joined, w_ref[...]), keep_ref, send_ref)
+
+
+def feed_kernel(
+    own_ref, pair_ref, w_ref, down_ref, keep_ref, send_ref, normed_ref, gate_ref, upper_ref, inner_ref
+):
+    normed = join_rows(own_ref, pair_ref)
+    normed_ref[...] = normed
+    flat = (normed.shape[1], w_ref.shape[3])
+    gate = dot(normed, w_ref[:, 0].reshape(flat))
+    upper = dot(normed, w_ref[:, 1].reshape(flat))
+    gate_ref[...] = gate
+    upper_ref[...] = upper
+    inner = (gate / (1.0 + jnp.exp(-gate)) * upper).astype(bf16)
+    inner_ref[...] = inner
+    part_rows(dot(inner, down_ref[...]), keep_ref, send_ref)
+
+
+def feed_back_kernel(
+    own_ref, pair_ref, w_ref, down_ref, gate_ref, upper_ref,
+    keep_ref, send_ref, down_in_ref, grad_gate_ref, grad_upper_ref,
+):
+    down_in = join_rows(own_ref, pair_ref)
+    down_in_ref[...] = down_in
+    flat = (down_in.shape[1], w_ref.shape[3])
+    grad_inner = dot_t(down_in, down_ref[...])
+    gate, upper = gate_ref[...], upper_ref[...]
+    sigmoid = 1.0 / (1.0 + jnp.exp(-gate))
+    slope = sigmoid * (1.0 + gate * (1.0 - sigmoid))
+    grad_gate = (grad_inner * upper * slope).astype(bf16)
+    grad_upper = (grad_inner * (gate * sigmoid)).astype(bf16)
+    grad_gate_ref[...] = grad_gate
+    grad_upper_ref[...] = grad_upper
+    partial = dot_t(grad_gate, w_ref[:, 0].reshape(flat)) + dot_t(grad_upper, w_ref[:, 1].reshape(flat))
+    part_rows(partial, keep_ref, send_ref)
+
+
+def combine_kernel(keep_ref, arrived_ref, own_ref, x_ref, y_ref, d_ref):
+    own_ref[...] = keep_ref[0] + arrived_ref[0].astype(f32)
+    for k, ref in ((1, x_ref), (2, y_ref), (3, d_ref)):
+        ref[...] = (keep_ref[k] + arrived_ref[k].astype(f32)).astype(bf16)
+
+
+def received(own_ref, x_ref, y_ref, d_ref):
+    return own_ref[...] + x_ref[...].astype(f32) + (y_ref[...].astype(f32) + d_ref[...].astype(f32))
+
+
+def norm_first_kernel(state_ref, gain_ref, shift_ref, normed_ref):
+    xhat, _ = normalize(state_ref[...])
+    normed_ref[...] = (xhat * gain_ref[...] + shift_ref[...]).astype(bf16)
+
+
+def norm_kernel(state_ref, own_ref, x_ref, y_ref, d_ref, gain_ref, shift_ref, new_ref, normed_ref):
+    state = state_ref[...] + received(own_ref, x_ref, y_ref, d_ref)
+    new_ref[...] = state
+    xhat, _ = normalize(state)
+    normed_ref[...] = (xhat * gain_ref[...] + shift_ref[...]).astype(bf16)
+
+
+def last_kernel(state_ref, own_ref, x_ref, y_ref, d_ref, out_ref):
+    out_ref[...] = (state_ref[...] + received(own_ref, x_ref, y_ref, d_ref)).astype(bf16)
+
+
+def norm_back_kernel(
+    grad_ref, own_ref, x_ref, y_ref, d_ref, state_ref, gain_ref, new_ref, low_ref, sums_ref
+):
+    grad_normed = received(own_ref, x_ref, y_ref, d_ref)
+    xhat, inverse = normalize(state_ref[...])
+    scaled = grad_normed * gain_ref[...]
+    inner = jnp.mean(scaled * xhat, axis=-1, keepdims=True)
+    back = inverse * (scaled - jnp.mean(scaled, axis=-1, keepdims=True) - xhat * inner)
+    grad = grad_ref[...] + back
+    new_ref[...] = grad
+    low_ref[...] = grad.astype(bf16)
+    sums_ref[0:1] = jnp.sum(grad_normed * xhat, axis=0, keepdims=True)
+    sums_ref[1:2] = jnp.sum(grad_normed, axis=0, keepdims=True)
+
+
+def weight_rows_kernel(first_ref, second_ref, first_grad_ref, second_grad_ref, out_ref):
+    product = t_dot(first_ref[...], first_grad_ref[...]) + t_dot(second_ref[...], second_grad_ref[...])
+    product = product.astype(bf16)
+    half = product.shape[0] // 2
+    out_ref[0] = product[:half].reshape(out_ref.shape[1:])
+    out_ref[1] = product[half:].reshape(out_ref.shape[1:])
+
+
+def make_cube(mesh):
+    shards, reps = 8, 4
+
+    def swap(values, bit):
+        return lax.ppermute(values, "shard", [(i, i ^ bit) for i in range(shards)])
+
+    def local(
+        hidden_in,
+        segments,
+        ln1_gain,
+        ln1_bias,
+        qkv_weight,
+        qkv_bias,
+        out_weight,
+        ln2_gain,
+        ln2_bias,
+        gate_weight,
+        up_weight,
+        down_weight,
+        cotangent,
+    ):
+        layers, rows = qkv_weight.shape[:2]
+        width = hidden_in.shape[2]
+        tokens = hidden_in.shape[1]
+        part = tokens // 2
+        head_size = width // HEADS
+        heads = HEADS // shards
+        cols = heads * head_size
+        hidden = down_weight.shape[1]
+        chips = shards // 2
+        many = chips * tokens
+        step = 2 * tokens
+        me = lax.axis_index("shard")
+        core = me % 2
+        rep = lax.axis_index("rep")
+        lower = rep < 2
+        within = (rep == 1) | (rep == 2)
+
+        smalls = (ln1_gain, ln1_bias, ln2_gain, ln2_bias, qkv_bias, segments.astype(bf16))
+        small = lax.all_gather(
+            jnp.concatenate([v.reshape(-1) for v in smalls]), "shard", axis=0, tiled=False
+        )
+        cuts = [0]
+        for v in smalls:
+            cuts.append(cuts[-1] + v.size)
+
+        def whole_of(index):
+            like = smalls[index]
+            cut = small[:, cuts[index] : cuts[index + 1]].reshape(shards, layers, like.shape[1])
+            return cut.transpose(1, 0, 2).reshape(layers, -1).astype(f32)
+
+        gain1, shift1, gain2, shift2 = (whole_of(i) for i in range(4))
+        bias_all = whole_of(4).reshape(layers, 3, shards, cols)
+        bias_own = lax.dynamic_index_in_dim(bias_all, me, axis=2, keepdims=False)
+        bias_own = bias_own.reshape(layers, 1, 3 * cols)
+        all_segments = small[:, cuts[5] : cuts[6]]
+
+        places = jnp.arange(tokens, dtype=jnp.int32)
+        places = jnp.where(core == 0, places, (places + part) % tokens)
+        exponents = jnp.arange(HALF, dtype=f32) * (2.0 / ROTARY)
+        inverse = 10000.0 ** (-exponents)
+        masks, tables = [], []
+        for h in range(2):
+            wanted = (me // 2 ^ jnp.arange(chips)) * 2 + h
+            picked = (wanted[:, None] == jnp.arange(shards)[None]).astype(bf16)
+            numbers = dot(picked, all_segments)
+            numbers = jnp.where(core == 0, numbers, jnp.roll(numbers, part, axis=1))
+            earlier = numbers[:, None, :] < numbers[:, :, None]
+            positions = places - jnp.sum(earlier.astype(jnp.int32), axis=-1)
+            allowed = (numbers[:, None, :] == numbers[:, :, None]) & (
+                places[None, :] <= places[:, None]
+            )
+            masks.append(allowed.astype(f32))
+            angles = positions.astype(f32).reshape(many, 1) * inverse
+            cosine, sine = jnp.cos(angles), jnp.sin(angles)
+            zero8 = jnp.zeros_like(sine)
+            rest = jnp.zeros((many, head_size - ROTARY), f32)
+            tables.append(
+                [
+                    jnp.tile(jnp.concatenate(pieces, axis=1), (1, heads))
+                    for pieces in (
+                        (cosine, cosine, rest + 1.0),
+                        (-sine, zero8, rest),
+                        (zero8, sine, rest),
+                    )
+                ]
+            )
+
+        def spread(blocks):
+            return lax.all_to_all(blocks, "shard", split_axis=0, concat_axis=0, tiled=False)
+
+        def qkv_columns(weight):
+            cut = weight.reshape(rows, 3, shards, cols).transpose(2, 0, 1, 3)
+            return spread(cut.reshape(shards, rows, 3 * cols)).reshape(width, 3 * cols)
+
+        def feed_columns(gate, up):
+            both = jnp.stack([v.reshape(rows, shards, hidden).transpose(1, 0, 2) for v in (gate, up)], axis=1)
+            return spread(both)
+
+        proj_in, feed_in = [], []
+        for layer in range(layers):
+            proj_in.append(qkv_columns(qkv_weight[layer]))
+            feed_in.append(feed_columns(gate_weight[layer], up_weight[layer]))
+
+        def gather(own):
+            x, y, d = swap(own, 2), swap(own, 4), swap(own, 6)
+            mine = jnp.stack([own, x, y, d])
+            return mine, swap(mine, 1)
+
+        combine = call(
+            combine_kernel,
+            None,
+            [pl.BlockSpec(memory_space=pltpu.VMEM)] * 2,
+            [pl.BlockSpec(memory_space=pltpu.VMEM)] * 4,
+            [shape_of((part, width), f32)] + [shape_of((part, width), bf16)] * 3,
+            1 << 20,
+            5 << 20,
+            16,
+        )
+
+        def scatter_sum(keep, send):
+            own, x, y, d = combine(keep, swap(send, 1))
+            return own, swap(x, 2), swap(y, 4), swap(d, 6)
+
+        steps = chips // 2
+        piece = pl.BlockSpec((2, part, width), lambda i: (i, 0, 0))
+
+        def row_block(n):
+            return pl.BlockSpec((step, n), lambda i: (i, 0))
+
+        mask_block = pl.BlockSpec((2, tokens, tokens), lambda i: (i, 0, 0))
+        table_blocks = [row_block(cols)] * 3
+        part_shapes = [
+            shape_of((chips, part, width), f32),
+            shape_of((chips, part, width), bf16),
+        ]
+        options = dict(heads=heads, head_size=head_size)
+        attend_flops = 2 * many * width * 4 * cols
+        feed_flops = 2 * many * width * 3 * hidden
+        attend = call(
+            functools.partial(attend_kernel, **options),
+            (steps,),
+            [piece, piece, whole((width, 3 * cols)), whole((1, 3 * cols))]
+            + table_blocks
+            + [mask_block, whole((cols, width))],
+            [piece, piece, row_block(width)] + [row_block(cols)] * 4,
+            part_shapes + [shape_of((many, width), bf16)] + [shape_of((many, cols), bf16)] * 4,
+            attend_flops,
+            16 << 20,
+        )
+        attend_back = call(
+            functools.partial(attend_back_kernel, **options),
+            (steps,),
+            [piece, piece, whole((width, 3 * cols))]
+            + table_blocks
+            + [mask_block, whole((cols, width))]
+            + [row_block(cols)] * 3,
+            [piece, piece, row_block(width), row_block(3 * cols), pl.BlockSpec((1, 3 * cols), lambda i: (0, 0))],
+            part_shapes
+            + [shape_of((many, width), bf16), shape_of((many, 3 * cols), bf16), shape_of((1, 3 * cols), f32)],
+            attend_flops,
+            16 << 20,
+        )
+        feed_weights = [whole((shards, 2, rows, hidden)), whole((hidden, width))]
+        feed = call(
+            feed_kernel,
+            (steps,),
+            [piece, piece] + feed_weights,
+            [piece, piece, row_block(width)] + [row_block(hidden)] * 3,
+            part_shapes
+            + [shape_of((many, width), bf16)]
+            + [shape_of((many, hidden), f32)] * 2
+            + [shape_of((many, hidden), bf16)],
+            feed_flops,
+            24 << 20,
+        )
+        feed_back = call(
+            feed_back_kernel,
+            (steps,),
+            [piece, piece] + feed_weights + [row_block(hidden)] * 2,
+            [piece, piece, row_block(width)] + [row_block(hidden)] * 2,
+            part_shapes + [shape_of((many, width), bf16)] + [shape_of((many, hidden), bf16)] * 2,
+            feed_flops,
+            24 << 20,
+        )
+
+        def small_call(kernel, n_in, out_shape):
+            vmem = pl.BlockSpec(memory_space=pltpu.VMEM)
+            return call(kernel, None, [vmem] * n_in, [vmem] * len(out_shape), out_shape, 1 << 20, 3 << 20, 16)
+
+        low_shape, state_shape = shape_of((part, width), bf16), shape_of((part, width), f32)
+        norm_first = small_call(norm_first_kernel, 3, [low_shape])
+        norm = small_call(norm_kernel, 7, [state_shape, low_shape])
+        last = small_call(last_kernel, 5, [low_shape])
+        norm_back = small_call(norm_back_kernel, 7, [state_shape, low_shape, shape_of((2, width), f32)])
+
+        def weight_columns(lefts, rights):
+            n = rights[0].shape[1]
+            left = pl.BlockSpec((many, rows), lambda s: (0, s))
+            return call(
+                weight_rows_kernel,
+                (shards,),
+                [left, left, whole((many, n)), whole((many, n))],
+                pl.BlockSpec((2, 1, rows // 2, n), lambda s: (0, s, 0, 0)),
+                shape_of((2, shards, rows // 2, n), bf16),
+                4 * many * width * n,
+                8 << 20,
+                32,
+            )(*lefts, *rights)
+
+        def weight_rows(lefts, rights):
+            m = lefts[0].shape[1]
+            right = pl.BlockSpec((many, 512), lambda s: (0, s))
+            return call(
+                weight_rows_kernel,
+                (width // 512,),
+                [whole((many, m)), whole((many, m)), right, right],
+                pl.BlockSpec((2, m // 2, 512), lambda s: (0, 0, s)),
+                shape_of((2, m // 2, width), bf16),
+                4 * many * width * m,
+                8 << 20,
+                32,
+            )(*lefts, *rights)
+
+        def total(grad, turn=lambda v: v):
+            inward = lax.ppermute(grad, "rep", [(0, 1), (3, 2)])
+            gone = jnp.where(lower, 0, 1)
+
+            def add(index):
+                picked = [lax.dynamic_index_in_dim(v, index, 0, keepdims=False) for v in (grad, inward)]
+                return picked[0].astype(f32) + picked[1].astype(f32)
+
+            middle = lax.ppermute(add(gone).astype(bf16), "rep", [(1, 2), (2, 1)])
+            final = turn((add(1 - gone) + middle.astype(f32)).astype(bf16))
+            other = lax.ppermute(final, "rep", [(1, 2), (2, 1)])
+            final_out = lax.ppermute(final, "rep", [(1, 0), (2, 3)])
+            other_out = lax.ppermute(other, "rep", [(1, 0), (2, 3)])
+            mine = jnp.where(within, final, final_out)
+            theirs = jnp.where(within, other, other_out)
+            return jnp.where(lower, theirs, mine), jnp.where(lower, mine, theirs)
+
+        def from_rows(grad):
+            return jnp.concatenate(total(grad), axis=0).astype(f32)
+
+        def from_columns(grad):
+            halves = [v.transpose(1, 0, 2).reshape(rows // 2, -1) for v in total(grad, spread)]
+            return jnp.concatenate(halves, axis=0).astype(f32)
+
+        def from_qkv(grad):
+            halves = [
+                v.reshape(shards, rows // 2, 3, cols).transpose(1, 2, 0, 3).reshape(rows // 2, -1)
+                for v in total(grad, spread)
+            ]
+            return jnp.concatenate(halves, axis=0).astype(f32)
+
+        def share(values):
+            first, second = values[:part], values[part:]
+            kept = jnp.where(core == 0, first, second)
+            arrived = swap(jnp.where(core == 0, second, first), 1)
+            return [jnp.where(core == 0, kept, arrived), jnp.where(core == 0, arrived, kept)]
+
+        def unshare(halves):
+            kept = jnp.where(core == 0, halves[0], halves[1])
+            arrived = swap(jnp.where(core == 0, halves[1], halves[0]), 1)
+            both = [jnp.where(core == 0, kept, arrived), jnp.where(core == 0, arrived, kept)]
+            return jnp.concatenate(both, axis=0)[None]
+
+        states = [v.astype(f32) for v in share(hidden_in[0])]
+        lows = [norm_first(states[h], gain1[:1], shift1[:1])[0] for h in range(2)]
+        cotangents = share(cotangent[0])
+        outs = [None, None]
+        saved = [[None, None] for _ in range(layers)]
+        for layer in range(layers):
+            for h in range(2):
+                gathered = gather(lows[h])
+                keep, send, normed1, q, k, v, mixed = attend(
+                    *gathered, proj_in[layer], bias_own[layer], *tables[h], masks[h], out_weight[layer]
+                )
+                state_mid, low = norm(
+                    states[h], *scatter_sum(keep, send), gain2[layer : layer + 1], shift2[layer : layer + 1]
+                )
+                gathered = gather(low)
+                keep, send, normed2, gate, upper, inner = feed(
+                    *gathered, feed_in[layer], down_weight[layer]
+                )
+                saved[layer][h] = (
+                    (states[h], normed1, q, k, v, mixed, state_mid, normed2, gate, upper, inner)
+                )
+                arrived = scatter_sum(keep, send)
+                if layer + 1 < layers:
+                    states[h], lows[h] = norm(
+                        state_mid, *arrived, gain1[layer + 1 : layer + 2], shift1[layer + 1 : layer + 2]
+                    )
+                else:
+                    outs[h] = last(state_mid, *arrived)[0]
+        block_out = unshare(outs)
+
+        lows = cotangents
+        grads = [v.astype(f32) for v in cotangents]
+        weight_grads = [None] * layers
+        small_grads = [None] * layers
+        for layer in reversed(range(layers)):
+            down_ins, gate_grads, up_grads, branches, joineds = [], [], [], [], []
+            sums2, sums1, bias_sums = [], [], []
+            for h in range(2):
+                states1, normed1, q, k, v, mixed, state_mid, normed2, gate, upper, inner = saved[layer][h]
+                keep, send, down_in, grad_gate, grad_up = feed_back(
+                    *gather(lows[h]), feed_in[layer], down_weight[layer], gate, upper
+                )
+                grad_mid, low, sums = norm_back(
+                    grads[h], *scatter_sum(keep, send), state_mid, gain2[layer : layer + 1]
+                )
+                sums2.append(sums)
+                keep, send, branch, joined, bias_sum = attend_back(
+                    *gather(low), proj_in[layer], *tables[h], masks[h], out_weight[layer], q, k, v
+                )
+                grads[h], lows[h], sums = norm_back(
+                    grad_mid, *scatter_sum(keep, send), states1, gain1[layer : layer + 1]
+                )
+                sums1.append(sums)
+                bias_sums.append(bias_sum)
+                for kept, value in zip(
+                    (down_ins, gate_grads, up_grads, branches, joineds),
+                    (down_in, grad_gate, grad_up, branch, joined),
+                ):
+                    kept.append(value)
+
+            def both(index):
+                return [saved[layer][h][index] for h in range(2)]
+
+            weight_grads[layer] = (
+                from_qkv(weight_columns(both(1), joineds)),
+                from_rows(weight_rows(both(5), branches)),
+                from_columns(weight_columns(both(7), gate_grads)),
+                from_columns(weight_columns(both(7), up_grads)),
+                from_rows(weight_rows(both(10), down_ins)),
+            )
+            placed = jnp.where(
+                (jnp.arange(shards) == me)[None, :, None],
+                (bias_sums[0] + bias_sums[1]).reshape(3, 1, cols),
+                0.0,
+            )
+            small_grads[layer] = jnp.concatenate(
+                [(sums1[0] + sums1[1]).reshape(-1), (sums2[0] + sums2[1]).reshape(-1), placed.reshape(-1)]
+            )
+        input_grad = unshare(lows)
+
+        summed = jnp.stack(small_grads)
+        for bit in (1, 2, 4):
+            summed = summed + swap(summed, bit)
+        for bit in (1, 2):
+            summed = summed + lax.ppermute(summed, "rep", [(i, i ^ bit) for i in range(reps)])
+
+        def owned(begin, count):
+            cut = summed[:, begin : begin + count].reshape(layers, shards, count // shards)
+            return lax.dynamic_index_in_dim(cut, me, axis=1, keepdims=False)
+
+        stacked = [
+            jnp.stack([weight_grads[layer][index] for layer in range(layers)]) for index in range(5)
+        ]
+        return (
+            block_out,
+            input_grad,
+            owned(0, width),
+            owned(width, width),
+            stacked[0],
+            owned(4 * width, 3 * width),
+            stacked[1],
+            owned(2 * width, width),
+            owned(3 * width, width),
+            stacked[2],
+            stacked[3],
+            stacked[4],
+        )
+
+    return local
 
 
 class Exchange:
@@ -123,7 +729,7 @@
         return jnp.where((rep == 1) | (rep == 2), whole, outward).astype(f32)
 
 
-def make_local(mesh):
+def make_general(mesh):
     net = Exchange(mesh)
     shards = net.shards
 
@@ -370,6 +976,8 @@
         matrix,
         matrix,
     )
+    cube = mesh.shape["shard"] == 8 and mesh.shape["rep"] == 4
+    local = make_cube(mesh) if cube else make_general(mesh)
     return jax.shard_map(
-        make_local(mesh), mesh=mesh, in_specs=in_specs, out_specs=out_specs, check_vma=False
+        local, mesh=mesh, in_specs=in_specs, out_specs=out_specs, check_vma=False
     )

time: 1920 us -> 1910 us (level)
  Pallas kernels: 0 us -> 273 us
  matrix products: 178 us -> 0.37 us
  starting transfers between devices: 365 us -> 282 us
  other arithmetic: 247 us -> 167 us
  local copies, waits for them, and re-layouts: 255 us -> 310 us
  blocking collectives: 10.7 us -> 39.4 us
  waiting for transfers between devices: 840 us -> 818 us
    pallas_call x0 -> x60, Pallas kernels: none -> 273 us  [the longest x4 52.2 us: local(): attend_back(*gather(low), proj_in[layer], *tables[h], masks[h], out_weigh...]
    psum x1 -> x0, waiting for transfers between devices: 162 us -> none  [local(): summed = lax.psum(jnp.stack(small_grads), ('shard', 'rep'))]
    ppermute x107 -> x177, waiting for transfers between devices: 664 us -> 812 us  [the longest x135 254 us: swap(): return lax.ppermute(values, 'shard', [(i, i ^ bit) for i in range(shards)])]
    dot_general x30 -> x0, matrix products: 126 us -> none  [the longest x10 65.6 us: t_dot(): lax.dot_general(a, b, (((0,), (0,)), ((), ())), preferred_element_type=f32)]
    ppermute x107 -> x177, starting transfers between devices: 299 us -> 220 us  [the longest x135 119 us: swap(): return lax.ppermute(values, 'shard', [(i, i ^ bit) for i in range(shards)])]
    unnamed x449 -> x510, local copies, waits for them, and re-layouts: 103 us -> 155 us
    dot_general x10 -> x2, matrix products: 46.8 us -> 0.37 us  [dot(): return jnp.dot(a, b, preferred_element_type=f32)]
    select_n x30 -> x15, other arithmetic: 69 us -> 23.4 us  [the longest x6 18.9 us: total(): return (jnp.where(lower, theirs, mine), jnp.where(lower, mine, theirs))]
  transfers between devices with their start and end apart: 130 -> 197, of which waited for: 42 -> 54; matrix products, arithmetic and copies ran while one was open for 27% -> 20% of each run, Pallas kernels for 0% -> 14%
where the time goes in v2:
time: 1910 us; the launch traced here: 1890 us
  waiting for transfers between devices  818 us (43%)
  local copies, waits for them, and re-layouts  310 us (16%)
  starting transfers between devices  282 us (15%)
  Pallas kernels  273 us (14%)
  other arithmetic  167 us (9%)
  blocking collectives  39.4 us (2%)
    ppermute x135, waiting for transfers between devices, swap(): return lax.ppermute(values, 'shard', [(i, i ^ bit) for i in range(shards)])  254 us
    ppermute x10, waiting for transfers between devices, total(): inward = lax.ppermute(grad, 'rep', [(0, 1), (3, 2)])  220 us
    ppermute x10, waiting for transfers between devices, total(): other_out = lax.ppermute(other, 'rep', [(1, 0), (2, 3)])  160 us
    unnamed x510, local copies, waits for them, and re-layouts  155 us
    ppermute x10, waiting for transfers between devices, total(): final_out = lax.ppermute(final, 'rep', [(1, 0), (2, 3)])  146 us
    ppermute x135, starting transfers between devices, swap(): return lax.ppermute(values, 'shard', [(i, i ^ bit) for i in range(shards)])  119 us
    pallas_call x4, Pallas kernels, local(): attend_back(*gather(low), proj_in[layer], *tables[h], masks[h], out_weigh...  52.2 us
    pallas_call x4, Pallas kernels, local(): feed_back(*gather(lows[h]), feed_in[layer], down_weight[layer], gate, upper)  50.2 us
  transfers between devices with their start and end apart: 197, of which 54 were waited for; matrix products, arithmetic and copies ran while one was open for 20% of the time, Pallas kernels for 14%

profile of v2, /device:TPU:0, one launch (start us, length us, event | category | flops | bytes accessed | tf_op | source)
XLA Modules:
  0.0 1893.9 jit_solution(8497272405729850958)
XLA Ops:
  2.9 6.3 fusion.43
  21.2 39.4 %all-gather.1 = bf16[8,1,3712]{2,1,0:T(2,128)(2,1)S(1)} all-gather(bf16[1,1,3712]{2,1,0:T(2,128)(2,1)S(1)} %reshape.712), channel_id=2, replica_groups=mesh['shard'=8,'rep'=4] {'shard'}, dimensions={0}, use_global_device_ids=true | all-gather | bytes 66816 | tf_op jit(solution)/shard_map/all_gather | solution.py:340
  60.6 5.6 fusion.45
  109.3 60.3 %collective-permute-done.35 = bf16[64,2048]{1,0:T(8,128)(2,1)S(1)} collective-permute-done((bf16[64,2048]{1,0:T(8,128)(2,1)S(1)}, bf16[64,2048]{1,0:T(8,128)(2,1)S(1)}, u32[]{:S(2)}, u32[]{:S(2)}) %collective-permute-start.35) | collective-permute-done | bytes 262176 | tf_op jit(solution)/shard_map/ppermute | solution.py:305
  187.0 11.1 shard_map.234
  211.0 11.2 shard_map.221
  227.2 6.6 collective-permute-done.43
  259.7 6.2 slice_bitcast_fusion
  265.8 30.2 %collective-permute-done.6.x_ref = bf16[64,2048]{1,0:T(8,128)(2,1)S(1)} collective-permute-done((bf16[64,2048]{1,0:T(8,128)(2,1)S(1)}, bf16[64,2048]{1,0:T(8,128)(2,1)S(1)}, u32[]{:S(2)}, u32[]{:S(2)}) %collective-permute-start.6) | collective-permute-done | bytes 262176 | tf_op jit(solution)/shard_map/ppermute | solution.py:305
  296.1 6.1 collective-permute-done.8.d_ref
  307.5 8.4 copy.224.w_ref
  315.9 10.2 shard_map.237
  361.8 10.2 shard_map.224
  379.7 55.9 %collective-permute-done.14.x_ref = bf16[64,2048]{1,0:T(8,128)(2,1)S(1)} collective-permute-done((bf16[64,2048]{1,0:T(8,128)(2,1)S(1)}, bf16[64,2048]{1,0:T(8,128)(2,1)S(1)}, u32[]{:S(2)}, u32[]{:S(2)}) %collective-permute-start.14) | collective-permute-done | bytes 262176 | tf_op jit(solution)/shard_map/ppermute | solution.py:305
  451.8 10.6 shard_map.240
  469.0 10.3 shard_map.227
  492.3 8.6 collective-permute-done.58
  523.8 8.6 copy.234.w_ref
  538.2 10.2 shard_map.243
  550.5 13.0 shard_map.258
  565.2 10.5 shard_map.230
  582.8 12.2 shard_map.246
  599.9 6.6 collective-permute-done.109
  618.7 5.6 shard_map.275
  658.7 13.0 shard_map.261
  677.5 6.8 collective-permute-done.64.d_ref
  689.3 5.6 shard_map.277
  717.2 13.5 shard_map.249
  732.2 7.2 collective-permute-done.113.y_ref
  740.9 5.6 shard_map.271
  791.6 33.4 %collective-permute-done.172 = bf16[2,8,128,704]{2,3,1,0:T(8,128)(2,1)} collective-permute-done((bf16[2,8,128,704]{2,3,1,0:T(8,128)(2,1)}, bf16[2,8,128,704]{2,3,1,0:T(8,128)(2,1)}, u32[]{:S(2)}, u32[]{:S(2)}) %collective-permute-start.172) | collective-permute-done | bytes 2883616 | tf_op jit(solution)/shard_map/ppermute | solution.py:526
  831.7 14.4 collective-permute-done.152
  848.2 6.2 collective-permute-start.142
  869.0 12.6 shard_map.264
  885.0 12.5 shard_map.252
  952.1 51.1 %collective-permute-done.156 = bf16[128,2048]{1,0:T(8,128)(2,1)} collective-permute-done((bf16[128,2048]{1,0:T(8,128)(2,1)}, bf16[128,2048]{1,0:T(8,128)(2,1)}, u32[]{:S(2)}, u32[]{:S(2)}) %collective-permute-start.156) | collective-permute-done | bytes 524320 | tf_op jit(solution)/shard_map/ppermute | solution.py:536
  1004.5 8.0 collective-permute-done.155
  1036.1 5.6 shard_map.274
  1048.8 5.7 shard_map.276
  1075.8 14.9 collective-permute-start.157
  1111.2 5.7 all-to-all-done.9
  1131.4 13.0 shard_map.267
  1145.2 12.7 shard_map.255
  1165.1 6.4 shard_map.270
  1180.4 33.6 %collective-permute-done.167 = bf16[2,8,128,704]{2,3,1,0:T(8,128)(2,1)} collective-permute-done((bf16[2,8,128,704]{2,3,1,0:T(8,128)(2,1)}, bf16[2,8,128,704]{2,3,1,0:T(8,128)(2,1)}, u32[]{:S(2)}, u32[]{:S(2)}) %collective-permute-start.167) | collective-permute-done | bytes 2883616 | tf_op jit(solution)/shard_map/ppermute | solution.py:526
  1215.3 59.6 %collective-permute-done.177 = bf16[2,352,2048]{2,1,0:T(8,128)(2,1)} collective-permute-done((bf16[2,352,2048]{2,1,0:T(8,128)(2,1)}, bf16[2,352,2048]{2,1,0:T(8,128)(2,1)}, u32[]{:S(2)}, u32[]{:S(2)}) %collective-permute-start.177) | collective-permute-done | bytes 2883616 | tf_op jit(solution)/shard_map/ppermute | solution.py:526
  1322.1 7.4 collective-permute-start.137
  1337.6 79.2 %collective-permute-done.147 = bf16[2,128,2048]{2,1,0:T(8,128)(2,1)S(1)} collective-permute-done((bf16[2,128,2048]{2,1,0:T(8,128)(2,1)S(1)}, bf16[2,128,2048]{2,1,0:T(8,128)(2,1)S(1)}, u32[]{:S(2)}, u32[]{:S(2)}) %collective-permute-start.147) | collective-permute-done | bytes 1048608 | tf_op jit(solution)/shard_map/ppermute | solution.py:526
  1449.1 5.7 collective-permute-start.135
  1478.2 30.9 %collective-permute-done.136 = f32[2,14336]{1,0:T(2,128)} collective-permute-done((f32[2,14336]{1,0:T(2,128)S(1)}, f32[2,14336]{1,0:T(2,128)}, u32[]{:S(2)}, u32[]{:S(2)}) %collective-permute-start.136) | collective-permute-done | bytes 114720 | tf_op jit(solution)/shard_map/ppermute | solution.py:652
  1527.8 41.3 %collective-permute-done.151 = bf16[128,2048]{1,0:T(8,128)(2,1)} collective-permute-done((bf16[128,2048]{1,0:T(8,128)(2,1)}, bf16[128,2048]{1,0:T(8,128)(2,1)}, u32[]{:S(2)}, u32[]{:S(2)}) %collective-permute-start.151) | collective-permute-done | bytes 524320 | tf_op jit(solution)/shard_map/ppermute | solution.py:536
  1582.4 31.6 %collective-permute-done.150 = bf16[128,2048]{1,0:T(8,128)(2,1)} collective-permute-done((bf16[128,2048]{1,0:T(8,128)(2,1)}, bf16[128,2048]{1,0:T(8,128)(2,1)}, u32[]{:S(2)}, u32[]{:S(2)}) %collective-permute-start.150) | collective-permute-done | bytes 524320 | tf_op jit(solution)/shard_map/ppermute | solution.py:537
  1636.0 8.9 collective-permute-done.181
  1647.5 28.3 %collective-permute-done.180 = bf16[352,2048]{1,0:T(8,128)(2,1)} collective-permute-done((bf16[352,2048]{1,0:T(8,128)(2,1)}, bf16[352,2048]{1,0:T(8,128)(2,1)}, u32[]{:S(2)}, u32[]{:S(2)}) %collective-permute-start.180) | collective-permute-done | bytes 1441824 | tf_op jit(solution)/shard_map/ppermute | solution.py:537
  1679.9 6.1 maximum_convert_fusion.3
  1686.1 20.7 %collective-permute-done.161 = bf16[8,128,704]{1,2,0:T(8,128)(2,1)} collective-permute-done((bf16[8,128,704]{1,2,0:T(8,128)(2,1)}, bf16[8,128,704]{1,2,0:T(8,128)(2,1)}, u32[]{:S(2)}, u32[]{:S(2)}) %collective-permute-start.161) | collective-permute-done | bytes 1441824 | tf_op jit(solution)/shard_map/ppermute | solution.py:536
  1706.7 30.9 %collective-permute-done.160 = bf16[8,128,704]{1,2,0:T(8,128)(2,1)} collective-permute-done((bf16[8,128,704]{1,2,0:T(8,128)(2,1)}, bf16[8,128,704]{1,2,0:T(8,128)(2,1)}, u32[]{:S(2)}, u32[]{:S(2)}) %collective-permute-start.160) | collective-permute-done | bytes 1441824 | tf_op jit(solution)/shard_map/ppermute | solution.py:537
  1747.1 11.9 copy.292
  1759.0 9.5 collective-permute-done.171
  1768.5 30.9 %collective-permute-done.170 = bf16[8,128,704]{1,2,0:T(8,128)(2,1)} collective-permute-done((bf16[8,128,704]{1,2,0:T(8,128)(2,1)}, bf16[8,128,704]{1,2,0:T(8,128)(2,1)}, u32[]{:S(2)}, u32[]{:S(2)}) %collective-permute-start.170) | collective-permute-done | bytes 1441824 | tf_op jit(solution)/shard_map/ppermute | solution.py:537
  1806.2 11.9 copy.293
  1818.2 15.0 collective-permute-done.141
  1833.1 29.8 %collective-permute-done.140 = bf16[8,128,768]{2,1,0:T(8,128)(2,1)} collective-permute-done((bf16[8,128,768]{2,1,0:T(8,128)(2,1)}, bf16[8,128,768]{2,1,0:T(8,128)(2,1)}, u32[]{:S(2)}, u32[]{:S(2)}) %collective-permute-start.140) | collective-permute-done | bytes 1572896 | tf_op jit(solution)/shard_map/ppermute | solution.py:537
  1881.1 12.6 copy.291
  (1077 shorter events, 766.5 us)
Async XLA Ops:
  2.4 98.8 %collective-permute-start = (bf16[64,2048]{1,0:T(8,128)(2,1)}, bf16[64,2048]{1,0:T(8,128)(2,1)S(1)}, u32[]{:S(2)}, u32[]{:S(2)}) collective-permute-start(bf16[64,2048]{1,0:T(8,128)(2,1)} %select_bitcast_fusion.9), channel_id=1, source_target_pairs={{0,4},{4,0},{8,12},{12,8},{16,20},{20,16},{24,28},{28,24},{1,5},{5... | collective-permute-start | bytes 786440 | tf_op jit(solution)/shard_map/ppermute | solution.py:305
  14.3 76.7 %all-to-all-start = ((bf16[8,256,768]{1,2,0:T(8,128)(2,1)}), bf16[8,256,768]{1,2,0:T(8,128)(2,1)S(1)}, u32[]{:S(2)}, u32[]{:S(2)}) async-start(bf16[8,256,768]{1,2,0:T(8,128)(2,1)} %bitcast.385), calls=%async_computation | async-start | bytes 6291456 | tf_op jit(solution)/shard_map/all_to_all | solution.py:390
  92.6 155.8 %all-to-all-start.1 = ((bf16[8,2,256,704]{2,3,1,0:T(8,128)(2,1)}), bf16[8,2,256,704]{2,3,1,0:T(8,128)(2,1)}, u32[]{:S(2)}, u32[]{:S(2)}) async-start(bf16[8,2,256,704]{2,3,1,0:T(8,128)(2,1)} %copy.223), calls=%async_computation.1 | async-start | bytes 11534336 | tf_op jit(solution)/shard_map/all_to_all | solution.py:390
  103.4 66.1 %collective-permute-start.35 = (bf16[64,2048]{1,0:T(8,128)(2,1)S(1)}, bf16[64,2048]{1,0:T(8,128)(2,1)S(1)}, u32[]{:S(2)}, u32[]{:S(2)}) collective-permute-start(bf16[64,2048]{1,0:T(8,128)(2,1)S(1)} %shard_map.233), channel_id=1, source_target_pairs={{0,24},{4,28},{8,16},{12,20},{16,8},{20,12},{24,0},{28,4},{1,25},{... | collective-permute-start | bytes 786440 | tf_op jit(solution)/shard_map/ppermute | solution.py:305
  106.3 67.5 %collective-permute-start.34 = (bf16[64,2048]{1,0:T(8,128)(2,1)S(1)}, bf16[64,2048]{1,0:T(8,128)(2,1)}, u32[]{:S(2)}, u32[]{:S(2)}) collective-permute-start(bf16[64,2048]{1,0:T(8,128)(2,1)S(1)} %shard_map.233), channel_id=1, source_target_pairs={{0,16},{4,20},{8,24},{12,28},{16,0},{20,4},{24,8},{28,12},{1,17},{... | collective-permute-start | bytes 786440 | tf_op jit(solution)/shard_map/ppermute | solution.py:305
  106.8 67.0 %collective-permute-start.33 = (bf16[64,2048]{1,0:T(8,128)(2,1)S(1)}, bf16[64,2048]{1,0:T(8,128)(2,1)}, u32[]{:S(2)}, u32[]{:S(2)}) collective-permute-start(bf16[64,2048]{1,0:T(8,128)(2,1)S(1)} %shard_map.233), channel_id=1, source_target_pairs={{0,8},{4,12},{8,0},{12,4},{16,24},{20,28},{24,16},{28,20},{1,9},{5... | collective-permute-start | bytes 786440 | tf_op jit(solution)/shard_map/ppermute | solution.py:305
  239.9 76.0 %collective-permute-start.44 = (bf16[4,64,2048]{2,1,0:T(8,128)(2,1)}, bf16[4,64,2048]{2,1,0:T(8,128)(2,1)}, u32[]{:S(2)}, u32[]{:S(2)}) collective-permute-start(bf16[4,64,2048]{2,1,0:T(8,128)(2,1)} %pad_maximum_fusion.7.own_ref), channel_id=1, source_target_pairs={{0,4},{4,0},{8,12},{12,8},{16,20},{20,16},{24,28},{28,24},{1,5},{5... | collective-permute-start | bytes 3145736 | tf_op jit(solution)/shard_map/ppermute | solution.py:305
  248.4 108.2 %all-to-all-start.2 = ((bf16[8,256,768]{1,2,0:T(8,128)(2,1)}), bf16[8,256,768]{1,2,0:T(8,128)(2,1)}, u32[]{:S(2)}, u32[]{:S(2)}) async-start(bf16[8,256,768]{1,2,0:T(8,128)(2,1)} %bitcast.384), calls=%async_computation.2 | async-start | bytes 6291456 | tf_op jit(solution)/shard_map/all_to_all | solution.py:390
  356.6 167.2 %all-to-all-start.3 = ((bf16[8,2,256,704]{2,3,1,0:T(8,128)(2,1)}), bf16[8,2,256,704]{2,3,1,0:T(8,128)(2,1)}, u32[]{:S(2)}, u32[]{:S(2)}) async-start(bf16[8,2,256,704]{2,3,1,0:T(8,128)(2,1)} %copy.233), calls=%async_computation.3 | async-start | bytes 11534336 | tf_op jit(solution)/shard_map/all_to_all | solution.py:390
  375.8 75.0 %collective-permute-start.52 = (bf16[4,64,2048]{2,1,0:T(8,128)(2,1)}, bf16[4,64,2048]{2,1,0:T(8,128)(2,1)}, u32[]{:S(2)}, u32[]{:S(2)}) collective-permute-start(bf16[4,64,2048]{2,1,0:T(8,128)(2,1)} %pad_maximum_fusion.8.own_ref), channel_id=1, source_target_pairs={{0,4},{4,0},{8,12},{12,8},{16,20},{20,16},{24,28},{28,24},{1,5},{5... | collective-permute-start | bytes 3145736 | tf_op jit(solution)/shard_map/ppermute | solution.py:305
  376.1 59.6 %collective-permute-start.14 = (bf16[64,2048]{1,0:T(8,128)(2,1)S(1)}, bf16[64,2048]{1,0:T(8,128)(2,1)S(1)}, u32[]{:S(2)}, u32[]{:S(2)}) collective-permute-start(bf16[64,2048]{1,0:T(8,128)(2,1)S(1)} %get-tuple-element.213), channel_id=1, source_target_pairs={{0,8},{4,12},{8,0},{12,4},{16,24},{20,28},{24,16},{28,20},{1,9},{5... | collective-permute-start | bytes 786440 | tf_op jit(solution)/shard_map/ppermute | solution.py:305
  378.2 57.5 %collective-permute-start.15 = (bf16[64,2048]{1,0:T(8,128)(2,1)S(1)}, bf16[64,2048]{1,0:T(8,128)(2,1)S(1)}, u32[]{:S(2)}, u32[]{:S(2)}) collective-permute-start(bf16[64,2048]{1,0:T(8,128)(2,1)S(1)} %get-tuple-element.214), channel_id=1, source_target_pairs={{0,16},{4,20},{8,24},{12,28},{16,0},{20,4},{24,8},{28,12},{1,17},{... | collective-permute-start | bytes 786440 | tf_op jit(solution)/shard_map/ppermute | solution.py:305
  379.7 61.2 %collective-permute-start.16 = (bf16[64,2048]{1,0:T(8,128)(2,1)S(1)}, bf16[64,2048]{1,0:T(8,128)(2,1)S(1)}, u32[]{:S(2)}, u32[]{:S(2)}) collective-permute-start(bf16[64,2048]{1,0:T(8,128)(2,1)S(1)} %get-tuple-element.215), channel_id=1, source_target_pairs={{0,24},{4,28},{8,16},{12,20},{16,8},{20,12},{24,0},{28,4},{1,25},{... | collective-permute-start | bytes 786440 | tf_op jit(solution)/shard_map/ppermute | solution.py:305
  634.5 120.5 %collective-permute-start.162 = (bf16[2,8,128,704]{2,3,1,0:T(8,128)(2,1)}, bf16[2,8,128,704]{2,3,1,0:T(8,128)(2,1)}, u32[]{:S(2)}, u32[]{:S(2)}) collective-permute-start(bf16[2,8,128,704]{2,3,1,0:T(8,128)(2,1)} %copy.273), channel_id=1, source_target_pairs={{0,1},{3,2},{4,5},{7,6},{8,9},{11,10},{12,13},{15,14},{16,17},{19,... | collective-permute-start | bytes 8650760 | tf_op jit(solution)/shard_map/ppermute | solution.py:526
  653.1 114.2 %collective-permute-start.182 = (bf16[2,352,2048]{2,1,0:T(8,128)(2,1)}, bf16[2,352,2048]{2,1,0:T(8,128)(2,1)}, u32[]{:S(2)}, u32[]{:S(2)}) collective-permute-start(bf16[2,352,2048]{2,1,0:T(8,128)(2,1)} %shard_map.279), channel_id=1, source_target_pairs={{0,1},{3,2},{4,5},{7,6},{8,9},{11,10},{12,13},{15,14},{16,17},{19,... | collective-permute-start | bytes 8650760 | tf_op jit(solution)/shard_map/ppermute | solution.py:526
  701.2 123.8 %collective-permute-start.172 = (bf16[2,8,128,704]{2,3,1,0:T(8,128)(2,1)}, bf16[2,8,128,704]{2,3,1,0:T(8,128)(2,1)}, u32[]{:S(2)}, u32[]{:S(2)}) collective-permute-start(bf16[2,8,128,704]{2,3,1,0:T(8,128)(2,1)} %copy.285), channel_id=1, source_target_pairs={{0,1},{3,2},{4,5},{7,6},{8,9},{11,10},{12,13},{15,14},{16,17},{19,... | collective-permute-start | bytes 8650760 | tf_op jit(solution)/shard_map/ppermute | solution.py:526
  755.0 91.0 %collective-permute-start.152 = (bf16[2,128,2048]{2,1,0:T(8,128)(2,1)}, bf16[2,128,2048]{2,1,0:T(8,128)(2,1)}, u32[]{:S(2)}, u32[]{:S(2)}) collective-permute-start(bf16[2,128,2048]{2,1,0:T(8,128)(2,1)} %shard_map.273), channel_id=1, source_target_pairs={{0,1},{3,2},{4,5},{7,6},{8,9},{11,10},{12,13},{15,14},{16,17},{19,... | collective-permute-start | bytes 3145736 | tf_op jit(solution)/shard_map/ppermute | solution.py:526
  783.3 84.9 %collective-permute-start.118 = (bf16[4,64,2048]{2,1,0:T(8,128)(2,1)}, bf16[4,64,2048]{2,1,0:T(8,128)(2,1)}, u32[]{:S(2)}, u32[]{:S(2)}) collective-permute-start(bf16[4,64,2048]{2,1,0:T(8,128)(2,1)} %pad_maximum_fusion.16.own_ref), channel_id=1, source_target_pairs={{0,4},{4,0},{8,12},{12,8},{16,20},{20,16},{24,28},{28,24},{1,5},{5... | collective-permute-start | bytes 3145736 | tf_op jit(solution)/shard_map/ppermute | solution.py:305
  789.2 59.0 %collective-permute-start.85 = (bf16[64,2048]{1,0:T(8,128)(2,1)}, bf16[64,2048]{1,0:T(8,128)(2,1)}, u32[]{:S(2)}, u32[]{:S(2)}) collective-permute-start(bf16[64,2048]{1,0:T(8,128)(2,1)} %get-tuple-element.282), channel_id=1, source_target_pairs={{0,24},{4,28},{8,16},{12,20},{16,8},{20,12},{24,0},{28,4},{1,25},{... | collective-permute-start | bytes 786440 | tf_op jit(solution)/shard_map/ppermute | solution.py:305
  790.6 63.7 %collective-permute-start.84 = (bf16[64,2048]{1,0:T(8,128)(2,1)}, bf16[64,2048]{1,0:T(8,128)(2,1)}, u32[]{:S(2)}, u32[]{:S(2)}) collective-permute-start(bf16[64,2048]{1,0:T(8,128)(2,1)} %get-tuple-element.282), channel_id=1, source_target_pairs={{0,16},{4,20},{8,24},{12,28},{16,0},{20,4},{24,8},{28,12},{1,17},{... | collective-permute-start | bytes 786440 | tf_op jit(solution)/shard_map/ppermute | solution.py:305
  848.2 78.4 %collective-permute-start.142 = (bf16[2,8,128,768]{3,2,1,0:T(8,128)(2,1)}, bf16[2,8,128,768]{3,2,1,0:T(8,128)(2,1)}, u32[]{:S(2)}, u32[]{:S(2)}) collective-permute-start(bf16[2,8,128,768]{3,2,1,0:T(8,128)(2,1)} %copy-done.23), channel_id=1, source_target_pairs={{0,1},{3,2},{4,5},{7,6},{8,9},{11,10},{12,13},{15,14},{16,17},{19,... | collective-permute-start | bytes 9437192 | tf_op jit(solution)/shard_map/ppermute | solution.py:526
  903.4 110.9 %collective-permute-start.184 = (bf16[352,2048]{1,0:T(8,128)(2,1)}, bf16[352,2048]{1,0:T(8,128)(2,1)}, u32[]{:S(2)}, u32[]{:S(2)}) collective-permute-start(bf16[352,2048]{1,0:T(8,128)(2,1)} %fusion.6), channel_id=1, source_target_pairs={{1,2},{2,1},{5,6},{6,5},{9,10},{10,9},{13,14},{14,13},{17,18},{18,... | collective-permute-start | bytes 4325384 | tf_op jit(solution)/shard_map/ppermute | solution.py:535
  926.5 76.7 %collective-permute-start.156 = (bf16[128,2048]{1,0:T(8,128)(2,1)}, bf16[128,2048]{1,0:T(8,128)(2,1)}, u32[]{:S(2)}, u32[]{:S(2)}) collective-permute-start(bf16[128,2048]{1,0:T(8,128)(2,1)} %copy-done.202), channel_id=1, source_target_pairs={{1,0},{2,3},{5,4},{6,7},{9,8},{10,11},{13,12},{14,15},{17,16},{18,... | collective-permute-start | bytes 1572872 | tf_op jit(solution)/shard_map/ppermute | solution.py:536
  927.8 84.7 %collective-permute-start.155 = (bf16[128,2048]{1,0:T(8,128)(2,1)}, bf16[128,2048]{1,0:T(8,128)(2,1)}, u32[]{:S(2)}, u32[]{:S(2)}) collective-permute-start(bf16[128,2048]{1,0:T(8,128)(2,1)} %copy-done.212), channel_id=1, source_target_pairs={{1,0},{2,3},{5,4},{6,7},{9,8},{10,11},{13,12},{14,15},{17,16},{18,... | collective-permute-start | bytes 1572872 | tf_op jit(solution)/shard_map/ppermute | solution.py:537
  929.1 86.7 %collective-permute-start.88 = (bf16[64,2048]{1,0:T(8,128)(2,1)}, bf16[64,2048]{1,0:T(8,128)(2,1)}, u32[]{:S(2)}, u32[]{:S(2)}) collective-permute-start(bf16[64,2048]{1,0:T(8,128)(2,1)} %get-tuple-element.288), channel_id=1, source_target_pairs={{0,8},{4,12},{8,0},{12,4},{16,24},{20,28},{24,16},{28,20},{1,9},{5... | collective-permute-start | bytes 786440 | tf_op jit(solution)/shard_map/ppermute | solution.py:305
  929.8 87.6 %collective-permute-start.89 = (bf16[64,2048]{1,0:T(8,128)(2,1)}, bf16[64,2048]{1,0:T(8,128)(2,1)}, u32[]{:S(2)}, u32[]{:S(2)}) collective-permute-start(bf16[64,2048]{1,0:T(8,128)(2,1)} %get-tuple-element.289), channel_id=1, source_target_pairs={{0,16},{4,20},{8,24},{12,28},{16,0},{20,4},{24,8},{28,12},{1,17},{... | collective-permute-start | bytes 786440 | tf_op jit(solution)/shard_map/ppermute | solution.py:305
  937.8 155.2 %all-to-all-start.7 = ((bf16[8,128,704]{1,2,0:T(8,128)(2,1)}), bf16[8,128,704]{1,2,0:T(8,128)(2,1)}, u32[]{:S(2)}, u32[]{:S(2)}) async-start(bf16[8,128,704]{1,2,0:T(8,128)(2,1)} %copy.278), calls=%async_computation.7 | async-start | bytes 2883584 | tf_op jit(solution)/shard_map/all_to_all | solution.py:390
  1003.2 94.0 %collective-permute-start.186 = (bf16[352,2048]{1,0:T(8,128)(2,1)}, bf16[352,2048]{1,0:T(8,128)(2,1)}, u32[]{:S(2)}, u32[]{:S(2)}) collective-permute-start(bf16[352,2048]{1,0:T(8,128)(2,1)} %fusion.6), channel_id=1, source_target_pairs={{1,0},{2,3},{5,4},{6,7},{9,8},{10,11},{13,12},{14,15},{17,16},{18,... | collective-permute-start | bytes 4325384 | tf_op jit(solution)/shard_map/ppermute | solution.py:536
  1012.5 90.5 %collective-permute-start.143 = (bf16[8,128,768]{2,1,0:T(8,128)(2,1)}, bf16[8,128,768]{2,1,0:T(8,128)(2,1)}, u32[]{:S(2)}, u32[]{:S(2)}) collective-permute-start(bf16[8,128,768]{2,1,0:T(8,128)(2,1)} %fusion.9), channel_id=1, source_target_pairs={{1,2},{2,1},{5,6},{6,5},{9,10},{10,9},{13,14},{14,13},{17,18},{18,... | collective-permute-start | bytes 4718600 | tf_op jit(solution)/shard_map/ppermute | solution.py:533
  1014.3 85.9 %collective-permute-start.185 = (bf16[352,2048]{1,0:T(8,128)(2,1)}, bf16[352,2048]{1,0:T(8,128)(2,1)}, u32[]{:S(2)}, u32[]{:S(2)}) collective-permute-start(bf16[352,2048]{1,0:T(8,128)(2,1)} %collective-permute-done.184), channel_id=1, source_target_pairs={{1,0},{2,3},{5,4},{6,7},{9,8},{10,11},{13,12},{14,15},{17,16},{18,... | collective-permute-start | bytes 4325384 | tf_op jit(solution)/shard_map/ppermute | solution.py:537
  1075.8 97.0 %collective-permute-start.157 = (bf16[2,8,128,704]{2,3,1,0:T(8,128)(2,1)}, bf16[2,8,128,704]{2,3,1,0:T(8,128)(2,1)}, u32[]{:S(2)}, u32[]{:S(2)}) collective-permute-start(bf16[2,8,128,704]{2,3,1,0:T(8,128)(2,1)} %copy.267), channel_id=1, source_target_pairs={{0,1},{3,2},{4,5},{7,6},{8,9},{11,10},{12,13},{15,14},{16,17},{19,... | collective-permute-start | bytes 8650760 | tf_op jit(solution)/shard_map/ppermute | solution.py:526
  1097.3 116.7 %collective-permute-start.167 = (bf16[2,8,128,704]{2,3,1,0:T(8,128)(2,1)}, bf16[2,8,128,704]{2,3,1,0:T(8,128)(2,1)}, u32[]{:S(2)}, u32[]{:S(2)}) collective-permute-start(bf16[2,8,128,704]{2,3,1,0:T(8,128)(2,1)} %copy.279), channel_id=1, source_target_pairs={{0,1},{3,2},{4,5},{7,6},{8,9},{11,10},{12,13},{15,14},{16,17},{19,... | collective-permute-start | bytes 8650760 | tf_op jit(solution)/shard_map/ppermute | solution.py:526
  1100.2 174.7 %collective-permute-start.177 = (bf16[2,352,2048]{2,1,0:T(8,128)(2,1)}, bf16[2,352,2048]{2,1,0:T(8,128)(2,1)}, u32[]{:S(2)}, u32[]{:S(2)}) collective-permute-start(bf16[2,352,2048]{2,1,0:T(8,128)(2,1)} %copy-done.24), channel_id=1, source_target_pairs={{0,1},{3,2},{4,5},{7,6},{8,9},{11,10},{12,13},{15,14},{16,17},{19,... | collective-permute-start | bytes 8650760 | tf_op jit(solution)/shard_map/ppermute | solution.py:526
  1105.7 52.3 %collective-permute-start.164 = (bf16[8,128,704]{1,2,0:T(8,128)(2,1)}, bf16[8,128,704]{1,2,0:T(8,128)(2,1)}, u32[]{:S(2)}, u32[]{:S(2)}) collective-permute-start(bf16[8,128,704]{1,2,0:T(8,128)(2,1)} %all-to-all-done.7), channel_id=1, source_target_pairs={{1,2},{2,1},{5,6},{6,5},{9,10},{10,9},{13,14},{14,13},{17,18},{18,... | collective-permute-start | bytes 4325384 | tf_op jit(solution)/shard_map/ppermute | solution.py:535
  1116.9 54.6 %collective-permute-start.174 = (bf16[8,128,704]{1,2,0:T(8,128)(2,1)}, bf16[8,128,704]{1,2,0:T(8,128)(2,1)}, u32[]{:S(2)}, u32[]{:S(2)}) collective-permute-start(bf16[8,128,704]{1,2,0:T(8,128)(2,1)} %all-to-all-done.9), channel_id=1, source_target_pairs={{1,2},{2,1},{5,6},{6,5},{9,10},{10,9},{13,14},{14,13},{17,18},{18,... | collective-permute-start | bytes 4325384 | tf_op jit(solution)/shard_map/ppermute | solution.py:535
  1122.8 310.0 %all-to-all-start.5 = ((bf16[8,128,768]{2,1,0:T(8,128)(2,1)}), bf16[8,128,768]{2,1,0:T(8,128)(2,1)}, u32[]{:S(2)}, u32[]{:S(2)}) async-start(bf16[8,128,768]{2,1,0:T(8,128)(2,1)} %fusion.4), calls=%async_computation.5 | async-start | bytes 3145728 | tf_op jit(solution)/shard_map/all_to_all | solution.py:390
  1158.1 121.2 %collective-permute-start.127 = (bf16[4,64,2048]{2,1,0:T(8,128)(2,1)}, bf16[4,64,2048]{2,1,0:T(8,128)(2,1)}, u32[]{:S(2)}, u32[]{:S(2)}) collective-permute-start(bf16[4,64,2048]{2,1,0:T(8,128)(2,1)} %get-tuple-element.338), channel_id=1, source_target_pairs={{0,4},{4,0},{8,12},{12,8},{16,20},{20,16},{24,28},{28,24},{1,5},{5... | collective-permute-start | bytes 3145736 | tf_op jit(solution)/shard_map/ppermute | solution.py:305
  1171.5 131.5 %collective-permute-start.166 = (bf16[8,128,704]{1,2,0:T(8,128)(2,1)}, bf16[8,128,704]{1,2,0:T(8,128)(2,1)}, u32[]{:S(2)}, u32[]{:S(2)}) collective-permute-start(bf16[8,128,704]{1,2,0:T(8,128)(2,1)} %all-to-all-done.7), channel_id=1, source_target_pairs={{1,0},{2,3},{5,4},{6,7},{9,8},{10,11},{13,12},{14,15},{17,16},{18,... | collective-permute-start | bytes 4325384 | tf_op jit(solution)/shard_map/ppermute | solution.py:536
  1172.8 130.9 %collective-permute-start.165 = (bf16[8,128,704]{1,2,0:T(8,128)(2,1)}, bf16[8,128,704]{1,2,0:T(8,128)(2,1)}, u32[]{:S(2)}, u32[]{:S(2)}) collective-permute-start(bf16[8,128,704]{1,2,0:T(8,128)(2,1)} %collective-permute-done.164), channel_id=1, source_target_pairs={{1,0},{2,3},{5,4},{6,7},{9,8},{10,11},{13,12},{14,15},{17,16},{18,... | collective-permute-start | bytes 4325384 | tf_op jit(solution)/shard_map/ppermute | solution.py:537
  1214.0 97.8 %collective-permute-start.176 = (bf16[8,128,704]{1,2,0:T(8,128)(2,1)}, bf16[8,128,704]{1,2,0:T(8,128)(2,1)}, u32[]{:S(2)}, u32[]{:S(2)}) collective-permute-start(bf16[8,128,704]{1,2,0:T(8,128)(2,1)} %all-to-all-done.9), channel_id=1, source_target_pairs={{1,0},{2,3},{5,4},{6,7},{9,8},{10,11},{13,12},{14,15},{17,16},{18,... | collective-permute-start | bytes 4325384 | tf_op jit(solution)/shard_map/ppermute | solution.py:536
  1322.1 137.7 %collective-permute-start.137 = (bf16[2,8,128,768]{3,2,1,0:T(8,128)(2,1)}, bf16[2,8,128,768]{3,2,1,0:T(8,128)(2,1)}, u32[]{:S(2)}, u32[]{:S(2)}) collective-permute-start(bf16[2,8,128,768]{3,2,1,0:T(8,128)(2,1)} %shard_map.270), channel_id=1, source_target_pairs={{0,1},{3,2},{4,5},{7,6},{8,9},{11,10},{12,13},{15,14},{16,17},{19,... | collective-permute-start | bytes 9437192 | tf_op jit(solution)/shard_map/ppermute | solution.py:526
  1329.5 87.3 %collective-permute-start.147 = (bf16[2,128,2048]{2,1,0:T(8,128)(2,1)S(1)}, bf16[2,128,2048]{2,1,0:T(8,128)(2,1)S(1)}, u32[]{:S(2)}, u32[]{:S(2)}) collective-permute-start(bf16[2,128,2048]{2,1,0:T(8,128)(2,1)S(1)} %copy-done.22), channel_id=1, source_target_pairs={{0,1},{3,2},{4,5},{7,6},{8,9},{11,10},{12,13},{15,14},{16,17},{19,... | collective-permute-start | bytes 3145736 | tf_op jit(solution)/shard_map/ppermute | solution.py:526
  1332.3 100.5 %collective-permute-start.158 = (bf16[8,128,704]{1,2,0:T(8,128)(2,1)}, bf16[8,128,704]{1,2,0:T(8,128)(2,1)}, u32[]{:S(2)}, u32[]{:S(2)}) collective-permute-start(bf16[8,128,704]{1,2,0:T(8,128)(2,1)} %copy.270), channel_id=1, source_target_pairs={{1,2},{2,1},{5,6},{6,5},{9,10},{10,9},{13,14},{14,13},{17,18},{18,... | collective-permute-start | bytes 4325384 | tf_op jit(solution)/shard_map/ppermute | solution.py:533
  1334.1 134.1 %collective-permute-start.178 = (bf16[352,2048]{1,0:T(8,128)(2,1)}, bf16[352,2048]{1,0:T(8,128)(2,1)}, u32[]{:S(2)}, u32[]{:S(2)}) collective-permute-start(bf16[352,2048]{1,0:T(8,128)(2,1)} %fusion.14), channel_id=1, source_target_pairs={{1,2},{2,1},{5,6},{6,5},{9,10},{10,9},{13,14},{14,13},{17,18},{18,... | collective-permute-start | bytes 4325384 | tf_op jit(solution)/shard_map/ppermute | solution.py:533
  1337.5 81.8 %collective-permute-start.132 = (f32[2,14336]{1,0:T(2,128)S(1)}, f32[2,14336]{1,0:T(2,128)S(1)}, u32[]{:S(2)}, u32[]{:S(2)}) collective-permute-start(f32[2,14336]{1,0:T(2,128)S(1)} %pad_maximum_fusion.22), channel_id=1, source_target_pairs={{0,4},{4,0},{8,12},{12,8},{16,20},{20,16},{24,28},{28,24},{1,5},{5... | collective-permute-start | bytes 344072 | tf_op jit(solution)/shard_map/ppermute | solution.py:305
  1432.9 93.0 %collective-permute-start.144 = (bf16[8,128,768]{2,1,0:T(8,128)(2,1)}, bf16[8,128,768]{2,1,0:T(8,128)(2,1)}, u32[]{:S(2)}, u32[]{:S(2)}) collective-permute-start(bf16[8,128,768]{2,1,0:T(8,128)(2,1)} %all-to-all-done.5), channel_id=1, source_target_pairs={{1,2},{2,1},{5,6},{6,5},{9,10},{10,9},{13,14},{14,13},{17,18},{18,... | collective-permute-start | bytes 4718600 | tf_op jit(solution)/shard_map/ppermute | solution.py:535
  1444.8 72.9 %all-to-all-start.6 = ((bf16[8,128,704]{1,2,0:T(8,128)(2,1)}), bf16[8,128,704]{1,2,0:T(8,128)(2,1)}, u32[]{:S(2)}, u32[]{:S(2)}) async-start(bf16[8,128,704]{1,2,0:T(8,128)(2,1)} %copy.272), calls=%async_computation.6 | async-start | bytes 2883584 | tf_op jit(solution)/shard_map/all_to_all | solution.py:390
  1458.5 119.0 %collective-permute-start.146 = (bf16[8,128,768]{2,1,0:T(8,128)(2,1)}, bf16[8,128,768]{2,1,0:T(8,128)(2,1)}, u32[]{:S(2)}, u32[]{:S(2)}) collective-permute-start(bf16[8,128,768]{2,1,0:T(8,128)(2,1)} %all-to-all-done.5), channel_id=1, source_target_pairs={{1,0},{2,3},{5,4},{6,7},{9,8},{10,11},{13,12},{14,15},{17,16},{18,... | collective-permute-start | bytes 4718600 | tf_op jit(solution)/shard_map/ppermute | solution.py:536
  1468.2 102.2 %collective-permute-start.138 = (bf16[8,128,768]{2,1,0:T(8,128)(2,1)}, bf16[8,128,768]{2,1,0:T(8,128)(2,1)}, u32[]{:S(2)}, u32[]{:S(2)}) collective-permute-start(bf16[8,128,768]{2,1,0:T(8,128)(2,1)} %fusion.8), channel_id=1, source_target_pairs={{1,2},{2,1},{5,6},{6,5},{9,10},{10,9},{13,14},{14,13},{17,18},{18,... | collective-permute-start | bytes 4718600 | tf_op jit(solution)/shard_map/ppermute | solution.py:533
  1473.7 50.3 %collective-permute-start.149 = (bf16[128,2048]{1,0:T(8,128)(2,1)}, bf16[128,2048]{1,0:T(8,128)(2,1)}, u32[]{:S(2)}, u32[]{:S(2)}) collective-permute-start(bf16[128,2048]{1,0:T(8,128)(2,1)} %fusion.17), channel_id=1, source_target_pairs={{1,2},{2,1},{5,6},{6,5},{9,10},{10,9},{13,14},{14,13},{17,18},{18,... | collective-permute-start | bytes 1572872 | tf_op jit(solution)/shard_map/ppermute | solution.py:535
  1509.2 106.6 %collective-permute-start.179 = (bf16[352,2048]{1,0:T(8,128)(2,1)}, bf16[352,2048]{1,0:T(8,128)(2,1)}, u32[]{:S(2)}, u32[]{:S(2)}) collective-permute-start(bf16[352,2048]{1,0:T(8,128)(2,1)} %fusion.7), channel_id=1, source_target_pairs={{1,2},{2,1},{5,6},{6,5},{9,10},{10,9},{13,14},{14,13},{17,18},{18,... | collective-permute-start | bytes 4325384 | tf_op jit(solution)/shard_map/ppermute | solution.py:535
  1517.7 61.0 %all-to-all-start.8 = ((bf16[8,128,704]{1,2,0:T(8,128)(2,1)}), bf16[8,128,704]{1,2,0:T(8,128)(2,1)}, u32[]{:S(2)}, u32[]{:S(2)}) async-start(bf16[8,128,704]{1,2,0:T(8,128)(2,1)} %copy.284), calls=%async_computation.8 | async-start | bytes 2883584 | tf_op jit(solution)/shard_map/all_to_all | solution.py:390
  1525.9 95.7 %collective-permute-start.145 = (bf16[8,128,768]{2,1,0:T(8,128)(2,1)}, bf16[8,128,768]{2,1,0:T(8,128)(2,1)S(1)}, u32[]{:S(2)}, u32[]{:S(2)}) collective-permute-start(bf16[8,128,768]{2,1,0:T(8,128)(2,1)} %collective-permute-done.144), channel_id=1, source_target_pairs={{1,0},{2,3},{5,4},{6,7},{9,8},{10,11},{13,12},{14,15},{17,16},{18,... | collective-permute-start | bytes 4718600 | tf_op jit(solution)/shard_map/ppermute | solution.py:537
  1570.4 52.5 %collective-permute-start.159 = (bf16[8,128,704]{1,2,0:T(8,128)(2,1)}, bf16[8,128,704]{1,2,0:T(8,128)(2,1)}, u32[]{:S(2)}, u32[]{:S(2)}) collective-permute-start(bf16[8,128,704]{1,2,0:T(8,128)(2,1)} %all-to-all-done.6), channel_id=1, source_target_pairs={{1,2},{2,1},{5,6},{6,5},{9,10},{10,9},{13,14},{14,13},{17,18},{18,... | collective-permute-start | bytes 4325384 | tf_op jit(solution)/shard_map/ppermute | solution.py:535
  1577.5 67.5 %collective-permute-start.181 = (bf16[352,2048]{1,0:T(8,128)(2,1)}, bf16[352,2048]{1,0:T(8,128)(2,1)}, u32[]{:S(2)}, u32[]{:S(2)}) collective-permute-start(bf16[352,2048]{1,0:T(8,128)(2,1)} %fusion.7), channel_id=1, source_target_pairs={{1,0},{2,3},{5,4},{6,7},{9,8},{10,11},{13,12},{14,15},{17,16},{18,... | collective-permute-start | bytes 4325384 | tf_op jit(solution)/shard_map/ppermute | solution.py:536
  1578.8 97.1 %all-to-all-start.4 = ((bf16[8,128,768]{2,1,0:T(8,128)(2,1)}), bf16[8,128,768]{2,1,0:T(8,128)(2,1)S(1)}, u32[]{:S(2)}, u32[]{:S(2)}) async-start(bf16[8,128,768]{2,1,0:T(8,128)(2,1)} %fusion.5), calls=%async_computation.4 | async-start | bytes 3145728 | tf_op jit(solution)/shard_map/all_to_all | solution.py:390
  1615.8 60.0 %collective-permute-start.180 = (bf16[352,2048]{1,0:T(8,128)(2,1)}, bf16[352,2048]{1,0:T(8,128)(2,1)}, u32[]{:S(2)}, u32[]{:S(2)}) collective-permute-start(bf16[352,2048]{1,0:T(8,128)(2,1)} %collective-permute-done.179), channel_id=1, source_target_pairs={{1,0},{2,3},{5,4},{6,7},{9,8},{10,11},{13,12},{14,15},{17,16},{18,... | collective-permute-start | bytes 4325384 | tf_op jit(solution)/shard_map/ppermute | solution.py:537
  1621.6 85.1 %collective-permute-start.161 = (bf16[8,128,704]{1,2,0:T(8,128)(2,1)}, bf16[8,128,704]{1,2,0:T(8,128)(2,1)}, u32[]{:S(2)}, u32[]{:S(2)}) collective-permute-start(bf16[8,128,704]{1,2,0:T(8,128)(2,1)} %all-to-all-done.6), channel_id=1, source_target_pairs={{1,0},{2,3},{5,4},{6,7},{9,8},{10,11},{13,12},{14,15},{17,16},{18,... | collective-permute-start | bytes 4325384 | tf_op jit(solution)/shard_map/ppermute | solution.py:536
  1622.9 114.7 %collective-permute-start.160 = (bf16[8,128,704]{1,2,0:T(8,128)(2,1)}, bf16[8,128,704]{1,2,0:T(8,128)(2,1)}, u32[]{:S(2)}, u32[]{:S(2)}) collective-permute-start(bf16[8,128,704]{1,2,0:T(8,128)(2,1)} %collective-permute-done.159), channel_id=1, source_target_pairs={{1,0},{2,3},{5,4},{6,7},{9,8},{10,11},{13,12},{14,15},{17,16},{18,... | collective-permute-start | bytes 4325384 | tf_op jit(solution)/shard_map/ppermute | solution.py:537
  1644.9 123.6 %collective-permute-start.171 = (bf16[8,128,704]{1,2,0:T(8,128)(2,1)}, bf16[8,128,704]{1,2,0:T(8,128)(2,1)}, u32[]{:S(2)}, u32[]{:S(2)}) collective-permute-start(bf16[8,128,704]{1,2,0:T(8,128)(2,1)} %all-to-all-done.8), channel_id=1, source_target_pairs={{1,0},{2,3},{5,4},{6,7},{9,8},{10,11},{13,12},{14,15},{17,16},{18,... | collective-permute-start | bytes 4325384 | tf_op jit(solution)/shard_map/ppermute | solution.py:536
  1646.2 153.2 %collective-permute-start.170 = (bf16[8,128,704]{1,2,0:T(8,128)(2,1)}, bf16[8,128,704]{1,2,0:T(8,128)(2,1)}, u32[]{:S(2)}, u32[]{:S(2)}) collective-permute-start(bf16[8,128,704]{1,2,0:T(8,128)(2,1)} %collective-permute-done.169), channel_id=1, source_target_pairs={{1,0},{2,3},{5,4},{6,7},{9,8},{10,11},{13,12},{14,15},{17,16},{18,... | collective-permute-start | bytes 4325384 | tf_op jit(solution)/shard_map/ppermute | solution.py:537
  1675.8 65.2 %collective-permute-start.139 = (bf16[8,128,768]{2,1,0:T(8,128)(2,1)S(1)}, bf16[8,128,768]{2,1,0:T(8,128)(2,1)}, u32[]{:S(2)}, u32[]{:S(2)}) collective-permute-start(bf16[8,128,768]{2,1,0:T(8,128)(2,1)S(1)} %all-to-all-done.4), channel_id=1, source_target_pairs={{1,2},{2,1},{5,6},{6,5},{9,10},{10,9},{13,14},{14,13},{17,18},{18,... | collective-permute-start | bytes 4718600 | tf_op jit(solution)/shard_map/ppermute | solution.py:535
  1739.7 93.4 %collective-permute-start.141 = (bf16[8,128,768]{2,1,0:T(8,128)(2,1)S(1)}, bf16[8,128,768]{2,1,0:T(8,128)(2,1)}, u32[]{:S(2)}, u32[]{:S(2)}) collective-permute-start(bf16[8,128,768]{2,1,0:T(8,128)(2,1)S(1)} %all-to-all-done.4), channel_id=1, source_target_pairs={{1,0},{2,3},{5,4},{6,7},{9,8},{10,11},{13,12},{14,15},{17,16},{18,... | collective-permute-start | bytes 4718600 | tf_op jit(solution)/shard_map/ppermute | solution.py:536
  1741.0 121.9 %collective-permute-start.140 = (bf16[8,128,768]{2,1,0:T(8,128)(2,1)}, bf16[8,128,768]{2,1,0:T(8,128)(2,1)}, u32[]{:S(2)}, u32[]{:S(2)}) collective-permute-start(bf16[8,128,768]{2,1,0:T(8,128)(2,1)} %collective-permute-done.139), channel_id=1, source_target_pairs={{1,0},{2,3},{5,4},{6,7},{9,8},{10,11},{13,12},{14,15},{17,16},{18,... | collective-permute-start | bytes 4718600 | tf_op jit(solution)/shard_map/ppermute | solution.py:537
  (365 other events, 4952.8 us)

commit v3 on v1

--- a/solution.py
+++ b/solution.py
@@ -1,6 +1,10 @@
+import functools
+
 import jax
 import jax.numpy as jnp
 from jax import lax
+from jax.experimental import pallas as pl
+from jax.experimental.pallas import tpu as pltpu
 from jax.sharding import PartitionSpec as P
 
 HEADS = 32
@@ -68,6 +72,946 @@
         ],
         axis=-1,
     )
+
+
+def corner(values):
+    if values.size < 1 << 20:
+        return values
+    short = values.reshape(-1, values.shape[-1])
+    return lax.slice(short, (0, 0), (8, 128))
+
+
+microsecond = 1_150_000_000
+
+
+def call(kernel, grid, in_specs, out_specs, out_shape, vmem=48, aliases=None, weight=1000):
+    reads = len(in_specs)
+
+    def run(*operands, after=()):
+        after = [corner(v) for v in after]
+
+        def body(*refs):
+            kernel(*refs[:reads], *refs[reads + len(after) :])
+
+        specs = list(in_specs) + [pl.BlockSpec(memory_space=pl.ANY)] * len(after)
+        return pl.pallas_call(
+            body,
+            grid=grid or (),
+            in_specs=specs,
+            out_specs=out_specs,
+            out_shape=out_shape,
+            input_output_aliases=aliases or {},
+            compiler_params=pltpu.CompilerParams(vmem_limit_bytes=vmem << 20),
+            cost_estimate=pl.CostEstimate(flops=weight, bytes_accessed=1000, transcendentals=0),
+        )(*operands, *after)
+
+    return run
+
+
+def hold(values, after):
+    anywhere = pl.BlockSpec(memory_space=pl.ANY)
+    shape = jax.ShapeDtypeStruct(values.shape, values.dtype)
+    return call(lambda *_: None, None, [anywhere], anywhere, shape, 48, aliases={0: 0})(values, after=after)
+
+
+def whole(shape, layer=None):
+    at = (layer or 0,) + (0,) * (len(shape) - 1)
+    return pl.BlockSpec(shape, lambda *_: at, pipeline_mode=pl.Buffered(1))
+
+
+def shape_of(shape, dtype):
+    return jax.ShapeDtypeStruct(shape, dtype)
+
+
+def head_lanes(values, head, head_size):
+    lanes = lax.broadcasted_iota(jnp.int32, values.shape, 1)
+    inside = (lanes >= head * head_size) & (lanes < (head + 1) * head_size)
+    return jnp.where(inside, values, jnp.zeros_like(values))
+
+
+def stack_heads(values, heads, head_size):
+    return jnp.concatenate([head_lanes(values, h, head_size) for h in range(heads)], axis=0)
+
+
+def own_lanes(blocks, heads, head_size):
+    tokens = blocks.shape[0] // heads
+    total = None
+    for h in range(heads):
+        term = head_lanes(blocks[h * tokens : (h + 1) * tokens], h, head_size)
+        total = term if total is None else total + term
+    return total
+
+
+def attention(q_heads, keys, mask, heads, head_size):
+    allowed = jnp.concatenate([mask] * heads, axis=0) > 0.5
+    scores = dot_t(q_heads, keys) * head_size ** (-0.5)
+    masked = jnp.where(allowed, scores, -1000000000.0)
+    raised = jnp.exp(masked - jnp.max(masked, axis=-1, keepdims=True))
+    return raised / jnp.sum(raised, axis=-1, keepdims=True)
+
+
+def join_rows(own_ref, pair_ref):
+    pieces = []
+    for s in range(own_ref.shape[0]):
+        pieces += [own_ref[s], pair_ref[s]]
+    return jnp.concatenate(pieces, axis=0)
+
+
+def part_rows(values, keep_ref, send_ref):
+    count, half, _ = keep_ref.shape
+    for s in range(count):
+        first = 2 * s * half
+        keep_ref[s] = values[first : first + half]
+        send_ref[s] = values[first + half : first + 2 * half].astype(bf16)
+
+
+def attend_kernel(
+    own_ref, pair_ref, w_ref, bias_ref, cos_ref, low_ref, high_ref, mask_ref, out_w_ref,
+    keep_ref, send_ref, normed_ref, q_ref, k_ref, v_ref, mixed_ref,
+    *, heads, head_size,
+):
+    cols = heads * head_size
+    normed = join_rows(own_ref, pair_ref)
+    normed_ref[...] = normed
+    joined = dot(normed, w_ref[...]) + bias_ref[...]
+    cosine, low, high = cos_ref[...], low_ref[...], high_ref[...]
+
+    def turn(v):
+        return v * cosine + pltpu.roll(v, cols - HALF, 1) * low + pltpu.roll(v, HALF, 1) * high
+
+    q = turn(joined[:, :cols]).astype(bf16)
+    k = turn(joined[:, cols : 2 * cols]).astype(bf16)
+    v = joined[:, 2 * cols :].astype(bf16)
+    q_ref[...] = q
+    k_ref[...] = k
+    v_ref[...] = v
+    tokens = mask_ref.shape[1]
+    mixed = []
+    for s in range(mask_ref.shape[0]):
+        at = slice(s * tokens, (s + 1) * tokens)
+        probs = attention(stack_heads(q[at], heads, head_size), k[at], mask_ref[s], heads, head_size)
+        terms = dot(probs.astype(bf16), v[at])
+        mixed.append(own_lanes(terms, heads, head_size).astype(bf16))
+    mixed = jnp.concatenate(mixed, axis=0)
+    mixed_ref[...] = mixed
+    part_rows(dot(mixed, out_w_ref[0]), keep_ref, send_ref)
+
+
+def attend_back_kernel(
+    own_ref, pair_ref, w_ref, cos_ref, low_ref, high_ref, mask_ref, out_w_ref, q_ref, k_ref, v_ref,
+    keep_ref, send_ref, branch_ref, joined_ref, bias_ref,
+    *, heads, head_size,
+):
+    cols = heads * head_size
+    scale = head_size ** (-0.5)
+    branch = join_rows(own_ref, pair_ref)
+    branch_ref[...] = branch
+    grad_mixed = dot_t(branch, out_w_ref[0]).astype(bf16)
+    cosine, low, high = cos_ref[...], low_ref[...], high_ref[...]
+
+    def turn_back(v):
+        return v * cosine - pltpu.roll(v, cols - HALF, 1) * low - pltpu.roll(v, HALF, 1) * high
+
+    q, k, v = q_ref[...], k_ref[...], v_ref[...]
+    tokens = mask_ref.shape[1]
+    grad_q, grad_k, grad_v = [], [], []
+    for s in range(mask_ref.shape[0]):
+        at = slice(s * tokens, (s + 1) * tokens)
+        q_heads = stack_heads(q[at], heads, head_size)
+        g_heads = stack_heads(grad_mixed[at], heads, head_size)
+        probs = attention(q_heads, k[at], mask_ref[s], heads, head_size)
+        grad_probs = dot_t(g_heads, v[at])
+        inner = jnp.sum(probs * grad_probs, axis=-1, keepdims=True)
+        grad_scores = (probs * (grad_probs - inner)).astype(bf16)
+        sums = (
+            own_lanes(dot(grad_scores, k[at]), heads, head_size),
+            t_dot(grad_scores, q_heads),
+            t_dot(probs.astype(bf16), g_heads),
+        )
+        grad_q.append(sums[0] * scale)
+        grad_k.append(sums[1] * scale)
+        grad_v.append(sums[2])
+    joined = jnp.concatenate(
+        [
+            turn_back(jnp.concatenate(grad_q, axis=0)),
+            turn_back(jnp.concatenate(grad_k, axis=0)),
+            jnp.concatenate(grad_v, axis=0),
+        ],
+        axis=1,
+    ).astype(bf16)
+    joined_ref[...] = joined
+
+    @pl.when(pl.program_id(0) == 0)
+    def _():
+        bias_ref[...] = jnp.zeros_like(bias_ref)
+
+    bias_ref[...] += jnp.sum(joined.astype(f32), axis=0, keepdims=True)
+    part_rows(dot_t(joined, w_ref[...]), keep_ref, send_ref)
+
+
+def feed_kernel(own_ref, pair_ref, w_ref, down_ref, keep_ref, send_ref, both_ref):
+    both = dot(join_rows(own_ref, pair_ref), w_ref[...])
+    both_ref[...] = both
+    hidden = both.shape[1] // 2
+    gate, upper = both[:, :hidden], both[:, hidden:]
+    inner = (gate / (1.0 + jnp.exp(-gate)) * upper).astype(bf16)
+    part_rows(dot(inner, down_ref[0]), keep_ref, send_ref)
+
+
+def feed_back_kernel(own_ref, pair_ref, w_ref, down_ref, both_ref, keep_ref, send_ref):
+    grad_inner = dot_t(join_rows(own_ref, pair_ref), down_ref[0])
+    hidden = grad_inner.shape[1]
+    gate, upper = both_ref[:, :hidden], both_ref[:, hidden:]
+    sigmoid = 1.0 / (1.0 + jnp.exp(-gate))
+    slope = sigmoid * (1.0 + gate * (1.0 - sigmoid))
+    grad_gate = (grad_inner * upper * slope).astype(bf16)
+    grad_upper = (grad_inner * (gate * sigmoid)).astype(bf16)
+    grad_both = jnp.concatenate([grad_gate, grad_upper], axis=1)
+    part_rows(dot_t(grad_both, w_ref[...]), keep_ref, send_ref)
+
+
+def feed_again_kernel(normed_ref, down_in_ref, w_ref, down_ref, *refs):
+    grad_both_ref, inner_ref, token_ref = refs[-3:]
+    token_ref[...] = jnp.zeros_like(token_ref)
+    both = dot(normed_ref[...], w_ref[...])
+    grad_inner = dot_t(down_in_ref[...], down_ref[0])
+    hidden = grad_inner.shape[1]
+    gate, upper = both[:, :hidden], both[:, hidden:]
+    sigmoid = 1.0 / (1.0 + jnp.exp(-gate))
+    silu = gate * sigmoid
+    inner_ref[...] = (silu * upper).astype(bf16)
+    slope = sigmoid * (1.0 + gate * (1.0 - sigmoid))
+    grad_both_ref[:, :hidden] = (grad_inner * upper * slope).astype(bf16)
+    grad_both_ref[:, hidden:] = (grad_inner * silu).astype(bf16)
+
+
+def all_rows_kernel(first_ref, second_ref, right_ref, out_ref):
+    count = first_ref.shape[0]
+    total = t_dot(first_ref[...], right_ref[:count]) + t_dot(second_ref[...], right_ref[count:])
+    out_ref[0] = total.astype(bf16)
+
+
+def all_down_kernel(left_ref, first_ref, second_ref, *refs):
+    count = first_ref.shape[0]
+    refs[-1][0] = t_dot(left_ref[:count], first_ref[...]) + t_dot(left_ref[count:], second_ref[...])
+
+
+def weight_quarters_kernel(first_ref, second_ref, first_grad_ref, second_grad_ref, *refs):
+    out_ref = refs[-1]
+    product = t_dot(first_ref[...], first_grad_ref[...]) + t_dot(second_ref[...], second_grad_ref[...])
+    product = product.astype(bf16)
+    quarter = product.shape[0] // out_ref.shape[0]
+    for k in range(out_ref.shape[0]):
+        out_ref[k, 0] = product[k * quarter : (k + 1) * quarter]
+
+
+def write_blocks_kernel(blocks_ref, *refs, place, outputs):
+    place(blocks_ref, *refs[len(refs) - outputs :])
+
+
+def combine_kernel(keep_ref, arrived_ref, own_ref, x_ref, y_ref, d_ref):
+    own_ref[...] = keep_ref[0] + arrived_ref[0].astype(f32)
+    for k, ref in ((1, x_ref), (2, y_ref), (3, d_ref)):
+        ref[...] = (keep_ref[k] + arrived_ref[k].astype(f32)).astype(bf16)
+
+
+def received(own_ref, x_ref, y_ref, d_ref):
+    return own_ref[...] + x_ref[...].astype(f32) + (y_ref[...].astype(f32) + d_ref[...].astype(f32))
+
+
+def norm_first_kernel(state_ref, gain_ref, shift_ref, normed_ref):
+    xhat, _ = normalize(state_ref[...])
+    normed_ref[...] = (xhat * gain_ref[...] + shift_ref[...]).astype(bf16)
+
+
+def norm_kernel(state_ref, own_ref, x_ref, y_ref, d_ref, gain_ref, shift_ref, new_ref, normed_ref):
+    state = state_ref[...] + received(own_ref, x_ref, y_ref, d_ref)
+    new_ref[...] = state
+    xhat, _ = normalize(state)
+    normed_ref[...] = (xhat * gain_ref[...] + shift_ref[...]).astype(bf16)
+
+
+def last_kernel(state_ref, own_ref, x_ref, y_ref, d_ref, out_ref):
+    out_ref[...] = (state_ref[...] + received(own_ref, x_ref, y_ref, d_ref)).astype(bf16)
+
+
+def norm_back_kernel(
+    grad_ref, own_ref, x_ref, y_ref, d_ref, state_ref, gain_ref, new_ref, low_ref, sums_ref
+):
+    grad_normed = received(own_ref, x_ref, y_ref, d_ref)
+    xhat, inverse = normalize(state_ref[...])
+    scaled = grad_normed * gain_ref[...]
+    inner = jnp.mean(scaled * xhat, axis=-1, keepdims=True)
+    back = inverse * (scaled - jnp.mean(scaled, axis=-1, keepdims=True) - xhat * inner)
+    grad = grad_ref[...] + back
+    new_ref[...] = grad
+    low_ref[...] = grad.astype(bf16)
+    sums_ref[0:1] = jnp.sum(grad_normed * xhat, axis=0, keepdims=True)
+    sums_ref[1:2] = jnp.sum(grad_normed, axis=0, keepdims=True)
+
+
+def cut_qkv_kernel(weight_ref, out_ref):
+    shards, _, n = out_ref.shape
+    cols = n // 3
+    for s in range(shards):
+        for t in range(3):
+            first = (t * shards + s) * cols
+            out_ref[s, :, t * cols : (t + 1) * cols] = weight_ref[0, :, first : first + cols]
+
+
+def cut_feed_kernel(gate_ref, up_ref, out_ref):
+    shards, _, n = out_ref.shape
+    n = n // 2
+    for s in range(shards):
+        out_ref[s, :, :n] = gate_ref[0, :, s * n : (s + 1) * n]
+        out_ref[s, :, n:] = up_ref[0, :, s * n : (s + 1) * n]
+
+
+def stack_kernel(a_ref, b_ref, c_ref, d_ref, out_ref):
+    for k, ref in enumerate((a_ref, b_ref, c_ref, d_ref)):
+        out_ref[k] = ref[...]
+
+
+def join_kernel(first_ref, second_ref, out_ref):
+    out_ref[0] = first_ref[...]
+    out_ref[1] = second_ref[...]
+
+
+def unpack_kernel(packed_ref, out_ref):
+    out_ref[...] = packed_ref[:, :, : out_ref.shape[2]]
+
+
+def pack_kernel(first_ref, packed_ref, out_ref):
+    n = first_ref.shape[2]
+    out_ref[:, :, :n] = first_ref[...]
+    out_ref[:, :, n:] = packed_ref[:, :, n:]
+
+
+def place_blocks(ref, out_ref):
+    n = ref.shape[2]
+    for s in range(ref.shape[0]):
+        out_ref[0, :, s * n : (s + 1) * n] = ref[s].astype(f32)
+
+
+def place_feed(ref, gate_ref, up_ref):
+    shards, _, n = ref.shape
+    n = n // 2
+    for s in range(shards):
+        gate_ref[0, :, s * n : (s + 1) * n] = ref[s, :, :n].astype(f32)
+        up_ref[0, :, s * n : (s + 1) * n] = ref[s, :, n:].astype(f32)
+
+
+def place_qkv(ref, out_ref):
+    shards, _, n = ref.shape
+    cols = n // 3
+    for s in range(shards):
+        for t in range(3):
+            first = (t * shards + s) * cols
+            out_ref[0, :, first : first + cols] = ref[s, :, t * cols : (t + 1) * cols].astype(f32)
+
+
+def make_cube(mesh):
+    shards, reps = 8, 4
+
+    def swap(values, bit):
+        return lax.ppermute(values, "shard", [(i, i ^ bit) for i in range(shards)])
+
+    def local(
+        hidden_in,
+        segments,
+        ln1_gain,
+        ln1_bias,
+        qkv_weight,
+        qkv_bias,
+        out_weight,
+        ln2_gain,
+        ln2_bias,
+        gate_weight,
+        up_weight,
+        down_weight,
+        cotangent,
+    ):
+        layers, rows = qkv_weight.shape[:2]
+        width = hidden_in.shape[2]
+        tokens = hidden_in.shape[1]
+        part = tokens // 2
+        head_size = width // HEADS
+        heads = HEADS // shards
+        cols = heads * head_size
+        hidden = down_weight.shape[1]
+        chips = shards // 2
+        many = chips * tokens
+        step = 2 * tokens
+        me = lax.axis_index("shard")
+        core = me % 2
+
+        smalls = (ln1_gain, ln1_bias, ln2_gain, ln2_bias, qkv_bias, segments.astype(bf16))
+        small = lax.all_gather(
+            jnp.concatenate([v.reshape(-1) for v in smalls]), "shard", axis=0, tiled=False
+        )
+        cuts = [0]
+        for v in smalls:
+            cuts.append(cuts[-1] + v.size)
+
+        def whole_of(index):
+            like = smalls[index]
+            cut = small[:, cuts[index] : cuts[index + 1]].reshape(shards, layers, like.shape[1])
+            return cut.transpose(1, 0, 2).reshape(layers, -1).astype(f32)
+
+        gain1, shift1, gain2, shift2 = (whole_of(i) for i in range(4))
+        bias_all = whole_of(4).reshape(layers, 3, shards, cols)
+        bias_own = lax.dynamic_index_in_dim(bias_all, me, axis=2, keepdims=False)
+        bias_own = bias_own.reshape(layers, 1, 3 * cols)
+        all_segments = small[:, cuts[5] : cuts[6]]
+
+        places = jnp.arange(tokens, dtype=jnp.int32)
+        places = jnp.where(core == 0, places, (places + part) % tokens)
+        exponents = jnp.arange(HALF, dtype=f32) * (2.0 / ROTARY)
+        inverse = 10000.0 ** (-exponents)
+        masks, tables = [], []
+        for h in range(2):
+            wanted = (me // 2 ^ jnp.arange(chips)) * 2 + h
+            picked = (wanted[:, None] == jnp.arange(shards)[None]).astype(bf16)
+            numbers = dot(picked, all_segments)
+            numbers = jnp.where(core == 0, numbers, jnp.roll(numbers, part, axis=1))
+            earlier = numbers[:, None, :] < numbers[:, :, None]
+            positions = places - jnp.sum(earlier.astype(jnp.int32), axis=-1)
+            allowed = (numbers[:, None, :] == numbers[:, :, None]) & (
+                places[None, :] <= places[:, None]
+            )
+            masks.append(allowed.astype(f32))
+            angles = positions.astype(f32).reshape(many, 1) * inverse
+            cosine, sine = jnp.cos(angles), jnp.sin(angles)
+            zero8 = jnp.zeros_like(sine)
+            rest = jnp.zeros((many, head_size - ROTARY), f32)
+            tables.append(
+                [
+                    jnp.tile(jnp.concatenate(pieces, axis=1), (1, heads))
+                    for pieces in (
+                        (cosine, cosine, rest + 1.0),
+                        (-sine, zero8, rest),
+                        (zero8, sine, rest),
+                    )
+                ]
+            )
+
+        def spread(blocks):
+            return lax.all_to_all(blocks, "shard", split_axis=0, concat_axis=0, tiled=False)
+
+        def cut_columns(kernel, arrays, layer, n, after):
+            cut_rows = rows // 4
+            block = pl.BlockSpec((1, cut_rows, arrays[0].shape[2]), lambda i: (layer, i, 0))
+            return call(
+                kernel,
+                (4,),
+                [block] * len(arrays),
+                pl.BlockSpec((shards, cut_rows, n), lambda i: (0, i, 0)),
+                shape_of((shards, rows, n), bf16),
+                24,
+            )(*arrays, after=after)
+
+        def cut_qkv(layer, after):
+            return cut_columns(cut_qkv_kernel, [qkv_weight], layer, 3 * cols, after)
+
+        def cut_feed(layer, after):
+            return cut_columns(cut_feed_kernel, [gate_weight, up_weight], layer, 2 * hidden, after)
+
+        def turned(blocks):
+            return spread(blocks).reshape(width, blocks.shape[2])
+
+        stack = call(
+            stack_kernel,
+            None,
+            [pl.BlockSpec(memory_space=pltpu.VMEM)] * 4,
+            pl.BlockSpec(memory_space=pltpu.VMEM),
+            shape_of((chips, part, width), bf16),
+            16,
+        )
+        combine = call(
+            combine_kernel,
+            None,
+            [pl.BlockSpec(memory_space=pltpu.VMEM)] * 2,
+            [pl.BlockSpec(memory_space=pltpu.VMEM)] * 4,
+            [shape_of((part, width), f32)] + [shape_of((part, width), bf16)] * 3,
+            16,
+        )
+
+        steps = chips // 2
+        piece = pl.BlockSpec((2, part, width), lambda i: (i, 0, 0))
+
+        def row_block(n):
+            return pl.BlockSpec((step, n), lambda i: (i, 0))
+
+        mask_block = pl.BlockSpec((2, tokens, tokens), lambda i: (i, 0, 0))
+        table_blocks = [row_block(cols)] * 3
+        part_shapes = [
+            shape_of((chips, part, width), f32),
+            shape_of((chips, part, width), bf16),
+        ]
+        options = dict(heads=heads, head_size=head_size)
+        def attend(layer, *operands, after=()):
+            return call(
+                functools.partial(attend_kernel, **options),
+                (steps,),
+                [piece, piece, whole((width, 3 * cols)), whole((1, 3 * cols))]
+                + table_blocks
+                + [mask_block, whole((1, cols, width), layer)],
+                [piece, piece, row_block(width)] + [row_block(cols)] * 4,
+                part_shapes + [shape_of((many, width), bf16)] + [shape_of((many, cols), bf16)] * 4,
+                weight=12 * microsecond,
+            )(*operands, after=after)
+
+        def attend_back(layer, *operands, after=()):
+            bias_block = pl.BlockSpec((1, 3 * cols), lambda i: (0, 0))
+            bias_shape = shape_of((1, 3 * cols), f32)
+            return call(
+                functools.partial(attend_back_kernel, **options),
+                (steps,),
+                [piece, piece, whole((width, 3 * cols))]
+                + table_blocks
+                + [mask_block, whole((1, cols, width), layer)]
+                + [row_block(cols)] * 3,
+                [piece, piece, row_block(width), row_block(3 * cols), bias_block],
+                part_shapes
+                + [shape_of((many, width), bf16), shape_of((many, 3 * cols), bf16), bias_shape],
+                weight=12 * microsecond,
+            )(*operands, after=after)
+
+        def feed_weights(layer):
+            return [whole((width, 2 * hidden)), whole((1, hidden, width), layer)]
+
+        def feed(layer, *operands, after=()):
+            return call(
+                feed_kernel,
+                (steps,),
+                [piece, piece] + feed_weights(layer),
+                [piece, piece, row_block(2 * hidden)],
+                part_shapes + [shape_of((many, 2 * hidden), f32)],
+                weight=12 * microsecond,
+            )(*operands, after=after)
+
+        def feed_back(layer, *operands, after=()):
+            return call(
+                feed_back_kernel,
+                (steps,),
+                [piece, piece] + feed_weights(layer) + [row_block(2 * hidden)],
+                [piece, piece],
+                part_shapes,
+                weight=12 * microsecond,
+            )(*operands, after=after)
+
+        def small_call(kernel, n_in, out_shape):
+            vmem = pl.BlockSpec(memory_space=pltpu.VMEM)
+            return call(kernel, None, [vmem] * n_in, [vmem] * len(out_shape), out_shape, 16)
+
+        low_shape, state_shape = shape_of((part, width), bf16), shape_of((part, width), f32)
+        norm_first = small_call(norm_first_kernel, 3, [low_shape])
+        norm = small_call(norm_kernel, 7, [state_shape, low_shape])
+        last = small_call(last_kernel, 5, [low_shape])
+        norm_back = small_call(norm_back_kernel, 7, [state_shape, low_shape, shape_of((2, width), f32)])
+
+        written = {}
+        shapes_of = dict(
+            qkv=[qkv_weight.shape],
+            feed=[gate_weight.shape, up_weight.shape],
+            out=[out_weight.shape],
+            down=[down_weight.shape],
+        )
+        places_of = dict(qkv=place_qkv, feed=place_feed, out=place_blocks)
+
+        def write_blocks(layer, name, blocks, n, cut, first, at=0):
+            parts, a, r, _ = blocks.shape
+            shapes = shapes_of[name]
+            earlier = written.get(name, [])
+            each = r // cut
+            begin = first // cut
+            written[name] = call(
+                functools.partial(write_blocks_kernel, place=places_of[name], outputs=len(shapes)),
+                (parts, each),
+                [pl.BlockSpec((None, a, cut, n), lambda i, j: (i, 0, j, at))]
+                + [pl.BlockSpec(memory_space=pl.ANY)] * len(earlier),
+                [pl.BlockSpec((1, cut, v[2]), lambda i, j: (layer, begin + i * each + j, 0)) for v in shapes],
+                [shape_of(v, f32) for v in shapes],
+                32,
+                aliases={1 + k: k for k in range(len(earlier))},
+            )(blocks, *earlier)
+
+        quarter = rows // reps
+        packed_shape = shape_of((reps, shards, quarter, 4 * cols), bf16)
+
+        def weight_quarters(normed, joined, mixed, branch, after=()):
+            left = pl.BlockSpec((many, rows), lambda s: (0, s))
+            packed = call(
+                weight_quarters_kernel,
+                (shards,),
+                [left, left, whole((many, 3 * cols)), whole((many, 3 * cols))],
+                pl.BlockSpec((reps, 1, quarter, 3 * cols), lambda s: (0, s, 0, 0)),
+                packed_shape,
+                32,
+            )(*normed, *joined, after=after)
+            right = pl.BlockSpec((many, cols), lambda s: (0, s))
+            return call(
+                weight_quarters_kernel,
+                (shards,),
+                [whole((many, cols)), whole((many, cols)), right, right, pl.BlockSpec(memory_space=pl.ANY)],
+                pl.BlockSpec((reps, 1, quarter, cols), lambda s: (0, s, 0, 3)),
+                packed_shape,
+                32,
+                aliases={4: 0},
+            )(*mixed, *branch, packed)
+
+        def scatter_quarters(packed):
+            return lax.psum_scatter(packed, "rep", scatter_dimension=0, tiled=False)
+
+        def turn_quarters(own, after):
+            vmem = pl.BlockSpec(memory_space=pltpu.VMEM)
+            shape = shape_of((shards, quarter, 3 * cols), bf16)
+            return spread(call(unpack_kernel, None, [vmem], vmem, shape, 16)(own, after=after))
+
+        def gather_quarters(columns, own, after):
+            vmem = pl.BlockSpec(memory_space=pltpu.VMEM)
+            full = shape_of((shards, quarter, 4 * cols), bf16)
+            own = call(pack_kernel, None, [vmem] * 2, vmem, full, 16)(columns, own, after=after)
+            return lax.all_gather(own, "rep", axis=0, tiled=False)
+
+        all_tokens = shards * reps * tokens
+        half_tokens = all_tokens // 2
+
+        def gather_all(halves, after=()):
+            joined = call(
+                join_kernel,
+                None,
+                [pl.BlockSpec(memory_space=pltpu.VMEM)] * 2,
+                pl.BlockSpec(memory_space=pltpu.VMEM),
+                shape_of((2, chips, part, width), bf16),
+                24,
+            )(*halves, after=after)
+            return lax.all_gather(joined, "rep", axis=0, tiled=False).reshape(half_tokens, width)
+
+        def with_pair(own, after):
+            own = hold(own, after)
+            return own, swap(own, 1)
+
+        def feed_again(layer, normed, down_in, piece_at, count, earlier, after=()):
+            block_rows = 2 * tokens
+            side, piece = divmod(piece_at, count // 2)
+            steps_in = all_tokens // count // block_rows
+            source = pl.BlockSpec((block_rows, width), lambda i: (piece * steps_in + i, 0))
+
+            def rows_of(n):
+                return pl.BlockSpec((block_rows, n), lambda i: (piece_at * steps_in + i, 0))
+
+            return call(
+                feed_again_kernel,
+                (steps_in,),
+                [source, source]
+                + feed_weights(layer)
+                + [pl.BlockSpec(memory_space=pl.ANY)] * len(earlier),
+                [rows_of(2 * hidden), rows_of(hidden), pl.BlockSpec((8, 128), lambda i: (0, 0))],
+                [
+                    shape_of((all_tokens, 2 * hidden), bf16),
+                    shape_of((all_tokens, hidden), bf16),
+                    shape_of((8, 128), f32),
+                ],
+                aliases={4 + k: k for k in range(len(earlier))},
+                weight=20 * microsecond,
+            )(normed[side], down_in[side], feed_in[layer], down_weight, *earlier, after=after)
+
+        def all_columns(normed, grad_both, piece_at, count, after=()):
+            n = grad_both.shape[1]
+            r = rows // count
+            left = pl.BlockSpec((half_tokens, r), lambda s: (0, s * count + piece_at))
+            return call(
+                all_rows_kernel,
+                (shards,),
+                [left, left, whole((all_tokens, n))],
+                pl.BlockSpec((1, r, n), lambda s: (s, 0, 0)),
+                shape_of((shards, r, n), bf16),
+                weight=30 * microsecond,
+            )(*normed, grad_both, after=after)
+
+        def all_down(layer, inner, down_in, after=()):
+            earlier = written.get("down", [])
+            right = pl.BlockSpec((half_tokens, 256), lambda s: (0, s))
+            written["down"] = call(
+                all_down_kernel,
+                (width // 256,),
+                [whole((all_tokens, hidden)), right, right]
+                + [pl.BlockSpec(memory_space=pl.ANY)] * len(earlier),
+                [pl.BlockSpec((1, hidden, 256), lambda s: (layer, 0, s))],
+                [shape_of(down_weight.shape, f32)],
+                aliases={3 + k: k for k in range(len(earlier))},
+                weight=20 * microsecond,
+            )(inner, *down_in, *earlier, after=after)
+
+        class Feed:
+            def __init__(self, layer, normed, down_in, pieces, cuts):
+                self.layer, self.normed, self.down_in = layer, normed, down_in
+                self.pieces, self.cuts, self.done = pieces, cuts, 0
+                self.carried, self.blocks = [], []
+
+            def again(self, after):
+                *self.carried, token = feed_again(
+                    self.layer, self.normed, self.down_in, self.done, self.pieces, self.carried, after=after
+                )
+                self.done += 1
+                return [token]
+
+            def columns(self, after, before=()):
+                got = all_columns(self.normed, self.carried[0], len(self.blocks), self.cuts, after=after)
+                got = hold(got, self.blocks[-1:] + list(before))
+                self.blocks.append(spread(got))
+                return [got]
+
+            def down(self, after):
+                all_down(self.layer, self.carried[1], self.down_in, after=after)
+                return after
+
+            def write(self):
+                r = rows // self.cuts
+                for k, blocks in enumerate(self.blocks):
+                    write_blocks(self.layer, "feed", blocks[None], blocks.shape[2], 32, k * r)
+
+        def share(values):
+            first, second = values[:part], values[part:]
+            kept = jnp.where(core == 0, first, second)
+            arrived = swap(jnp.where(core == 0, second, first), 1)
+            return [jnp.where(core == 0, kept, arrived), jnp.where(core == 0, arrived, kept)]
+
+        def unshare(halves):
+            kept = jnp.where(core == 0, halves[0], halves[1])
+            arrived = swap(jnp.where(core == 0, halves[1], halves[0]), 1)
+            both = [jnp.where(core == 0, kept, arrived), jnp.where(core == 0, arrived, kept)]
+            return jnp.concatenate(both, axis=0)[None]
+
+        def row(values, layer):
+            return values[layer : layer + 1]
+
+        def send_low(low):
+            return low, [swap(low, 2), swap(low, 4), swap(low, 6)]
+
+        def collect(sent, after):
+            mine = stack(sent[0], *sent[1], after=after)
+            return mine, swap(mine, 1)
+
+        def send_sums(outputs, after):
+            own, x, y, d = combine(outputs[0], swap(outputs[1], 1), after=after)
+            return own, swap(x, 2), swap(y, 4), swap(d, 6)
+
+        def block(run, finish, ready, after=(), due=None, filler=None):
+            (gathered, other), sent = ready[:2], ready[2]
+            first = run(0, gathered, list(after))
+            if other is None:
+                other = collect(sent, [first[0]])
+            if due is None:
+                sums = send_sums(first, [other[0]])
+                second = run(1, other, [sums[0]])
+            else:
+                second = run(1, other, [first[0]])
+                sums = send_sums(first, [second[0]] + list(due))
+            later = send_sums(second, [sums[0]])
+            done = finish(0, sums, [later[0]])
+            wait = [done[0]]
+            sent = send_low(done[1]) if len(done) > 1 else None
+            if filler:
+                wait += filler(wait)
+            end = finish(1, later, wait)
+            if sent is None:
+                return (first, second), (done, end), None, (gathered, other)
+            inputs = (gathered, other)
+            gathered, sent = collect(sent, [end[0]]), send_low(end[1])
+            other = None if due is None else collect(sent, [gathered[0]])
+            return (first, second), (done, end), (gathered, other, sent), inputs
+
+        states = [v.astype(f32) for v in share(hidden_in[0])]
+        cotangents = share(cotangent[0])
+        lows = [norm_first(states[h], row(gain1, 0), row(shift1, 0))[0] for h in range(2)]
+        proj_in, feed_in = [None] * layers, [None] * layers
+        proj_in[0] = turned(cut_qkv(0, lows))
+        sent = [send_low(low) for low in lows]
+        gathered = collect(sent[0], [lows[1]] + masks + tables[0] + tables[1])
+        ready = (gathered, collect(sent[1], [gathered[0]]), None)
+        all_normed2, all_down_in = [None] * layers, [None] * layers
+        saved = []
+        for layer in range(layers):
+            blocks = hold(cut_feed(layer, []), [proj_in[layer], ready[1][0]])
+            feed_in[layer] = turned(blocks)
+            first, done, ready, _ = block(
+                lambda h, gathered, after: attend(
+                    layer,
+                    *gathered,
+                    proj_in[layer],
+                    bias_own[layer],
+                    *tables[h],
+                    masks[h],
+                    out_weight,
+                    after=after,
+                ),
+                lambda h, sums, after: norm(
+                    states[h], *sums, row(gain2, layer), row(shift2, layer), after=after
+                ),
+                ready,
+                [blocks],
+                [feed_in[layer]],
+            )
+            mids = [v[0] for v in done]
+            if layer == 0:
+                sent = [send_low(hold(v, [mids[1]])) for v in cotangents]
+                one = collect(sent[0], [ready[1][0]])
+                back_ready = (one, collect(sent[1], [one[0]]), None)
+                gathering = [gather_all([v[0] for v in back_ready[:2]])]
+            if layer + 1 < layers:
+                blocks = hold(cut_qkv(layer + 1, []), [feed_in[layer], ready[1][0]])
+                proj_in[layer + 1] = turned(blocks)
+                due = [proj_in[layer + 1]]
+            else:
+                blocks = ready[1][0]
+                due = None
+            second, done, ready, inputs = block(
+                lambda h, gathered, after: feed(layer, *gathered, feed_in[layer], down_weight, after=after),
+                lambda h, sums, after: (
+                    norm(mids[h], *sums, row(gain1, layer + 1), row(shift1, layer + 1), after=after)
+                    if layer + 1 < layers
+                    else last(mids[h], *sums, after=after)
+                ),
+                ready,
+                [blocks] + (gathering[:1] if layer + 1 == layers else []),
+                due,
+            )
+            if layer + 1 == layers:
+                all_down_in[-1] = with_pair(gathering[0], [second[0][0]])
+                all_normed2[0] = with_pair(gathering[1], [second[1][0]])
+            gathering.append(gather_all([v[0] for v in inputs]))
+            saved.append(
+                [(states[h],) + tuple(first[h][2:]) + (mids[h], second[h][2]) for h in range(2)]
+            )
+            if layer + 1 < layers:
+                states = [v[0] for v in done]
+        block_out = unshare([v[0] for v in done])
+
+        grads = [v.astype(f32) for v in cotangents]
+        small_grads, quarters, own = [None] * layers, [None] * layers, []
+        fed = [None] * layers
+        ready = back_ready
+        starts = [second[0][2], second[1][2]]
+        for layer in reversed(range(layers)):
+
+            def both(index):
+                return [saved[layer][h][index] for h in range(2)]
+
+            filler = None
+            if layer + 1 < layers:
+                all_normed2[layer + 1] = with_pair(gathering[2], [ends[1][0]])
+                fed[layer + 1] = Feed(layer + 1, all_normed2[layer + 1], all_down_in[layer + 1], 4, 1)
+
+                def filler(wait):
+                    return fed[layer + 1].again(wait)
+
+                starts = starts + [all_normed2[layer + 1][0]]
+            first, back, ready, inputs = block(
+                lambda h, gathered, after: feed_back(
+                    layer, *gathered, feed_in[layer], down_weight, saved[layer][h][7], after=after
+                ),
+                lambda h, sums, after: norm_back(
+                    grads[h], *sums, saved[layer][h][6], row(gain2, layer), after=after
+                ),
+                ready,
+                starts,
+                filler=filler,
+            )
+            if layer + 1 < layers:
+                gathering.append(gather_all([v[0] for v in inputs], [quarters[layer + 1]]))
+            sums2 = back[0][2] + back[1][2]
+            ahead = gathering[1:2] + [block_out] if layer > 0 else []
+            if layer + 1 < layers:
+
+                def filler(wait):
+                    return fed[layer + 1].again(wait + own)
+
+            second, ends, ready, _ = block(
+                lambda h, gathered, after: attend_back(
+                    layer,
+                    *gathered,
+                    proj_in[layer],
+                    *tables[h],
+                    masks[h],
+                    out_weight,
+                    *saved[layer][h][2:5],
+                    after=after,
+                ),
+                lambda h, sums, after: norm_back(
+                    back[h][0], *sums, saved[layer][h][0], row(gain1, layer), after=after
+                ),
+                ready,
+                ahead,
+                filler=filler,
+            )
+            branches, joineds = [v[2] for v in second], [v[3] for v in second]
+            ended = [ends[0][0]] if layer > 0 else [ends[1][0]]
+            quarters[layer] = weight_quarters(both(1), joineds, both(5), branches, after=ended)
+            starts = [quarters[layer]]
+            own.insert(0, scatter_quarters(quarters[layer]))
+            grads, lows = [v[0] for v in ends], [v[1] for v in ends]
+            sums1 = ends[0][2] + ends[1][2]
+            placed = jnp.where(
+                (jnp.arange(shards) == me)[None, :, None],
+                (second[0][4] + second[1][4]).reshape(3, 1, cols),
+                0.0,
+            )
+            small_grads[layer] = jnp.concatenate([sums1.reshape(-1), sums2.reshape(-1), placed.reshape(-1)])
+        input_grad = unshare(lows)
+
+        summed = [jnp.stack(small_grads)]
+
+        def small_step():
+            k, last_sum = len(summed) - 1, summed[-1]
+            if k < 3:
+                arrived = swap(last_sum, 1 << k)
+            else:
+                arrived = lax.ppermute(last_sum, "rep", [(i, i ^ (1 << (k - 3))) for i in range(reps)])
+            summed.append(last_sum + arrived)
+            return [summed[-1]]
+
+        turned1 = turn_quarters(own[1], [second[1][2]])
+        wait = fed[1].again([quarters[0], input_grad] + small_step())
+        wait = fed[1].again(wait + small_step())
+        wait = fed[1].columns(wait + small_step(), [turned1])
+        all_down_in[0] = with_pair(gathering[3], wait)
+        fed[0] = Feed(0, all_normed2[0], all_down_in[0], 2, 2)
+        wait = fed[0].again(wait + small_step())
+        packed1 = gather_quarters(turned1, own[1], wait + own[:1])
+        wait = fed[0].again(wait + small_step())
+        turned0 = turn_quarters(own[0], wait + [fed[1].blocks[0]])
+        wait = fed[0].columns(wait, [turned0])
+        packed0 = gather_quarters(turned0, own[0], wait)
+        wait = fed[0].columns(wait)
+        fed[1].down(wait)
+        fed[0].down(wait)
+        summed = summed[-1]
+        for layer, packed in ((1, packed1), (0, packed0)):
+            fed[layer].write()
+            write_blocks(layer, "qkv", packed, 3 * cols, 32, 0)
+            write_blocks(layer, "out", packed, cols, quarter, 0, 3)
+
+        def owned(begin, count):
+            cut = summed[:, begin : begin + count].reshape(layers, shards, count // shards)
+            return lax.dynamic_index_in_dim(cut, me, axis=1, keepdims=False)
+
+        return (
+            block_out,
+            input_grad,
+            owned(0, width),
+            owned(width, width),
+            written["qkv"][0],
+            owned(4 * width, 3 * width),
+            written["out"][0],
+            owned(2 * width, width),
+            owned(3 * width, width),
+            *written["feed"],
+            written["down"][0],
+        )
+
+    return local
 
 
 class Exchange:
@@ -123,7 +1067,7 @@
         return jnp.where((rep == 1) | (rep == 2), whole, outward).astype(f32)
 
 
-def make_local(mesh):
+def make_general(mesh):
     net = Exchange(mesh)
     shards = net.shards
 
@@ -370,6 +1314,8 @@
         matrix,
         matrix,
     )
+    cube = mesh.shape["shard"] == 8 and mesh.shape["rep"] == 4
+    local = make_cube(mesh) if cube else make_general(mesh)
     return jax.shard_map(
-        make_local(mesh), mesh=mesh, in_specs=in_specs, out_specs=out_specs, check_vma=False
+        local, mesh=mesh, in_specs=in_specs, out_specs=out_specs, check_vma=False
     )

time: 1920 us -> 1220 us (0.64)
  Pallas kernels: 0 us -> 479 us
  waiting for transfers between devices: 840 us -> 387 us
  other arithmetic: 247 us -> 13.9 us
  starting transfers between devices: 365 us -> 154 us
  matrix products: 178 us -> 0.37 us
  local copies, waits for them, and re-layouts: 255 us -> 153 us
    pallas_call x0 -> x112, Pallas kernels: none -> 479 us  [run(): pl.pallas_call(body, grid=grid or (), in_specs=specs, out_specs=out_specs...]
    ppermute x117 -> x141, waiting for transfers between devices: 664 us -> 276 us  [the longest x139 250 us: swap(): return lax.ppermute(values, 'shard', [(i, i ^ bit) for i in range(shards)])]
    ppermute x117 -> x141, starting transfers between devices: 313 us -> 113 us  [the longest x139 113 us: swap(): return lax.ppermute(values, 'shard', [(i, i ^ bit) for i in range(shards)])]
    psum x1 -> x0, waiting for transfers between devices: 162 us -> none  [local(): summed = lax.psum(jnp.stack(small_grads), ('shard', 'rep'))]
    dot_general x30 -> x0, matrix products: 126 us -> none  [the longest x10 65.6 us: t_dot(): lax.dot_general(a, b, (((0,), (0,)), ((), ())), preferred_element_type=f32)]
    all_to_all x12 -> x9, waiting for transfers between devices: 13.8 us -> 101 us  [spread(): lax.all_to_all(blocks, 'shard', split_axis=0, concat_axis=0, tiled=False)]
    convert_element_type x47 -> x9, other arithmetic: 86.3 us -> 4.13 us  [the longest x1 2.04 us: local(): grads = [v.astype(f32) for v in cotangents]]
    select_n x30 -> x8, other arithmetic: 69 us -> 3.68 us  [the longest x2 1.79 us: share(): arrived = swap(jnp.where(core == 0, second, first), 1)]
  transfers between devices with their start and end apart: 130 -> 158, of which waited for: 42 -> 70; matrix products, arithmetic and copies ran while one was open for 27% -> 3% of each run, Pallas kernels for 0% -> 39%
where the time goes in v3:
time: 1220 us; the launch traced here: 1210 us
  Pallas kernels  479 us (39%)
  waiting for transfers between devices  387 us (32%)
  starting transfers between devices  154 us (13%)
  local copies, waits for them, and re-layouts  153 us (13%)
  between operations  17 us (1%)
  other arithmetic  13.9 us (1%)
    pallas_call x112, Pallas kernels, run(): pl.pallas_call(body, grid=grid or (), in_specs=specs, out_specs=out_specs...  479 us
    ppermute x139, waiting for transfers between devices, swap(): return lax.ppermute(values, 'shard', [(i, i ^ bit) for i in range(shards)])  250 us
    unnamed x451, local copies, waits for them, and re-layouts  132 us
    ppermute x139, starting transfers between devices, swap(): return lax.ppermute(values, 'shard', [(i, i ^ bit) for i in range(shards)])  113 us
    all_to_all x9, waiting for transfers between devices, spread(): lax.all_to_all(blocks, 'shard', split_axis=0, concat_axis=0, tiled=False)  101 us
    all_to_all x9, starting transfers between devices, spread(): lax.all_to_all(blocks, 'shard', split_axis=0, concat_axis=0, tiled=False)  39.7 us
    ppermute x2, waiting for transfers between devices, small_step(): lax.ppermute(last_sum, 'rep', [(i, i ^ 1 << k - 3) for i in range(reps)])  25.9 us
  transfers between devices with their start and end apart: 158, of which 70 were waited for; matrix products, arithmetic and copies ran while one was open for 3% of the time, Pallas kernels for 39%

profile of v3, /device:TPU:0, one launch (start us, length us, event | category | flops | bytes accessed | tf_op | source)
XLA Modules:
  0.0 1214.6 jit_solution(7023642689503468118)
XLA Ops:
  14.1 10.3 all-gather.7
  47.3 33.1 %collective-permute-done.1.refs_1_ = bf16[64,2048]{1,0:T(8,128)(2,1)S(1)} collective-permute-done((bf16[64,2048]{1,0:T(8,128)(2,1)S(1)}, bf16[64,2048]{1,0:T(8,128)(2,1)S(1)}, u32[]{:S(2)}, u32[]{:S(2)}) %collective-permute-start.1) | collective-permute-done | bytes 262176 | tf_op jit(solution)/shard_map/ppermute | solution.py:417
  110.4 4.7 all-to-all-start.1
  123.0 8.6 shard_map.227
  132.5 8.6 shard_map.228
  145.3 35.9 %all-to-all-done.1 = bf16[8,256,1408]{2,1,0:T(8,128)(2,1)} async-done(((bf16[8,256,1408]{2,1,0:T(8,128)(2,1)}), bf16[8,256,1408]{2,1,0:T(8,128)(2,1)}, u32[]{:S(2)}, u32[]{:S(2)}) %all-to-all-start.1) | async-done | bytes 5767200 | tf_op jit(solution)/shard_map/all_to_all | solution.py:499
  191.0 4.9 collective-permute-done.10.refs_2_
  196.4 5.5 collective-permute-done.11.refs_3_
  207.9 5.3 collective-permute-done.18.refs_3_
  219.0 5.4 collective-permute-done.15.refs_2_
  230.3 5.4 collective-permute-done.22.refs_2_
  241.7 5.2 collective-permute-done.58.refs_2_
  247.0 5.3 collective-permute-done.60.refs_1_
  273.2 9.9 shard_map.237
  284.8 10.0 shard_map.238
  296.3 12.5 %all-to-all-done.2 = bf16[8,256,768]{2,1,0:T(8,128)(2,1)} async-done(((bf16[8,256,768]{2,1,0:T(8,128)(2,1)}), bf16[8,256,768]{2,1,0:T(8,128)(2,1)}, u32[]{:S(2)}, u32[]{:S(2)}) %all-to-all-start.2) | async-done | bytes 3145760 | tf_op jit(solution)/shard_map/all_to_all | solution.py:499
  335.4 5.5 collective-permute-done.34.refs_3_
  357.4 4.8 collective-permute-done.38.refs_2_
  364.2 4.7 all-to-all-start.3
  378.0 8.6 shard_map.247
  387.6 8.5 shard_map.248
  399.3 35.6 %all-to-all-done.3 = bf16[8,256,1408]{2,1,0:T(8,128)(2,1)} async-done(((bf16[8,256,1408]{2,1,0:T(8,128)(2,1)}), bf16[8,256,1408]{2,1,0:T(8,128)(2,1)}, u32[]{:S(2)}, u32[]{:S(2)}) %all-to-all-start.3) | async-done | bytes 5767200 | tf_op jit(solution)/shard_map/all_to_all | solution.py:499
  450.2 5.5 collective-permute-done.43.refs_3_
  461.4 5.5 collective-permute-done.50.refs_3_
  467.3 4.9 collective-permute-done.46.refs_1_
  472.2 4.8 collective-permute-done.47.refs_2_
  480.7 5.6 collective-permute-done.53.refs_1_
  486.3 5.2 collective-permute-done.54.refs_2_
  493.3 10.8 shard_map.260
  510.5 9.5 shard_map.262
  520.0 11.7 shard_map.266
  536.1 10.7 shard_map.268
  563.5 10.5 collective-permute-done.76.refs_3_
  580.4 4.9 collective-permute-done.70.refs_3_
  601.5 6.1 collective-permute-done.81.refs_2_
  621.1 10.0 shard_map.274
  636.9 9.7 shard_map.277
  656.5 11.3 collective-permute-done.92.refs_3_
  678.6 4.9 collective-permute-done.97.refs_2_
  683.7 5.6 shard_map.282.refs_4_
  699.4 9.0 all-gather.19.cloned.1.call-done
  709.1 11.3 shard_map.286
  724.6 10.7 shard_map.289
  744.7 5.8 collective-permute-done.108.refs_3_
  758.4 16.0 %shard_map.293 = (bf16[4096,1408]{1,0:T(8,128)(2,1)}, bf16[4096,704]{1,0:T(8,128)(2,1)}, f32[8,128]{1,0:T(8,128)S(1)}) custom-call(bf16[2048,2048]{1,0:T(8,128)(2,1)} %shard_map.285.refs_0_, bf16[2048,2048]{1,0:T(8,128)(2,1)} %shard_map.292.refs_1_, bf16[2048,1408]{1,0:T(8,128)(2,1)} %bitcast.31.refs_2_, bf16[2,704,2048]{2,1,0:T(8,128)(2,1)} %refs_3_.27, ...), custom_call_target="tpu_custom_call" | custom-call | flops 23000000512 | bytes 1000 | tf_op jit(solution)/shard_map/pallas_call | solution.py:97
  788.7 9.9 shard_map.296
  804.7 10.2 shard_map.299
  839.6 16.2 %shard_map.302 = (bf16[4096,1408]{1,0:T(8,128)(2,1)}, bf16[4096,704]{1,0:T(8,128)(2,1)}, f32[8,128]{1,0:T(8,128)S(1)}) custom-call(bf16[2048,2048]{1,0:T(8,128)(2,1)} %shard_map.285.refs_0_, bf16[2048,2048]{1,0:T(8,128)(2,1)} %shard_map.292.refs_1_, bf16[2048,1408]{1,0:T(8,128)(2,1)} %bitcast.31.refs_2_, ...), custom_call_target="tpu_custom_call", output_to_operand_aliasing={{0}: (4, {}), {1}: (5, {})} | custom-call | flops 23000000512 | bytes 1000 | tf_op jit(solution)/shard_map/pallas_call | solution.py:97
  874.8 5.9 shard_map.304.refs_4_
  893.8 16.1 %shard_map.308 = (bf16[4096,1408]{1,0:T(8,128)(2,1)}, bf16[4096,704]{1,0:T(8,128)(2,1)}, f32[8,128]{1,0:T(8,128)S(1)}) custom-call(bf16[2048,2048]{1,0:T(8,128)(2,1)} %collective-permute-done.138.refs_0_.refs_1_, bf16[2048,2048]{1,0:T(8,128)(2,1)} %collective-permute-done.139.refs_1_.refs_2_, ...), custom_call_target="tpu_custom_call", output_to_operand_aliasing={{0}: (4, {}), {1}: (5, {})} | custom-call | flops 23000000512 | bytes 1000 | tf_op jit(solution)/shard_map/pallas_call | solution.py:97
  909.9 16.0 %shard_map.309 = (bf16[4096,1408]{1,0:T(8,128)(2,1)}, bf16[4096,704]{1,0:T(8,128)(2,1)}, f32[8,128]{1,0:T(8,128)S(1)}) custom-call(bf16[2048,2048]{1,0:T(8,128)(2,1)} %collective-permute-done.138.refs_0_.refs_1_, bf16[2048,2048]{1,0:T(8,128)(2,1)} %collective-permute-done.139.refs_1_.refs_2_, ...), custom_call_target="tpu_custom_call", output_to_operand_aliasing={{0}: (4, {}), {1}: (5, {})} | custom-call | flops 23000000512 | bytes 1000 | tf_op jit(solution)/shard_map/pallas_call | solution.py:97
  925.9 32.6 %shard_map.310.refs_0_ = bf16[8,256,1408]{2,1,0:T(8,128)(2,1)S(1)} custom-call(bf16[2048,2048]{1,0:T(8,128)(2,1)} %shard_map.285.refs_0_, bf16[2048,2048]{1,0:T(8,128)(2,1)} %collective-permute-done.138.refs_0_.refs_1_, bf16[4096,1408]{1,0:T(8,128)(2,1)} %get-tuple-element.381.refs_2_, f32[8,128]{1,0:T(8,128)S(1)} %get-tuple-element.382.refs_3_, ...), custom_call_target="tpu_custom_call" | custom-call | flops 34500001792 | bytes 1000 | tf_op jit(solution)/shard_map/pallas_call | solution.py:97
  966.7 11.2 collective-permute-done.135
  978.0 14.7 %collective-permute-done.136 = f32[2,14336]{1,0:T(2,128)S(1)} collective-permute-done((f32[2,14336]{1,0:T(2,128)S(1)}, f32[2,14336]{1,0:T(2,128)S(1)}, u32[]{:S(2)}, u32[]{:S(2)}) %collective-permute-start.136) | collective-permute-done | bytes 114720 | tf_op jit(solution)/shard_map/ppermute | solution.py:971
  992.8 27.3 %shard_map.314 = (bf16[4096,1408]{1,0:T(8,128)(2,1)}, bf16[4096,704]{1,0:T(8,128)(2,1)}, f32[8,128]{1,0:T(8,128)S(1)}) custom-call(bf16[2048,2048]{1,0:T(8,128)(2,1)} %shard_map.306.refs_0_, bf16[2048,2048]{1,0:T(8,128)(2,1)} %shard_map.313.refs_1_, bf16[2048,1408]{1,0:T(8,128)(2,1)} %bitcast.20.refs_2_, bf16[2,704,2048]{2,1,0:T(8,128)(2,1)} %refs_3_.27, ...), custom_call_target="tpu_custom_call" | custom-call | flops 23000000512 | bytes 1000 | tf_op jit(solution)/shard_map/pallas_call | solution.py:97
  1025.9 6.6 all-to-all-done.5
  1032.5 8.8 shard_map.327
  1041.9 27.1 %shard_map.315 = (bf16[4096,1408]{1,0:T(8,128)(2,1)}, bf16[4096,704]{1,0:T(8,128)(2,1)}, f32[8,128]{1,0:T(8,128)S(1)}) custom-call(bf16[2048,2048]{1,0:T(8,128)(2,1)} %collective-permute-done.137.refs_0_.refs_1_, bf16[2048,2048]{1,0:T(8,128)(2,1)} %collective-permute-done.140.refs_1_.refs_2_, ...), custom_call_target="tpu_custom_call", output_to_operand_aliasing={{0}: (4, {}), {1}: (5, {})} | custom-call | flops 23000000512 | bytes 1000 | tf_op jit(solution)/shard_map/pallas_call | solution.py:97
  1074.2 19.5 %shard_map.317.refs_0_ = bf16[8,128,1408]{2,1,0:T(8,128)(2,1)S(1)} custom-call(bf16[2048,2048]{1,0:T(8,128)(2,1)} %shard_map.306.refs_0_, bf16[2048,2048]{1,0:T(8,128)(2,1)} %collective-permute-done.137.refs_0_.refs_1_, bf16[4096,1408]{1,0:T(8,128)(2,1)} %get-tuple-element.387.refs_2_, f32[8,128]{1,0:T(8,128)S(1)} %get-tuple-element.386.refs_1_.refs_3_), custom_call_target="tpu_custom_call" | custom-call | flops 34500001792 | bytes 1000 | tf_op jit(solution)/shard_map/pallas_call | solution.py:97
  1102.9 19.5 %shard_map.325.refs_0_ = bf16[8,128,1408]{2,1,0:T(8,128)(2,1)S(1)} custom-call(bf16[2048,2048]{1,0:T(8,128)(2,1)} %shard_map.306.refs_0_, bf16[2048,2048]{1,0:T(8,128)(2,1)} %collective-permute-done.137.refs_0_.refs_1_, bf16[4096,1408]{1,0:T(8,128)(2,1)} %get-tuple-element.387.refs_2_, bf16[8,128]{1,0:T(8,128)(2,1)S(1)} %slice.282.refs_2_.refs_3_), custom_call_target="tpu_custom_call" | custom-call | flops 34500001792 | bytes 1000 | tf_op jit(solution)/shard_map/pallas_call | solution.py:97
  1124.0 10.5 all-to-all-done.7
  1149.8 20.6 %shard_map.330.refs_3_ = f32[2,704,2048]{2,1,0:T(8,128)} custom-call(bf16[4096,704]{1,0:T(8,128)(2,1)} %get-tuple-element.395.refs_0_, bf16[2048,2048]{1,0:T(8,128)(2,1)} %shard_map.292.refs_1_, bf16[2048,2048]{1,0:T(8,128)(2,1)} %collective-permute-done.139.refs_1_.refs_2_, bf16[8,128]{1,0:T(8,128)(2,1)S(1)} %slice.287.refs_3_.refs_4_), custom_call_target="tpu_custom_call" | custom-call | flops 23000000512 | bytes 1000 | tf_op jit(solution)/shard_map/pallas_call | solution.py:97
  1173.5 20.6 %shard_map.331 = f32[2,704,2048]{2,1,0:T(8,128)} custom-call(bf16[4096,704]{1,0:T(8,128)(2,1)} %get-tuple-element.394.refs_0_, bf16[2048,2048]{1,0:T(8,128)(2,1)} %shard_map.313.refs_1_, bf16[2048,2048]{1,0:T(8,128)(2,1)} %collective-permute-done.140.refs_1_.refs_2_, f32[2,704,2048]{2,1,0:T(8,128)} %shard_map.330.refs_3_, ...), custom_call_target="tpu_custom_call", output_to_operand_aliasing={{}: (3, {})} | custom-call | flops 23000000512 | bytes 1000 | tf_op jit(solution)/shard_map/pallas_call | solution.py:97
  1194.1 5.0 shard_map.329
  (925 shorter events, 471.1 us)
Async XLA Ops:
  32.9 76.8 %all-to-all-start = ((bf16[8,256,768]{2,1,0:T(8,128)(2,1)}), bf16[8,256,768]{2,1,0:T(8,128)(2,1)}, u32[]{:S(2)}, u32[]{:S(2)}) async-start(bf16[8,256,768]{2,1,0:T(8,128)(2,1)} %shard_map.223), calls=%async_computation | async-start | bytes 6291456 | tf_op jit(solution)/shard_map/all_to_all | solution.py:499
  38.8 41.6 %collective-permute-start.1 = (bf16[64,2048]{1,0:T(8,128)(2,1)S(1)}, bf16[64,2048]{1,0:T(8,128)(2,1)S(1)}, u32[]{:S(2)}, u32[]{:S(2)}) collective-permute-start(bf16[64,2048]{1,0:T(8,128)(2,1)S(1)} %shard_map.220.refs_0_.refs_1_), channel_id=1, source_target_pairs={{0,8},{4,12},{8,0},{12,4},{16,24},{20,28},{24,16},{28,20},{1,9},{5... | collective-permute-start | bytes 786440 | tf_op jit(solution)/shard_map/ppermute | solution.py:417
  42.4 57.5 %collective-permute-start.2 = (bf16[64,2048]{1,0:T(8,128)(2,1)S(1)}, bf16[64,2048]{1,0:T(8,128)(2,1)S(1)}, u32[]{:S(2)}, u32[]{:S(2)}) collective-permute-start(bf16[64,2048]{1,0:T(8,128)(2,1)S(1)} %shard_map.220.refs_0_.refs_1_), channel_id=1, source_target_pairs={{0,16},{4,20},{8,24},{12,28},{16,0},{20,4},{24,8},{28,12},{1,17},{... | collective-permute-start | bytes 786440 | tf_op jit(solution)/shard_map/ppermute | solution.py:417
  43.9 56.8 %collective-permute-start.3 = (bf16[64,2048]{1,0:T(8,128)(2,1)S(1)}, bf16[64,2048]{1,0:T(8,128)(2,1)S(1)}, u32[]{:S(2)}, u32[]{:S(2)}) collective-permute-start(bf16[64,2048]{1,0:T(8,128)(2,1)S(1)} %shard_map.220.refs_0_.refs_1_), channel_id=1, source_target_pairs={{0,24},{4,28},{8,16},{12,20},{16,8},{20,12},{24,0},{28,4},{1,25},{... | collective-permute-start | bytes 786440 | tf_op jit(solution)/shard_map/ppermute | solution.py:417
  44.0 64.6 %collective-permute-start.5 = (bf16[64,2048]{1,0:T(8,128)(2,1)S(1)}, bf16[64,2048]{1,0:T(8,128)(2,1)}, u32[]{:S(2)}, u32[]{:S(2)}) collective-permute-start(bf16[64,2048]{1,0:T(8,128)(2,1)S(1)} %shard_map.221.refs_4_.refs_2_.refs_0_), channel_id=1, source_target_pairs={{0,8},{4,12},{8,0},{12,4},{16,24},{20,28},{24,16},{28,20},{1,9},{5... | collective-permute-start | bytes 786440 | tf_op jit(solution)/shard_map/ppermute | solution.py:417
  45.9 62.7 %collective-permute-start.6 = (bf16[64,2048]{1,0:T(8,128)(2,1)S(1)}, bf16[64,2048]{1,0:T(8,128)(2,1)}, u32[]{:S(2)}, u32[]{:S(2)}) collective-permute-start(bf16[64,2048]{1,0:T(8,128)(2,1)S(1)} %shard_map.221.refs_4_.refs_2_.refs_0_), channel_id=1, source_target_pairs={{0,16},{4,20},{8,24},{12,28},{16,0},{20,4},{24,8},{28,12},{1,17},{... | collective-permute-start | bytes 786440 | tf_op jit(solution)/shard_map/ppermute | solution.py:417
  80.4 28.2 %collective-permute-start.7 = (bf16[64,2048]{1,0:T(8,128)(2,1)S(1)}, bf16[64,2048]{1,0:T(8,128)(2,1)}, u32[]{:S(2)}, u32[]{:S(2)}) collective-permute-start(bf16[64,2048]{1,0:T(8,128)(2,1)S(1)} %shard_map.221.refs_4_.refs_2_.refs_0_), channel_id=1, source_target_pairs={{0,24},{4,28},{8,16},{12,20},{16,8},{20,12},{24,0},{28,4},{1,25},{... | collective-permute-start | bytes 786440 | tf_op jit(solution)/shard_map/ppermute | solution.py:417
  110.4 70.7 %all-to-all-start.1 = ((bf16[8,256,1408]{2,1,0:T(8,128)(2,1)}), bf16[8,256,1408]{2,1,0:T(8,128)(2,1)}, u32[]{:S(2)}, u32[]{:S(2)}) async-start(bf16[8,256,1408]{2,1,0:T(8,128)(2,1)} %shard_map.226), calls=%async_computation.1 | async-start | bytes 11534336 | tf_op jit(solution)/shard_map/all_to_all | solution.py:499
  115.2 377.4 %all-gather.15.cloned.1.call-start = ((), (), s32[]{:S(2)}) async-start(), calls=%async_computation.13 | async-start | bytes 10485760 | tf_op jit(solution)/shard_map/all_gather | solution.py:689
  132.3 49.5 %collective-permute-start.8 = (bf16[4,64,2048]{2,1,0:T(8,128)(2,1)}, bf16[4,64,2048]{2,1,0:T(8,128)(2,1)}, u32[]{:S(2)}, u32[]{:S(2)}) collective-permute-start(bf16[4,64,2048]{2,1,0:T(8,128)(2,1)} %get-tuple-element.205), channel_id=1, source_target_pairs={{0,4},{4,0},{8,12},{12,8},{16,20},{20,16},{24,28},{28,24},{1,5},{5... | collective-permute-start | bytes 3145736 | tf_op jit(solution)/shard_map/ppermute | solution.py:417
  144.0 46.2 %collective-permute-start.13 = (bf16[4,64,2048]{2,1,0:T(8,128)(2,1)}, bf16[4,64,2048]{2,1,0:T(8,128)(2,1)S(1)}, u32[]{:S(2)}, u32[]{:S(2)}) collective-permute-start(bf16[4,64,2048]{2,1,0:T(8,128)(2,1)} %get-tuple-element.211), channel_id=1, source_target_pairs={{0,4},{4,0},{8,12},{12,8},{16,20},{20,16},{24,28},{28,24},{1,5},{5... | collective-permute-start | bytes 3145736 | tf_op jit(solution)/shard_map/ppermute | solution.py:417
  145.0 58.9 %collective-permute-start.56 = (bf16[64,2048]{1,0:T(8,128)(2,1)}, bf16[64,2048]{1,0:T(8,128)(2,1)}, u32[]{:S(2)}, u32[]{:S(2)}) collective-permute-start(bf16[64,2048]{1,0:T(8,128)(2,1)} %select_bitcast_fusion), channel_id=1, source_target_pairs={{0,4},{4,0},{8,12},{12,8},{16,20},{20,16},{24,28},{28,24},{1,5},{5... | collective-permute-start | bytes 786440 | tf_op jit(solution)/shard_map/ppermute | solution.py:417
  203.9 20.5 %collective-permute-start.15 = (bf16[64,2048]{1,0:T(8,128)(2,1)S(1)}, bf16[64,2048]{1,0:T(8,128)(2,1)S(1)}, u32[]{:S(2)}, u32[]{:S(2)}) collective-permute-start(bf16[64,2048]{1,0:T(8,128)(2,1)S(1)} %get-tuple-element.214.refs_0_), channel_id=1, source_target_pairs={{0,16},{4,20},{8,24},{12,28},{16,0},{20,4},{24,8},{28,12},{1,17},{... | collective-permute-start | bytes 786440 | tf_op jit(solution)/shard_map/ppermute | solution.py:417
  213.8 21.9 %collective-permute-start.22 = (bf16[64,2048]{1,0:T(8,128)(2,1)S(1)}, bf16[64,2048]{1,0:T(8,128)(2,1)S(1)}, u32[]{:S(2)}, u32[]{:S(2)}) collective-permute-start(bf16[64,2048]{1,0:T(8,128)(2,1)S(1)} %get-tuple-element.219.refs_0_), channel_id=1, source_target_pairs={{0,16},{4,20},{8,24},{12,28},{16,0},{20,4},{24,8},{28,12},{1,17},{... | collective-permute-start | bytes 786440 | tf_op jit(solution)/shard_map/ppermute | solution.py:417
  224.4 22.5 %collective-permute-start.58 = (bf16[64,2048]{1,0:T(8,128)(2,1)S(1)}, bf16[64,2048]{1,0:T(8,128)(2,1)S(1)}, u32[]{:S(2)}, u32[]{:S(2)}) collective-permute-start(bf16[64,2048]{1,0:T(8,128)(2,1)S(1)} %shard_map.255.refs_0_), channel_id=1, source_target_pairs={{0,16},{4,20},{8,24},{12,28},{16,0},{20,4},{24,8},{28,12},{1,17},{... | collective-permute-start | bytes 786440 | tf_op jit(solution)/shard_map/ppermute | solution.py:417
  235.7 21.3 %collective-permute-start.61 = (bf16[64,2048]{1,0:T(8,128)(2,1)S(1)}, bf16[64,2048]{1,0:T(8,128)(2,1)S(1)}, u32[]{:S(2)}, u32[]{:S(2)}) collective-permute-start(bf16[64,2048]{1,0:T(8,128)(2,1)S(1)} %shard_map.257.refs_0_), channel_id=1, source_target_pairs={{0,16},{4,20},{8,24},{12,28},{16,0},{20,4},{24,8},{28,12},{1,17},{... | collective-permute-start | bytes 786440 | tf_op jit(solution)/shard_map/ppermute | solution.py:417
  264.5 20.3 %collective-permute-start.25 = (bf16[4,64,2048]{2,1,0:T(8,128)(2,1)S(1)}, bf16[4,64,2048]{2,1,0:T(8,128)(2,1)}, u32[]{:S(2)}, u32[]{:S(2)}) collective-permute-start(bf16[4,64,2048]{2,1,0:T(8,128)(2,1)S(1)} %shard_map.235.refs_2_.refs_0_.refs_4_.refs_1_), channel_id=1, source_target_pairs={{0,4},{4,0},{8,12},{12,8},{16,20},{20,16},{24,28},{28,24},{1,5},{5... | collective-permute-start | bytes 3145736 | tf_op jit(solution)/shard_map/ppermute | solution.py:417
  266.4 42.4 %all-to-all-start.2 = ((bf16[8,256,768]{2,1,0:T(8,128)(2,1)}), bf16[8,256,768]{2,1,0:T(8,128)(2,1)}, u32[]{:S(2)}, u32[]{:S(2)}) async-start(bf16[8,256,768]{2,1,0:T(8,128)(2,1)} %shard_map.236), calls=%async_computation.2 | async-start | bytes 6291456 | tf_op jit(solution)/shard_map/all_to_all | solution.py:499
  270.9 339.2 %all-gather.17.cloned.1.call-start = ((), (), s32[]{:S(2)}) async-start(), calls=%async_computation.14 | async-start | bytes 10485760 | tf_op jit(solution)/shard_map/all_gather | solution.py:689
  284.5 25.0 %collective-permute-start.24 = (bf16[4,64,2048]{2,1,0:T(8,128)(2,1)}, bf16[4,64,2048]{2,1,0:T(8,128)(2,1)}, u32[]{:S(2)}, u32[]{:S(2)}) collective-permute-start(bf16[4,64,2048]{2,1,0:T(8,128)(2,1)} %get-tuple-element.221), channel_id=1, source_target_pairs={{0,4},{4,0},{8,12},{12,8},{16,20},{20,16},{24,28},{28,24},{1,5},{5... | collective-permute-start | bytes 3145736 | tf_op jit(solution)/shard_map/ppermute | solution.py:417
  296.1 21.7 %collective-permute-start.29 = (bf16[4,64,2048]{2,1,0:T(8,128)(2,1)}, bf16[4,64,2048]{2,1,0:T(8,128)(2,1)S(1)}, u32[]{:S(2)}, u32[]{:S(2)}) collective-permute-start(bf16[4,64,2048]{2,1,0:T(8,128)(2,1)} %get-tuple-element.227), channel_id=1, source_target_pairs={{0,4},{4,0},{8,12},{12,8},{16,20},{20,16},{24,28},{28,24},{1,5},{5... | collective-permute-start | bytes 3145736 | tf_op jit(solution)/shard_map/ppermute | solution.py:417
  330.2 23.2 %collective-permute-start.31 = (bf16[64,2048]{1,0:T(8,128)(2,1)S(1)}, bf16[64,2048]{1,0:T(8,128)(2,1)S(1)}, u32[]{:S(2)}, u32[]{:S(2)}) collective-permute-start(bf16[64,2048]{1,0:T(8,128)(2,1)S(1)} %get-tuple-element.230.refs_0_), channel_id=1, source_target_pairs={{0,16},{4,20},{8,24},{12,28},{16,0},{20,4},{24,8},{28,12},{1,17},{... | collective-permute-start | bytes 786440 | tf_op jit(solution)/shard_map/ppermute | solution.py:417
  341.5 20.7 %collective-permute-start.38 = (bf16[64,2048]{1,0:T(8,128)(2,1)S(1)}, bf16[64,2048]{1,0:T(8,128)(2,1)S(1)}, u32[]{:S(2)}, u32[]{:S(2)}) collective-permute-start(bf16[64,2048]{1,0:T(8,128)(2,1)S(1)} %get-tuple-element.235.refs_0_), channel_id=1, source_target_pairs={{0,16},{4,20},{8,24},{12,28},{16,0},{20,4},{24,8},{28,12},{1,17},{... | collective-permute-start | bytes 786440 | tf_op jit(solution)/shard_map/ppermute | solution.py:417
  364.2 70.7 %all-to-all-start.3 = ((bf16[8,256,1408]{2,1,0:T(8,128)(2,1)}), bf16[8,256,1408]{2,1,0:T(8,128)(2,1)}, u32[]{:S(2)}, u32[]{:S(2)}) async-start(bf16[8,256,1408]{2,1,0:T(8,128)(2,1)} %shard_map.246), calls=%async_computation.3 | async-start | bytes 11534336 | tf_op jit(solution)/shard_map/all_to_all | solution.py:499
  368.9 339.4 %all-gather.19.cloned.1.call-start = ((), (), s32[]{:S(2)}) async-start(), calls=%async_computation.15 | async-start | bytes 10485760 | tf_op jit(solution)/shard_map/all_gather | solution.py:689
  387.4 48.1 %collective-permute-start.40 = (bf16[4,64,2048]{2,1,0:T(8,128)(2,1)}, bf16[4,64,2048]{2,1,0:T(8,128)(2,1)}, u32[]{:S(2)}, u32[]{:S(2)}) collective-permute-start(bf16[4,64,2048]{2,1,0:T(8,128)(2,1)} %get-tuple-element.237), channel_id=1, source_target_pairs={{0,4},{4,0},{8,12},{12,8},{16,20},{20,16},{24,28},{28,24},{1,5},{5... | collective-permute-start | bytes 3145736 | tf_op jit(solution)/shard_map/ppermute | solution.py:417
  399.0 44.9 %collective-permute-start.45 = (bf16[4,64,2048]{2,1,0:T(8,128)(2,1)}, bf16[4,64,2048]{2,1,0:T(8,128)(2,1)}, u32[]{:S(2)}, u32[]{:S(2)}) collective-permute-start(bf16[4,64,2048]{2,1,0:T(8,128)(2,1)} %get-tuple-element.243), channel_id=1, source_target_pairs={{0,4},{4,0},{8,12},{12,8},{16,20},{20,16},{24,28},{28,24},{1,5},{5... | collective-permute-start | bytes 3145736 | tf_op jit(solution)/shard_map/ppermute | solution.py:417
  445.9 21.0 %collective-permute-start.50 = (bf16[64,2048]{1,0:T(8,128)(2,1)S(1)}, bf16[64,2048]{1,0:T(8,128)(2,1)S(1)}, u32[]{:S(2)}, u32[]{:S(2)}) collective-permute-start(bf16[64,2048]{1,0:T(8,128)(2,1)S(1)} %get-tuple-element.248), channel_id=1, source_target_pairs={{0,16},{4,20},{8,24},{12,28},{16,0},{20,4},{24,8},{28,12},{1,17},{... | collective-permute-start | bytes 786440 | tf_op jit(solution)/shard_map/ppermute | solution.py:417
  507.3 330.1 %reduce-scatter.3.cloned.1.call-start = ((), (), s32[]{:S(2)}) async-start(), calls=%async_computation.11 | async-start | bytes 5242880 | tf_op jit(solution)/shard_map/reduce_scatter | solution.py:664
  550.8 23.3 %collective-permute-start.76 = (bf16[64,2048]{1,0:T(8,128)(2,1)S(1)}, bf16[64,2048]{1,0:T(8,128)(2,1)S(1)}, u32[]{:S(2)}, u32[]{:S(2)}) collective-permute-start(bf16[64,2048]{1,0:T(8,128)(2,1)S(1)} %get-tuple-element.270), channel_id=1, source_target_pairs={{0,16},{4,20},{8,24},{12,28},{16,0},{20,4},{24,8},{28,12},{1,17},{... | collective-permute-start | bytes 786440 | tf_op jit(solution)/shard_map/ppermute | solution.py:417
  551.3 23.2 %collective-permute-start.77 = (bf16[64,2048]{1,0:T(8,128)(2,1)S(1)}, bf16[64,2048]{1,0:T(8,128)(2,1)S(1)}, u32[]{:S(2)}, u32[]{:S(2)}) collective-permute-start(bf16[64,2048]{1,0:T(8,128)(2,1)S(1)} %get-tuple-element.271), channel_id=1, source_target_pairs={{0,24},{4,28},{8,16},{12,20},{16,8},{20,12},{24,0},{28,4},{1,25},{... | collective-permute-start | bytes 786440 | tf_op jit(solution)/shard_map/ppermute | solution.py:417
  558.1 20.8 %collective-permute-start.69 = (bf16[64,2048]{1,0:T(8,128)(2,1)S(1)}, bf16[64,2048]{1,0:T(8,128)(2,1)S(1)}, u32[]{:S(2)}, u32[]{:S(2)}) collective-permute-start(bf16[64,2048]{1,0:T(8,128)(2,1)S(1)} %get-tuple-element.261), channel_id=1, source_target_pairs={{0,8},{4,12},{8,0},{12,4},{16,24},{20,28},{24,16},{28,20},{1,9},{5... | collective-permute-start | bytes 786440 | tf_op jit(solution)/shard_map/ppermute | solution.py:417
  562.0 23.2 %collective-permute-start.70 = (bf16[64,2048]{1,0:T(8,128)(2,1)S(1)}, bf16[64,2048]{1,0:T(8,128)(2,1)S(1)}, u32[]{:S(2)}, u32[]{:S(2)}) collective-permute-start(bf16[64,2048]{1,0:T(8,128)(2,1)S(1)} %get-tuple-element.262), channel_id=1, source_target_pairs={{0,16},{4,20},{8,24},{12,28},{16,0},{20,4},{24,8},{28,12},{1,17},{... | collective-permute-start | bytes 786440 | tf_op jit(solution)/shard_map/ppermute | solution.py:417
  576.0 20.4 %collective-permute-start.84 = (bf16[64,2048]{1,0:T(8,128)(2,1)S(1)}, bf16[64,2048]{1,0:T(8,128)(2,1)S(1)}, u32[]{:S(2)}, u32[]{:S(2)}) collective-permute-start(bf16[64,2048]{1,0:T(8,128)(2,1)S(1)} %get-tuple-element.278), channel_id=1, source_target_pairs={{0,16},{4,20},{8,24},{12,28},{16,0},{20,4},{24,8},{28,12},{1,17},{... | collective-permute-start | bytes 786440 | tf_op jit(solution)/shard_map/ppermute | solution.py:417
  585.5 22.0 %collective-permute-start.81 = (bf16[64,2048]{1,0:T(8,128)(2,1)S(1)}, bf16[64,2048]{1,0:T(8,128)(2,1)S(1)}, u32[]{:S(2)}, u32[]{:S(2)}) collective-permute-start(bf16[64,2048]{1,0:T(8,128)(2,1)S(1)} %get-tuple-element.276.refs_0_), channel_id=1, source_target_pairs={{0,16},{4,20},{8,24},{12,28},{16,0},{20,4},{24,8},{28,12},{1,17},{... | collective-permute-start | bytes 786440 | tf_op jit(solution)/shard_map/ppermute | solution.py:417
  647.3 20.4 %collective-permute-start.92 = (bf16[64,2048]{1,0:T(8,128)(2,1)S(1)}, bf16[64,2048]{1,0:T(8,128)(2,1)S(1)}, u32[]{:S(2)}, u32[]{:S(2)}) collective-permute-start(bf16[64,2048]{1,0:T(8,128)(2,1)S(1)} %get-tuple-element.289), channel_id=1, source_target_pairs={{0,16},{4,20},{8,24},{12,28},{16,0},{20,4},{24,8},{28,12},{1,17},{... | collective-permute-start | bytes 786440 | tf_op jit(solution)/shard_map/ppermute | solution.py:417
  652.2 21.1 %collective-permute-start.100 = (bf16[64,2048]{1,0:T(8,128)(2,1)S(1)}, bf16[64,2048]{1,0:T(8,128)(2,1)S(1)}, u32[]{:S(2)}, u32[]{:S(2)}) collective-permute-start(bf16[64,2048]{1,0:T(8,128)(2,1)S(1)} %get-tuple-element.300), channel_id=1, source_target_pairs={{0,16},{4,20},{8,24},{12,28},{16,0},{20,4},{24,8},{28,12},{1,17},{... | collective-permute-start | bytes 786440 | tf_op jit(solution)/shard_map/ppermute | solution.py:417
  652.6 22.2 %collective-permute-start.101 = (bf16[64,2048]{1,0:T(8,128)(2,1)S(1)}, bf16[64,2048]{1,0:T(8,128)(2,1)S(1)}, u32[]{:S(2)}, u32[]{:S(2)}) collective-permute-start(bf16[64,2048]{1,0:T(8,128)(2,1)S(1)} %get-tuple-element.301), channel_id=1, source_target_pairs={{0,24},{4,28},{8,16},{12,20},{16,8},{20,12},{24,0},{28,4},{1,25},{... | collective-permute-start | bytes 786440 | tf_op jit(solution)/shard_map/ppermute | solution.py:417
  683.6 25.5 %collective-permute-start.102 = (bf16[4,64,2048]{2,1,0:T(8,128)(2,1)S(1)}, bf16[4,64,2048]{2,1,0:T(8,128)(2,1)}, u32[]{:S(2)}, u32[]{:S(2)}) collective-permute-start(bf16[4,64,2048]{2,1,0:T(8,128)(2,1)S(1)} %shard_map.281.refs_0_), channel_id=1, source_target_pairs={{0,4},{4,0},{8,12},{12,8},{16,20},{20,16},{24,28},{28,24},{1,5},{5... | collective-permute-start | bytes 3145736 | tf_op jit(solution)/shard_map/ppermute | solution.py:417
  695.0 266.8 %all-gather.21.cloned.1.call-start = ((), (), s32[]{:S(2)}) async-start(), calls=%async_computation.16 | async-start | bytes 10485760 | tf_op jit(solution)/shard_map/all_gather | solution.py:689
  695.9 24.6 %collective-permute-start.104 = (bf16[64,2048]{1,0:T(8,128)(2,1)S(1)}, bf16[64,2048]{1,0:T(8,128)(2,1)S(1)}, u32[]{:S(2)}, u32[]{:S(2)}) collective-permute-start(bf16[64,2048]{1,0:T(8,128)(2,1)S(1)} %copy-done.143), channel_id=1, source_target_pairs={{0,8},{4,12},{8,0},{12,4},{16,24},{20,28},{24,16},{28,20},{1,9},{5... | collective-permute-start | bytes 786440 | tf_op jit(solution)/shard_map/ppermute | solution.py:417
  697.6 22.9 %collective-permute-start.105 = (bf16[64,2048]{1,0:T(8,128)(2,1)S(1)}, bf16[64,2048]{1,0:T(8,128)(2,1)}, u32[]{:S(2)}, u32[]{:S(2)}) collective-permute-start(bf16[64,2048]{1,0:T(8,128)(2,1)S(1)} %copy-done.143), channel_id=1, source_target_pairs={{0,16},{4,20},{8,24},{12,28},{16,0},{20,4},{24,8},{28,12},{1,17},{... | collective-permute-start | bytes 786440 | tf_op jit(solution)/shard_map/ppermute | solution.py:417
  697.9 22.6 %collective-permute-start.106 = (bf16[64,2048]{1,0:T(8,128)(2,1)S(1)}, bf16[64,2048]{1,0:T(8,128)(2,1)}, u32[]{:S(2)}, u32[]{:S(2)}) collective-permute-start(bf16[64,2048]{1,0:T(8,128)(2,1)S(1)} %copy-done.143), channel_id=1, source_target_pairs={{0,24},{4,28},{8,16},{12,20},{16,8},{20,12},{24,0},{28,4},{1,25},{... | collective-permute-start | bytes 786440 | tf_op jit(solution)/shard_map/ppermute | solution.py:417
  752.0 26.7 %collective-permute-start.112 = (bf16[64,2048]{1,0:T(8,128)(2,1)S(1)}, bf16[64,2048]{1,0:T(8,128)(2,1)S(1)}, u32[]{:S(2)}, u32[]{:S(2)}) collective-permute-start(bf16[64,2048]{1,0:T(8,128)(2,1)S(1)} %get-tuple-element.324.refs_0_), channel_id=1, source_target_pairs={{0,8},{4,12},{8,0},{12,4},{16,24},{20,28},{24,16},{28,20},{1,9},{5... | collective-permute-start | bytes 786440 | tf_op jit(solution)/shard_map/ppermute | solution.py:417
  753.5 25.2 %collective-permute-start.113 = (bf16[64,2048]{1,0:T(8,128)(2,1)S(1)}, bf16[64,2048]{1,0:T(8,128)(2,1)S(1)}, u32[]{:S(2)}, u32[]{:S(2)}) collective-permute-start(bf16[64,2048]{1,0:T(8,128)(2,1)S(1)} %get-tuple-element.324.refs_0_), channel_id=1, source_target_pairs={{0,16},{4,20},{8,24},{12,28},{16,0},{20,4},{24,8},{28,12},{1,17},{... | collective-permute-start | bytes 786440 | tf_op jit(solution)/shard_map/ppermute | solution.py:417
  754.1 24.6 %collective-permute-start.114 = (bf16[64,2048]{1,0:T(8,128)(2,1)S(1)}, bf16[64,2048]{1,0:T(8,128)(2,1)S(1)}, u32[]{:S(2)}, u32[]{:S(2)}) collective-permute-start(bf16[64,2048]{1,0:T(8,128)(2,1)S(1)} %get-tuple-element.324.refs_0_), channel_id=1, source_target_pairs={{0,24},{4,28},{8,16},{12,20},{16,8},{20,12},{24,0},{28,4},{1,25},{... | collective-permute-start | bytes 786440 | tf_op jit(solution)/shard_map/ppermute | solution.py:417
  755.5 21.7 %collective-permute-start.116 = (bf16[64,2048]{1,0:T(8,128)(2,1)S(1)}, bf16[64,2048]{1,0:T(8,128)(2,1)S(1)}, u32[]{:S(2)}, u32[]{:S(2)}) collective-permute-start(bf16[64,2048]{1,0:T(8,128)(2,1)S(1)} %get-tuple-element.326), channel_id=1, source_target_pairs={{0,16},{4,20},{8,24},{12,28},{16,0},{20,4},{24,8},{28,12},{1,17},{... | collective-permute-start | bytes 786440 | tf_op jit(solution)/shard_map/ppermute | solution.py:417
  756.7 20.6 %collective-permute-start.117 = (bf16[64,2048]{1,0:T(8,128)(2,1)S(1)}, bf16[64,2048]{1,0:T(8,128)(2,1)S(1)}, u32[]{:S(2)}, u32[]{:S(2)}) collective-permute-start(bf16[64,2048]{1,0:T(8,128)(2,1)S(1)} %get-tuple-element.327), channel_id=1, source_target_pairs={{0,24},{4,28},{8,16},{12,20},{16,8},{20,12},{24,0},{28,4},{1,25},{... | collective-permute-start | bytes 786440 | tf_op jit(solution)/shard_map/ppermute | solution.py:417
  801.1 92.7 %collective-permute-start.139 = (bf16[2048,2048]{1,0:T(8,128)(2,1)}, bf16[2048,2048]{1,0:T(8,128)(2,1)}, u32[]{:S(2)}, u32[]{:S(2)}) collective-permute-start(bf16[2048,2048]{1,0:T(8,128)(2,1)} %shard_map.292.refs_1_), channel_id=1, source_target_pairs={{0,4},{4,0},{8,12},{12,8},{16,20},{20,16},{24,28},{28,24},{1,5},{5... | collective-permute-start | bytes 25165832 | tf_op jit(solution)/shard_map/ppermute | solution.py:417
  822.3 71.5 %collective-permute-start.138 = (bf16[2048,2048]{1,0:T(8,128)(2,1)}, bf16[2048,2048]{1,0:T(8,128)(2,1)}, u32[]{:S(2)}, u32[]{:S(2)}) collective-permute-start(bf16[2048,2048]{1,0:T(8,128)(2,1)} %shard_map.285.refs_0_), channel_id=1, source_target_pairs={{0,4},{4,0},{8,12},{12,8},{16,20},{20,16},{24,28},{28,24},{1,5},{5... | collective-permute-start | bytes 25165832 | tf_op jit(solution)/shard_map/ppermute | solution.py:417
  826.2 29.6 %collective-permute-start.128 = (bf16[64,2048]{1,0:T(8,128)(2,1)}, bf16[64,2048]{1,0:T(8,128)(2,1)S(1)}, u32[]{:S(2)}, u32[]{:S(2)}) collective-permute-start(bf16[64,2048]{1,0:T(8,128)(2,1)} %get-tuple-element.347), channel_id=1, source_target_pairs={{0,8},{4,12},{8,0},{12,4},{16,24},{20,28},{24,16},{28,20},{1,9},{5... | collective-permute-start | bytes 786440 | tf_op jit(solution)/shard_map/ppermute | solution.py:417
  831.4 25.1 %collective-permute-start.129 = (bf16[64,2048]{1,0:T(8,128)(2,1)}, bf16[64,2048]{1,0:T(8,128)(2,1)}, u32[]{:S(2)}, u32[]{:S(2)}) collective-permute-start(bf16[64,2048]{1,0:T(8,128)(2,1)} %get-tuple-element.348), channel_id=1, source_target_pairs={{0,16},{4,20},{8,24},{12,28},{16,0},{20,4},{24,8},{28,12},{1,17},{... | collective-permute-start | bytes 786440 | tf_op jit(solution)/shard_map/ppermute | solution.py:417
  832.0 24.5 %collective-permute-start.130 = (bf16[64,2048]{1,0:T(8,128)(2,1)}, bf16[64,2048]{1,0:T(8,128)(2,1)}, u32[]{:S(2)}, u32[]{:S(2)}) collective-permute-start(bf16[64,2048]{1,0:T(8,128)(2,1)} %get-tuple-element.349), channel_id=1, source_target_pairs={{0,24},{4,28},{8,16},{12,20},{16,8},{20,12},{24,0},{28,4},{1,25},{... | collective-permute-start | bytes 786440 | tf_op jit(solution)/shard_map/ppermute | solution.py:417
  861.5 180.4 %collective-permute-start.137 = (bf16[2048,2048]{1,0:T(8,128)(2,1)}, bf16[2048,2048]{1,0:T(8,128)(2,1)}, u32[]{:S(2)}, u32[]{:S(2)}) collective-permute-start(bf16[2048,2048]{1,0:T(8,128)(2,1)} %shard_map.306.refs_0_), channel_id=1, source_target_pairs={{0,4},{4,0},{8,12},{12,8},{16,20},{20,16},{24,28},{28,24},{1,5},{5... | collective-permute-start | bytes 25165832 | tf_op jit(solution)/shard_map/ppermute | solution.py:417
  862.9 98.2 %all-to-all-start.4 = ((bf16[8,64,768]{2,1,0:T(8,128)(2,1)}), bf16[8,64,768]{2,1,0:T(8,128)(2,1)S(1)}, u32[]{:S(2)}, u32[]{:S(2)}) async-start(bf16[8,64,768]{2,1,0:T(8,128)(2,1)} %shard_map.311), calls=%async_computation.6 | async-start | bytes 1572864 | tf_op jit(solution)/shard_map/all_to_all | solution.py:499
  866.5 154.1 %reduce-scatter.5.cloned.1.call-start = ((), (), s32[]{:S(2)}) async-start(), calls=%async_computation.12 | async-start | bytes 5242880 | tf_op jit(solution)/shard_map/reduce_scatter | solution.py:664
  866.7 20.3 %collective-permute-start.133 = (f32[2,14336]{1,0:T(2,128)S(1)}, f32[2,14336]{1,0:T(2,128)}, u32[]{:S(2)}, u32[]{:S(2)}) collective-permute-start(f32[2,14336]{1,0:T(2,128)S(1)} %fusion.15.refs_8_), channel_id=1, source_target_pairs={{0,8},{4,12},{8,0},{12,4},{16,24},{20,28},{24,16},{28,20},{1,9},{5... | collective-permute-start | bytes 344072 | tf_op jit(solution)/shard_map/ppermute | solution.py:417
  961.8 80.1 %collective-permute-start.140 = (bf16[2048,2048]{1,0:T(8,128)(2,1)}, bf16[2048,2048]{1,0:T(8,128)(2,1)}, u32[]{:S(2)}, u32[]{:S(2)}) collective-permute-start(bf16[2048,2048]{1,0:T(8,128)(2,1)} %shard_map.313.refs_1_), channel_id=1, source_target_pairs={{0,4},{4,0},{8,12},{12,8},{16,20},{20,16},{24,28},{28,24},{1,5},{5... | collective-permute-start | bytes 25165832 | tf_op jit(solution)/shard_map/ppermute | solution.py:417
  961.8 70.7 %all-to-all-start.5 = ((bf16[8,256,1408]{2,1,0:T(8,128)(2,1)}), bf16[8,256,1408]{2,1,0:T(8,128)(2,1)}, u32[]{:S(2)}, u32[]{:S(2)}) async-start(bf16[8,256,1408]{2,1,0:T(8,128)(2,1)} %shard_map.312), calls=%async_computation.7 | async-start | bytes 11534336 | tf_op jit(solution)/shard_map/all_to_all | solution.py:499
  966.5 168.0 %all-gather.25.cloned.1.call-start = ((), (), s32[]{:S(2)}) async-start(), calls=%async_computation.18 | async-start | bytes 5242880 | tf_op jit(solution)/shard_map/all_gather | solution.py:675
  1070.0 23.8 %all-to-all-start.6 = ((bf16[8,64,768]{2,1,0:T(8,128)(2,1)}), bf16[8,64,768]{2,1,0:T(8,128)(2,1)}, u32[]{:S(2)}, u32[]{:S(2)}) async-start(bf16[8,64,768]{2,1,0:T(8,128)(2,1)} %shard_map.316), calls=%async_computation.8 | async-start | bytes 1572864 | tf_op jit(solution)/shard_map/all_to_all | solution.py:499
  1095.4 39.2 %all-to-all-start.7 = ((bf16[8,128,1408]{2,1,0:T(8,128)(2,1)}), bf16[8,128,1408]{2,1,0:T(8,128)(2,1)S(1)}, u32[]{:S(2)}, u32[]{:S(2)}) async-start(bf16[8,128,1408]{2,1,0:T(8,128)(2,1)} %copy-done.12), calls=%async_computation.9 | async-start | bytes 5767168 | tf_op jit(solution)/shard_map/all_to_all | solution.py:499
  1099.5 99.6 %all-gather.23.cloned.1.call-start = ((), (), s32[]{:S(2)}) async-start(), calls=%async_computation.17 | async-start | bytes 5242880 | tf_op jit(solution)/shard_map/all_gather | solution.py:675
  1144.4 49.6 %all-to-all-start.8 = ((bf16[8,128,1408]{2,1,0:T(8,128)(2,1)}), bf16[8,128,1408]{2,1,0:T(8,128)(2,1)}, u32[]{:S(2)}, u32[]{:S(2)}) async-start(bf16[8,128,1408]{2,1,0:T(8,128)(2,1)} %copy-done.15), calls=%async_computation.10 | async-start | bytes 5767168 | tf_op jit(solution)/shard_map/all_to_all | solution.py:499
  (300 other events, 3254.2 us)
Sparse Core Ops, SparseCore 0:
  259.6 149.8 all-gather.14
  411.0 147.8 all-gather.16
  560.5 147.8 all-gather.18
  711.1 74.9 reduce-scatter.2
  787.6 150.1 all-gather.20
  940.6 79.8 reduce-scatter.4
  1023.0 81.1 all-gather.24
  1105.8 79.2 all-gather.22

commit v4 on v3

--- a/solution.py
+++ b/solution.py
@@ -87,8 +87,8 @@
 def call(kernel, grid, in_specs, out_specs, out_shape, vmem=48, aliases=None, weight=1000):
     reads = len(in_specs)
 
-    def run(*operands, after=()):
-        after = [corner(v) for v in after]
+    def run(*operands, after=(), pieces=True):
+        after = [corner(v) for v in after] if pieces else list(after)
 
         def body(*refs):
             kernel(*refs[:reads], *refs[reads + len(after) :])
@@ -111,7 +111,8 @@
 def hold(values, after):
     anywhere = pl.BlockSpec(memory_space=pl.ANY)
     shape = jax.ShapeDtypeStruct(values.shape, values.dtype)
-    return call(lambda *_: None, None, [anywhere], anywhere, shape, 48, aliases={0: 0})(values, after=after)
+    run = call(lambda *_: None, None, [anywhere], anywhere, shape, 62, aliases={0: 0})
+    return run(values, after=after, pieces=False)
 
 
 def whole(shape, layer=None):
@@ -619,7 +620,7 @@
         )
         places_of = dict(qkv=place_qkv, feed=place_feed, out=place_blocks)
 
-        def write_blocks(layer, name, blocks, n, cut, first, at=0):
+        def write_blocks(layer, name, blocks, n, cut, first, at=0, after=()):
             parts, a, r, _ = blocks.shape
             shapes = shapes_of[name]
             earlier = written.get(name, [])
@@ -634,7 +635,7 @@
                 [shape_of(v, f32) for v in shapes],
                 32,
                 aliases={1 + k: k for k in range(len(earlier))},
-            )(blocks, *earlier)
+            )(blocks, *earlier, after=after)
 
         quarter = rows // reps
         packed_shape = shape_of((reps, shards, quarter, 4 * cols), bf16)
@@ -757,20 +758,27 @@
                 self.done += 1
                 return [token]
 
-            def columns(self, after, before=()):
-                got = all_columns(self.normed, self.carried[0], len(self.blocks), self.cuts, after=after)
-                got = hold(got, self.blocks[-1:] + list(before))
+            def columns_now(self, after):
+                self.got = all_columns(self.normed, self.carried[0], len(self.blocks), self.cuts, after=after)
+                return [self.got]
+
+            def columns_held(self, before=()):
+                got = hold(self.got, self.blocks[-1:] + list(before))
                 self.blocks.append(spread(got))
                 return [got]
+
+            def columns(self, after, before=()):
+                self.columns_now(after)
+                return self.columns_held(before)
 
             def down(self, after):
                 all_down(self.layer, self.carried[1], self.down_in, after=after)
                 return after
 
-            def write(self):
+            def write(self, after=()):
                 r = rows // self.cuts
                 for k, blocks in enumerate(self.blocks):
-                    write_blocks(self.layer, "feed", blocks[None], blocks.shape[2], 32, k * r)
+                    write_blocks(self.layer, "feed", blocks[None], blocks.shape[2], 32, k * r, after=after)
 
         def share(values):
             first, second = values[:part], values[part:]
@@ -803,6 +811,8 @@
             first = run(0, gathered, list(after))
             if other is None:
                 other = collect(sent, [first[0]])
+            if finish is None:
+                return (first, run(1, other, [first[0]])), None, None, None
             if due is None:
                 sums = send_sums(first, [other[0]])
                 second = run(1, other, [sums[0]])
@@ -819,12 +829,14 @@
             if sent is None:
                 return (first, second), (done, end), None, (gathered, other)
             inputs = (gathered, other)
-            gathered, sent = collect(sent, [end[0]]), send_low(end[1])
+            other_sent = send_low(end[1])
+            wait = [end[0]] + (filler([end[0]]) if filler else [])
+            gathered, sent = collect(sent, wait), other_sent
             other = None if due is None else collect(sent, [gathered[0]])
             return (first, second), (done, end), (gathered, other, sent), inputs
 
+        cotangents = share(cotangent[0])
         states = [v.astype(f32) for v in share(hidden_in[0])]
-        cotangents = share(cotangent[0])
         lows = [norm_first(states[h], row(gain1, 0), row(shift1, 0))[0] for h in range(2)]
         proj_in, feed_in = [None] * layers, [None] * layers
         proj_in[0] = turned(cut_qkv(0, lows))
@@ -867,13 +879,16 @@
             else:
                 blocks = ready[1][0]
                 due = None
-            second, done, ready, inputs = block(
+            inputs = ready[:2]
+            second, done, ready, _ = block(
                 lambda h, gathered, after: feed(layer, *gathered, feed_in[layer], down_weight, after=after),
-                lambda h, sums, after: (
-                    norm(mids[h], *sums, row(gain1, layer + 1), row(shift1, layer + 1), after=after)
-                    if layer + 1 < layers
-                    else last(mids[h], *sums, after=after)
-                ),
+                (
+                    lambda h, sums, after: norm(
+                        mids[h], *sums, row(gain1, layer + 1), row(shift1, layer + 1), after=after
+                    )
+                )
+                if layer + 1 < layers
+                else None,
                 ready,
                 [blocks] + (gathering[:1] if layer + 1 == layers else []),
                 due,
@@ -887,7 +902,7 @@
             )
             if layer + 1 < layers:
                 states = [v[0] for v in done]
-        block_out = unshare([v[0] for v in done])
+        out_sums, out_mids = second, mids
 
         grads = [v.astype(f32) for v in cotangents]
         small_grads, quarters, own = [None] * layers, [None] * layers, []
@@ -907,7 +922,6 @@
                 def filler(wait):
                     return fed[layer + 1].again(wait)
 
-                starts = starts + [all_normed2[layer + 1][0]]
             first, back, ready, inputs = block(
                 lambda h, gathered, after: feed_back(
                     layer, *gathered, feed_in[layer], down_weight, saved[layer][h][7], after=after
@@ -922,7 +936,7 @@
             if layer + 1 < layers:
                 gathering.append(gather_all([v[0] for v in inputs], [quarters[layer + 1]]))
             sums2 = back[0][2] + back[1][2]
-            ahead = gathering[1:2] + [block_out] if layer > 0 else []
+            ahead = gathering[1:2] if layer > 0 else []
             if layer + 1 < layers:
 
                 def filler(wait):
@@ -964,49 +978,59 @@
         summed = [jnp.stack(small_grads)]
 
         def small_step():
-            k, last_sum = len(summed) - 1, summed[-1]
-            if k < 3:
-                arrived = swap(last_sum, 1 << k)
-            else:
-                arrived = lax.ppermute(last_sum, "rep", [(i, i ^ (1 << (k - 3))) for i in range(reps)])
-            summed.append(last_sum + arrived)
+            summed.append(summed[-1] + swap(summed[-1], 1 << (len(summed) - 1)))
             return [summed[-1]]
 
         turned1 = turn_quarters(own[1], [second[1][2]])
-        wait = fed[1].again([quarters[0], input_grad] + small_step())
-        wait = fed[1].again(wait + small_step())
-        wait = fed[1].columns(wait + small_step(), [turned1])
+        steps3 = small_step() + small_step() + small_step()
+        wait = fed[1].columns([quarters[0], input_grad] + steps3, [turned1])
+        packed1 = gather_quarters(turned1, own[1], wait)
+        fed[1].down(wait)
+        wait = [written["down"][0][1, :8, :128]]
         all_down_in[0] = with_pair(gathering[3], wait)
         fed[0] = Feed(0, all_normed2[0], all_down_in[0], 2, 2)
-        wait = fed[0].again(wait + small_step())
-        packed1 = gather_quarters(turned1, own[1], wait + own[:1])
-        wait = fed[0].again(wait + small_step())
-        turned0 = turn_quarters(own[0], wait + [fed[1].blocks[0]])
-        wait = fed[0].columns(wait, [turned0])
+        wait = fed[0].again(wait)
+        wait = fed[0].again(wait)
+        out_moving = [send_sums(out_sums[h], wait) for h in range(2)]
+        wait = fed[0].columns(wait, fed[1].blocks)
+        wait = fed[0].columns_now(wait)
+        outs = [last(out_mids[h], *out_moving[h], after=wait)[0] for h in range(2)]
+        block_out = unshare(outs)
+        turned0 = turn_quarters(own[0], wait + fed[0].blocks)
+        fed[1].write(wait)
         packed0 = gather_quarters(turned0, own[0], wait)
-        wait = fed[0].columns(wait)
-        fed[1].down(wait)
+        wait = fed[0].columns_held([turned0])
         fed[0].down(wait)
-        summed = summed[-1]
+
+        norms = summed[-1][:, : 4 * width].reshape(layers, 4, shards, rows)
+        biases = summed[-1][:, 4 * width :].reshape(layers, shards, 3 * rows)
+        mine = jnp.concatenate(
+            [
+                lax.dynamic_index_in_dim(norms, me, axis=2, keepdims=False).reshape(layers, 4 * rows),
+                lax.dynamic_index_in_dim(biases, me, axis=1, keepdims=False),
+            ],
+            axis=1,
+        )
+        mine = lax.all_gather(mine, "rep", axis=0, tiled=False)
+        mine = (mine[0] + mine[1]) + (mine[2] + mine[3])
+        fed[0].write()
         for layer, packed in ((1, packed1), (0, packed0)):
-            fed[layer].write()
             write_blocks(layer, "qkv", packed, 3 * cols, 32, 0)
             write_blocks(layer, "out", packed, cols, quarter, 0, 3)
 
-        def owned(begin, count):
-            cut = summed[:, begin : begin + count].reshape(layers, shards, count // shards)
-            return lax.dynamic_index_in_dim(cut, me, axis=1, keepdims=False)
+        def owned(k):
+            return mine[:, k * rows : (k + 1) * rows]
 
         return (
             block_out,
             input_grad,
-            owned(0, width),
-            owned(width, width),
+            owned(0),
+            owned(1),
             written["qkv"][0],
-            owned(4 * width, 3 * width),
+            mine[:, 4 * rows :],
             written["out"][0],
-            owned(2 * width, width),
-            owned(3 * width, width),
+            owned(2),
+            owned(3),
             *written["feed"],
             written["down"][0],
         )

time: 1220 us -> 1200 us (0.984)
  waiting for transfers between devices: 387 us -> 352 us
  blocking collectives: 10.3 us -> 38.5 us
  local copies, waits for them, and re-layouts: 153 us -> 138 us
    ppermute x2 -> x0, waiting for transfers between devices: 25.9 us -> none  [small_step(): lax.ppermute(last_sum, 'rep', [(i, i ^ 1 << k - 3) for i in range(reps)])]
    ppermute x139, waiting for transfers between devices: 250 us -> 231 us  [swap(): return lax.ppermute(values, 'shard', [(i, i ^ bit) for i in range(shards)])]
    unnamed x451 -> x447, local copies, waits for them, and re-layouts: 132 us -> 114 us
    all_to_all x0 -> x1, blocking collectives: none -> 15.1 us  [spread(): lax.all_to_all(blocks, 'shard', split_axis=0, concat_axis=0, tiled=False)]
    all_gather x0 -> x1, blocking collectives: none -> 13.1 us  [local(): mine = lax.all_gather(mine, 'rep', axis=0, tiled=False)]
    all_to_all x9 -> x8, waiting for transfers between devices: 101 us -> 110 us  [spread(): lax.all_to_all(blocks, 'shard', split_axis=0, concat_axis=0, tiled=False)]
    all_to_all x9 -> x8, starting transfers between devices: 39.7 us -> 36.7 us  [spread(): lax.all_to_all(blocks, 'shard', split_axis=0, concat_axis=0, tiled=False)]
  transfers between devices with their start and end apart: 158 -> 155, of which waited for: 70 -> 66; matrix products, arithmetic and copies ran while one was open for 3% -> 3% of each run, Pallas kernels for 39% -> 40%
where the time goes in v4:
time: 1200 us; the launch traced here: 1190 us
  Pallas kernels  484 us (40%)
  waiting for transfers between devices  352 us (29%)
  starting transfers between devices  154 us (13%)
  local copies, waits for them, and re-layouts  138 us (12%)
  blocking collectives  38.5 us (3%)
  between operations  16.9 us (1%)
    pallas_call x112, Pallas kernels, run(): pl.pallas_call(body, grid=grid or (), in_specs=specs, out_specs=out_specs...  484 us
    ppermute x139, waiting for transfers between devices, swap(): return lax.ppermute(values, 'shard', [(i, i ^ bit) for i in range(shards)])  231 us
    ppermute x139, starting transfers between devices, swap(): return lax.ppermute(values, 'shard', [(i, i ^ bit) for i in range(shards)])  115 us
    unnamed x447, local copies, waits for them, and re-layouts  114 us
    all_to_all x8, waiting for transfers between devices, spread(): lax.all_to_all(blocks, 'shard', split_axis=0, concat_axis=0, tiled=False)  110 us
    all_to_all x8, starting transfers between devices, spread(): lax.all_to_all(blocks, 'shard', split_axis=0, concat_axis=0, tiled=False)  36.7 us
  transfers between devices with their start and end apart: 155, of which 66 were waited for; matrix products, arithmetic and copies ran while one was open for 3% of the time, Pallas kernels for 40%

profile of v4, /device:TPU:0, one launch (start us, length us, event | category | flops | bytes accessed | tf_op | source)
XLA Modules:
  0.0 1194.6 jit_solution(14712636590593060222)
XLA Ops:
  14.1 10.3 all-gather.8
  44.3 34.3 %collective-permute-done.1.refs_1_ = bf16[64,2048]{1,0:T(8,128)(2,1)S(1)} collective-permute-done((bf16[64,2048]{1,0:T(8,128)(2,1)S(1)}, bf16[64,2048]{1,0:T(8,128)(2,1)S(1)}, u32[]{:S(2)}, u32[]{:S(2)}) %collective-permute-start.1) | collective-permute-done | bytes 262176 | tf_op jit(solution)/shard_map/ppermute | solution.py:418
  109.8 4.9 all-to-all-start.1
  123.0 8.7 shard_map.227
  134.0 8.6 shard_map.228
  146.7 34.0 %all-to-all-done.1 = bf16[8,256,1408]{2,1,0:T(8,128)(2,1)} async-done(((bf16[8,256,1408]{2,1,0:T(8,128)(2,1)}), bf16[8,256,1408]{2,1,0:T(8,128)(2,1)}, u32[]{:S(2)}, u32[]{:S(2)}) %all-to-all-start.1) | async-done | bytes 5767200 | tf_op jit(solution)/shard_map/all_to_all | solution.py:500
  190.5 4.9 collective-permute-done.10.refs_2_
  195.9 5.5 collective-permute-done.11.refs_3_
  207.3 5.4 collective-permute-done.18.refs_3_
  218.5 5.4 collective-permute-done.15.refs_2_
  267.3 4.8 all-to-all-start.2
  272.9 10.1 shard_map.237
  284.8 10.0 shard_map.238
  294.8 15.2 %all-to-all-done.2 = bf16[8,256,768]{2,1,0:T(8,128)(2,1)} async-done(((bf16[8,256,768]{2,1,0:T(8,128)(2,1)}), bf16[8,256,768]{2,1,0:T(8,128)(2,1)}, u32[]{:S(2)}, u32[]{:S(2)}) %all-to-all-start.2) | async-done | bytes 3145760 | tf_op jit(solution)/shard_map/all_to_all | solution.py:500
  323.8 5.5 collective-permute-done.27.refs_3_
  335.1 5.5 collective-permute-done.34.refs_3_
  363.9 4.8 all-to-all-start.3
  374.4 8.7 shard_map.247
  384.7 8.5 shard_map.248
  395.7 39.0 %all-to-all-done.3 = bf16[8,256,1408]{2,1,0:T(8,128)(2,1)} async-done(((bf16[8,256,1408]{2,1,0:T(8,128)(2,1)}), bf16[8,256,1408]{2,1,0:T(8,128)(2,1)}, u32[]{:S(2)}, u32[]{:S(2)}) %all-to-all-start.3) | async-done | bytes 5767200 | tf_op jit(solution)/shard_map/all_to_all | solution.py:500
  450.0 5.5 collective-permute-done.43.refs_3_
  461.3 5.5 collective-permute-done.50.refs_3_
  467.1 4.9 collective-permute-done.46.refs_1_
  472.0 4.8 collective-permute-done.47.refs_2_
  480.5 5.6 collective-permute-done.53.refs_1_
  486.1 5.2 collective-permute-done.54.refs_2_
  496.1 10.1 shard_map.260
  507.2 9.5 shard_map.262
  518.0 11.3 shard_map.264
  533.7 11.0 shard_map.266
  555.8 5.8 collective-permute-done.69.refs_3_
  567.0 5.8 collective-permute-done.77.refs_3_
  576.8 6.1 collective-permute-done.74.refs_2_
  591.0 9.8 shard_map.271
  606.4 9.7 shard_map.274
  625.7 4.9 collective-permute-done.85.refs_3_
  631.3 5.6 shard_map.279.refs_4_
  653.9 5.8 collective-permute-done.93.refs_3_
  672.9 10.8 shard_map.281
  687.9 11.5 shard_map.288
  719.1 16.2 %shard_map.291 = (bf16[4096,1408]{1,0:T(8,128)(2,1)}, bf16[4096,704]{1,0:T(8,128)(2,1)}, f32[8,128]{1,0:T(8,128)S(1)}) custom-call(bf16[2048,2048]{1,0:T(8,128)(2,1)} %shard_map.285.refs_0_, bf16[2048,2048]{1,0:T(8,128)(2,1)} %shard_map.286.refs_1_, bf16[2048,1408]{1,0:T(8,128)(2,1)} %bitcast.31.refs_2_, bf16[2,704,2048]{2,1,0:T(8,128)(2,1)} %refs_3_.27, ...), custom_call_target="tpu_custom_call" | custom-call | flops 23000000512 | bytes 1000 | tf_op jit(solution)/shard_map/pallas_call | solution.py:97
  739.6 16.3 %shard_map.293 = (bf16[4096,1408]{1,0:T(8,128)(2,1)}, bf16[4096,704]{1,0:T(8,128)(2,1)}, f32[8,128]{1,0:T(8,128)S(1)}) custom-call(bf16[2048,2048]{1,0:T(8,128)(2,1)} %shard_map.285.refs_0_, bf16[2048,2048]{1,0:T(8,128)(2,1)} %shard_map.286.refs_1_, bf16[2048,1408]{1,0:T(8,128)(2,1)} %bitcast.31.refs_2_, ...), custom_call_target="tpu_custom_call", output_to_operand_aliasing={{0}: (4, {}), {1}: (5, {})} | custom-call | flops 23000000512 | bytes 1000 | tf_op jit(solution)/shard_map/pallas_call | solution.py:97
  761.7 9.6 shard_map.295
  777.6 10.2 shard_map.298
  800.0 5.6 collective-permute-start.123
  820.7 16.3 %shard_map.301 = (bf16[4096,1408]{1,0:T(8,128)(2,1)}, bf16[4096,704]{1,0:T(8,128)(2,1)}, f32[8,128]{1,0:T(8,128)S(1)}) custom-call(bf16[2048,2048]{1,0:T(8,128)(2,1)} %collective-permute-done.99.refs_0_.refs_1_, bf16[2048,2048]{1,0:T(8,128)(2,1)} %collective-permute-done.100.refs_1_.refs_2_, ...), custom_call_target="tpu_custom_call", output_to_operand_aliasing={{0}: (4, {}), {1}: (5, {})} | custom-call | flops 23000000512 | bytes 1000 | tf_op jit(solution)/shard_map/pallas_call | solution.py:97
  840.4 5.6 shard_map.304.refs_4_
  853.1 16.0 %shard_map.303 = (bf16[4096,1408]{1,0:T(8,128)(2,1)}, bf16[4096,704]{1,0:T(8,128)(2,1)}, f32[8,128]{1,0:T(8,128)}) custom-call(bf16[2048,2048]{1,0:T(8,128)(2,1)} %collective-permute-done.99.refs_0_.refs_1_, bf16[2048,2048]{1,0:T(8,128)(2,1)} %collective-permute-done.100.refs_1_.refs_2_, ...), custom_call_target="tpu_custom_call", output_to_operand_aliasing={{0}: (4, {}), {1}: (5, {})} | custom-call | flops 23000000512 | bytes 1000 | tf_op jit(solution)/shard_map/pallas_call | solution.py:97
  875.0 33.6 %shard_map.306.refs_0_ = bf16[8,256,1408]{2,1,0:T(8,128)(2,1)} custom-call(bf16[2048,2048]{1,0:T(8,128)(2,1)} %shard_map.285.refs_0_, bf16[2048,2048]{1,0:T(8,128)(2,1)} %collective-permute-done.99.refs_0_.refs_1_, bf16[4096,1408]{1,0:T(8,128)(2,1)} %get-tuple-element.350.refs_2_, bf16[8,128]{1,0:T(8,128)(2,1)S(1)} %slice.303.refs_3_, ...), custom_call_target="tpu_custom_call" | custom-call | flops 34500001792 | bytes 1000 | tf_op jit(solution)/shard_map/pallas_call | solution.py:97
  911.7 20.6 %shard_map.309.refs_3_ = f32[2,704,2048]{2,1,0:T(8,128)} custom-call(bf16[4096,704]{1,0:T(8,128)(2,1)} %get-tuple-element.349.refs_0_, bf16[2048,2048]{1,0:T(8,128)(2,1)} %shard_map.286.refs_1_, bf16[2048,2048]{1,0:T(8,128)(2,1)} %collective-permute-done.100.refs_1_.refs_2_, bf16[8,128]{1,0:T(8,128)(2,1)S(1)} %slice.304.refs_3_.refs_2_), custom_call_target="tpu_custom_call" | custom-call | flops 23000000512 | bytes 1000 | tf_op jit(solution)/shard_map/pallas_call | solution.py:97
  937.5 5.2 all-to-all-start.5
  943.9 27.5 %shard_map.311 = (bf16[4096,1408]{1,0:T(8,128)(2,1)}, bf16[4096,704]{1,0:T(8,128)(2,1)}, f32[8,128]{1,0:T(8,128)S(1)}) custom-call(bf16[2048,2048]{1,0:T(8,128)(2,1)} %shard_map.263.refs_0_, bf16[2048,2048]{1,0:T(8,128)(2,1)} %shard_map.310.refs_1_, bf16[2048,1408]{1,0:T(8,128)(2,1)} %bitcast.20.refs_1_.refs_2_, bf16[2,704,2048]{2,1,0:T(8,128)(2,1)} %refs_3_.27, ...), custom_call_target="tpu_custom_call" | custom-call | flops 23000000512 | bytes 1000 | tf_op jit(solution)/shard_map/pallas_call | solution.py:97
  971.4 27.1 %shard_map.312 = (bf16[4096,1408]{1,0:T(8,128)(2,1)}, bf16[4096,704]{1,0:T(8,128)(2,1)}, f32[8,128]{1,0:T(8,128)S(1)}) custom-call(bf16[2048,2048]{1,0:T(8,128)(2,1)} %collective-permute-done.65.refs_0_.refs_1_, bf16[2048,2048]{1,0:T(8,128)(2,1)} %collective-permute-done.130.refs_1_.refs_2_, ...), custom_call_target="tpu_custom_call", output_to_operand_aliasing={{0}: (4, {}), {1}: (5, {})} | custom-call | flops 23000000512 | bytes 1000 | tf_op jit(solution)/shard_map/pallas_call | solution.py:97
  998.5 19.5 %shard_map.314.refs_0_ = bf16[8,128,1408]{2,1,0:T(8,128)(2,1)S(1)} custom-call(bf16[2048,2048]{1,0:T(8,128)(2,1)} %shard_map.263.refs_0_, bf16[2048,2048]{1,0:T(8,128)(2,1)} %collective-permute-done.65.refs_0_.refs_1_, bf16[4096,1408]{1,0:T(8,128)(2,1)} %get-tuple-element.381.refs_2_, f32[8,128]{1,0:T(8,128)S(1)} %get-tuple-element.376.refs_2_.refs_3_), custom_call_target="tpu_custom_call" | custom-call | flops 34500001792 | bytes 1000 | tf_op jit(solution)/shard_map/pallas_call | solution.py:97
  1024.3 20.2 %shard_map.316.refs_0_ = bf16[8,128,1408]{2,1,0:T(8,128)(2,1)S(1)} custom-call(bf16[2048,2048]{1,0:T(8,128)(2,1)} %shard_map.263.refs_0_, bf16[2048,2048]{1,0:T(8,128)(2,1)} %collective-permute-done.65.refs_0_.refs_1_, bf16[4096,1408]{1,0:T(8,128)(2,1)} %get-tuple-element.381.refs_2_, bf16[8,128]{1,0:T(8,128)(2,1)S(1)} %slice.306.refs_3_), custom_call_target="tpu_custom_call" | custom-call | flops 34500001792 | bytes 1000 | tf_op jit(solution)/shard_map/pallas_call | solution.py:97
  1046.0 12.6 %all-to-all-done.6.refs_1_ = bf16[8,128,1408]{2,1,0:T(8,128)(2,1)S(1)} async-done(((bf16[8,128,1408]{2,1,0:T(8,128)(2,1)}), bf16[8,128,1408]{2,1,0:T(8,128)(2,1)S(1)}, u32[]{:S(2)}, u32[]{:S(2)}) %all-to-all-start.6) | async-done | bytes 2883616 | tf_op jit(solution)/shard_map/all_to_all | solution.py:500
  1060.7 15.1 %all_to_all.45.refs_0_.refs_2_ = bf16[8,64,768]{2,1,0:T(8,128)(2,1)S(1)} all-to-all(bf16[8,64,768]{2,1,0:T(8,128)(2,1)S(1)} %shard_map.320), channel_id=1, replica_groups=mesh['shard'=8,'rep'=4] {'shard'}, dimensions={0} | all-to-all | bytes 1572864 | tf_op jit(solution)/shard_map/all_to_all | solution.py:500
  1092.5 13.1 %all-gather.9 = f32[4,2,1792]{2,1,0:T(2,128)S(1)} all-gather(f32[1,2,1792]{2,1,0:T(2,128)S(1)} %maximum_bitcast_fusion.2), channel_id=7, replica_groups=mesh['shard'=8,'rep'=4] {'rep'}, dimensions={0}, use_global_device_ids=true | all-gather | bytes 71680 | tf_op jit(solution)/shard_map/all_gather | solution.py:1014
  1118.6 8.8 shard_map.328
  1127.3 4.9 all-to-all-start.8
  1137.9 20.6 %shard_map.331 = f32[2,704,2048]{2,1,0:T(8,128)} custom-call(bf16[4096,704]{1,0:T(8,128)(2,1)} %get-tuple-element.393.refs_0_, bf16[2048,2048]{1,0:T(8,128)(2,1)} %shard_map.310.refs_1_, bf16[2048,2048]{1,0:T(8,128)(2,1)} %collective-permute-done.130.refs_1_.refs_2_, f32[2,704,2048]{2,1,0:T(8,128)} %shard_map.309.refs_3_, ...), custom_call_target="tpu_custom_call", output_to_operand_aliasing={{}: (3, {})} | custom-call | flops 23000000512 | bytes 1000 | tf_op jit(solution)/shard_map/pallas_call | solution.py:97
  1158.5 8.8 all-to-all-done.8
  1167.3 5.0 shard_map.330
  1172.3 7.0 all-gather.25.cloned.1.call-done
  (917 shorter events, 449.2 us)
Async XLA Ops:
  31.2 78.6 %all-to-all-start = ((bf16[8,256,768]{2,1,0:T(8,128)(2,1)}), bf16[8,256,768]{2,1,0:T(8,128)(2,1)}, u32[]{:S(2)}, u32[]{:S(2)}) async-start(bf16[8,256,768]{2,1,0:T(8,128)(2,1)} %shard_map.223), calls=%async_computation | async-start | bytes 6291456 | tf_op jit(solution)/shard_map/all_to_all | solution.py:500
  37.1 41.6 %collective-permute-start.1 = (bf16[64,2048]{1,0:T(8,128)(2,1)S(1)}, bf16[64,2048]{1,0:T(8,128)(2,1)S(1)}, u32[]{:S(2)}, u32[]{:S(2)}) collective-permute-start(bf16[64,2048]{1,0:T(8,128)(2,1)S(1)} %shard_map.220.refs_0_.refs_1_), channel_id=1, source_target_pairs={{0,8},{4,12},{8,0},{12,4},{16,24},{20,28},{24,16},{28,20},{1,9},{5... | collective-permute-start | bytes 786440 | tf_op jit(solution)/shard_map/ppermute | solution.py:418
  39.3 60.9 %collective-permute-start.2 = (bf16[64,2048]{1,0:T(8,128)(2,1)S(1)}, bf16[64,2048]{1,0:T(8,128)(2,1)}, u32[]{:S(2)}, u32[]{:S(2)}) collective-permute-start(bf16[64,2048]{1,0:T(8,128)(2,1)S(1)} %shard_map.220.refs_0_.refs_1_), channel_id=1, source_target_pairs={{0,16},{4,20},{8,24},{12,28},{16,0},{20,4},{24,8},{28,12},{1,17},{... | collective-permute-start | bytes 786440 | tf_op jit(solution)/shard_map/ppermute | solution.py:418
  40.9 59.4 %collective-permute-start.3 = (bf16[64,2048]{1,0:T(8,128)(2,1)S(1)}, bf16[64,2048]{1,0:T(8,128)(2,1)}, u32[]{:S(2)}, u32[]{:S(2)}) collective-permute-start(bf16[64,2048]{1,0:T(8,128)(2,1)S(1)} %shard_map.220.refs_0_.refs_1_), channel_id=1, source_target_pairs={{0,24},{4,28},{8,16},{12,20},{16,8},{20,12},{24,0},{28,4},{1,25},{... | collective-permute-start | bytes 786440 | tf_op jit(solution)/shard_map/ppermute | solution.py:418
  41.0 65.7 %collective-permute-start.5 = (bf16[64,2048]{1,0:T(8,128)(2,1)S(1)}, bf16[64,2048]{1,0:T(8,128)(2,1)}, u32[]{:S(2)}, u32[]{:S(2)}) collective-permute-start(bf16[64,2048]{1,0:T(8,128)(2,1)S(1)} %shard_map.221.refs_4_.refs_2_.refs_0_), channel_id=1, source_target_pairs={{0,8},{4,12},{8,0},{12,4},{16,24},{20,28},{24,16},{28,20},{1,9},{5... | collective-permute-start | bytes 786440 | tf_op jit(solution)/shard_map/ppermute | solution.py:418
  42.9 63.8 %collective-permute-start.6 = (bf16[64,2048]{1,0:T(8,128)(2,1)S(1)}, bf16[64,2048]{1,0:T(8,128)(2,1)}, u32[]{:S(2)}, u32[]{:S(2)}) collective-permute-start(bf16[64,2048]{1,0:T(8,128)(2,1)S(1)} %shard_map.221.refs_4_.refs_2_.refs_0_), channel_id=1, source_target_pairs={{0,16},{4,20},{8,24},{12,28},{16,0},{20,4},{24,8},{28,12},{1,17},{... | collective-permute-start | bytes 786440 | tf_op jit(solution)/shard_map/ppermute | solution.py:418
  78.6 28.0 %collective-permute-start.7 = (bf16[64,2048]{1,0:T(8,128)(2,1)S(1)}, bf16[64,2048]{1,0:T(8,128)(2,1)}, u32[]{:S(2)}, u32[]{:S(2)}) collective-permute-start(bf16[64,2048]{1,0:T(8,128)(2,1)S(1)} %shard_map.221.refs_4_.refs_2_.refs_0_), channel_id=1, source_target_pairs={{0,24},{4,28},{8,16},{12,20},{16,8},{20,12},{24,0},{28,4},{1,25},{... | collective-permute-start | bytes 786440 | tf_op jit(solution)/shard_map/ppermute | solution.py:418
  109.8 70.9 %all-to-all-start.1 = ((bf16[8,256,1408]{2,1,0:T(8,128)(2,1)}), bf16[8,256,1408]{2,1,0:T(8,128)(2,1)}, u32[]{:S(2)}, u32[]{:S(2)}) async-start(bf16[8,256,1408]{2,1,0:T(8,128)(2,1)} %shard_map.226), calls=%async_computation.1 | async-start | bytes 11534336 | tf_op jit(solution)/shard_map/all_to_all | solution.py:500
  114.7 380.7 %all-gather.17.cloned.1.call-start = ((), (), s32[]{:S(2)}) async-start(), calls=%async_computation.13 | async-start | bytes 10485760 | tf_op jit(solution)/shard_map/all_gather | solution.py:690
  115.5 18.5 %collective-permute-start.9 = (bf16[4,64,2048]{2,1,0:T(8,128)(2,1)}, bf16[4,64,2048]{2,1,0:T(8,128)(2,1)S(1)}, u32[]{:S(2)}, u32[]{:S(2)}) collective-permute-start(bf16[4,64,2048]{2,1,0:T(8,128)(2,1)} %copy-done.71), channel_id=1, source_target_pairs={{0,4},{4,0},{8,12},{12,8},{16,20},{20,16},{24,28},{28,24},{1,5},{5... | collective-permute-start | bytes 3145736 | tf_op jit(solution)/shard_map/ppermute | solution.py:418
  133.8 47.5 %collective-permute-start.8 = (bf16[4,64,2048]{2,1,0:T(8,128)(2,1)}, bf16[4,64,2048]{2,1,0:T(8,128)(2,1)}, u32[]{:S(2)}, u32[]{:S(2)}) collective-permute-start(bf16[4,64,2048]{2,1,0:T(8,128)(2,1)} %get-tuple-element.204), channel_id=1, source_target_pairs={{0,4},{4,0},{8,12},{12,8},{16,20},{20,16},{24,28},{28,24},{1,5},{5... | collective-permute-start | bytes 3145736 | tf_op jit(solution)/shard_map/ppermute | solution.py:418
  145.4 44.3 %collective-permute-start.13 = (bf16[4,64,2048]{2,1,0:T(8,128)(2,1)}, bf16[4,64,2048]{2,1,0:T(8,128)(2,1)S(1)}, u32[]{:S(2)}, u32[]{:S(2)}) collective-permute-start(bf16[4,64,2048]{2,1,0:T(8,128)(2,1)} %get-tuple-element.210), channel_id=1, source_target_pairs={{0,4},{4,0},{8,12},{12,8},{16,20},{20,16},{24,28},{28,24},{1,5},{5... | collective-permute-start | bytes 3145736 | tf_op jit(solution)/shard_map/ppermute | solution.py:418
  146.5 57.5 %collective-permute-start.56 = (bf16[64,2048]{1,0:T(8,128)(2,1)}, bf16[64,2048]{1,0:T(8,128)(2,1)S(1)}, u32[]{:S(2)}, u32[]{:S(2)}) collective-permute-start(bf16[64,2048]{1,0:T(8,128)(2,1)} %select_bitcast_fusion), channel_id=1, source_target_pairs={{0,4},{4,0},{8,12},{12,8},{16,20},{20,16},{24,28},{28,24},{1,5},{5... | collective-permute-start | bytes 786440 | tf_op jit(solution)/shard_map/ppermute | solution.py:418
  204.1 19.9 %collective-permute-start.15 = (bf16[64,2048]{1,0:T(8,128)(2,1)}, bf16[64,2048]{1,0:T(8,128)(2,1)S(1)}, u32[]{:S(2)}, u32[]{:S(2)}) collective-permute-start(bf16[64,2048]{1,0:T(8,128)(2,1)} %get-tuple-element.213.refs_0_), channel_id=1, source_target_pairs={{0,16},{4,20},{8,24},{12,28},{16,0},{20,4},{24,8},{28,12},{1,17},{... | collective-permute-start | bytes 786440 | tf_op jit(solution)/shard_map/ppermute | solution.py:418
  214.7 20.4 %collective-permute-start.22 = (bf16[64,2048]{1,0:T(8,128)(2,1)}, bf16[64,2048]{1,0:T(8,128)(2,1)S(1)}, u32[]{:S(2)}, u32[]{:S(2)}) collective-permute-start(bf16[64,2048]{1,0:T(8,128)(2,1)} %get-tuple-element.218.refs_0_), channel_id=1, source_target_pairs={{0,16},{4,20},{8,24},{12,28},{16,0},{20,4},{24,8},{28,12},{1,17},{... | collective-permute-start | bytes 786440 | tf_op jit(solution)/shard_map/ppermute | solution.py:418
  218.0 17.9 %collective-permute-start.23 = (bf16[64,2048]{1,0:T(8,128)(2,1)}, bf16[64,2048]{1,0:T(8,128)(2,1)}, u32[]{:S(2)}, u32[]{:S(2)}) collective-permute-start(bf16[64,2048]{1,0:T(8,128)(2,1)} %get-tuple-element.218.refs_0_), channel_id=1, source_target_pairs={{0,24},{4,28},{8,16},{12,20},{16,8},{20,12},{24,0},{28,4},{1,25},{... | collective-permute-start | bytes 786440 | tf_op jit(solution)/shard_map/ppermute | solution.py:418
  223.9 23.4 %collective-permute-start.58 = (bf16[64,2048]{1,0:T(8,128)(2,1)}, bf16[64,2048]{1,0:T(8,128)(2,1)S(1)}, u32[]{:S(2)}, u32[]{:S(2)}) collective-permute-start(bf16[64,2048]{1,0:T(8,128)(2,1)} %shard_map.255.refs_0_), channel_id=1, source_target_pairs={{0,16},{4,20},{8,24},{12,28},{16,0},{20,4},{24,8},{28,12},{1,17},{... | collective-permute-start | bytes 786440 | tf_op jit(solution)/shard_map/ppermute | solution.py:418
  235.9 20.5 %collective-permute-start.61 = (bf16[64,2048]{1,0:T(8,128)(2,1)}, bf16[64,2048]{1,0:T(8,128)(2,1)S(1)}, u32[]{:S(2)}, u32[]{:S(2)}) collective-permute-start(bf16[64,2048]{1,0:T(8,128)(2,1)} %shard_map.257.refs_0_), channel_id=1, source_target_pairs={{0,16},{4,20},{8,24},{12,28},{16,0},{20,4},{24,8},{28,12},{1,17},{... | collective-permute-start | bytes 786440 | tf_op jit(solution)/shard_map/ppermute | solution.py:418
  259.0 324.9 %all-gather.19.cloned.1.call-start = ((), (), s32[]{:S(2)}) async-start(), calls=%async_computation.14 | async-start | bytes 10485760 | tf_op jit(solution)/shard_map/all_gather | solution.py:690
  267.3 42.7 %all-to-all-start.2 = ((bf16[8,256,768]{2,1,0:T(8,128)(2,1)}), bf16[8,256,768]{2,1,0:T(8,128)(2,1)}, u32[]{:S(2)}, u32[]{:S(2)}) async-start(bf16[8,256,768]{2,1,0:T(8,128)(2,1)} %shard_map.236), calls=%async_computation.2 | async-start | bytes 6291456 | tf_op jit(solution)/shard_map/all_to_all | solution.py:500
  284.3 26.4 %collective-permute-start.24 = (bf16[4,64,2048]{2,1,0:T(8,128)(2,1)}, bf16[4,64,2048]{2,1,0:T(8,128)(2,1)}, u32[]{:S(2)}, u32[]{:S(2)}) collective-permute-start(bf16[4,64,2048]{2,1,0:T(8,128)(2,1)} %get-tuple-element.220), channel_id=1, source_target_pairs={{0,4},{4,0},{8,12},{12,8},{16,20},{20,16},{24,28},{28,24},{1,5},{5... | collective-permute-start | bytes 3145736 | tf_op jit(solution)/shard_map/ppermute | solution.py:418
  294.8 22.7 %collective-permute-start.29 = (bf16[4,64,2048]{2,1,0:T(8,128)(2,1)}, bf16[4,64,2048]{2,1,0:T(8,128)(2,1)}, u32[]{:S(2)}, u32[]{:S(2)}) collective-permute-start(bf16[4,64,2048]{2,1,0:T(8,128)(2,1)} %get-tuple-element.226), channel_id=1, source_target_pairs={{0,4},{4,0},{8,12},{12,8},{16,20},{20,16},{24,28},{28,24},{1,5},{5... | collective-permute-start | bytes 3145736 | tf_op jit(solution)/shard_map/ppermute | solution.py:418
  319.6 20.9 %collective-permute-start.34 = (bf16[64,2048]{1,0:T(8,128)(2,1)S(1)}, bf16[64,2048]{1,0:T(8,128)(2,1)S(1)}, u32[]{:S(2)}, u32[]{:S(2)}) collective-permute-start(bf16[64,2048]{1,0:T(8,128)(2,1)S(1)} %get-tuple-element.231), channel_id=1, source_target_pairs={{0,16},{4,20},{8,24},{12,28},{16,0},{20,4},{24,8},{28,12},{1,17},{... | collective-permute-start | bytes 786440 | tf_op jit(solution)/shard_map/ppermute | solution.py:418
  330.3 22.8 %collective-permute-start.31 = (bf16[64,2048]{1,0:T(8,128)(2,1)S(1)}, bf16[64,2048]{1,0:T(8,128)(2,1)S(1)}, u32[]{:S(2)}, u32[]{:S(2)}) collective-permute-start(bf16[64,2048]{1,0:T(8,128)(2,1)S(1)} %get-tuple-element.229.refs_0_), channel_id=1, source_target_pairs={{0,16},{4,20},{8,24},{12,28},{16,0},{20,4},{24,8},{28,12},{1,17},{... | collective-permute-start | bytes 786440 | tf_op jit(solution)/shard_map/ppermute | solution.py:418
  334.5 18.6 %collective-permute-start.32 = (bf16[64,2048]{1,0:T(8,128)(2,1)S(1)}, bf16[64,2048]{1,0:T(8,128)(2,1)S(1)}, u32[]{:S(2)}, u32[]{:S(2)}) collective-permute-start(bf16[64,2048]{1,0:T(8,128)(2,1)S(1)} %get-tuple-element.229.refs_0_), channel_id=1, source_target_pairs={{0,24},{4,28},{8,16},{12,20},{16,8},{20,12},{24,0},{28,4},{1,25},{... | collective-permute-start | bytes 786440 | tf_op jit(solution)/shard_map/ppermute | solution.py:418
  341.5 20.3 %collective-permute-start.38 = (bf16[64,2048]{1,0:T(8,128)(2,1)S(1)}, bf16[64,2048]{1,0:T(8,128)(2,1)S(1)}, u32[]{:S(2)}, u32[]{:S(2)}) collective-permute-start(bf16[64,2048]{1,0:T(8,128)(2,1)S(1)} %get-tuple-element.234.refs_0_), channel_id=1, source_target_pairs={{0,16},{4,20},{8,24},{12,28},{16,0},{20,4},{24,8},{28,12},{1,17},{... | collective-permute-start | bytes 786440 | tf_op jit(solution)/shard_map/ppermute | solution.py:418
  363.9 70.8 %all-to-all-start.3 = ((bf16[8,256,1408]{2,1,0:T(8,128)(2,1)}), bf16[8,256,1408]{2,1,0:T(8,128)(2,1)}, u32[]{:S(2)}, u32[]{:S(2)}) async-start(bf16[8,256,1408]{2,1,0:T(8,128)(2,1)} %shard_map.246), calls=%async_computation.3 | async-start | bytes 11534336 | tf_op jit(solution)/shard_map/all_to_all | solution.py:500
  368.7 339.3 %all-gather.23.cloned.1.call-start = ((), (), s32[]{:S(2)}) async-start(), calls=%async_computation.16 | async-start | bytes 10485760 | tf_op jit(solution)/shard_map/all_gather | solution.py:690
  384.5 50.9 %collective-permute-start.40 = (bf16[4,64,2048]{2,1,0:T(8,128)(2,1)}, bf16[4,64,2048]{2,1,0:T(8,128)(2,1)}, u32[]{:S(2)}, u32[]{:S(2)}) collective-permute-start(bf16[4,64,2048]{2,1,0:T(8,128)(2,1)} %get-tuple-element.236), channel_id=1, source_target_pairs={{0,4},{4,0},{8,12},{12,8},{16,20},{20,16},{24,28},{28,24},{1,5},{5... | collective-permute-start | bytes 3145736 | tf_op jit(solution)/shard_map/ppermute | solution.py:418
  395.3 48.4 %collective-permute-start.45 = (bf16[4,64,2048]{2,1,0:T(8,128)(2,1)}, bf16[4,64,2048]{2,1,0:T(8,128)(2,1)S(1)}, u32[]{:S(2)}, u32[]{:S(2)}) collective-permute-start(bf16[4,64,2048]{2,1,0:T(8,128)(2,1)} %get-tuple-element.242), channel_id=1, source_target_pairs={{0,4},{4,0},{8,12},{12,8},{16,20},{20,16},{24,28},{28,24},{1,5},{5... | collective-permute-start | bytes 3145736 | tf_op jit(solution)/shard_map/ppermute | solution.py:418
  444.5 22.2 %collective-permute-start.50 = (bf16[64,2048]{1,0:T(8,128)(2,1)S(1)}, bf16[64,2048]{1,0:T(8,128)(2,1)S(1)}, u32[]{:S(2)}, u32[]{:S(2)}) collective-permute-start(bf16[64,2048]{1,0:T(8,128)(2,1)S(1)} %get-tuple-element.247), channel_id=1, source_target_pairs={{0,16},{4,20},{8,24},{12,28},{16,0},{20,4},{24,8},{28,12},{1,17},{... | collective-permute-start | bytes 786440 | tf_op jit(solution)/shard_map/ppermute | solution.py:418
  457.5 19.3 %collective-permute-start.47 = (bf16[64,2048]{1,0:T(8,128)(2,1)S(1)}, bf16[64,2048]{1,0:T(8,128)(2,1)S(1)}, u32[]{:S(2)}, u32[]{:S(2)}) collective-permute-start(bf16[64,2048]{1,0:T(8,128)(2,1)S(1)} %get-tuple-element.245.refs_0_), channel_id=1, source_target_pairs={{0,16},{4,20},{8,24},{12,28},{16,0},{20,4},{24,8},{28,12},{1,17},{... | collective-permute-start | bytes 786440 | tf_op jit(solution)/shard_map/ppermute | solution.py:418
  476.9 19.2 %collective-permute-start.52 = (bf16[4,64,2048]{2,1,0:T(8,128)(2,1)S(1)}, bf16[4,64,2048]{2,1,0:T(8,128)(2,1)}, u32[]{:S(2)}, u32[]{:S(2)}) collective-permute-start(bf16[4,64,2048]{2,1,0:T(8,128)(2,1)S(1)} %shard_map.253.refs_4_.refs_0_), channel_id=1, source_target_pairs={{0,4},{4,0},{8,12},{12,8},{16,20},{20,16},{24,28},{28,24},{1,5},{5... | collective-permute-start | bytes 3145736 | tf_op jit(solution)/shard_map/ppermute | solution.py:418
  480.5 37.5 %collective-permute-start.66 = (bf16[4,64,2048]{2,1,0:T(8,128)(2,1)S(1)}, bf16[4,64,2048]{2,1,0:T(8,128)(2,1)}, u32[]{:S(2)}, u32[]{:S(2)}) collective-permute-start(bf16[4,64,2048]{2,1,0:T(8,128)(2,1)S(1)} %copy-done.23), channel_id=1, source_target_pairs={{0,4},{4,0},{8,12},{12,8},{16,20},{20,16},{24,28},{28,24},{1,5},{5... | collective-permute-start | bytes 3145736 | tf_op jit(solution)/shard_map/ppermute | solution.py:418
  495.2 314.6 %reduce-scatter.3.cloned.1.call-start = ((), (), s32[]{:S(2)}) async-start(), calls=%async_computation.11 | async-start | bytes 5242880 | tf_op jit(solution)/shard_map/reduce_scatter | solution.py:665
  550.5 22.3 %collective-permute-start.77 = (bf16[64,2048]{1,0:T(8,128)(2,1)S(1)}, bf16[64,2048]{1,0:T(8,128)(2,1)S(1)}, u32[]{:S(2)}, u32[]{:S(2)}) collective-permute-start(bf16[64,2048]{1,0:T(8,128)(2,1)S(1)} %get-tuple-element.268), channel_id=1, source_target_pairs={{0,16},{4,20},{8,24},{12,28},{16,0},{20,4},{24,8},{28,12},{1,17},{... | collective-permute-start | bytes 786440 | tf_op jit(solution)/shard_map/ppermute | solution.py:418
  554.2 18.6 %collective-permute-start.78 = (bf16[64,2048]{1,0:T(8,128)(2,1)S(1)}, bf16[64,2048]{1,0:T(8,128)(2,1)S(1)}, u32[]{:S(2)}, u32[]{:S(2)}) collective-permute-start(bf16[64,2048]{1,0:T(8,128)(2,1)S(1)} %get-tuple-element.269), channel_id=1, source_target_pairs={{0,24},{4,28},{8,16},{12,20},{16,8},{20,12},{24,0},{28,4},{1,25},{... | collective-permute-start | bytes 786440 | tf_op jit(solution)/shard_map/ppermute | solution.py:418
  562.7 20.2 %collective-permute-start.74 = (bf16[64,2048]{1,0:T(8,128)(2,1)S(1)}, bf16[64,2048]{1,0:T(8,128)(2,1)S(1)}, u32[]{:S(2)}, u32[]{:S(2)}) collective-permute-start(bf16[64,2048]{1,0:T(8,128)(2,1)S(1)} %get-tuple-element.266.refs_0_), channel_id=1, source_target_pairs={{0,16},{4,20},{8,24},{12,28},{16,0},{20,4},{24,8},{28,12},{1,17},{... | collective-permute-start | bytes 786440 | tf_op jit(solution)/shard_map/ppermute | solution.py:418
  642.6 294.8 %all-gather.21.cloned.1.call-start = ((), (), s32[]{:S(2)}) async-start(), calls=%async_computation.15 | async-start | bytes 10485760 | tf_op jit(solution)/shard_map/all_gather | solution.py:690
  704.4 111.2 %collective-permute-start.100 = (bf16[2048,2048]{1,0:T(8,128)(2,1)}, bf16[2048,2048]{1,0:T(8,128)(2,1)}, u32[]{:S(2)}, u32[]{:S(2)}) collective-permute-start(bf16[2048,2048]{1,0:T(8,128)(2,1)} %shard_map.286.refs_1_), channel_id=1, source_target_pairs={{0,4},{4,0},{8,12},{12,8},{16,20},{20,16},{24,28},{28,24},{1,5},{5... | collective-permute-start | bytes 25165832 | tf_op jit(solution)/shard_map/ppermute | solution.py:418
  708.0 110.5 %collective-permute-start.99 = (bf16[2048,2048]{1,0:T(8,128)(2,1)}, bf16[2048,2048]{1,0:T(8,128)(2,1)}, u32[]{:S(2)}, u32[]{:S(2)}) collective-permute-start(bf16[2048,2048]{1,0:T(8,128)(2,1)} %shard_map.285.refs_0_), channel_id=1, source_target_pairs={{0,4},{4,0},{8,12},{12,8},{16,20},{20,16},{24,28},{28,24},{1,5},{5... | collective-permute-start | bytes 25165832 | tf_op jit(solution)/shard_map/ppermute | solution.py:418
  711.2 24.1 %collective-permute-start.107 = (bf16[64,2048]{1,0:T(8,128)(2,1)S(1)}, bf16[64,2048]{1,0:T(8,128)(2,1)S(1)}, u32[]{:S(2)}, u32[]{:S(2)}) collective-permute-start(bf16[64,2048]{1,0:T(8,128)(2,1)S(1)} %get-tuple-element.316), channel_id=1, source_target_pairs={{0,8},{4,12},{8,0},{12,4},{16,24},{20,28},{24,16},{28,20},{1,9},{5... | collective-permute-start | bytes 786440 | tf_op jit(solution)/shard_map/ppermute | solution.py:418
  715.8 21.5 %collective-permute-start.108 = (bf16[64,2048]{1,0:T(8,128)(2,1)S(1)}, bf16[64,2048]{1,0:T(8,128)(2,1)S(1)}, u32[]{:S(2)}, u32[]{:S(2)}) collective-permute-start(bf16[64,2048]{1,0:T(8,128)(2,1)S(1)} %get-tuple-element.317), channel_id=1, source_target_pairs={{0,16},{4,20},{8,24},{12,28},{16,0},{20,4},{24,8},{28,12},{1,17},{... | collective-permute-start | bytes 786440 | tf_op jit(solution)/shard_map/ppermute | solution.py:418
  717.4 21.5 %collective-permute-start.109 = (bf16[64,2048]{1,0:T(8,128)(2,1)S(1)}, bf16[64,2048]{1,0:T(8,128)(2,1)S(1)}, u32[]{:S(2)}, u32[]{:S(2)}) collective-permute-start(bf16[64,2048]{1,0:T(8,128)(2,1)S(1)} %get-tuple-element.318), channel_id=1, source_target_pairs={{0,24},{4,28},{8,16},{12,20},{16,8},{20,12},{24,0},{28,4},{1,25},{... | collective-permute-start | bytes 786440 | tf_op jit(solution)/shard_map/ppermute | solution.py:418
  735.3 20.6 %collective-permute-start.110 = (bf16[64,2048]{1,0:T(8,128)(2,1)S(1)}, bf16[64,2048]{1,0:T(8,128)(2,1)S(1)}, u32[]{:S(2)}, u32[]{:S(2)}) collective-permute-start(bf16[64,2048]{1,0:T(8,128)(2,1)S(1)} %get-tuple-element.323.refs_0_), channel_id=1, source_target_pairs={{0,8},{4,12},{8,0},{12,4},{16,24},{20,28},{24,16},{28,20},{1,9},{5... | collective-permute-start | bytes 786440 | tf_op jit(solution)/shard_map/ppermute | solution.py:418
  737.3 18.6 %collective-permute-start.111 = (bf16[64,2048]{1,0:T(8,128)(2,1)S(1)}, bf16[64,2048]{1,0:T(8,128)(2,1)S(1)}, u32[]{:S(2)}, u32[]{:S(2)}) collective-permute-start(bf16[64,2048]{1,0:T(8,128)(2,1)S(1)} %get-tuple-element.323.refs_0_), channel_id=1, source_target_pairs={{0,16},{4,20},{8,24},{12,28},{16,0},{20,4},{24,8},{28,12},{1,17},{... | collective-permute-start | bytes 786440 | tf_op jit(solution)/shard_map/ppermute | solution.py:418
  798.7 172.7 %collective-permute-start.65 = (bf16[2048,2048]{1,0:T(8,128)(2,1)}, bf16[2048,2048]{1,0:T(8,128)(2,1)}, u32[]{:S(2)}, u32[]{:S(2)}) collective-permute-start(bf16[2048,2048]{1,0:T(8,128)(2,1)} %shard_map.263.refs_0_), channel_id=1, source_target_pairs={{0,4},{4,0},{8,12},{12,8},{16,20},{20,16},{24,28},{28,24},{1,5},{5... | collective-permute-start | bytes 25165832 | tf_op jit(solution)/shard_map/ppermute | solution.py:418
  800.0 37.1 %collective-permute-start.123 = (bf16[64,2048]{1,0:T(8,128)(2,1)}, bf16[64,2048]{1,0:T(8,128)(2,1)}, u32[]{:S(2)}, u32[]{:S(2)}) collective-permute-start(bf16[64,2048]{1,0:T(8,128)(2,1)} %get-tuple-element.344), channel_id=1, source_target_pairs={{0,8},{4,12},{8,0},{12,4},{16,24},{20,28},{24,16},{28,20},{1,9},{5... | collective-permute-start | bytes 786440 | tf_op jit(solution)/shard_map/ppermute | solution.py:418
  805.6 31.5 %collective-permute-start.124 = (bf16[64,2048]{1,0:T(8,128)(2,1)}, bf16[64,2048]{1,0:T(8,128)(2,1)}, u32[]{:S(2)}, u32[]{:S(2)}) collective-permute-start(bf16[64,2048]{1,0:T(8,128)(2,1)} %get-tuple-element.345), channel_id=1, source_target_pairs={{0,16},{4,20},{8,24},{12,28},{16,0},{20,4},{24,8},{28,12},{1,17},{... | collective-permute-start | bytes 786440 | tf_op jit(solution)/shard_map/ppermute | solution.py:418
  812.0 98.1 %all-to-all-start.4 = ((bf16[8,64,768]{2,1,0:T(8,128)(2,1)}), bf16[8,64,768]{2,1,0:T(8,128)(2,1)S(1)}, u32[]{:S(2)}, u32[]{:S(2)}) async-start(bf16[8,64,768]{2,1,0:T(8,128)(2,1)} %shard_map.307), calls=%async_computation.5 | async-start | bytes 1572864 | tf_op jit(solution)/shard_map/all_to_all | solution.py:500
  815.5 243.1 %reduce-scatter.5.cloned.1.call-start = ((), (), s32[]{:S(2)}) async-start(), calls=%async_computation.12 | async-start | bytes 5242880 | tf_op jit(solution)/shard_map/reduce_scatter | solution.py:665
  815.6 21.5 %collective-permute-start.125 = (bf16[64,2048]{1,0:T(8,128)(2,1)}, bf16[64,2048]{1,0:T(8,128)(2,1)S(1)}, u32[]{:S(2)}, u32[]{:S(2)}) collective-permute-start(bf16[64,2048]{1,0:T(8,128)(2,1)} %copy-done.175), channel_id=1, source_target_pairs={{0,24},{4,28},{8,16},{12,20},{16,8},{20,12},{24,0},{28,4},{1,25},{... | collective-permute-start | bytes 786440 | tf_op jit(solution)/shard_map/ppermute | solution.py:418
  839.9 30.6 %collective-permute-start.126 = (bf16[64,2048]{1,0:T(8,128)(2,1)}, bf16[64,2048]{1,0:T(8,128)(2,1)}, u32[]{:S(2)}, u32[]{:S(2)}) collective-permute-start(bf16[64,2048]{1,0:T(8,128)(2,1)} %broadcast_select_fusion.8), channel_id=1, source_target_pairs={{0,4},{4,0},{8,12},{12,8},{16,20},{20,16},{24,28},{28,24},{1,5},{5... | collective-permute-start | bytes 786440 | tf_op jit(solution)/shard_map/ppermute | solution.py:418
  937.4 34.0 %collective-permute-start.130 = (bf16[2048,2048]{1,0:T(8,128)(2,1)}, bf16[2048,2048]{1,0:T(8,128)(2,1)}, u32[]{:S(2)}, u32[]{:S(2)}) collective-permute-start(bf16[2048,2048]{1,0:T(8,128)(2,1)} %shard_map.310.refs_1_), channel_id=1, source_target_pairs={{0,4},{4,0},{8,12},{12,8},{16,20},{20,16},{24,28},{28,24},{1,5},{5... | collective-permute-start | bytes 25165832 | tf_op jit(solution)/shard_map/ppermute | solution.py:418
  937.5 82.1 %all-to-all-start.5 = ((bf16[8,256,1408]{2,1,0:T(8,128)(2,1)}), bf16[8,256,1408]{2,1,0:T(8,128)(2,1)}, u32[]{:S(2)}, u32[]{:S(2)}) async-start(bf16[8,256,1408]{2,1,0:T(8,128)(2,1)} %shard_map.308), calls=%async_computation.6 | async-start | bytes 11534336 | tf_op jit(solution)/shard_map/all_to_all | solution.py:500
  942.7 167.6 %all-gather.27.cloned.1.call-start = ((), (), s32[]{:S(2)}) async-start(), calls=%async_computation.18 | async-start | bytes 5242880 | tf_op jit(solution)/shard_map/all_gather | solution.py:676
  1019.5 39.1 %all-to-all-start.6 = ((bf16[8,128,1408]{2,1,0:T(8,128)(2,1)}), bf16[8,128,1408]{2,1,0:T(8,128)(2,1)S(1)}, u32[]{:S(2)}, u32[]{:S(2)}) async-start(bf16[8,128,1408]{2,1,0:T(8,128)(2,1)} %shard_map.315), calls=%async_computation.8 | async-start | bytes 5767168 | tf_op jit(solution)/shard_map/all_to_all | solution.py:500
  1023.6 155.7 %all-gather.25.cloned.1.call-start = ((), (), s32[]{:S(2)}) async-start(), calls=%async_computation.17 | async-start | bytes 5242880 | tf_op jit(solution)/shard_map/all_gather | solution.py:676
  1083.3 22.4 %collective-permute-start.132 = (bf16[64,2048]{1,0:T(8,128)(2,1)S(1)}, bf16[64,2048]{1,0:T(8,128)(2,1)S(1)}, u32[]{:S(2)}, u32[]{:S(2)}) collective-permute-start(bf16[64,2048]{1,0:T(8,128)(2,1)S(1)} %get-tuple-element.379), channel_id=1, source_target_pairs={{0,16},{4,20},{8,24},{12,28},{16,0},{20,4},{24,8},{28,12},{1,17},{... | collective-permute-start | bytes 786440 | tf_op jit(solution)/shard_map/ppermute | solution.py:418
  1083.8 21.8 %collective-permute-start.133 = (bf16[64,2048]{1,0:T(8,128)(2,1)S(1)}, bf16[64,2048]{1,0:T(8,128)(2,1)S(1)}, u32[]{:S(2)}, u32[]{:S(2)}) collective-permute-start(bf16[64,2048]{1,0:T(8,128)(2,1)S(1)} %get-tuple-element.380), channel_id=1, source_target_pairs={{0,24},{4,28},{8,16},{12,20},{16,8},{20,12},{24,0},{28,4},{1,25},{... | collective-permute-start | bytes 786440 | tf_op jit(solution)/shard_map/ppermute | solution.py:418
  1086.4 19.5 %collective-permute-start.135 = (bf16[64,2048]{1,0:T(8,128)(2,1)S(1)}, bf16[64,2048]{1,0:T(8,128)(2,1)S(1)}, u32[]{:S(2)}, u32[]{:S(2)}) collective-permute-start(bf16[64,2048]{1,0:T(8,128)(2,1)S(1)} %get-tuple-element.384), channel_id=1, source_target_pairs={{0,8},{4,12},{8,0},{12,4},{16,24},{20,28},{24,16},{28,20},{1,9},{5... | collective-permute-start | bytes 786440 | tf_op jit(solution)/shard_map/ppermute | solution.py:418
  1087.0 21.2 %collective-permute-start.136 = (bf16[64,2048]{1,0:T(8,128)(2,1)S(1)}, bf16[64,2048]{1,0:T(8,128)(2,1)S(1)}, u32[]{:S(2)}, u32[]{:S(2)}) collective-permute-start(bf16[64,2048]{1,0:T(8,128)(2,1)S(1)} %get-tuple-element.385), channel_id=1, source_target_pairs={{0,16},{4,20},{8,24},{12,28},{16,0},{20,4},{24,8},{28,12},{1,17},{... | collective-permute-start | bytes 786440 | tf_op jit(solution)/shard_map/ppermute | solution.py:418
  1109.1 23.1 %collective-permute-start.138 = (bf16[64,2048]{1,0:T(8,128)(2,1)}, bf16[64,2048]{1,0:T(8,128)(2,1)}, u32[]{:S(2)}, u32[]{:S(2)}) collective-permute-start(bf16[64,2048]{1,0:T(8,128)(2,1)} %broadcast_select_fusion.4), channel_id=1, source_target_pairs={{0,4},{4,0},{8,12},{12,8},{16,20},{20,16},{24,28},{28,24},{1,5},{5... | collective-permute-start | bytes 786440 | tf_op jit(solution)/shard_map/ppermute | solution.py:418
  1127.3 40.0 %all-to-all-start.8 = ((bf16[8,128,1408]{2,1,0:T(8,128)(2,1)}), bf16[8,128,1408]{2,1,0:T(8,128)(2,1)}, u32[]{:S(2)}, u32[]{:S(2)}) async-start(bf16[8,128,1408]{2,1,0:T(8,128)(2,1)} %shard_map.327), calls=%async_computation.10 | async-start | bytes 5767168 | tf_op jit(solution)/shard_map/all_to_all | solution.py:500
  (300 other events, 3747.9 us)
Sparse Core Ops, SparseCore 0:
  259.2 149.8 all-gather.16
  410.6 147.8 all-gather.18
  560.1 147.8 all-gather.22
  710.7 74.9 reduce-scatter.2
  787.2 150.1 all-gather.20
  940.2 74.9 reduce-scatter.4
  1016.8 81.6 all-gather.26
  1100.1 79.1 all-gather.24

commit v5 on v4

--- a/solution.py
+++ b/solution.py
@@ -130,6 +130,11 @@
     return jnp.where(inside, values, jnp.zeros_like(values))
 
 
+def widen(ref, cols):
+    values = ref[...]
+    return jnp.concatenate([values] * (cols // values.shape[1]), axis=1)
+
+
 def stack_heads(values, heads, head_size):
     return jnp.concatenate([head_lanes(values, h, head_size) for h in range(heads)], axis=0)
 
@@ -175,7 +180,7 @@
     normed = join_rows(own_ref, pair_ref)
     normed_ref[...] = normed
     joined = dot(normed, w_ref[...]) + bias_ref[...]
-    cosine, low, high = cos_ref[...], low_ref[...], high_ref[...]
+    cosine, low, high = (widen(ref, cols) for ref in (cos_ref, low_ref, high_ref))
 
     def turn(v):
         return v * cosine + pltpu.roll(v, cols - HALF, 1) * low + pltpu.roll(v, HALF, 1) * high
@@ -208,7 +213,7 @@
     branch = join_rows(own_ref, pair_ref)
     branch_ref[...] = branch
     grad_mixed = dot_t(branch, out_w_ref[0]).astype(bf16)
-    cosine, low, high = cos_ref[...], low_ref[...], high_ref[...]
+    cosine, low, high = (widen(ref, cols) for ref in (cos_ref, low_ref, high_ref))
 
     def turn_back(v):
         return v * cosine - pltpu.roll(v, cols - HALF, 1) * low - pltpu.roll(v, HALF, 1) * high
@@ -487,7 +492,7 @@
             rest = jnp.zeros((many, head_size - ROTARY), f32)
             tables.append(
                 [
-                    jnp.tile(jnp.concatenate(pieces, axis=1), (1, heads))
+                    jnp.tile(jnp.concatenate(pieces, axis=1), (1, heads // 2))
                     for pieces in (
                         (cosine, cosine, rest + 1.0),
                         (-sine, zero8, rest),
@@ -544,7 +549,7 @@
             return pl.BlockSpec((step, n), lambda i: (i, 0))
 
         mask_block = pl.BlockSpec((2, tokens, tokens), lambda i: (i, 0, 0))
-        table_blocks = [row_block(cols)] * 3
+        table_blocks = [row_block(cols // 2)] * 3
         part_shapes = [
             shape_of((chips, part, width), f32),
             shape_of((chips, part, width), bf16),

time: 1200 us -> 1190 us (level)
    unnamed x447 -> x451, local copies, waits for them, and re-layouts: 114 us -> 113 us
where the time goes in v5:
time: 1190 us
  Pallas kernels  485 us (41%)
  waiting for transfers between devices  353 us (30%)
  starting transfers between devices  151 us (13%)
  local copies, waits for them, and re-layouts  130 us (11%)
  blocking collectives  38.5 us (3%)
  between operations  17 us (1%)
    pallas_call x112, Pallas kernels, run(): pl.pallas_call(body, grid=grid or (), in_specs=specs, out_specs=out_specs...  485 us
    ppermute x139, waiting for transfers between devices, swap(): return lax.ppermute(values, 'shard', [(i, i ^ bit) for i in range(shards)])  236 us
    unnamed x451, local copies, waits for them, and re-layouts  113 us
    ppermute x139, starting transfers between devices, swap(): return lax.ppermute(values, 'shard', [(i, i ^ bit) for i in range(shards)])  112 us
    all_to_all x8, waiting for transfers between devices, spread(): lax.all_to_all(blocks, 'shard', split_axis=0, concat_axis=0, tiled=False)  109 us
    all_to_all x8, starting transfers between devices, spread(): lax.all_to_all(blocks, 'shard', split_axis=0, concat_axis=0, tiled=False)  36.7 us
  transfers between devices with their start and end apart: 155, of which 66 were waited for; matrix products, arithmetic and copies ran while one was open for 3% of the time, Pallas kernels for 40%

profile of v5, /device:TPU:0, one launch (start us, length us, event | category | flops | bytes accessed | tf_op | source)
XLA Modules:
  0.0 1185.6 jit_solution(16326332461845508790)
XLA Ops:
  14.1 10.3 all-gather.8
  46.1 34.3 %collective-permute-done.1.refs_1_ = bf16[64,2048]{1,0:T(8,128)(2,1)S(1)} collective-permute-done((bf16[64,2048]{1,0:T(8,128)(2,1)S(1)}, bf16[64,2048]{1,0:T(8,128)(2,1)S(1)}, u32[]{:S(2)}, u32[]{:S(2)}) %collective-permute-start.1) | collective-permute-done | bytes 262176 | tf_op jit(solution)/shard_map/ppermute | solution.py:423
  101.0 4.9 all-to-all-start.1
  114.8 8.6 shard_map.227
  124.4 8.6 shard_map.228
  137.1 34.7 %all-to-all-done.1 = bf16[8,256,1408]{2,1,0:T(8,128)(2,1)} async-done(((bf16[8,256,1408]{2,1,0:T(8,128)(2,1)}), bf16[8,256,1408]{2,1,0:T(8,128)(2,1)}, u32[]{:S(2)}, u32[]{:S(2)}) %all-to-all-start.1) | async-done | bytes 5767200 | tf_op jit(solution)/shard_map/all_to_all | solution.py:505
  181.7 4.9 collective-permute-done.10.refs_2_
  187.1 5.5 collective-permute-done.11.refs_3_
  198.5 5.4 collective-permute-done.18.refs_3_
  209.7 5.4 collective-permute-done.15.refs_2_
  258.4 4.8 all-to-all-start.2
  264.0 10.1 shard_map.237
  275.9 10.0 shard_map.238
  285.9 15.3 %all-to-all-done.2 = bf16[8,256,768]{2,1,0:T(8,128)(2,1)} async-done(((bf16[8,256,768]{2,1,0:T(8,128)(2,1)}), bf16[8,256,768]{2,1,0:T(8,128)(2,1)}, u32[]{:S(2)}, u32[]{:S(2)}) %all-to-all-start.2) | async-done | bytes 3145760 | tf_op jit(solution)/shard_map/all_to_all | solution.py:505
  314.9 5.5 collective-permute-done.27.refs_3_
  326.2 5.5 collective-permute-done.34.refs_3_
  348.2 4.8 collective-permute-done.38.refs_2_
  355.0 4.9 all-to-all-start.3
  367.2 8.7 shard_map.247
  376.8 8.5 shard_map.248
  388.4 37.4 %all-to-all-done.3 = bf16[8,256,1408]{2,1,0:T(8,128)(2,1)} async-done(((bf16[8,256,1408]{2,1,0:T(8,128)(2,1)}), bf16[8,256,1408]{2,1,0:T(8,128)(2,1)}, u32[]{:S(2)}, u32[]{:S(2)}) %all-to-all-start.3) | async-done | bytes 5767200 | tf_op jit(solution)/shard_map/all_to_all | solution.py:505
  441.1 5.5 collective-permute-done.43.refs_3_
  452.4 5.5 collective-permute-done.50.refs_3_
  458.2 4.9 collective-permute-done.46.refs_1_
  463.1 4.8 collective-permute-done.47.refs_2_
  471.6 5.6 collective-permute-done.53.refs_1_
  477.2 5.2 collective-permute-done.54.refs_2_
  487.2 10.1 shard_map.260
  498.3 9.5 shard_map.262
  509.1 11.3 shard_map.264
  524.8 11.0 shard_map.266
  546.8 5.8 collective-permute-done.69.refs_3_
  558.1 5.8 collective-permute-done.77.refs_3_
  567.9 6.1 collective-permute-done.74.refs_2_
  582.2 9.8 shard_map.271
  597.6 9.7 shard_map.274
  616.9 4.9 collective-permute-done.85.refs_3_
  623.1 5.6 shard_map.279.refs_4_
  645.7 5.8 collective-permute-done.93.refs_3_
  665.7 10.8 shard_map.281
  680.7 11.5 shard_map.288
  712.2 16.3 %shard_map.291 = (bf16[4096,1408]{1,0:T(8,128)(2,1)}, bf16[4096,704]{1,0:T(8,128)(2,1)}, f32[8,128]{1,0:T(8,128)S(1)}) custom-call(bf16[2048,2048]{1,0:T(8,128)(2,1)} %shard_map.285.refs_0_, bf16[2048,2048]{1,0:T(8,128)(2,1)} %shard_map.286.refs_1_, bf16[2048,1408]{1,0:T(8,128)(2,1)} %bitcast.31.refs_2_, bf16[2,704,2048]{2,1,0:T(8,128)(2,1)} %refs_3_.27, ...), custom_call_target="tpu_custom_call" | custom-call | flops 23000000512 | bytes 1000 | tf_op jit(solution)/shard_map/pallas_call | solution.py:97
  732.8 16.4 %shard_map.293 = (bf16[4096,1408]{1,0:T(8,128)(2,1)}, bf16[4096,704]{1,0:T(8,128)(2,1)}, f32[8,128]{1,0:T(8,128)S(1)}) custom-call(bf16[2048,2048]{1,0:T(8,128)(2,1)} %shard_map.285.refs_0_, bf16[2048,2048]{1,0:T(8,128)(2,1)} %shard_map.286.refs_1_, bf16[2048,1408]{1,0:T(8,128)(2,1)} %bitcast.31.refs_2_, ...), custom_call_target="tpu_custom_call", output_to_operand_aliasing={{0}: (4, {}), {1}: (5, {})} | custom-call | flops 23000000512 | bytes 1000 | tf_op jit(solution)/shard_map/pallas_call | solution.py:97
  754.9 9.4 shard_map.295
  770.7 10.2 shard_map.298
  814.0 16.4 %shard_map.301 = (bf16[4096,1408]{1,0:T(8,128)(2,1)}, bf16[4096,704]{1,0:T(8,128)(2,1)}, f32[8,128]{1,0:T(8,128)S(1)}) custom-call(bf16[2048,2048]{1,0:T(8,128)(2,1)} %collective-permute-done.99.refs_0_.refs_1_, bf16[2048,2048]{1,0:T(8,128)(2,1)} %collective-permute-done.100.refs_1_.refs_2_, ...), custom_call_target="tpu_custom_call", output_to_operand_aliasing={{0}: (4, {}), {1}: (5, {})} | custom-call | flops 23000000512 | bytes 1000 | tf_op jit(solution)/shard_map/pallas_call | solution.py:97
  833.8 5.6 shard_map.304.refs_4_
  846.4 15.9 %shard_map.303 = (bf16[4096,1408]{1,0:T(8,128)(2,1)}, bf16[4096,704]{1,0:T(8,128)(2,1)}, f32[8,128]{1,0:T(8,128)}) custom-call(bf16[2048,2048]{1,0:T(8,128)(2,1)} %collective-permute-done.99.refs_0_.refs_1_, bf16[2048,2048]{1,0:T(8,128)(2,1)} %collective-permute-done.100.refs_1_.refs_2_, ...), custom_call_target="tpu_custom_call", output_to_operand_aliasing={{0}: (4, {}), {1}: (5, {})} | custom-call | flops 23000000512 | bytes 1000 | tf_op jit(solution)/shard_map/pallas_call | solution.py:97
  868.4 33.6 %shard_map.306.refs_0_ = bf16[8,256,1408]{2,1,0:T(8,128)(2,1)} custom-call(bf16[2048,2048]{1,0:T(8,128)(2,1)} %shard_map.285.refs_0_, bf16[2048,2048]{1,0:T(8,128)(2,1)} %collective-permute-done.99.refs_0_.refs_1_, bf16[4096,1408]{1,0:T(8,128)(2,1)} %get-tuple-element.350.refs_2_, bf16[8,128]{1,0:T(8,128)(2,1)S(1)} %slice.303.refs_3_, ...), custom_call_target="tpu_custom_call" | custom-call | flops 34500001792 | bytes 1000 | tf_op jit(solution)/shard_map/pallas_call | solution.py:97
  905.0 20.5 %shard_map.309.refs_3_ = f32[2,704,2048]{2,1,0:T(8,128)} custom-call(bf16[4096,704]{1,0:T(8,128)(2,1)} %get-tuple-element.349.refs_0_, bf16[2048,2048]{1,0:T(8,128)(2,1)} %shard_map.286.refs_1_, bf16[2048,2048]{1,0:T(8,128)(2,1)} %collective-permute-done.100.refs_1_.refs_2_, bf16[8,128]{1,0:T(8,128)(2,1)S(1)} %slice.304.refs_3_.refs_2_), custom_call_target="tpu_custom_call" | custom-call | flops 23000000512 | bytes 1000 | tf_op jit(solution)/shard_map/pallas_call | solution.py:97
  928.6 5.2 all-to-all-start.5
  935.0 27.5 %shard_map.311 = (bf16[4096,1408]{1,0:T(8,128)(2,1)}, bf16[4096,704]{1,0:T(8,128)(2,1)}, f32[8,128]{1,0:T(8,128)S(1)}) custom-call(bf16[2048,2048]{1,0:T(8,128)(2,1)} %shard_map.263.refs_0_, bf16[2048,2048]{1,0:T(8,128)(2,1)} %shard_map.310.refs_1_, bf16[2048,1408]{1,0:T(8,128)(2,1)} %bitcast.20.refs_1_.refs_2_, bf16[2,704,2048]{2,1,0:T(8,128)(2,1)} %refs_3_.27, ...), custom_call_target="tpu_custom_call" | custom-call | flops 23000000512 | bytes 1000 | tf_op jit(solution)/shard_map/pallas_call | solution.py:97
  962.5 27.1 %shard_map.312 = (bf16[4096,1408]{1,0:T(8,128)(2,1)}, bf16[4096,704]{1,0:T(8,128)(2,1)}, f32[8,128]{1,0:T(8,128)S(1)}) custom-call(bf16[2048,2048]{1,0:T(8,128)(2,1)} %collective-permute-done.65.refs_0_.refs_1_, bf16[2048,2048]{1,0:T(8,128)(2,1)} %collective-permute-done.130.refs_1_.refs_2_, ...), custom_call_target="tpu_custom_call", output_to_operand_aliasing={{0}: (4, {}), {1}: (5, {})} | custom-call | flops 23000000512 | bytes 1000 | tf_op jit(solution)/shard_map/pallas_call | solution.py:97
  989.6 19.5 %shard_map.314.refs_0_ = bf16[8,128,1408]{2,1,0:T(8,128)(2,1)S(1)} custom-call(bf16[2048,2048]{1,0:T(8,128)(2,1)} %shard_map.263.refs_0_, bf16[2048,2048]{1,0:T(8,128)(2,1)} %collective-permute-done.65.refs_0_.refs_1_, bf16[4096,1408]{1,0:T(8,128)(2,1)} %get-tuple-element.381.refs_2_, f32[8,128]{1,0:T(8,128)S(1)} %get-tuple-element.376.refs_2_.refs_3_), custom_call_target="tpu_custom_call" | custom-call | flops 34500001792 | bytes 1000 | tf_op jit(solution)/shard_map/pallas_call | solution.py:97
  1015.4 20.2 %shard_map.316.refs_0_ = bf16[8,128,1408]{2,1,0:T(8,128)(2,1)S(1)} custom-call(bf16[2048,2048]{1,0:T(8,128)(2,1)} %shard_map.263.refs_0_, bf16[2048,2048]{1,0:T(8,128)(2,1)} %collective-permute-done.65.refs_0_.refs_1_, bf16[4096,1408]{1,0:T(8,128)(2,1)} %get-tuple-element.381.refs_2_, bf16[8,128]{1,0:T(8,128)(2,1)S(1)} %slice.306.refs_3_), custom_call_target="tpu_custom_call" | custom-call | flops 34500001792 | bytes 1000 | tf_op jit(solution)/shard_map/pallas_call | solution.py:97
  1037.2 12.6 %all-to-all-done.6.refs_1_ = bf16[8,128,1408]{2,1,0:T(8,128)(2,1)S(1)} async-done(((bf16[8,128,1408]{2,1,0:T(8,128)(2,1)}), bf16[8,128,1408]{2,1,0:T(8,128)(2,1)S(1)}, u32[]{:S(2)}, u32[]{:S(2)}) %all-to-all-start.6) | async-done | bytes 2883616 | tf_op jit(solution)/shard_map/all_to_all | solution.py:505
  1051.9 15.1 %all_to_all.45.refs_0_.refs_2_ = bf16[8,64,768]{2,1,0:T(8,128)(2,1)S(1)} all-to-all(bf16[8,64,768]{2,1,0:T(8,128)(2,1)S(1)} %shard_map.320), channel_id=1, replica_groups=mesh['shard'=8,'rep'=4] {'shard'}, dimensions={0} | all-to-all | bytes 1572864 | tf_op jit(solution)/shard_map/all_to_all | solution.py:505
  1083.7 13.1 %all-gather.9 = f32[4,2,1792]{2,1,0:T(2,128)S(1)} all-gather(f32[1,2,1792]{2,1,0:T(2,128)S(1)} %maximum_bitcast_fusion.2), channel_id=7, replica_groups=mesh['shard'=8,'rep'=4] {'rep'}, dimensions={0}, use_global_device_ids=true | all-gather | bytes 71680 | tf_op jit(solution)/shard_map/all_gather | solution.py:1019
  1109.7 8.7 shard_map.328
  1118.5 4.9 all-to-all-start.8
  1129.0 20.6 %shard_map.331 = f32[2,704,2048]{2,1,0:T(8,128)} custom-call(bf16[4096,704]{1,0:T(8,128)(2,1)} %get-tuple-element.393.refs_0_, bf16[2048,2048]{1,0:T(8,128)(2,1)} %shard_map.310.refs_1_, bf16[2048,2048]{1,0:T(8,128)(2,1)} %collective-permute-done.130.refs_1_.refs_2_, f32[2,704,2048]{2,1,0:T(8,128)} %shard_map.309.refs_3_, ...), custom_call_target="tpu_custom_call", output_to_operand_aliasing={{}: (3, {})} | custom-call | flops 23000000512 | bytes 1000 | tf_op jit(solution)/shard_map/pallas_call | solution.py:97
  1149.6 8.8 all-to-all-done.8
  1158.4 5.0 shard_map.330
  1163.4 6.9 all-gather.25.cloned.1.call-done
  (921 shorter events, 442.1 us)
Async XLA Ops:
  8.3 18.0 %collective-permute-start = (bf16[64,2048]{1,0:T(8,128)(2,1)S(1)}, bf16[64,2048]{1,0:T(8,128)(2,1)S(1)}, u32[]{:S(2)}, u32[]{:S(2)}) collective-permute-start(bf16[64,2048]{1,0:T(8,128)(2,1)S(1)} %select_bitcast_fusion.1), channel_id=1, source_target_pairs={{0,4},{4,0},{8,12},{12,8},{16,20},{20,16},{24,28},{28,24},{1,5},{5... | collective-permute-start | bytes 786440 | tf_op jit(solution)/shard_map/ppermute | solution.py:423
  32.9 68.0 %all-to-all-start = ((bf16[8,256,768]{2,1,0:T(8,128)(2,1)}), bf16[8,256,768]{2,1,0:T(8,128)(2,1)}, u32[]{:S(2)}, u32[]{:S(2)}) async-start(bf16[8,256,768]{2,1,0:T(8,128)(2,1)} %shard_map.223), calls=%async_computation | async-start | bytes 6291456 | tf_op jit(solution)/shard_map/all_to_all | solution.py:505
  38.8 41.6 %collective-permute-start.1 = (bf16[64,2048]{1,0:T(8,128)(2,1)S(1)}, bf16[64,2048]{1,0:T(8,128)(2,1)S(1)}, u32[]{:S(2)}, u32[]{:S(2)}) collective-permute-start(bf16[64,2048]{1,0:T(8,128)(2,1)S(1)} %shard_map.220.refs_0_.refs_1_), channel_id=1, source_target_pairs={{0,8},{4,12},{8,0},{12,4},{16,24},{20,28},{24,16},{28,20},{1,9},{5... | collective-permute-start | bytes 786440 | tf_op jit(solution)/shard_map/ppermute | solution.py:423
  41.0 53.2 %collective-permute-start.2 = (bf16[64,2048]{1,0:T(8,128)(2,1)S(1)}, bf16[64,2048]{1,0:T(8,128)(2,1)}, u32[]{:S(2)}, u32[]{:S(2)}) collective-permute-start(bf16[64,2048]{1,0:T(8,128)(2,1)S(1)} %shard_map.220.refs_0_.refs_1_), channel_id=1, source_target_pairs={{0,16},{4,20},{8,24},{12,28},{16,0},{20,4},{24,8},{28,12},{1,17},{... | collective-permute-start | bytes 786440 | tf_op jit(solution)/shard_map/ppermute | solution.py:423
  42.6 51.7 %collective-permute-start.3 = (bf16[64,2048]{1,0:T(8,128)(2,1)S(1)}, bf16[64,2048]{1,0:T(8,128)(2,1)}, u32[]{:S(2)}, u32[]{:S(2)}) collective-permute-start(bf16[64,2048]{1,0:T(8,128)(2,1)S(1)} %shard_map.220.refs_0_.refs_1_), channel_id=1, source_target_pairs={{0,24},{4,28},{8,16},{12,20},{16,8},{20,12},{24,0},{28,4},{1,25},{... | collective-permute-start | bytes 786440 | tf_op jit(solution)/shard_map/ppermute | solution.py:423
  42.7 53.8 %collective-permute-start.5 = (bf16[64,2048]{1,0:T(8,128)(2,1)S(1)}, bf16[64,2048]{1,0:T(8,128)(2,1)}, u32[]{:S(2)}, u32[]{:S(2)}) collective-permute-start(bf16[64,2048]{1,0:T(8,128)(2,1)S(1)} %shard_map.221.refs_4_.refs_2_.refs_0_), channel_id=1, source_target_pairs={{0,8},{4,12},{8,0},{12,4},{16,24},{20,28},{24,16},{28,20},{1,9},{5... | collective-permute-start | bytes 786440 | tf_op jit(solution)/shard_map/ppermute | solution.py:423
  44.6 51.9 %collective-permute-start.6 = (bf16[64,2048]{1,0:T(8,128)(2,1)S(1)}, bf16[64,2048]{1,0:T(8,128)(2,1)}, u32[]{:S(2)}, u32[]{:S(2)}) collective-permute-start(bf16[64,2048]{1,0:T(8,128)(2,1)S(1)} %shard_map.221.refs_4_.refs_2_.refs_0_), channel_id=1, source_target_pairs={{0,16},{4,20},{8,24},{12,28},{16,0},{20,4},{24,8},{28,12},{1,17},{... | collective-permute-start | bytes 786440 | tf_op jit(solution)/shard_map/ppermute | solution.py:423
  101.0 70.9 %all-to-all-start.1 = ((bf16[8,256,1408]{2,1,0:T(8,128)(2,1)}), bf16[8,256,1408]{2,1,0:T(8,128)(2,1)}, u32[]{:S(2)}, u32[]{:S(2)}) async-start(bf16[8,256,1408]{2,1,0:T(8,128)(2,1)} %shard_map.226), calls=%async_computation.1 | async-start | bytes 11534336 | tf_op jit(solution)/shard_map/all_to_all | solution.py:505
  105.8 380.7 %all-gather.17.cloned.1.call-start = ((), (), s32[]{:S(2)}) async-start(), calls=%async_computation.13 | async-start | bytes 10485760 | tf_op jit(solution)/shard_map/all_gather | solution.py:695
  124.2 48.3 %collective-permute-start.8 = (bf16[4,64,2048]{2,1,0:T(8,128)(2,1)}, bf16[4,64,2048]{2,1,0:T(8,128)(2,1)}, u32[]{:S(2)}, u32[]{:S(2)}) collective-permute-start(bf16[4,64,2048]{2,1,0:T(8,128)(2,1)} %get-tuple-element.204), channel_id=1, source_target_pairs={{0,4},{4,0},{8,12},{12,8},{16,20},{20,16},{24,28},{28,24},{1,5},{5... | collective-permute-start | bytes 3145736 | tf_op jit(solution)/shard_map/ppermute | solution.py:423
  135.9 45.0 %collective-permute-start.13 = (bf16[4,64,2048]{2,1,0:T(8,128)(2,1)}, bf16[4,64,2048]{2,1,0:T(8,128)(2,1)S(1)}, u32[]{:S(2)}, u32[]{:S(2)}) collective-permute-start(bf16[4,64,2048]{2,1,0:T(8,128)(2,1)} %get-tuple-element.210), channel_id=1, source_target_pairs={{0,4},{4,0},{8,12},{12,8},{16,20},{20,16},{24,28},{28,24},{1,5},{5... | collective-permute-start | bytes 3145736 | tf_op jit(solution)/shard_map/ppermute | solution.py:423
  136.9 58.4 %collective-permute-start.56 = (bf16[64,2048]{1,0:T(8,128)(2,1)}, bf16[64,2048]{1,0:T(8,128)(2,1)S(1)}, u32[]{:S(2)}, u32[]{:S(2)}) collective-permute-start(bf16[64,2048]{1,0:T(8,128)(2,1)} %select_bitcast_fusion), channel_id=1, source_target_pairs={{0,4},{4,0},{8,12},{12,8},{16,20},{20,16},{24,28},{28,24},{1,5},{5... | collective-permute-start | bytes 786440 | tf_op jit(solution)/shard_map/ppermute | solution.py:423
  195.2 19.9 %collective-permute-start.15 = (bf16[64,2048]{1,0:T(8,128)(2,1)}, bf16[64,2048]{1,0:T(8,128)(2,1)S(1)}, u32[]{:S(2)}, u32[]{:S(2)}) collective-permute-start(bf16[64,2048]{1,0:T(8,128)(2,1)} %get-tuple-element.213.refs_0_), channel_id=1, source_target_pairs={{0,16},{4,20},{8,24},{12,28},{16,0},{20,4},{24,8},{28,12},{1,17},{... | collective-permute-start | bytes 786440 | tf_op jit(solution)/shard_map/ppermute | solution.py:423
  205.9 20.4 %collective-permute-start.22 = (bf16[64,2048]{1,0:T(8,128)(2,1)}, bf16[64,2048]{1,0:T(8,128)(2,1)S(1)}, u32[]{:S(2)}, u32[]{:S(2)}) collective-permute-start(bf16[64,2048]{1,0:T(8,128)(2,1)} %get-tuple-element.218.refs_0_), channel_id=1, source_target_pairs={{0,16},{4,20},{8,24},{12,28},{16,0},{20,4},{24,8},{28,12},{1,17},{... | collective-permute-start | bytes 786440 | tf_op jit(solution)/shard_map/ppermute | solution.py:423
  209.1 17.9 %collective-permute-start.23 = (bf16[64,2048]{1,0:T(8,128)(2,1)}, bf16[64,2048]{1,0:T(8,128)(2,1)}, u32[]{:S(2)}, u32[]{:S(2)}) collective-permute-start(bf16[64,2048]{1,0:T(8,128)(2,1)} %get-tuple-element.218.refs_0_), channel_id=1, source_target_pairs={{0,24},{4,28},{8,16},{12,20},{16,8},{20,12},{24,0},{28,4},{1,25},{... | collective-permute-start | bytes 786440 | tf_op jit(solution)/shard_map/ppermute | solution.py:423
  215.1 23.4 %collective-permute-start.58 = (bf16[64,2048]{1,0:T(8,128)(2,1)}, bf16[64,2048]{1,0:T(8,128)(2,1)S(1)}, u32[]{:S(2)}, u32[]{:S(2)}) collective-permute-start(bf16[64,2048]{1,0:T(8,128)(2,1)} %shard_map.255.refs_0_), channel_id=1, source_target_pairs={{0,16},{4,20},{8,24},{12,28},{16,0},{20,4},{24,8},{28,12},{1,17},{... | collective-permute-start | bytes 786440 | tf_op jit(solution)/shard_map/ppermute | solution.py:423
  227.0 20.6 %collective-permute-start.61 = (bf16[64,2048]{1,0:T(8,128)(2,1)}, bf16[64,2048]{1,0:T(8,128)(2,1)S(1)}, u32[]{:S(2)}, u32[]{:S(2)}) collective-permute-start(bf16[64,2048]{1,0:T(8,128)(2,1)} %shard_map.257.refs_0_), channel_id=1, source_target_pairs={{0,16},{4,20},{8,24},{12,28},{16,0},{20,4},{24,8},{28,12},{1,17},{... | collective-permute-start | bytes 786440 | tf_op jit(solution)/shard_map/ppermute | solution.py:423
  250.2 324.9 %all-gather.19.cloned.1.call-start = ((), (), s32[]{:S(2)}) async-start(), calls=%async_computation.14 | async-start | bytes 10485760 | tf_op jit(solution)/shard_map/all_gather | solution.py:695
  258.0 17.9 %collective-permute-start.25 = (bf16[4,64,2048]{2,1,0:T(8,128)(2,1)S(1)}, bf16[4,64,2048]{2,1,0:T(8,128)(2,1)}, u32[]{:S(2)}, u32[]{:S(2)}) collective-permute-start(bf16[4,64,2048]{2,1,0:T(8,128)(2,1)S(1)} %shard_map.235.refs_2_.refs_0_.refs_4_.refs_1_), channel_id=1, source_target_pairs={{0,4},{4,0},{8,12},{12,8},{16,20},{20,16},{24,28},{28,24},{1,5},{5... | collective-permute-start | bytes 3145736 | tf_op jit(solution)/shard_map/ppermute | solution.py:423
  258.4 42.7 %all-to-all-start.2 = ((bf16[8,256,768]{2,1,0:T(8,128)(2,1)}), bf16[8,256,768]{2,1,0:T(8,128)(2,1)}, u32[]{:S(2)}, u32[]{:S(2)}) async-start(bf16[8,256,768]{2,1,0:T(8,128)(2,1)} %shard_map.236), calls=%async_computation.2 | async-start | bytes 6291456 | tf_op jit(solution)/shard_map/all_to_all | solution.py:505
  275.4 26.4 %collective-permute-start.24 = (bf16[4,64,2048]{2,1,0:T(8,128)(2,1)}, bf16[4,64,2048]{2,1,0:T(8,128)(2,1)}, u32[]{:S(2)}, u32[]{:S(2)}) collective-permute-start(bf16[4,64,2048]{2,1,0:T(8,128)(2,1)} %get-tuple-element.220), channel_id=1, source_target_pairs={{0,4},{4,0},{8,12},{12,8},{16,20},{20,16},{24,28},{28,24},{1,5},{5... | collective-permute-start | bytes 3145736 | tf_op jit(solution)/shard_map/ppermute | solution.py:423
  285.9 22.8 %collective-permute-start.29 = (bf16[4,64,2048]{2,1,0:T(8,128)(2,1)}, bf16[4,64,2048]{2,1,0:T(8,128)(2,1)}, u32[]{:S(2)}, u32[]{:S(2)}) collective-permute-start(bf16[4,64,2048]{2,1,0:T(8,128)(2,1)} %get-tuple-element.226), channel_id=1, source_target_pairs={{0,4},{4,0},{8,12},{12,8},{16,20},{20,16},{24,28},{28,24},{1,5},{5... | collective-permute-start | bytes 3145736 | tf_op jit(solution)/shard_map/ppermute | solution.py:423
  310.8 20.9 %collective-permute-start.34 = (bf16[64,2048]{1,0:T(8,128)(2,1)S(1)}, bf16[64,2048]{1,0:T(8,128)(2,1)S(1)}, u32[]{:S(2)}, u32[]{:S(2)}) collective-permute-start(bf16[64,2048]{1,0:T(8,128)(2,1)S(1)} %get-tuple-element.231), channel_id=1, source_target_pairs={{0,16},{4,20},{8,24},{12,28},{16,0},{20,4},{24,8},{28,12},{1,17},{... | collective-permute-start | bytes 786440 | tf_op jit(solution)/shard_map/ppermute | solution.py:423
  321.4 22.8 %collective-permute-start.31 = (bf16[64,2048]{1,0:T(8,128)(2,1)S(1)}, bf16[64,2048]{1,0:T(8,128)(2,1)S(1)}, u32[]{:S(2)}, u32[]{:S(2)}) collective-permute-start(bf16[64,2048]{1,0:T(8,128)(2,1)S(1)} %get-tuple-element.229.refs_0_), channel_id=1, source_target_pairs={{0,16},{4,20},{8,24},{12,28},{16,0},{20,4},{24,8},{28,12},{1,17},{... | collective-permute-start | bytes 786440 | tf_op jit(solution)/shard_map/ppermute | solution.py:423
  325.6 18.6 %collective-permute-start.32 = (bf16[64,2048]{1,0:T(8,128)(2,1)S(1)}, bf16[64,2048]{1,0:T(8,128)(2,1)S(1)}, u32[]{:S(2)}, u32[]{:S(2)}) collective-permute-start(bf16[64,2048]{1,0:T(8,128)(2,1)S(1)} %get-tuple-element.229.refs_0_), channel_id=1, source_target_pairs={{0,24},{4,28},{8,16},{12,20},{16,8},{20,12},{24,0},{28,4},{1,25},{... | collective-permute-start | bytes 786440 | tf_op jit(solution)/shard_map/ppermute | solution.py:423
  332.6 20.3 %collective-permute-start.38 = (bf16[64,2048]{1,0:T(8,128)(2,1)S(1)}, bf16[64,2048]{1,0:T(8,128)(2,1)S(1)}, u32[]{:S(2)}, u32[]{:S(2)}) collective-permute-start(bf16[64,2048]{1,0:T(8,128)(2,1)S(1)} %get-tuple-element.234.refs_0_), channel_id=1, source_target_pairs={{0,16},{4,20},{8,24},{12,28},{16,0},{20,4},{24,8},{28,12},{1,17},{... | collective-permute-start | bytes 786440 | tf_op jit(solution)/shard_map/ppermute | solution.py:423
  355.0 70.8 %all-to-all-start.3 = ((bf16[8,256,1408]{2,1,0:T(8,128)(2,1)}), bf16[8,256,1408]{2,1,0:T(8,128)(2,1)}, u32[]{:S(2)}, u32[]{:S(2)}) async-start(bf16[8,256,1408]{2,1,0:T(8,128)(2,1)} %shard_map.246), calls=%async_computation.3 | async-start | bytes 11534336 | tf_op jit(solution)/shard_map/all_to_all | solution.py:505
  359.8 340.1 %all-gather.23.cloned.1.call-start = ((), (), s32[]{:S(2)}) async-start(), calls=%async_computation.16 | async-start | bytes 10485760 | tf_op jit(solution)/shard_map/all_gather | solution.py:695
  376.6 49.9 %collective-permute-start.40 = (bf16[4,64,2048]{2,1,0:T(8,128)(2,1)}, bf16[4,64,2048]{2,1,0:T(8,128)(2,1)}, u32[]{:S(2)}, u32[]{:S(2)}) collective-permute-start(bf16[4,64,2048]{2,1,0:T(8,128)(2,1)} %get-tuple-element.236), channel_id=1, source_target_pairs={{0,4},{4,0},{8,12},{12,8},{16,20},{20,16},{24,28},{28,24},{1,5},{5... | collective-permute-start | bytes 3145736 | tf_op jit(solution)/shard_map/ppermute | solution.py:423
  388.1 46.7 %collective-permute-start.45 = (bf16[4,64,2048]{2,1,0:T(8,128)(2,1)}, bf16[4,64,2048]{2,1,0:T(8,128)(2,1)S(1)}, u32[]{:S(2)}, u32[]{:S(2)}) collective-permute-start(bf16[4,64,2048]{2,1,0:T(8,128)(2,1)} %get-tuple-element.242), channel_id=1, source_target_pairs={{0,4},{4,0},{8,12},{12,8},{16,20},{20,16},{24,28},{28,24},{1,5},{5... | collective-permute-start | bytes 3145736 | tf_op jit(solution)/shard_map/ppermute | solution.py:423
  435.6 22.2 %collective-permute-start.50 = (bf16[64,2048]{1,0:T(8,128)(2,1)S(1)}, bf16[64,2048]{1,0:T(8,128)(2,1)S(1)}, u32[]{:S(2)}, u32[]{:S(2)}) collective-permute-start(bf16[64,2048]{1,0:T(8,128)(2,1)S(1)} %get-tuple-element.247), channel_id=1, source_target_pairs={{0,16},{4,20},{8,24},{12,28},{16,0},{20,4},{24,8},{28,12},{1,17},{... | collective-permute-start | bytes 786440 | tf_op jit(solution)/shard_map/ppermute | solution.py:423
  448.6 19.3 %collective-permute-start.47 = (bf16[64,2048]{1,0:T(8,128)(2,1)S(1)}, bf16[64,2048]{1,0:T(8,128)(2,1)S(1)}, u32[]{:S(2)}, u32[]{:S(2)}) collective-permute-start(bf16[64,2048]{1,0:T(8,128)(2,1)S(1)} %get-tuple-element.245.refs_0_), channel_id=1, source_target_pairs={{0,16},{4,20},{8,24},{12,28},{16,0},{20,4},{24,8},{28,12},{1,17},{... | collective-permute-start | bytes 786440 | tf_op jit(solution)/shard_map/ppermute | solution.py:423
  468.0 19.2 %collective-permute-start.52 = (bf16[4,64,2048]{2,1,0:T(8,128)(2,1)S(1)}, bf16[4,64,2048]{2,1,0:T(8,128)(2,1)}, u32[]{:S(2)}, u32[]{:S(2)}) collective-permute-start(bf16[4,64,2048]{2,1,0:T(8,128)(2,1)S(1)} %shard_map.253.refs_4_.refs_0_), channel_id=1, source_target_pairs={{0,4},{4,0},{8,12},{12,8},{16,20},{20,16},{24,28},{28,24},{1,5},{5... | collective-permute-start | bytes 3145736 | tf_op jit(solution)/shard_map/ppermute | solution.py:423
  471.6 37.5 %collective-permute-start.66 = (bf16[4,64,2048]{2,1,0:T(8,128)(2,1)S(1)}, bf16[4,64,2048]{2,1,0:T(8,128)(2,1)}, u32[]{:S(2)}, u32[]{:S(2)}) collective-permute-start(bf16[4,64,2048]{2,1,0:T(8,128)(2,1)S(1)} %copy-done.23), channel_id=1, source_target_pairs={{0,4},{4,0},{8,12},{12,8},{16,20},{20,16},{24,28},{28,24},{1,5},{5... | collective-permute-start | bytes 3145736 | tf_op jit(solution)/shard_map/ppermute | solution.py:423
  486.3 316.9 %reduce-scatter.3.cloned.1.call-start = ((), (), s32[]{:S(2)}) async-start(), calls=%async_computation.11 | async-start | bytes 5242880 | tf_op jit(solution)/shard_map/reduce_scatter | solution.py:670
  541.6 22.3 %collective-permute-start.77 = (bf16[64,2048]{1,0:T(8,128)(2,1)S(1)}, bf16[64,2048]{1,0:T(8,128)(2,1)S(1)}, u32[]{:S(2)}, u32[]{:S(2)}) collective-permute-start(bf16[64,2048]{1,0:T(8,128)(2,1)S(1)} %get-tuple-element.268), channel_id=1, source_target_pairs={{0,16},{4,20},{8,24},{12,28},{16,0},{20,4},{24,8},{28,12},{1,17},{... | collective-permute-start | bytes 786440 | tf_op jit(solution)/shard_map/ppermute | solution.py:423
  545.3 18.6 %collective-permute-start.78 = (bf16[64,2048]{1,0:T(8,128)(2,1)S(1)}, bf16[64,2048]{1,0:T(8,128)(2,1)S(1)}, u32[]{:S(2)}, u32[]{:S(2)}) collective-permute-start(bf16[64,2048]{1,0:T(8,128)(2,1)S(1)} %get-tuple-element.269), channel_id=1, source_target_pairs={{0,24},{4,28},{8,16},{12,20},{16,8},{20,12},{24,0},{28,4},{1,25},{... | collective-permute-start | bytes 786440 | tf_op jit(solution)/shard_map/ppermute | solution.py:423
  553.8 20.2 %collective-permute-start.74 = (bf16[64,2048]{1,0:T(8,128)(2,1)S(1)}, bf16[64,2048]{1,0:T(8,128)(2,1)S(1)}, u32[]{:S(2)}, u32[]{:S(2)}) collective-permute-start(bf16[64,2048]{1,0:T(8,128)(2,1)S(1)} %get-tuple-element.266.refs_0_), channel_id=1, source_target_pairs={{0,16},{4,20},{8,24},{12,28},{16,0},{20,4},{24,8},{28,12},{1,17},{... | collective-permute-start | bytes 786440 | tf_op jit(solution)/shard_map/ppermute | solution.py:423
  634.4 294.1 %all-gather.21.cloned.1.call-start = ((), (), s32[]{:S(2)}) async-start(), calls=%async_computation.15 | async-start | bytes 10485760 | tf_op jit(solution)/shard_map/all_gather | solution.py:695
  697.1 111.8 %collective-permute-start.100 = (bf16[2048,2048]{1,0:T(8,128)(2,1)}, bf16[2048,2048]{1,0:T(8,128)(2,1)}, u32[]{:S(2)}, u32[]{:S(2)}) collective-permute-start(bf16[2048,2048]{1,0:T(8,128)(2,1)} %shard_map.286.refs_1_), channel_id=1, source_target_pairs={{0,4},{4,0},{8,12},{12,8},{16,20},{20,16},{24,28},{28,24},{1,5},{5... | collective-permute-start | bytes 25165832 | tf_op jit(solution)/shard_map/ppermute | solution.py:423
  699.9 111.8 %collective-permute-start.99 = (bf16[2048,2048]{1,0:T(8,128)(2,1)}, bf16[2048,2048]{1,0:T(8,128)(2,1)}, u32[]{:S(2)}, u32[]{:S(2)}) collective-permute-start(bf16[2048,2048]{1,0:T(8,128)(2,1)} %shard_map.285.refs_0_), channel_id=1, source_target_pairs={{0,4},{4,0},{8,12},{12,8},{16,20},{20,16},{24,28},{28,24},{1,5},{5... | collective-permute-start | bytes 25165832 | tf_op jit(solution)/shard_map/ppermute | solution.py:423
  703.5 24.9 %collective-permute-start.107 = (bf16[64,2048]{1,0:T(8,128)(2,1)S(1)}, bf16[64,2048]{1,0:T(8,128)(2,1)S(1)}, u32[]{:S(2)}, u32[]{:S(2)}) collective-permute-start(bf16[64,2048]{1,0:T(8,128)(2,1)S(1)} %get-tuple-element.316), channel_id=1, source_target_pairs={{0,8},{4,12},{8,0},{12,4},{16,24},{20,28},{24,16},{28,20},{1,9},{5... | collective-permute-start | bytes 786440 | tf_op jit(solution)/shard_map/ppermute | solution.py:423
  708.4 21.6 %collective-permute-start.108 = (bf16[64,2048]{1,0:T(8,128)(2,1)S(1)}, bf16[64,2048]{1,0:T(8,128)(2,1)S(1)}, u32[]{:S(2)}, u32[]{:S(2)}) collective-permute-start(bf16[64,2048]{1,0:T(8,128)(2,1)S(1)} %get-tuple-element.317), channel_id=1, source_target_pairs={{0,16},{4,20},{8,24},{12,28},{16,0},{20,4},{24,8},{28,12},{1,17},{... | collective-permute-start | bytes 786440 | tf_op jit(solution)/shard_map/ppermute | solution.py:423
  710.4 21.6 %collective-permute-start.109 = (bf16[64,2048]{1,0:T(8,128)(2,1)S(1)}, bf16[64,2048]{1,0:T(8,128)(2,1)S(1)}, u32[]{:S(2)}, u32[]{:S(2)}) collective-permute-start(bf16[64,2048]{1,0:T(8,128)(2,1)S(1)} %get-tuple-element.318), channel_id=1, source_target_pairs={{0,24},{4,28},{8,16},{12,20},{16,8},{20,12},{24,0},{28,4},{1,25},{... | collective-permute-start | bytes 786440 | tf_op jit(solution)/shard_map/ppermute | solution.py:423
  728.4 20.7 %collective-permute-start.110 = (bf16[64,2048]{1,0:T(8,128)(2,1)S(1)}, bf16[64,2048]{1,0:T(8,128)(2,1)S(1)}, u32[]{:S(2)}, u32[]{:S(2)}) collective-permute-start(bf16[64,2048]{1,0:T(8,128)(2,1)S(1)} %get-tuple-element.323.refs_0_), channel_id=1, source_target_pairs={{0,8},{4,12},{8,0},{12,4},{16,24},{20,28},{24,16},{28,20},{1,9},{5... | collective-permute-start | bytes 786440 | tf_op jit(solution)/shard_map/ppermute | solution.py:423
  729.9 19.2 %collective-permute-start.111 = (bf16[64,2048]{1,0:T(8,128)(2,1)S(1)}, bf16[64,2048]{1,0:T(8,128)(2,1)S(1)}, u32[]{:S(2)}, u32[]{:S(2)}) collective-permute-start(bf16[64,2048]{1,0:T(8,128)(2,1)S(1)} %get-tuple-element.323.refs_0_), channel_id=1, source_target_pairs={{0,16},{4,20},{8,24},{12,28},{16,0},{20,4},{24,8},{28,12},{1,17},{... | collective-permute-start | bytes 786440 | tf_op jit(solution)/shard_map/ppermute | solution.py:423
  791.9 170.6 %collective-permute-start.65 = (bf16[2048,2048]{1,0:T(8,128)(2,1)}, bf16[2048,2048]{1,0:T(8,128)(2,1)}, u32[]{:S(2)}, u32[]{:S(2)}) collective-permute-start(bf16[2048,2048]{1,0:T(8,128)(2,1)} %shard_map.263.refs_0_), channel_id=1, source_target_pairs={{0,4},{4,0},{8,12},{12,8},{16,20},{20,16},{24,28},{28,24},{1,5},{5... | collective-permute-start | bytes 25165832 | tf_op jit(solution)/shard_map/ppermute | solution.py:423
  796.2 34.2 %collective-permute-start.123 = (bf16[64,2048]{1,0:T(8,128)(2,1)}, bf16[64,2048]{1,0:T(8,128)(2,1)}, u32[]{:S(2)}, u32[]{:S(2)}) collective-permute-start(bf16[64,2048]{1,0:T(8,128)(2,1)} %get-tuple-element.344), channel_id=1, source_target_pairs={{0,8},{4,12},{8,0},{12,4},{16,24},{20,28},{24,16},{28,20},{1,9},{5... | collective-permute-start | bytes 786440 | tf_op jit(solution)/shard_map/ppermute | solution.py:423
  798.8 31.6 %collective-permute-start.124 = (bf16[64,2048]{1,0:T(8,128)(2,1)}, bf16[64,2048]{1,0:T(8,128)(2,1)}, u32[]{:S(2)}, u32[]{:S(2)}) collective-permute-start(bf16[64,2048]{1,0:T(8,128)(2,1)} %get-tuple-element.345), channel_id=1, source_target_pairs={{0,16},{4,20},{8,24},{12,28},{16,0},{20,4},{24,8},{28,12},{1,17},{... | collective-permute-start | bytes 786440 | tf_op jit(solution)/shard_map/ppermute | solution.py:423
  805.3 98.1 %all-to-all-start.4 = ((bf16[8,64,768]{2,1,0:T(8,128)(2,1)}), bf16[8,64,768]{2,1,0:T(8,128)(2,1)S(1)}, u32[]{:S(2)}, u32[]{:S(2)}) async-start(bf16[8,64,768]{2,1,0:T(8,128)(2,1)} %shard_map.307), calls=%async_computation.5 | async-start | bytes 1572864 | tf_op jit(solution)/shard_map/all_to_all | solution.py:505
  808.8 240.9 %reduce-scatter.5.cloned.1.call-start = ((), (), s32[]{:S(2)}) async-start(), calls=%async_computation.12 | async-start | bytes 5242880 | tf_op jit(solution)/shard_map/reduce_scatter | solution.py:670
  808.9 21.6 %collective-permute-start.125 = (bf16[64,2048]{1,0:T(8,128)(2,1)}, bf16[64,2048]{1,0:T(8,128)(2,1)S(1)}, u32[]{:S(2)}, u32[]{:S(2)}) collective-permute-start(bf16[64,2048]{1,0:T(8,128)(2,1)} %copy-done.172), channel_id=1, source_target_pairs={{0,24},{4,28},{8,16},{12,20},{16,8},{20,12},{24,0},{28,4},{1,25},{... | collective-permute-start | bytes 786440 | tf_op jit(solution)/shard_map/ppermute | solution.py:423
  833.3 30.5 %collective-permute-start.126 = (bf16[64,2048]{1,0:T(8,128)(2,1)}, bf16[64,2048]{1,0:T(8,128)(2,1)}, u32[]{:S(2)}, u32[]{:S(2)}) collective-permute-start(bf16[64,2048]{1,0:T(8,128)(2,1)} %broadcast_select_fusion.8), channel_id=1, source_target_pairs={{0,4},{4,0},{8,12},{12,8},{16,20},{20,16},{24,28},{28,24},{1,5},{5... | collective-permute-start | bytes 786440 | tf_op jit(solution)/shard_map/ppermute | solution.py:423
  928.5 34.0 %collective-permute-start.130 = (bf16[2048,2048]{1,0:T(8,128)(2,1)}, bf16[2048,2048]{1,0:T(8,128)(2,1)}, u32[]{:S(2)}, u32[]{:S(2)}) collective-permute-start(bf16[2048,2048]{1,0:T(8,128)(2,1)} %shard_map.310.refs_1_), channel_id=1, source_target_pairs={{0,4},{4,0},{8,12},{12,8},{16,20},{20,16},{24,28},{28,24},{1,5},{5... | collective-permute-start | bytes 25165832 | tf_op jit(solution)/shard_map/ppermute | solution.py:423
  928.6 82.1 %all-to-all-start.5 = ((bf16[8,256,1408]{2,1,0:T(8,128)(2,1)}), bf16[8,256,1408]{2,1,0:T(8,128)(2,1)}, u32[]{:S(2)}, u32[]{:S(2)}) async-start(bf16[8,256,1408]{2,1,0:T(8,128)(2,1)} %shard_map.308), calls=%async_computation.6 | async-start | bytes 11534336 | tf_op jit(solution)/shard_map/all_to_all | solution.py:505
  933.8 167.6 %all-gather.27.cloned.1.call-start = ((), (), s32[]{:S(2)}) async-start(), calls=%async_computation.18 | async-start | bytes 5242880 | tf_op jit(solution)/shard_map/all_gather | solution.py:681
  1010.7 39.1 %all-to-all-start.6 = ((bf16[8,128,1408]{2,1,0:T(8,128)(2,1)}), bf16[8,128,1408]{2,1,0:T(8,128)(2,1)S(1)}, u32[]{:S(2)}, u32[]{:S(2)}) async-start(bf16[8,128,1408]{2,1,0:T(8,128)(2,1)} %shard_map.315), calls=%async_computation.8 | async-start | bytes 5767168 | tf_op jit(solution)/shard_map/all_to_all | solution.py:505
  1014.7 155.6 %all-gather.25.cloned.1.call-start = ((), (), s32[]{:S(2)}) async-start(), calls=%async_computation.17 | async-start | bytes 5242880 | tf_op jit(solution)/shard_map/all_gather | solution.py:681
  1074.4 22.4 %collective-permute-start.132 = (bf16[64,2048]{1,0:T(8,128)(2,1)S(1)}, bf16[64,2048]{1,0:T(8,128)(2,1)S(1)}, u32[]{:S(2)}, u32[]{:S(2)}) collective-permute-start(bf16[64,2048]{1,0:T(8,128)(2,1)S(1)} %get-tuple-element.379), channel_id=1, source_target_pairs={{0,16},{4,20},{8,24},{12,28},{16,0},{20,4},{24,8},{28,12},{1,17},{... | collective-permute-start | bytes 786440 | tf_op jit(solution)/shard_map/ppermute | solution.py:423
  1075.0 21.8 %collective-permute-start.133 = (bf16[64,2048]{1,0:T(8,128)(2,1)S(1)}, bf16[64,2048]{1,0:T(8,128)(2,1)S(1)}, u32[]{:S(2)}, u32[]{:S(2)}) collective-permute-start(bf16[64,2048]{1,0:T(8,128)(2,1)S(1)} %get-tuple-element.380), channel_id=1, source_target_pairs={{0,24},{4,28},{8,16},{12,20},{16,8},{20,12},{24,0},{28,4},{1,25},{... | collective-permute-start | bytes 786440 | tf_op jit(solution)/shard_map/ppermute | solution.py:423
  1077.5 19.4 %collective-permute-start.135 = (bf16[64,2048]{1,0:T(8,128)(2,1)S(1)}, bf16[64,2048]{1,0:T(8,128)(2,1)S(1)}, u32[]{:S(2)}, u32[]{:S(2)}) collective-permute-start(bf16[64,2048]{1,0:T(8,128)(2,1)S(1)} %get-tuple-element.384), channel_id=1, source_target_pairs={{0,8},{4,12},{8,0},{12,4},{16,24},{20,28},{24,16},{28,20},{1,9},{5... | collective-permute-start | bytes 786440 | tf_op jit(solution)/shard_map/ppermute | solution.py:423
  1078.1 21.2 %collective-permute-start.136 = (bf16[64,2048]{1,0:T(8,128)(2,1)S(1)}, bf16[64,2048]{1,0:T(8,128)(2,1)S(1)}, u32[]{:S(2)}, u32[]{:S(2)}) collective-permute-start(bf16[64,2048]{1,0:T(8,128)(2,1)S(1)} %get-tuple-element.385), channel_id=1, source_target_pairs={{0,16},{4,20},{8,24},{12,28},{16,0},{20,4},{24,8},{28,12},{1,17},{... | collective-permute-start | bytes 786440 | tf_op jit(solution)/shard_map/ppermute | solution.py:423
  1100.3 23.1 %collective-permute-start.138 = (bf16[64,2048]{1,0:T(8,128)(2,1)}, bf16[64,2048]{1,0:T(8,128)(2,1)}, u32[]{:S(2)}, u32[]{:S(2)}) collective-permute-start(bf16[64,2048]{1,0:T(8,128)(2,1)} %broadcast_select_fusion.4), channel_id=1, source_target_pairs={{0,4},{4,0},{8,12},{12,8},{16,20},{20,16},{24,28},{28,24},{1,5},{5... | collective-permute-start | bytes 786440 | tf_op jit(solution)/shard_map/ppermute | solution.py:423
  1118.5 40.0 %all-to-all-start.8 = ((bf16[8,128,1408]{2,1,0:T(8,128)(2,1)}), bf16[8,128,1408]{2,1,0:T(8,128)(2,1)}, u32[]{:S(2)}, u32[]{:S(2)}) async-start(bf16[8,128,1408]{2,1,0:T(8,128)(2,1)} %shard_map.327), calls=%async_computation.10 | async-start | bytes 5767168 | tf_op jit(solution)/shard_map/all_to_all | solution.py:505
  (302 other events, 3747.0 us)
Sparse Core Ops, SparseCore 0:
  250.3 149.8 all-gather.16
  401.7 147.8 all-gather.18
  551.2 147.8 all-gather.22
  701.8 74.9 reduce-scatter.2
  778.4 150.1 all-gather.20
  931.3 74.9 reduce-scatter.4
  1007.9 81.5 all-gather.26
  1091.1 79.1 all-gather.24
